TPU v7x, 32 devices: a whole 2x2x4 slice. The times are simulated.
32 devices in a mesh: texel: 2 (over x), light: 4 (over z), view: 4 (over y, core).
Axes of the slice: x: 2, y: 2, z: 4, core: 2. Of those that a mesh axis runs over, the one named last changes fastest.
Arguments:
- slab: bfloat16 [80, 80, 2048], P('light', 'view', 'texel'), may hold values from -6 to 6
- basis: bfloat16 [80, 48], P('view'), may hold values from -0.625 to 0.625
Outputs:
- view_gram: float32 [80, 80], P('view')
- core: bfloat16 [48, 80, 2048], P('view', 'light', 'texel')
- light_gram: float32 [80, 80], P('light')
All inputs are finite; a program needn't handle non-finite values.
Results may differ from a plain program's by a relative error of at most 0.001.
Values may be sent and summed in bfloat16 or wider, within the bound.
No kernel may reach another device: no remote copies, remote signals or barrier semaphores. Data moves between devices by JAX's collectives and lax.ppermute only.
A program may use at most 64 MiB of HBM per device.

v0:
```python
import jax
import jax.numpy as jnp
from jax import lax
from jax.sharding import PartitionSpec as P


def row_total(partial_value):
    return lax.psum(partial_value, ("texel", "light"))


def body(slab, basis):
    lights_dev, views_dev, columns_dev = slab.shape
    ranks = basis.shape[1]
    light_count = lights_dev * lax.axis_size("light")
    columns_all = columns_dev * lax.axis_size("texel")
    view_scale = 1.0 / (light_count * columns_all)
    block = jnp.einsum(
        "lvc,lwc->vw",
        slab,
        lax.all_gather(slab, "view", axis=1, tiled=True),
        preferred_element_type=jnp.float32,
    )
    partial_value = block
    view_gram = row_total(partial_value * view_scale)
    core_sum = lax.psum_scatter(
        jnp.einsum("vr,lvc->rlc", basis, slab, preferred_element_type=jnp.float32),
        "view",
        scatter_dimension=0,
        tiled=True,
    )
    core = core_sum.astype(jnp.bfloat16)
    light_scale = 1.0 / (ranks * columns_all)
    block = jnp.einsum(
        "rlc,rmc->lm",
        core,
        lax.all_gather(core, "light", axis=1, tiled=True),
        preferred_element_type=jnp.float32,
    )
    light_gram = lax.psum(block * light_scale, ("texel", "view"))
    return (view_gram, core, light_gram)


def solution(mesh):
    return jax.shard_map(
        body,
        mesh=mesh,
        in_specs=(P("light", "view", "texel"), P("view", None)),
        out_specs=(P("view", None), P("view", "light", "texel"), P("light", None)),
        check_vma=False,
    )
```

profile of v0, /device:TPU:0, one launch (start us, length us, event | category | flops | bytes accessed | tf_op | source)
XLA Modules:
  0.0 191.5 jit_solution(5799079281131987230)
XLA Ops:
  7.2 0.0 copy-start
  7.2 0.0 reduce-scatter.2.cloned.1.call-start
  7.2 0.6 copy-done
  7.9 1.9 fusion.16
  9.8 4.4 %copy.10 = f32[48,20,1024]{2,1,0:T(8,128)} copy(f32[48,20,1024]{2,0,1:T(8,128)S(1)} %fusion.16) | data formatting | bytes 7864320 | tf_op jit(solution)/shard_map/vr,lvc->rlc/dot_general | solution.py:26
  14.2 0.0 copy-start.1
  14.2 0.0 reduce-scatter.2.cloned.1.call-update
  14.2 0.0 all-gather.3.cloned.1.call-start
  14.3 1.1 copy-done.1
  15.4 1.4 copy.8
  16.9 0.0 all-gather.3.cloned.1.call-update
  16.9 0.0 all-gather.5.cloned.1.call-start
  16.9 48.0 %reduce-scatter.2.cloned.1.call-done = f32[12,20,1024]{2,1,0:T(8,128)} async-done(((f32[48,20,1024]{2,1,0:T(8,128)}), f32[12,20,1024]{2,1,0:T(8,128)}) %reduce-scatter.2.cloned.1.call-update) | async-done | bytes 983056 | tf_op jit(solution)/shard_map/reduce_scatter | solution.py:25
  64.9 1.4 convert_element_type.3
  66.3 0.0 copy-start.2
  66.3 1.2 copy.11
  67.5 0.0 all-gather.5.cloned.1.call-update
  67.5 32.1 %all-gather.3.cloned.1.call-done = bf16[20,80,1024]{2,0,1:T(8,128)(2,1)} async-done(((bf16[20,20,1024]{2,0,1:T(8,128)(2,1)}), bf16[20,80,1024]{2,0,1:T(8,128)(2,1)}) %all-gather.3.cloned.1.call-update) | async-done | bytes 3276816 | tf_op jit(solution)/shard_map/all_gather | solution.py:20
  99.6 5.9 %fusion.10 = f32[20,80]{1,0:T(8,128)S(1)} fusion(bf16[20,20,1024]{2,1,0:T(8,128)(2,1)S(1)} %copy-done.1, bf16[20,80,1024]{2,0,1:T(8,128)(2,1)} %all-gather.3.cloned.1.call-done), kind=kOutput, calls=%fused_computation.6 | convolution fusion | flops 65537600 | bytes 4102400 | tf_op jit(solution)/shard_map/lvc,lwc->vw/dot_general | solution.py:17
  105.5 38.6 %psum.14 = f32[20,80]{1,0:T(8,128)} all-reduce(f32[20,80]{1,0:T(8,128)S(1)} %fusion.10), channel_id=1, replica_groups=mesh['texel'=2,'light'=4,'view'=4] {'texel','light'}, use_global_device_ids=true, to_apply=%region_0.0 | all-reduce | flops 1600 | bytes 12800 | tf_op jit(solution)/shard_map/psum | solution.py:8
  144.1 12.9 %all-gather.5.cloned.1.call-done = bf16[12,80,1024]{2,0,1:T(8,128)(2,1)} async-done(((bf16[12,20,1024]{2,0,1:T(8,128)(2,1)}), bf16[12,80,1024]{2,0,1:T(8,128)(2,1)}) %all-gather.5.cloned.1.call-update) | async-done | bytes 1966096 | tf_op jit(solution)/shard_map/all_gather | solution.py:36
  157.0 4.0 %fusion.13 = f32[20,80]{1,0:T(8,128)S(1)} fusion(bf16[12,20,1024]{2,1,0:T(8,128)(2,1)S(1)} %convert_element_type.3, bf16[12,80,1024]{2,0,1:T(8,128)(2,1)} %all-gather.5.cloned.1.call-done), kind=kOutput, calls=%fused_computation.7 | convolution fusion | flops 39323200 | bytes 2464000 | tf_op jit(solution)/shard_map/rlc,rmc->lm/dot_general | solution.py:33
  161.1 0.0 copy-done.2
  161.1 23.9 %psum.15 = f32[20,80]{1,0:T(8,128)} all-reduce(f32[20,80]{1,0:T(8,128)S(1)} %fusion.13), channel_id=1, replica_groups=mesh['texel'=2,'light'=4,'view'=4] {'texel','view'}, use_global_device_ids=true, to_apply=%region_2.0 | all-reduce | flops 1600 | bytes 12800 | tf_op jit(solution)/shard_map/psum | solution.py:39
Async XLA Ops:
  7.2 0.7 copy-start
  7.2 57.7 %reduce-scatter.2.cloned.1.call-start = ((), (), s32[]{:S(2)}) async-start(), calls=%async_computation.2 | async-start | bytes 5898240 | tf_op jit(solution)/shard_map/reduce_scatter | solution.py:25
  14.2 1.2 copy-start.1
  14.2 85.4 %all-gather.3.cloned.1.call-start = ((), (), s32[]{:S(2)}) async-start(), calls=%async_computation.1 | async-start | bytes 4915200 | tf_op jit(solution)/shard_map/all_gather | solution.py:20
  16.9 140.2 %all-gather.5.cloned.1.call-start = ((), (), s32[]{:S(2)}) async-start(), calls=%async_computation.3 | async-start | bytes 3276800 | tf_op jit(solution)/shard_map/all_gather | solution.py:36
  66.3 94.8 %copy-start.2 = (bf16[12,20,1024]{2,1,0:T(8,128)(2,1)}, bf16[12,20,1024]{2,1,0:T(8,128)(2,1)S(1)}, u32[]{:S(2)}) copy-start(bf16[12,20,1024]{2,1,0:T(8,128)(2,1)S(1)} %convert_element_type.3) | copy-start | bytes 1474564
Sparse Core Ops, SparseCore 0:
  14.4 50.5 reduce-scatter.1
  66.6 33.0 all-gather.2
  101.3 55.7 all-gather.4
where the time goes:
time: 192 us; the launch traced here: 191 us
  waiting for transfers between devices  93.1 us (48%)
  blocking collectives  62.5 us (33%)
  between operations  13.8 us (7%)
  matrix products  11.8 us (6%)
  local copies, waits for them, and re-layouts  8.85 us (5%)
    reduce_scatter x1, waiting for transfers between devices, body(): lax.psum_scatter(jnp.einsum('vr,lvc->rlc', basis, slab, preferred_element...  48 us
    psum x1, blocking collectives, row_total(): return lax.psum(partial_value, ('texel', 'light'))  38.6 us
    all_gather x1, waiting for transfers between devices, body(): lax.all_gather(slab, 'view', axis=1, tiled=True)  32.1 us
    psum x1, blocking collectives, body(): light_gram = lax.psum(block * light_scale, ('texel', 'view'))  23.9 us
    all_gather x1, waiting for transfers between devices, body(): lax.all_gather(core, 'light', axis=1, tiled=True)  12.9 us
    dot_general x1, matrix products, body(): jnp.einsum('lvc,lwc->vw', slab, lax.all_gather(slab, 'view', axis=1, tile...  5.85 us
    dot_general x1, local copies, waits for them, and re-layouts, body(): jnp.einsum('vr,lvc->rlc', basis, slab, preferred_element_type=jnp.float32)  4.43 us
    dot_general x1, matrix products, body(): jnp.einsum('rlc,rmc->lm', core, lax.all_gather(core, 'light', axis=1, til...  4.03 us
  transfers between devices with their start and end apart: 3, of which 3 were waited for; matrix products, arithmetic and copies ran while one was open for 5% of the time, Pallas kernels for 0%

commit v1 on v0

v1 whole, which is shorter than its diff:
```python
import functools

import jax
import jax.numpy as jnp
from jax import lax
from jax.experimental import pallas as pl
from jax.experimental.pallas import tpu as pltpu
from jax.sharding import PartitionSpec as P

VMEM = pl.BlockSpec(memory_space=pltpu.VMEM)
PARAMS = pltpu.CompilerParams(vmem_limit_bytes=32 * 1024 * 1024)
sds = jax.ShapeDtypeStruct


def swap(value, axis, step):
    return lax.ppermute(value, axis, [(i, i ^ step) for i in range(lax.axis_size(axis))])


def swaps(values, axis):
    moved = {k: swap(values[k], axis, k) for k in range(len(values) - 1, 0, -1)}
    return [values[0]] + [moved[k] for k in range(1, len(values))]


def doubled(value, axis):
    step = 1
    while step < lax.axis_size(axis):
        value = value + swap(value, axis, step)
        step *= 2
    return value


def call(kernel, out_shape, scratch, flops, *args):
    moved = sum(a.size * a.dtype.itemsize for a in list(args) + jax.tree.leaves(out_shape))
    return pl.pallas_call(
        kernel,
        out_shape=out_shape,
        in_specs=[VMEM] * len(args),
        out_specs=jax.tree.map(lambda _: VMEM, out_shape),
        scratch_shapes=scratch,
        compiler_params=PARAMS,
        cost_estimate=pl.CostEstimate(flops=flops, bytes_accessed=moved, transcendentals=0),
    )(*args)


def nt(a, b):
    return lax.dot_general(a, b, (((1,), (1,)), ((), ())), preferred_element_type=jnp.float32)


def pack_kernel(slab_ref, basis_ref, *outs):
    me = lax.axis_index("view")
    lights, rows, columns = slab_ref.shape
    ranks = basis_ref.shape[1]
    width = columns // len(outs)
    rest = outs[0].shape[0] - (lights + 1) * rows
    basis = jnp.pad(basis_ref[...], ((0, rest), (0, width - ranks)))
    for k in range(len(outs)):
        at = pl.ds(pl.multiple_of((me ^ k) * width, width), width)
        outs[k][...] = jnp.concatenate([slab_ref[l, :, at] for l in range(lights)] + [basis], axis=0)


def core_kernel(lights, rows, ranks, views, parts, scale, *refs):
    ins, refs = refs[:views], refs[views:]
    light_outs, refs = refs[:parts], refs[parts:]
    view_outs, refs = refs[:views], refs[views:]
    gram_outs, refs = refs[:views], refs[views:]
    whole, turned, pieces, grams = refs
    v, z = lax.axis_index("view"), lax.axis_index("light")
    width = whole.shape[2]
    for k in range(views):
        whole[v ^ k] = ins[k][...]
    body = lights * rows
    basis = jnp.concatenate([whole[k, body : body + rows, :128] for k in range(views)], axis=0)
    basis = basis.astype(jnp.float32).T[:ranks].astype(jnp.bfloat16)
    gram = jnp.zeros((views * rows, views * rows), jnp.float32)
    for l in range(lights):
        page = jnp.concatenate([whole[k, l * rows : (l + 1) * rows, :] for k in range(views)], axis=0)
        product = jnp.dot(basis, page, preferred_element_type=jnp.float32)
        for h in range(width // 128):
            turned[h, l * ranks : (l + 1) * ranks, :] = product[:, h * 128 : (h + 1) * 128]
        gram += nt(page, page)
    gram *= scale
    size = ranks // parts
    for j in range(parts):
        for h in range(width // 128):
            picked = [turned[h, pl.ds(j * size + r, lights, stride=ranks), :] for r in range(size)]
            pieces[j, :, h * 128 : (h + 1) * 128] = jnp.concatenate(picked, axis=0).astype(jnp.bfloat16)
    for k in range(parts):
        light_outs[k][...] = pieces[z ^ k]
    for k in range(views):
        grams[k] = gram[k * rows : (k + 1) * rows]
    for k in range(views):
        view_outs[k][...] = pieces[v ^ k]
        gram_outs[k][...] = grams[v ^ k]


def light_kernel(lights, parts, scale, *refs):
    ins, refs = refs[:parts], refs[parts:]
    extra, outs, whole, grams = refs[0], refs[1 : parts + 1], refs[-2], refs[-1]
    z = lax.axis_index("light")
    for k in range(parts):
        whole[z ^ k] = ins[k][...]
    gram = jnp.zeros((parts * lights, parts * lights), jnp.float32)
    for r in range(whole.shape[1] // lights):
        page = jnp.concatenate([whole[k, r * lights : (r + 1) * lights, :] for k in range(parts)], axis=0)
        gram += nt(page, page)
    gram *= scale
    for k in range(parts):
        grams[k] = gram[k * lights : (k + 1) * lights]
    for k in range(parts):
        outs[k][...] = jnp.concatenate([grams[z ^ k], extra[...]], axis=0)


def place_kernel(lights, *refs):
    ins, core_ref = refs[:-1], refs[-1]
    v = lax.axis_index("view")
    width = ins[0].shape[1]
    for k in range(len(ins)):
        at = pl.ds(pl.multiple_of((v ^ k) * width, width), width)
        for r in range(core_ref.shape[0]):
            core_ref[r, :, at] = ins[k][r * lights : (r + 1) * lights, :]


def body(slab, basis):
    views, parts = lax.axis_size("view"), lax.axis_size("light")
    lights, rows, columns = slab.shape
    ranks = basis.shape[1]
    columns_all = columns * lax.axis_size("texel")
    view_scale = 1.0 / (lights * parts * columns_all)
    light_scale = 1.0 / (ranks * columns_all)
    width = columns // views
    packed_rows = -(-(lights + 1) * rows // 16) * 16
    views_all, lights_all = views * rows, parts * lights
    piece = ranks // parts * lights
    bf16, f32 = jnp.bfloat16, jnp.float32

    packed = call(pack_kernel, [sds((packed_rows, width), bf16)] * views, [], 0, slab, basis)
    whole = swaps(packed, "view")
    made = call(
        functools.partial(core_kernel, lights, rows, ranks, views, parts, view_scale),
        [sds((piece, width), bf16)] * (parts + views) + [sds((rows, views_all), f32)] * views,
        [
            pltpu.VMEM((views, packed_rows, width), bf16),
            pltpu.VMEM((width // 128, lights * ranks, 128), f32),
            pltpu.VMEM((parts, piece, width), bf16),
            pltpu.VMEM((views, rows, views_all), f32),
        ],
        2 * views_all * lights * width * (views_all + ranks),
        *whole,
    )
    lit = swaps(made[:parts], "light")
    view_gram = sum(swaps(made[parts + views :], "view"))
    view_gram = doubled(view_gram, "texel")
    core_parts = swaps(made[parts : parts + views], "view")
    sums = call(
        functools.partial(light_kernel, lights, parts, light_scale),
        [sds((lights + rows, lights_all), f32)] * parts,
        [pltpu.VMEM((parts, piece, width), bf16), pltpu.VMEM((parts, lights, lights_all), f32)],
        2 * lights_all * lights_all * ranks // parts * width,
        *lit,
        view_gram,
    )
    total = sum(swaps(sums, "light"))
    view_gram = total[lights:]
    light_gram = sum(swaps([total[:lights]] * views, "view"))
    light_gram = doubled(light_gram, "texel")
    core = call(
        functools.partial(place_kernel, lights), sds((ranks // views, lights, columns), bf16), [], 0, *core_parts
    )
    return (view_gram, core, light_gram)


def solution(mesh):
    return jax.shard_map(
        body,
        mesh=mesh,
        in_specs=(P("light", "view", "texel"), P("view", None)),
        out_specs=(P("view", None), P("view", "light", "texel"), P("light", None)),
        check_vma=False,
    )
```

time: 192 us -> 54.7 us (0.28)
  waiting for transfers between devices: 93.1 us -> 26.6 us
  blocking collectives: 62.5 us -> 0 us
  starting transfers between devices: 0.12 us -> 21.7 us
  between operations: 13.8 us -> 0.69 us
  matrix products: 11.8 us -> 0 us
  local copies, waits for them, and re-layouts: 8.85 us -> 1.89 us
  Pallas kernels: 0 us -> 2.38 us
    psum x2 -> x0, blocking collectives: 62.5 us -> none  [the longest x1 38.6 us: row_total(): return lax.psum(partial_value, ('texel', 'light'))]
    reduce_scatter x1 -> x0, waiting for transfers between devices: 48 us -> none  [body(): lax.psum_scatter(jnp.einsum('vr,lvc->rlc', basis, slab, preferred_element...]
    all_gather x2 -> x0, waiting for transfers between devices: 45 us -> none  [the longest x1 32.1 us: body(): lax.all_gather(slab, 'view', axis=1, tiled=True)]
    ppermute x0 -> x20, waiting for transfers between devices: none -> 26.6 us  [swap(): lax.ppermute(value, axis, [(i, i ^ step) for i in range(lax.axis_size(axi...]
    ppermute x0 -> x20, starting transfers between devices: none -> 21.7 us  [swap(): lax.ppermute(value, axis, [(i, i ^ step) for i in range(lax.axis_size(axi...]
    dot_general x3 -> x0, matrix products: 11.8 us -> none  [the longest x1 5.85 us: body(): jnp.einsum('lvc,lwc->vw', slab, lax.all_gather(slab, 'view', axis=1, tile...]
    dot_general x1 -> x0, local copies, waits for them, and re-layouts: 4.43 us -> none  [body(): jnp.einsum('vr,lvc->rlc', basis, slab, preferred_element_type=jnp.float32)]
    pallas_call x0 -> x4, Pallas kernels: none -> 2.38 us  [call(): pl.pallas_call(kernel, out_shape=out_shape, in_specs=[VMEM] * len(args),...]
  transfers between devices with their start and end apart: 3 -> 20, of which waited for: 3 -> 9; matrix products, arithmetic and copies ran while one was open for 5% -> 1% of each run, Pallas kernels for 0% -> 2%
where the time goes in v1:
time: 54.7 us; the launch traced here: 54.5 us
  waiting for transfers between devices  26.6 us (49%)
  starting transfers between devices  21.7 us (40%)
  Pallas kernels  2.38 us (4%)
  local copies, waits for them, and re-layouts  1.89 us (3%)
  other arithmetic  1.23 us (2%)
  between operations  0.69 us (1%)
    ppermute x20, waiting for transfers between devices, swap(): lax.ppermute(value, axis, [(i, i ^ step) for i in range(lax.axis_size(axi...  26.6 us
    ppermute x20, starting transfers between devices, swap(): lax.ppermute(value, axis, [(i, i ^ step) for i in range(lax.axis_size(axi...  21.7 us
    pallas_call x4, Pallas kernels, call(): pl.pallas_call(kernel, out_shape=out_shape, in_specs=[VMEM] * len(args),...  2.38 us
    unnamed x4, local copies, waits for them, and re-layouts  1.89 us
  transfers between devices with their start and end apart: 20, of which 9 were waited for; matrix products, arithmetic and copies ran while one was open for 1% of the time, Pallas kernels for 2%

profile of v1, /device:TPU:0, one launch (start us, length us, event | category | flops | bytes accessed | tf_op | source)
XLA Modules:
  0.0 54.5 jit_solution(11797588404330312845)
XLA Ops:
  0.6 0.0 copy-start
  0.6 1.2 %copy-done = bf16[20,20,1024]{2,1,0:T(8,128)(2,1)S(1)} copy-done((bf16[20,20,1024]{2,1,0:T(8,128)(2,1)S(1)}, bf16[20,20,1024]{2,1,0:T(8,128)(2,1)}, u32[]{:S(2)}) %copy-start) | copy-done | bytes 819224
  1.8 0.0 copy-start.1
  1.8 0.7 %copy-done.1 = bf16[20,48]{1,0:T(8,128)(2,1)S(1)} copy-done((bf16[20,48]{1,0:T(8,128)(2,1)S(1)}, bf16[20,48]{1,0:T(8,128)(2,1)}, u32[]{:S(2)}) %copy-start.1) | copy-done | bytes 1944
  2.5 0.1 shard_map.49
  2.7 0.5 collective-permute-start
  3.2 2.6 %collective-permute-start.1 = (bf16[432,256]{1,0:T(8,128)(2,1)S(1)}, bf16[432,256]{1,0:T(8,128)(2,1)S(1)}, u32[]{:S(2)}, u32[]{:S(2)}) collective-permute-start(bf16[432,256]{1,0:T(8,128)(2,1)S(1)} %get-tuple-element.25), channel_id=1, source_target_pairs={{0,2},{1,3},{2,0},{3,1},{4,6},{5,7},{6,4},{7,5},{8,10},{9,11},{10,... | collective-permute-start | bytes 663560 | tf_op jit(solution)/shard_map/ppermute | solution.py:16
  5.8 0.1 collective-permute-start.2
  5.9 0.0 collective-permute-done.refs_1_
  5.9 6.2 %collective-permute-done.1.refs_2_ = bf16[432,256]{1,0:T(8,128)(2,1)S(1)} collective-permute-done((bf16[432,256]{1,0:T(8,128)(2,1)S(1)}, bf16[432,256]{1,0:T(8,128)(2,1)S(1)}, u32[]{:S(2)}, u32[]{:S(2)}) %collective-permute-start.1) | collective-permute-done | bytes 221216 | tf_op jit(solution)/shard_map/ppermute | solution.py:16
  12.1 4.2 %collective-permute-done.2.refs_3_ = bf16[432,256]{1,0:T(8,128)(2,1)S(1)} collective-permute-done((bf16[432,256]{1,0:T(8,128)(2,1)S(1)}, bf16[432,256]{1,0:T(8,128)(2,1)S(1)}, u32[]{:S(2)}, u32[]{:S(2)}) %collective-permute-start.2) | collective-permute-done | bytes 221216 | tf_op jit(solution)/shard_map/ppermute | solution.py:16
  16.3 1.0 %shard_map.50 = (bf16[240,256]{1,0:T(8,128)(2,1)S(1)}, bf16[240,256]{1,0:T(8,128)(2,1)S(1)}, bf16[240,256]{1,0:T(8,128)(2,1)S(1)}, bf16[240,256]{1,0:T(8,128)(2,...) custom-call(bf16[432,256]{1,0:T(8,128)(2,1)S(1)} %get-tuple-element., ...), custom_call_target="tpu_custom_call" | custom-call | flops 104857600 | bytes 1893376 | tf_op jit(solution)/shard_map/pallas_call | solution.py:34
  17.3 0.2 collective-permute-start.6
  17.5 1.7 %collective-permute-start.7 = (f32[20,80]{1,0:T(8,128)S(1)}, f32[20,80]{1,0:T(8,128)S(1)}, u32[]{:S(2)}, u32[]{:S(2)}) collective-permute-start(f32[20,80]{1,0:T(8,128)S(1)} %get-tuple-element.33), channel_id=1, source_target_pairs={{0,2},{1,3},{2,0},{3,1},{4,6},{5,7},{6,4},{7,5},{8,10},{9,11},{10,... | collective-permute-start | bytes 19208 | tf_op jit(solution)/shard_map/ppermute | solution.py:16
  19.2 0.0 collective-permute-start.8
  19.2 1.6 %collective-permute-start.3 = (bf16[240,256]{1,0:T(8,128)(2,1)S(1)}, bf16[240,256]{1,0:T(8,128)(2,1)S(1)}, u32[]{:S(2)}, u32[]{:S(2)}) collective-permute-start(bf16[240,256]{1,0:T(8,128)(2,1)S(1)} %get-tuple-element.28), channel_id=1, source_target_pairs={{0,4},{4,0},{8,12},{12,8},{1,5},{5,1},{9,13},{13,9},{2,6},{6,2},{1... | collective-permute-start | bytes 368648 | tf_op jit(solution)/shard_map/ppermute | solution.py:16
  20.8 2.6 %collective-permute-start.4 = (bf16[240,256]{1,0:T(8,128)(2,1)S(1)}, bf16[240,256]{1,0:T(8,128)(2,1)S(1)}, u32[]{:S(2)}, u32[]{:S(2)}) collective-permute-start(bf16[240,256]{1,0:T(8,128)(2,1)S(1)} %get-tuple-element.29), channel_id=1, source_target_pairs={{0,8},{4,12},{8,0},{12,4},{1,9},{5,13},{9,1},{13,5},{2,10},{6,14},... | collective-permute-start | bytes 368648 | tf_op jit(solution)/shard_map/ppermute | solution.py:16
  23.4 0.0 collective-permute-done.6
  23.4 0.2 collective-permute-start.5
  23.6 0.0 collective-permute-done.7
  23.6 0.0 collective-permute-done.8
  23.6 1.6 %collective-permute-start.9 = (f32[20,80]{1,0:T(8,128)S(1)}, f32[20,80]{1,0:T(8,128)S(1)}, u32[]{:S(2)}, u32[]{:S(2)}) collective-permute-start(f32[20,80]{1,0:T(8,128)S(1)} %add_add_fusion.2), channel_id=1, source_target_pairs={{0,16},{16,0},{1,17},{17,1},{2,18},{18,2},{3,19},{19,3},{4,20},{20... | collective-permute-start | bytes 19208 | tf_op jit(solution)/shard_map/ppermute | solution.py:16
  25.2 2.2 %collective-permute-done.9 = f32[20,80]{1,0:T(8,128)S(1)} collective-permute-done((f32[20,80]{1,0:T(8,128)S(1)}, f32[20,80]{1,0:T(8,128)S(1)}, u32[]{:S(2)}, u32[]{:S(2)}) %collective-permute-start.9) | collective-permute-done | bytes 6432 | tf_op jit(solution)/shard_map/ppermute | solution.py:16
  27.4 0.0 collective-permute-done.3.refs_1_
  27.4 5.8 %collective-permute-done.4.refs_2_ = bf16[240,256]{1,0:T(8,128)(2,1)S(1)} collective-permute-done((bf16[240,256]{1,0:T(8,128)(2,1)S(1)}, bf16[240,256]{1,0:T(8,128)(2,1)S(1)}, u32[]{:S(2)}, u32[]{:S(2)}) %collective-permute-start.4) | collective-permute-done | bytes 122912 | tf_op jit(solution)/shard_map/ppermute | solution.py:16
  33.2 0.0 collective-permute-done.5.refs_3_
  33.2 0.3 shard_map.51
  33.5 2.6 %collective-permute-start.10 = (f32[40,80]{1,0:T(8,128)S(1)}, f32[40,80]{1,0:T(8,128)S(1)}, u32[]{:S(2)}, u32[]{:S(2)}) collective-permute-start(f32[40,80]{1,0:T(8,128)S(1)} %get-tuple-element.36), channel_id=1, source_target_pairs={{0,4},{4,0},{8,12},{12,8},{1,5},{5,1},{9,13},{13,9},{2,6},{6,2},{1... | collective-permute-start | bytes 38408 | tf_op jit(solution)/shard_map/ppermute | solution.py:16
  36.2 1.1 %collective-permute-start.11 = (f32[40,80]{1,0:T(8,128)S(1)}, f32[40,80]{1,0:T(8,128)S(1)}, u32[]{:S(2)}, u32[]{:S(2)}) collective-permute-start(f32[40,80]{1,0:T(8,128)S(1)} %get-tuple-element.37), channel_id=1, source_target_pairs={{0,8},{4,12},{8,0},{12,4},{1,9},{5,13},{9,1},{13,5},{2,10},{6,14},... | collective-permute-start | bytes 38408 | tf_op jit(solution)/shard_map/ppermute | solution.py:16
  37.2 1.4 %collective-permute-start.12 = (f32[40,80]{1,0:T(8,128)S(1)}, f32[40,80]{1,0:T(8,128)S(1)}, u32[]{:S(2)}, u32[]{:S(2)}) collective-permute-start(f32[40,80]{1,0:T(8,128)S(1)} %get-tuple-element.38), channel_id=1, source_target_pairs={{0,12},{4,8},{8,4},{12,0},{1,13},{5,9},{9,5},{13,1},{2,14},{6,10},... | collective-permute-start | bytes 38408 | tf_op jit(solution)/shard_map/ppermute | solution.py:16
  38.6 0.0 collective-permute-done.10
  38.6 2.2 %collective-permute-done.11 = f32[40,80]{1,0:T(8,128)S(1)} collective-permute-done((f32[40,80]{1,0:T(8,128)S(1)}, f32[40,80]{1,0:T(8,128)S(1)}, u32[]{:S(2)}, u32[]{:S(2)}) %collective-permute-start.11) | collective-permute-done | bytes 12832 | tf_op jit(solution)/shard_map/ppermute | solution.py:16
  40.8 2.0 %collective-permute-done.12 = f32[40,80]{1,0:T(8,128)S(1)} collective-permute-done((f32[40,80]{1,0:T(8,128)S(1)}, f32[40,80]{1,0:T(8,128)S(1)}, u32[]{:S(2)}, u32[]{:S(2)}) %collective-permute-start.12) | collective-permute-done | bytes 12832 | tf_op jit(solution)/shard_map/ppermute | solution.py:16
  42.8 1.6 %collective-permute-start.17 = (f32[20,80]{1,0:T(8,128)S(1)}, f32[20,80]{1,0:T(8,128)S(1)}, u32[]{:S(2)}, u32[]{:S(2)}) collective-permute-start(f32[20,80]{1,0:T(8,128)S(1)} %slice.9), channel_id=1, source_target_pairs={{0,2},{1,3},{2,0},{3,1},{4,6},{5,7},{6,4},{7,5},{8,10},{9,11},{10,... | collective-permute-start | bytes 19208 | tf_op jit(solution)/shard_map/ppermute | solution.py:16
  44.4 0.0 collective-permute-start.18
  44.4 0.6 %collective-permute-start.16 = (f32[20,80]{1,0:T(8,128)S(1)}, f32[20,80]{1,0:T(8,128)S(1)}, u32[]{:S(2)}, u32[]{:S(2)}) collective-permute-start(f32[20,80]{1,0:T(8,128)S(1)} %slice.9), channel_id=1, source_target_pairs={{0,1},{1,0},{2,3},{3,2},{4,5},{5,4},{6,7},{7,6},{8,9},{9,8},{10,11... | collective-permute-start | bytes 19208 | tf_op jit(solution)/shard_map/ppermute | solution.py:16
  45.1 0.0 collective-permute-start.13
  45.1 1.5 %collective-permute-start.14 = (bf16[240,256]{1,0:T(8,128)(2,1)S(1)}, bf16[240,256]{1,0:T(8,128)(2,1)S(1)}, u32[]{:S(2)}, u32[]{:S(2)}) collective-permute-start(bf16[240,256]{1,0:T(8,128)(2,1)S(1)} %get-tuple-element.41), channel_id=1, source_target_pairs={{0,2},{1,3},{2,0},{3,1},{4,6},{5,7},{6,4},{7,5},{8,10},{9,11},{10,... | collective-permute-start | bytes 368648 | tf_op jit(solution)/shard_map/ppermute | solution.py:16
  46.6 0.0 collective-permute-done.17
  46.6 0.3 collective-permute-start.15
  46.9 0.6 %collective-permute-done.18 = f32[20,80]{1,0:T(8,128)S(1)} collective-permute-done((f32[20,80]{1,0:T(8,128)S(1)}, f32[20,80]{1,0:T(8,128)S(1)}, u32[]{:S(2)}, u32[]{:S(2)}) %collective-permute-start.18) | collective-permute-done | bytes 6432 | tf_op jit(solution)/shard_map/ppermute | solution.py:16
  47.6 0.0 collective-permute-done.16
  47.6 0.6 %add_add_fusion.1 = (f32[20,80]{1,0:T(8,128)S(1)}, f32[20,80]{1,0:T(8,128)}) fusion(f32[20,80]{1,0:T(8,128)S(1)} %collective-permute-done.18, f32[20,80]{1,0:T(8,128)S(1)} %collective-permute-done.17, f32[20,80]{1,0:T(8,128)S(1)} %collective-permute-done.16, f32[40,80]{1,0:T(8,128)S(1)} %add_add_fusion), kind=kLoop, calls=%fused_computation.1 | loop fusion | flops 4800 | bytes 44800 | tf_op jit(solution)/shard_map/add | solution.py:164
  48.2 1.5 %collective-permute-start.19 = (f32[20,80]{1,0:T(8,128)S(1)}, f32[20,80]{1,0:T(8,128)S(1)}, u32[]{:S(2)}, u32[]{:S(2)}) collective-permute-start(f32[20,80]{1,0:T(8,128)S(1)} %get-tuple-element.43), channel_id=1, source_target_pairs={{0,16},{16,0},{1,17},{17,1},{2,18},{18,2},{3,19},{19,3},{4,20},{20... | collective-permute-start | bytes 19208 | tf_op jit(solution)/shard_map/ppermute | solution.py:16
  49.7 0.0 collective-permute-done.13.refs_1_
  49.7 1.5 %collective-permute-done.14.refs_2_ = bf16[240,256]{1,0:T(8,128)(2,1)S(1)} collective-permute-done((bf16[240,256]{1,0:T(8,128)(2,1)S(1)}, bf16[240,256]{1,0:T(8,128)(2,1)S(1)}, u32[]{:S(2)}, u32[]{:S(2)}) %collective-permute-start.14) | collective-permute-done | bytes 122912 | tf_op jit(solution)/shard_map/ppermute | solution.py:16
  51.2 1.9 %collective-permute-done.15.refs_3_ = bf16[240,256]{1,0:T(8,128)(2,1)S(1)} collective-permute-done((bf16[240,256]{1,0:T(8,128)(2,1)S(1)}, bf16[240,256]{1,0:T(8,128)(2,1)S(1)}, u32[]{:S(2)}, u32[]{:S(2)}) %collective-permute-start.15) | collective-permute-done | bytes 122912 | tf_op jit(solution)/shard_map/ppermute | solution.py:16
  53.0 0.9 %shard_map.52 = bf16[12,20,1024]{2,1,0:T(8,128)(2,1)} custom-call(bf16[240,256]{1,0:T(8,128)(2,1)S(1)} %get-tuple-element.39.refs_0_, bf16[240,256]{1,0:T(8,128)(2,1)S(1)} %collective-permute-done.13.refs_1_, bf16[240,256]{1,0:T(8,128)(2,1)S(1)} %collective-permute-done.14.refs_2_, bf16[240,256]{1,0:T(8,128)(2,1)S(1)} %collective-permute-done.15.refs_3_), custom_call_target="tpu_custom_call" | custom-call | bytes 983040 | tf_op jit(solution)/shard_map/pallas_call | solution.py:34
  53.9 0.0 collective-permute-done.19
  53.9 0.6 %add.43 = f32[20,80]{1,0:T(8,128)} add(f32[20,80]{1,0:T(8,128)S(1)} %get-tuple-element.43, f32[20,80]{1,0:T(8,128)S(1)} %collective-permute-done.19) | non-fusion elementwise | flops 1600 | bytes 19200 | tf_op jit(solution)/shard_map/add | solution.py:27
  (4 shorter events, 0.0 us)
Async XLA Ops:
  0.6 1.2 %copy-start = (bf16[20,20,1024]{2,1,0:T(8,128)(2,1)S(1)}, bf16[20,20,1024]{2,1,0:T(8,128)(2,1)}, u32[]{:S(2)}) copy-start(bf16[20,20,1024]{2,1,0:T(8,128)(2,1)} %slab_ref.1) | copy-start | bytes 2457604
  1.8 0.7 %copy-start.1 = (bf16[20,48]{1,0:T(8,128)(2,1)S(1)}, bf16[20,48]{1,0:T(8,128)(2,1)}, u32[]{:S(2)}) copy-start(bf16[20,48]{1,0:T(8,128)(2,1)} %basis_ref.1) | copy-start | bytes 5764
  2.7 3.2 %collective-permute-start = (bf16[432,256]{1,0:T(8,128)(2,1)S(1)}, bf16[432,256]{1,0:T(8,128)(2,1)S(1)}, u32[]{:S(2)}, u32[]{:S(2)}) collective-permute-start(bf16[432,256]{1,0:T(8,128)(2,1)S(1)} %get-tuple-element.24), channel_id=1, source_target_pairs={{0,1},{1,0},{2,3},{3,2},{4,5},{5,4},{6,7},{7,6},{8,9},{9,8},{10,11... | collective-permute-start | bytes 663560 | tf_op jit(solution)/shard_map/ppermute | solution.py:16
  3.2 8.9 %collective-permute-start.1 = (bf16[432,256]{1,0:T(8,128)(2,1)S(1)}, bf16[432,256]{1,0:T(8,128)(2,1)S(1)}, u32[]{:S(2)}, u32[]{:S(2)}) collective-permute-start(bf16[432,256]{1,0:T(8,128)(2,1)S(1)} %get-tuple-element.25), channel_id=1, source_target_pairs={{0,2},{1,3},{2,0},{3,1},{4,6},{5,7},{6,4},{7,5},{8,10},{9,11},{10,... | collective-permute-start | bytes 663560 | tf_op jit(solution)/shard_map/ppermute | solution.py:16
  5.8 10.5 %collective-permute-start.2 = (bf16[432,256]{1,0:T(8,128)(2,1)S(1)}, bf16[432,256]{1,0:T(8,128)(2,1)S(1)}, u32[]{:S(2)}, u32[]{:S(2)}) collective-permute-start(bf16[432,256]{1,0:T(8,128)(2,1)S(1)} %get-tuple-element.26), channel_id=1, source_target_pairs={{0,3},{1,2},{2,1},{3,0},{4,7},{5,6},{6,5},{7,4},{8,11},{9,10},{10,... | collective-permute-start | bytes 663560 | tf_op jit(solution)/shard_map/ppermute | solution.py:16
  17.3 6.1 %collective-permute-start.6 = (f32[20,80]{1,0:T(8,128)S(1)}, f32[20,80]{1,0:T(8,128)S(1)}, u32[]{:S(2)}, u32[]{:S(2)}) collective-permute-start(f32[20,80]{1,0:T(8,128)S(1)} %get-tuple-element.32), channel_id=1, source_target_pairs={{0,1},{1,0},{2,3},{3,2},{4,5},{5,4},{6,7},{7,6},{8,9},{9,8},{10,11... | collective-permute-start | bytes 19208 | tf_op jit(solution)/shard_map/ppermute | solution.py:16
  17.5 6.2 %collective-permute-start.7 = (f32[20,80]{1,0:T(8,128)S(1)}, f32[20,80]{1,0:T(8,128)S(1)}, u32[]{:S(2)}, u32[]{:S(2)}) collective-permute-start(f32[20,80]{1,0:T(8,128)S(1)} %get-tuple-element.33), channel_id=1, source_target_pairs={{0,2},{1,3},{2,0},{3,1},{4,6},{5,7},{6,4},{7,5},{8,10},{9,11},{10,... | collective-permute-start | bytes 19208 | tf_op jit(solution)/shard_map/ppermute | solution.py:16
  19.2 4.4 %collective-permute-start.8 = (f32[20,80]{1,0:T(8,128)S(1)}, f32[20,80]{1,0:T(8,128)S(1)}, u32[]{:S(2)}, u32[]{:S(2)}) collective-permute-start(f32[20,80]{1,0:T(8,128)S(1)} %get-tuple-element.34), channel_id=1, source_target_pairs={{0,3},{1,2},{2,1},{3,0},{4,7},{5,6},{6,5},{7,4},{8,11},{9,10},{10,... | collective-permute-start | bytes 19208 | tf_op jit(solution)/shard_map/ppermute | solution.py:16
  19.2 8.2 %collective-permute-start.3 = (bf16[240,256]{1,0:T(8,128)(2,1)S(1)}, bf16[240,256]{1,0:T(8,128)(2,1)S(1)}, u32[]{:S(2)}, u32[]{:S(2)}) collective-permute-start(bf16[240,256]{1,0:T(8,128)(2,1)S(1)} %get-tuple-element.28), channel_id=1, source_target_pairs={{0,4},{4,0},{8,12},{12,8},{1,5},{5,1},{9,13},{13,9},{2,6},{6,2},{1... | collective-permute-start | bytes 368648 | tf_op jit(solution)/shard_map/ppermute | solution.py:16
  20.8 12.4 %collective-permute-start.4 = (bf16[240,256]{1,0:T(8,128)(2,1)S(1)}, bf16[240,256]{1,0:T(8,128)(2,1)S(1)}, u32[]{:S(2)}, u32[]{:S(2)}) collective-permute-start(bf16[240,256]{1,0:T(8,128)(2,1)S(1)} %get-tuple-element.29), channel_id=1, source_target_pairs={{0,8},{4,12},{8,0},{12,4},{1,9},{5,13},{9,1},{13,5},{2,10},{6,14},... | collective-permute-start | bytes 368648 | tf_op jit(solution)/shard_map/ppermute | solution.py:16
  23.4 9.8 %collective-permute-start.5 = (bf16[240,256]{1,0:T(8,128)(2,1)S(1)}, bf16[240,256]{1,0:T(8,128)(2,1)S(1)}, u32[]{:S(2)}, u32[]{:S(2)}) collective-permute-start(bf16[240,256]{1,0:T(8,128)(2,1)S(1)} %get-tuple-element.30), channel_id=1, source_target_pairs={{0,12},{4,8},{8,4},{12,0},{1,13},{5,9},{9,5},{13,1},{2,14},{6,10},... | collective-permute-start | bytes 368648 | tf_op jit(solution)/shard_map/ppermute | solution.py:16
  23.6 3.8 %collective-permute-start.9 = (f32[20,80]{1,0:T(8,128)S(1)}, f32[20,80]{1,0:T(8,128)S(1)}, u32[]{:S(2)}, u32[]{:S(2)}) collective-permute-start(f32[20,80]{1,0:T(8,128)S(1)} %add_add_fusion.2), channel_id=1, source_target_pairs={{0,16},{16,0},{1,17},{17,1},{2,18},{18,2},{3,19},{19,3},{4,20},{20... | collective-permute-start | bytes 19208 | tf_op jit(solution)/shard_map/ppermute | solution.py:16
  33.5 5.1 %collective-permute-start.10 = (f32[40,80]{1,0:T(8,128)S(1)}, f32[40,80]{1,0:T(8,128)S(1)}, u32[]{:S(2)}, u32[]{:S(2)}) collective-permute-start(f32[40,80]{1,0:T(8,128)S(1)} %get-tuple-element.36), channel_id=1, source_target_pairs={{0,4},{4,0},{8,12},{12,8},{1,5},{5,1},{9,13},{13,9},{2,6},{6,2},{1... | collective-permute-start | bytes 38408 | tf_op jit(solution)/shard_map/ppermute | solution.py:16
  36.2 4.7 %collective-permute-start.11 = (f32[40,80]{1,0:T(8,128)S(1)}, f32[40,80]{1,0:T(8,128)S(1)}, u32[]{:S(2)}, u32[]{:S(2)}) collective-permute-start(f32[40,80]{1,0:T(8,128)S(1)} %get-tuple-element.37), channel_id=1, source_target_pairs={{0,8},{4,12},{8,0},{12,4},{1,9},{5,13},{9,1},{13,5},{2,10},{6,14},... | collective-permute-start | bytes 38408 | tf_op jit(solution)/shard_map/ppermute | solution.py:16
  37.2 5.6 %collective-permute-start.12 = (f32[40,80]{1,0:T(8,128)S(1)}, f32[40,80]{1,0:T(8,128)S(1)}, u32[]{:S(2)}, u32[]{:S(2)}) collective-permute-start(f32[40,80]{1,0:T(8,128)S(1)} %get-tuple-element.38), channel_id=1, source_target_pairs={{0,12},{4,8},{8,4},{12,0},{1,13},{5,9},{9,5},{13,1},{2,14},{6,10},... | collective-permute-start | bytes 38408 | tf_op jit(solution)/shard_map/ppermute | solution.py:16
  42.8 3.8 %collective-permute-start.17 = (f32[20,80]{1,0:T(8,128)S(1)}, f32[20,80]{1,0:T(8,128)S(1)}, u32[]{:S(2)}, u32[]{:S(2)}) collective-permute-start(f32[20,80]{1,0:T(8,128)S(1)} %slice.9), channel_id=1, source_target_pairs={{0,2},{1,3},{2,0},{3,1},{4,6},{5,7},{6,4},{7,5},{8,10},{9,11},{10,... | collective-permute-start | bytes 19208 | tf_op jit(solution)/shard_map/ppermute | solution.py:16
  44.4 3.1 %collective-permute-start.18 = (f32[20,80]{1,0:T(8,128)S(1)}, f32[20,80]{1,0:T(8,128)S(1)}, u32[]{:S(2)}, u32[]{:S(2)}) collective-permute-start(f32[20,80]{1,0:T(8,128)S(1)} %slice.9), channel_id=1, source_target_pairs={{0,3},{1,2},{2,1},{3,0},{4,7},{5,6},{6,5},{7,4},{8,11},{9,10},{10,... | collective-permute-start | bytes 19208 | tf_op jit(solution)/shard_map/ppermute | solution.py:16
  44.4 3.1 %collective-permute-start.16 = (f32[20,80]{1,0:T(8,128)S(1)}, f32[20,80]{1,0:T(8,128)S(1)}, u32[]{:S(2)}, u32[]{:S(2)}) collective-permute-start(f32[20,80]{1,0:T(8,128)S(1)} %slice.9), channel_id=1, source_target_pairs={{0,1},{1,0},{2,3},{3,2},{4,5},{5,4},{6,7},{7,6},{8,9},{9,8},{10,11... | collective-permute-start | bytes 19208 | tf_op jit(solution)/shard_map/ppermute | solution.py:16
  45.1 4.6 %collective-permute-start.13 = (bf16[240,256]{1,0:T(8,128)(2,1)S(1)}, bf16[240,256]{1,0:T(8,128)(2,1)S(1)}, u32[]{:S(2)}, u32[]{:S(2)}) collective-permute-start(bf16[240,256]{1,0:T(8,128)(2,1)S(1)} %get-tuple-element.40), channel_id=1, source_target_pairs={{0,1},{1,0},{2,3},{3,2},{4,5},{5,4},{6,7},{7,6},{8,9},{9,8},{10,11... | collective-permute-start | bytes 368648 | tf_op jit(solution)/shard_map/ppermute | solution.py:16
  45.1 6.1 %collective-permute-start.14 = (bf16[240,256]{1,0:T(8,128)(2,1)S(1)}, bf16[240,256]{1,0:T(8,128)(2,1)S(1)}, u32[]{:S(2)}, u32[]{:S(2)}) collective-permute-start(bf16[240,256]{1,0:T(8,128)(2,1)S(1)} %get-tuple-element.41), channel_id=1, source_target_pairs={{0,2},{1,3},{2,0},{3,1},{4,6},{5,7},{6,4},{7,5},{8,10},{9,11},{10,... | collective-permute-start | bytes 368648 | tf_op jit(solution)/shard_map/ppermute | solution.py:16
  46.6 6.4 %collective-permute-start.15 = (bf16[240,256]{1,0:T(8,128)(2,1)S(1)}, bf16[240,256]{1,0:T(8,128)(2,1)S(1)}, u32[]{:S(2)}, u32[]{:S(2)}) collective-permute-start(bf16[240,256]{1,0:T(8,128)(2,1)S(1)} %get-tuple-element.42), channel_id=1, source_target_pairs={{0,3},{1,2},{2,1},{3,0},{4,7},{5,6},{6,5},{7,4},{8,11},{9,10},{10,... | collective-permute-start | bytes 368648 | tf_op jit(solution)/shard_map/ppermute | solution.py:16
  48.2 5.8 %collective-permute-start.19 = (f32[20,80]{1,0:T(8,128)S(1)}, f32[20,80]{1,0:T(8,128)S(1)}, u32[]{:S(2)}, u32[]{:S(2)}) collective-permute-start(f32[20,80]{1,0:T(8,128)S(1)} %get-tuple-element.43), channel_id=1, source_target_pairs={{0,16},{16,0},{1,17},{17,1},{2,18},{18,2},{3,19},{19,3},{4,20},{20... | collective-permute-start | bytes 19208 | tf_op jit(solution)/shard_map/ppermute | solution.py:16

commit v2 on v0

v2 whole, which is shorter than its diff:
```python
import functools

import jax
import jax.numpy as jnp
from jax import lax
from jax.experimental import pallas as pl
from jax.experimental.pallas import tpu as pltpu
from jax.sharding import PartitionSpec as P

VMEM = pl.BlockSpec(memory_space=pltpu.VMEM)
ANY = pl.BlockSpec(memory_space=pl.ANY)
sds = jax.ShapeDtypeStruct
bf16, f32 = jnp.bfloat16, jnp.float32


def swap(value, axis, step):
    return lax.ppermute(value, axis, [(i, i ^ step) for i in range(lax.axis_size(axis))])


def farthest_first(n):
    return list(range(n - 1, -1, -1))


def swaps(values, axis):
    moved = {k: swap(values[k], axis, k) for k in farthest_first(len(values))[:-1]}
    return [values[0]] + [moved[k] for k in range(1, len(values))]


def summed(values):
    total = values[-1]
    for value in values[-2::-1]:
        total = total + value
    return total


def doubled(value, axis):
    step = 1
    while step < lax.axis_size(axis):
        value = value + swap(value, axis, step)
        step *= 2
    return value


def call(kernel, out_shape, scratch, flops, args, unused=()):
    moved = sum(a.size * a.dtype.itemsize for a in list(args) + jax.tree.leaves(out_shape))
    return pl.pallas_call(
        kernel,
        out_shape=out_shape,
        in_specs=[VMEM] * len(args) + [ANY] * len(unused),
        out_specs=jax.tree.map(lambda _: VMEM, out_shape),
        scratch_shapes=scratch,
        compiler_params=pltpu.CompilerParams(vmem_limit_bytes=32 * 1024 * 1024),
        cost_estimate=pl.CostEstimate(flops=flops, bytes_accessed=moved, transcendentals=0),
    )(*args, *unused)


def nt(a, b):
    return lax.dot_general(a, b, (((1,), (1,)), ((), ())), preferred_element_type=f32)


def cut(refs, *counts):
    out, at = [], 0
    for count in counts:
        out.append(refs[at : at + count])
        at += count
    return out + [refs[at:]]


def blank_kernel(out_ref):
    out_ref[...] = jnp.zeros_like(out_ref)


def pack_kernel(spans, groups, ranks, views, slab_ref, *refs):
    me = lax.axis_index("view")
    outs = refs[-len(spans) :]
    rows, columns = slab_ref.shape[1:]
    width = columns // views
    head = []
    if groups:
        deep = rows // groups
        wide = refs[0][...].astype(f32)
        wide = jnp.concatenate([wide[g * deep : (g + 1) * deep] for g in range(groups)], axis=1)
        head = [jnp.pad(wide, ((0, -deep % 8), (0, width - groups * ranks))).astype(bf16)]
    for (k, begin, count), out in zip(spans, outs):
        at = pl.ds(pl.multiple_of((me ^ k) * width, width), width)
        out[...] = jnp.concatenate(head + [slab_ref[l, :, at] for l in range(begin, begin + count)], axis=0)


def core_kernel(lights, head, starts, rows, ranks, views, parts, groups, spare, *refs):
    first = groups > 0
    ins, old, _, light_outs, (pieces, *outs) = cut(refs[:-2], views, 0 if first else 1, spare, parts)
    whole, turned = refs[-2:]
    v, z = lax.axis_index("view"), lax.axis_index("light")
    width = whole.shape[2]
    for i, k in enumerate(farthest_first(views)):
        whole[v ^ k] = ins[i][starts[i] : starts[i] + whole.shape[1], :]
    if first:
        deep = rows // groups
        wide = [whole[k, :head, :].astype(f32)[:deep] for k in range(views)]
        basis = jnp.concatenate([w[:, g * ranks : (g + 1) * ranks] for w in wide for g in range(groups)], axis=0)
        basis = jnp.pad(basis, ((0, 0), (0, 128 - ranks))).T[:ranks].astype(bf16)
    else:
        basis = old[0][...]
    for l in range(lights):
        at = head + l * rows
        page = jnp.concatenate([whole[k, at : at + rows, :] for k in range(views)], axis=0)
        product = jnp.dot(basis, page, preferred_element_type=f32)
        for h in range(width // 128):
            turned[h, l * ranks : (l + 1) * ranks, :] = product[:, h * 128 : (h + 1) * 128]
    size = ranks // parts
    for j in range(parts):
        for h in range(width // 128):
            picked = [turned[h, pl.ds(j * size + r, lights, stride=ranks), :] for r in range(size)]
            pieces[j, :, h * 128 : (h + 1) * 128] = jnp.concatenate(picked, axis=0).astype(bf16)
    for k in range(parts):
        light_outs[k][...] = pieces[z ^ k]
    if first:
        outs[0][...] = basis


def back_kernel(chunks, *refs):
    v, outs = lax.axis_index("view"), refs[-refs[0].shape[0] :]
    for k, out in enumerate(outs):
        out[...] = jnp.concatenate([ref[v ^ k] for ref in refs[:chunks]], axis=0)


def view_kernel(lights, rows, views, spans, scale, *refs):
    ins, (out, whole) = cut(refs, len(spans))
    v = lax.axis_index("view")
    for (k, begin), ref in zip(spans, ins):
        whole[v ^ k, begin : begin + ref.shape[0], :] = ref[...]
    head = whole.shape[1] - lights * rows
    gram = jnp.zeros((views * rows, views * rows), f32)
    for l in range(lights):
        at = head + l * rows
        page = jnp.concatenate([whole[k, at : at + rows, :] for k in range(views)], axis=0)
        gram += nt(page, page)
    gram *= scale
    half = views * rows // 2
    quarters = jnp.concatenate([gram[:half], gram[half:, half:]], axis=1)
    out[...] = jnp.pad(quarters, ((0, 0), (0, out.shape[1] - 3 * half)))


def deal_kernel(lights, rows, views, *refs):
    ins, outs, (blocks,) = cut(refs, len(refs) - views - 1, views)
    v = lax.axis_index("view")
    total = summed([ref[...] for ref in ins])
    light, quarters = total[:lights, : outs[0].shape[1]], total[lights:]
    half = views * rows // 2
    cross = quarters[:, half : 2 * half]
    lower = jnp.concatenate([cross.T, quarters[:, 2 * half : 3 * half]], axis=1)
    gram = jnp.concatenate([quarters[:, : 2 * half], lower], axis=0)
    for k in range(views):
        blocks[k] = gram[k * rows : (k + 1) * rows]
    for k in range(views):
        outs[k][...] = jnp.concatenate([light, blocks[v ^ k]], axis=0)


def sum_kernel(*refs):
    refs[-1][...] = summed([ref[...] for ref in refs[:-1]])


def light_kernel(counts, spare, parts, scale, *refs):
    ins, (view,), _, outs, wholes, (blocks,) = cut(refs, parts * len(counts), 1, spare, parts, len(counts))
    z, lights = lax.axis_index("light"), sum(counts)
    for c, whole in enumerate(wholes):
        for i, k in enumerate(farthest_first(parts)):
            whole[z ^ k] = ins[c * parts + i][...]
    gram = jnp.zeros((parts * lights, parts * lights), f32)
    for r in range(wholes[0].shape[1] // counts[0]):
        page = [wholes[c][k, r * n : (r + 1) * n, :] for k in range(parts) for c, n in enumerate(counts)]
        page = jnp.concatenate(page, axis=0)
        gram += nt(page, page)
    gram *= scale
    for k in range(parts):
        blocks[k] = gram[k * lights : (k + 1) * lights]
    for k in range(parts):
        block = jnp.pad(blocks[z ^ k], ((0, 0), (0, view.shape[1] - parts * lights)))
        outs[k][...] = jnp.concatenate([block, view[...]], axis=0)


def place_kernel(counts, *refs):
    ins, core_ref = refs[:-1], refs[-1]
    v = lax.axis_index("view")
    ranks, width = core_ref.shape[0], ins[0].shape[1]
    for k in range(len(ins)):
        at = pl.ds(pl.multiple_of((v ^ k) * width, width), width)
        for r in range(ranks):
            begin, page = 0, []
            for n in counts:
                page.append(ins[k][begin + r * n : begin + (r + 1) * n, :])
                begin += ranks * n
            core_ref[r, :, at] = jnp.concatenate(page, axis=0)


def body(slab, basis):
    views, parts = lax.axis_size("view"), lax.axis_size("light")
    lights, rows, columns = slab.shape
    ranks = basis.shape[1]
    columns_all = columns * lax.axis_size("texel")
    view_scale = 1.0 / (lights * parts * columns_all)
    light_scale = 1.0 / (ranks * columns_all)
    width = columns // views
    views_all, lights_all = views * rows, parts * lights
    size = ranks // parts
    groups = max(g for g in range(1, width // ranks + 1) if rows % g == 0)
    head = -(-(rows // groups) // 8) * 8

    one = lights * 2 // 5 // 4 * 4
    counts, half = [one, lights - one], views // 2
    tall = [head + one * rows, (lights - one) * rows]

    blank = call(blank_kernel, sds((8, 128), f32), [], 10**9, [])

    spans = [(k, 0, lights if k < half else one) for k in range(views)]
    packed = call(
        functools.partial(pack_kernel, spans, groups, ranks, views),
        [sds((head + count * rows, width), bf16) for _, _, count in spans],
        [],
        0,
        [slab, basis],
        [blank],
    )
    came = swaps(packed, "view")
    near, whole = came[:half], [came[half:]]
    spans = [(k, one, lights - one) for k in range(half, views)]
    packed = call(
        functools.partial(pack_kernel, spans, 0, ranks, views),
        [sds((tall[1], width), bf16)] * len(spans),
        [],
        0,
        [slab],
        whole[0][1:],
    )
    moved = {k: swap(packed[k - half], "view", k) for k in farthest_first(views)[:half]}
    whole.append([moved[k] for k in range(half, views)])

    lit, carried, pieces = [], [], []
    for c, count in enumerate(counts):
        outs = [sds((size * count, width), bf16)] * parts + [sds((parts, size * count, width), bf16)]
        if c == 0:
            outs += [sds((ranks, views_all), bf16)]
        waits = [] if c else []
        made = call(
            functools.partial(
                core_kernel, count, 0 if c else head, [0] * half + [tall[0] * c] * half, rows, ranks, views, parts,
                0 if c else groups, len(waits),
            ),
            outs,
            [
                pltpu.VMEM((views, tall[c], width), bf16),
                pltpu.VMEM((width // 128, count * ranks, 128), f32),
            ],
            2 * views_all * count * width * ranks,
            whole[c][::-1] + near[::-1] + carried,
            waits,
        )
        lit += swaps(made[:parts], "light")[::-1]
        pieces.append(made[parts])
        carried = list(made[parts + 1 :])
    back = call(
        functools.partial(back_kernel, 2), [sds((size * lights, width), bf16)] * views, [], 0, pieces, lit[: parts - 1]
    )
    spans = [(k, 0) for k in range(half)] + [(k, c * tall[0]) for c in range(2) for k in range(half, views)]
    wide = -(-max(3 * views_all // 2, lights_all) // 128) * 128
    view_part = call(
        functools.partial(view_kernel, lights, rows, views, spans, view_scale),
        sds((views_all // 2, wide), f32),
        [pltpu.VMEM((views, head + lights * rows, width), bf16)],
        2 * views_all * lights * width * views_all,
        near + whole[0] + whole[1],
    )
    returned = swaps(back, "view")
    sums = call(
        functools.partial(light_kernel, counts, 1, parts, light_scale),
        [sds((lights + views_all // 2, wide), f32)] * parts,
        [pltpu.VMEM((parts, size * count, width), bf16) for count in counts]
        + [pltpu.VMEM((parts, lights, lights_all), f32)],
        2 * lights_all * lights_all * size * width,
        lit + [view_part],
        [returned[1]],
    )
    dealt = call(
        functools.partial(deal_kernel, lights, rows, views),
        [sds((lights + rows, lights_all), f32)] * views,
        [pltpu.VMEM((views, rows, views_all), f32)],
        0,
        swaps(sums, "light")[::-1],
    )
    total = call(sum_kernel, sds((lights + rows, lights_all), f32), [], 0, swaps(dealt, "view")[::-1])
    total = doubled(total, "texel")
    core = call(
        functools.partial(place_kernel, counts),
        sds((ranks // views, lights, columns), bf16),
        [],
        0,
        returned,
    )
    return (total[lights:], core, total[:lights])


def solution(mesh):
    return jax.shard_map(
        body,
        mesh=mesh,
        in_specs=(P("light", "view", "texel"), P("view", None)),
        out_specs=(P("view", None), P("view", "light", "texel"), P("light", None)),
        check_vma=False,
    )
```

time: 192 us -> 51.1 us (0.27)
  waiting for transfers between devices: 93.1 us -> 19.6 us
  blocking collectives: 62.5 us -> 0 us
  starting transfers between devices: 0.12 us -> 25.7 us
  between operations: 13.8 us -> 0.73 us
  matrix products: 11.8 us -> 0 us
  local copies, waits for them, and re-layouts: 8.85 us -> 1.79 us
  Pallas kernels: 0 us -> 3.08 us
    psum x2 -> x0, blocking collectives: 62.5 us -> none  [the longest x1 38.6 us: row_total(): return lax.psum(partial_value, ('texel', 'light'))]
    reduce_scatter x1 -> x0, waiting for transfers between devices: 48 us -> none  [body(): lax.psum_scatter(jnp.einsum('vr,lvc->rlc', basis, slab, preferred_element...]
    all_gather x2 -> x0, waiting for transfers between devices: 45 us -> none  [the longest x1 32.1 us: body(): lax.all_gather(slab, 'view', axis=1, tiled=True)]
    ppermute x0 -> x21, starting transfers between devices: none -> 25.7 us  [swap(): lax.ppermute(value, axis, [(i, i ^ step) for i in range(lax.axis_size(axi...]
    ppermute x0 -> x21, waiting for transfers between devices: none -> 19.6 us  [swap(): lax.ppermute(value, axis, [(i, i ^ step) for i in range(lax.axis_size(axi...]
    dot_general x3 -> x0, matrix products: 11.8 us -> none  [the longest x1 5.85 us: body(): jnp.einsum('lvc,lwc->vw', slab, lax.all_gather(slab, 'view', axis=1, tile...]
    dot_general x1 -> x0, local copies, waits for them, and re-layouts: 4.43 us -> none  [body(): jnp.einsum('vr,lvc->rlc', basis, slab, preferred_element_type=jnp.float32)]
    pallas_call x0 -> x11, Pallas kernels: none -> 3.08 us  [call(): pl.pallas_call(kernel, out_shape=out_shape, in_specs=[VMEM] * len(args) +...]
  transfers between devices with their start and end apart: 3 -> 21, of which waited for: 3 -> 10; matrix products, arithmetic and copies ran while one was open for 5% -> 0% of each run, Pallas kernels for 0% -> 6%
where the time goes in v2:
time: 51.1 us; the launch traced here: 51 us
  starting transfers between devices  25.7 us (50%)
  waiting for transfers between devices  19.6 us (38%)
  Pallas kernels  3.08 us (6%)
  local copies, waits for them, and re-layouts  1.79 us (4%)
  between operations  0.73 us (1%)
    ppermute x21, starting transfers between devices, swap(): lax.ppermute(value, axis, [(i, i ^ step) for i in range(lax.axis_size(axi...  25.7 us
    ppermute x21, waiting for transfers between devices, swap(): lax.ppermute(value, axis, [(i, i ^ step) for i in range(lax.axis_size(axi...  19.6 us
    pallas_call x11, Pallas kernels, call(): pl.pallas_call(kernel, out_shape=out_shape, in_specs=[VMEM] * len(args) +...  3.08 us
    unnamed x4, local copies, waits for them, and re-layouts  1.18 us
  transfers between devices with their start and end apart: 21, of which 10 were waited for; matrix products, arithmetic and copies ran while one was open for 0% of the time, Pallas kernels for 6%

profile of v2, /device:TPU:0, one launch (start us, length us, event | category | flops | bytes accessed | tf_op | source)
XLA Modules:
  0.0 51.0 jit_solution(10346755592226001883)
XLA Ops:
  0.6 0.0 copy-start
  0.6 0.0 copy-start.1
  0.7 1.2 %copy-done = bf16[20,20,1024]{2,1,0:T(8,128)(2,1)S(1)} copy-done((bf16[20,20,1024]{2,1,0:T(8,128)(2,1)S(1)}, bf16[20,20,1024]{2,1,0:T(8,128)(2,1)}, u32[]{:S(2)}) %copy-start) | copy-done | bytes 819224
  1.8 0.0 copy-done.1
  1.8 0.1 shard_map.50
  2.0 0.5 %collective-permute-start.2 = (bf16[408,256]{1,0:T(8,128)(2,1)S(1)}, bf16[408,256]{1,0:T(8,128)(2,1)S(1)}, u32[]{:S(2)}, u32[]{:S(2)}) collective-permute-start(bf16[408,256]{1,0:T(8,128)(2,1)S(1)} %get-tuple-element.34), channel_id=1, source_target_pairs={{0,1},{1,0},{2,3},{3,2},{4,5},{5,4},{6,7},{7,6},{8,9},{9,8},{10,11... | collective-permute-start | bytes 626696 | tf_op jit(solution)/shard_map/ppermute | solution.py:17
  2.5 2.6 %collective-permute-start = (bf16[168,256]{1,0:T(8,128)(2,1)S(1)}, bf16[168,256]{1,0:T(8,128)(2,1)S(1)}, u32[]{:S(2)}, u32[]{:S(2)}) collective-permute-start(bf16[168,256]{1,0:T(8,128)(2,1)S(1)} %get-tuple-element.32), channel_id=1, source_target_pairs={{0,3},{1,2},{2,1},{3,0},{4,7},{5,6},{6,5},{7,4},{8,11},{9,10},{10,... | collective-permute-start | bytes 258056 | tf_op jit(solution)/shard_map/ppermute | solution.py:17
  5.1 2.8 %collective-permute-done.refs_0_.refs_3_ = bf16[168,256]{1,0:T(8,128)(2,1)S(1)} collective-permute-done((bf16[168,256]{1,0:T(8,128)(2,1)S(1)}, bf16[168,256]{1,0:T(8,128)(2,1)S(1)}, u32[]{:S(2)}, u32[]{:S(2)}) %collective-permute-start) | collective-permute-done | bytes 86048 | tf_op jit(solution)/shard_map/ppermute | solution.py:17
  8.0 1.5 %collective-permute-start.6 = (bf16[240,256]{1,0:T(8,128)(2,1)S(1)}, bf16[240,256]{1,0:T(8,128)(2,1)S(1)}, u32[]{:S(2)}, u32[]{:S(2)}) collective-permute-start(bf16[240,256]{1,0:T(8,128)(2,1)S(1)} %get-tuple-element.40), channel_id=1, source_target_pairs={{0,3},{1,2},{2,1},{3,0},{4,7},{5,6},{6,5},{7,4},{8,11},{9,10},{10,... | collective-permute-start | bytes 368648 | tf_op jit(solution)/shard_map/ppermute | solution.py:17
  9.4 0.3 collective-permute-start.7
  9.8 1.7 %collective-permute-start.1 = (bf16[168,256]{1,0:T(8,128)(2,1)S(1)}, bf16[168,256]{1,0:T(8,128)(2,1)S(1)}, u32[]{:S(2)}, u32[]{:S(2)}) collective-permute-start(bf16[168,256]{1,0:T(8,128)(2,1)S(1)} %get-tuple-element.33), channel_id=1, source_target_pairs={{0,2},{1,3},{2,0},{3,1},{4,6},{5,7},{6,4},{7,5},{8,10},{9,11},{10,... | collective-permute-start | bytes 258056 | tf_op jit(solution)/shard_map/ppermute | solution.py:17
  11.5 6.7 %collective-permute-done.1.refs_1_.refs_2_ = bf16[168,256]{1,0:T(8,128)(2,1)S(1)} collective-permute-done((bf16[168,256]{1,0:T(8,128)(2,1)S(1)}, bf16[168,256]{1,0:T(8,128)(2,1)S(1)}, u32[]{:S(2)}, u32[]{:S(2)}) %collective-permute-start.1) | collective-permute-done | bytes 86048 | tf_op jit(solution)/shard_map/ppermute | solution.py:17
  18.1 0.0 collective-permute-done.2.refs_2_.refs_1_
  18.1 0.5 shard_map.51
  18.6 3.6 %collective-permute-start.3 = (bf16[96,256]{1,0:T(8,128)(2,1)S(1)}, bf16[96,256]{1,0:T(8,128)(2,1)S(1)}, u32[]{:S(2)}, u32[]{:S(2)}) collective-permute-start(bf16[96,256]{1,0:T(8,128)(2,1)S(1)} %get-tuple-element.36), channel_id=1, source_target_pairs={{0,12},{4,8},{8,4},{12,0},{1,13},{5,9},{9,5},{13,1},{2,14},{6,10},... | collective-permute-start | bytes 147464 | tf_op jit(solution)/shard_map/ppermute | solution.py:17
  22.2 0.0 collective-permute-start.4
  22.2 0.9 %collective-permute-start.5 = (bf16[96,256]{1,0:T(8,128)(2,1)S(1)}, bf16[96,256]{1,0:T(8,128)(2,1)S(1)}, u32[]{:S(2)}, u32[]{:S(2)}) collective-permute-start(bf16[96,256]{1,0:T(8,128)(2,1)S(1)} %get-tuple-element.38), channel_id=1, source_target_pairs={{0,4},{4,0},{8,12},{12,8},{1,5},{5,1},{9,13},{13,9},{2,6},{6,2},{1... | collective-permute-start | bytes 147464 | tf_op jit(solution)/shard_map/ppermute | solution.py:17
  23.1 0.0 collective-permute-done.6.refs_0_.refs_5_
  23.1 0.0 collective-permute-done.7.refs_1_.refs_4_
  23.1 0.5 shard_map.53
  23.6 3.6 %collective-permute-start.8 = (bf16[144,256]{1,0:T(8,128)(2,1)S(1)}, bf16[144,256]{1,0:T(8,128)(2,1)S(1)}, u32[]{:S(2)}, u32[]{:S(2)}) collective-permute-start(bf16[144,256]{1,0:T(8,128)(2,1)S(1)} %get-tuple-element.43), channel_id=1, source_target_pairs={{0,12},{4,8},{8,4},{12,0},{1,13},{5,9},{9,5},{13,1},{2,14},{6,10},... | collective-permute-start | bytes 221192 | tf_op jit(solution)/shard_map/ppermute | solution.py:17
  27.2 0.0 collective-permute-done.3.refs_2_.refs_0_
  27.2 1.1 %collective-permute-done.4.refs_3_.refs_1_ = bf16[96,256]{1,0:T(8,128)(2,1)S(1)} collective-permute-done((bf16[96,256]{1,0:T(8,128)(2,1)S(1)}, bf16[96,256]{1,0:T(8,128)(2,1)S(1)}, u32[]{:S(2)}, u32[]{:S(2)}) %collective-permute-start.4) | collective-permute-done | bytes 49184 | tf_op jit(solution)/shard_map/ppermute | solution.py:17
  28.3 0.0 collective-permute-done.5.refs_4_.refs_2_
  28.4 0.1 collective-permute-start.11
  28.4 1.0 %collective-permute-start.9 = (bf16[144,256]{1,0:T(8,128)(2,1)S(1)}, bf16[144,256]{1,0:T(8,128)(2,1)S(1)}, u32[]{:S(2)}, u32[]{:S(2)}) collective-permute-start(bf16[144,256]{1,0:T(8,128)(2,1)S(1)} %get-tuple-element.44), channel_id=1, source_target_pairs={{0,8},{4,12},{8,0},{12,4},{1,9},{5,13},{9,1},{13,5},{2,10},{6,14},... | collective-permute-start | bytes 221192 | tf_op jit(solution)/shard_map/ppermute | solution.py:17
  29.4 0.8 %collective-permute-start.10 = (bf16[144,256]{1,0:T(8,128)(2,1)S(1)}, bf16[144,256]{1,0:T(8,128)(2,1)S(1)}, u32[]{:S(2)}, u32[]{:S(2)}) collective-permute-start(bf16[144,256]{1,0:T(8,128)(2,1)S(1)} %get-tuple-element.45), channel_id=1, source_target_pairs={{0,4},{4,0},{8,12},{12,8},{1,5},{5,1},{9,13},{13,9},{2,6},{6,2},{1... | collective-permute-start | bytes 221192 | tf_op jit(solution)/shard_map/ppermute | solution.py:17
  30.3 1.3 %collective-permute-start.19 = (bf16[240,256]{1,0:T(8,128)(2,1)S(1)}, bf16[240,256]{1,0:T(8,128)(2,1)S(1)}, u32[]{:S(2)}, u32[]{:S(2)}) collective-permute-start(bf16[240,256]{1,0:T(8,128)(2,1)S(1)} %get-tuple-element.59), channel_id=1, source_target_pairs={{0,2},{1,3},{2,0},{3,1},{4,6},{5,7},{6,4},{7,5},{8,10},{9,11},{10,... | collective-permute-start | bytes 368648 | tf_op jit(solution)/shard_map/ppermute | solution.py:17
  31.5 0.0 collective-permute-done.8.refs_4_
  31.5 0.0 collective-permute-start.20
  31.5 0.5 shard_map.54.refs_8_
  32.0 2.4 %collective-permute-done.9.refs_5_ = bf16[144,256]{1,0:T(8,128)(2,1)S(1)} collective-permute-done((bf16[144,256]{1,0:T(8,128)(2,1)S(1)}, bf16[144,256]{1,0:T(8,128)(2,1)S(1)}, u32[]{:S(2)}, u32[]{:S(2)}) %collective-permute-start.9) | collective-permute-done | bytes 73760 | tf_op jit(solution)/shard_map/ppermute | solution.py:17
  34.5 0.9 %collective-permute-done.10.refs_6_ = bf16[144,256]{1,0:T(8,128)(2,1)S(1)} collective-permute-done((bf16[144,256]{1,0:T(8,128)(2,1)S(1)}, bf16[144,256]{1,0:T(8,128)(2,1)S(1)}, u32[]{:S(2)}, u32[]{:S(2)}) %collective-permute-start.10) | collective-permute-done | bytes 73760 | tf_op jit(solution)/shard_map/ppermute | solution.py:17
  35.3 0.0 collective-permute-done.11.refs_9_.refs_1_
  35.3 0.3 shard_map.56
  35.7 1.5 %collective-permute-start.12 = (f32[60,128]{1,0:T(8,128)S(1)}, f32[60,128]{1,0:T(8,128)S(1)}, u32[]{:S(2)}, u32[]{:S(2)}) collective-permute-start(f32[60,128]{1,0:T(8,128)S(1)} %get-tuple-element.50), channel_id=1, source_target_pairs={{0,12},{4,8},{8,4},{12,0},{1,13},{5,9},{9,5},{13,1},{2,14},{6,10},... | collective-permute-start | bytes 92168 | tf_op jit(solution)/shard_map/ppermute | solution.py:17
  37.2 0.3 collective-permute-start.13
  37.6 2.6 %collective-permute-start.14 = (f32[60,128]{1,0:T(8,128)S(1)}, f32[60,128]{1,0:T(8,128)S(1)}, u32[]{:S(2)}, u32[]{:S(2)}) collective-permute-start(f32[60,128]{1,0:T(8,128)S(1)} %get-tuple-element.52), channel_id=1, source_target_pairs={{0,4},{4,0},{8,12},{12,8},{1,5},{5,1},{9,13},{13,9},{2,6},{6,2},{1... | collective-permute-start | bytes 92168 | tf_op jit(solution)/shard_map/ppermute | solution.py:17
  40.2 1.5 %collective-permute-done.12.refs_0_ = f32[60,128]{1,0:T(8,128)S(1)} collective-permute-done((f32[60,128]{1,0:T(8,128)S(1)}, f32[60,128]{1,0:T(8,128)S(1)}, u32[]{:S(2)}, u32[]{:S(2)}) %collective-permute-start.12) | collective-permute-done | bytes 30752 | tf_op jit(solution)/shard_map/ppermute | solution.py:17
  41.7 0.7 %collective-permute-done.13.refs_1_ = f32[60,128]{1,0:T(8,128)S(1)} collective-permute-done((f32[60,128]{1,0:T(8,128)S(1)}, f32[60,128]{1,0:T(8,128)S(1)}, u32[]{:S(2)}, u32[]{:S(2)}) %collective-permute-start.13) | collective-permute-done | bytes 30752 | tf_op jit(solution)/shard_map/ppermute | solution.py:17
  42.4 0.0 collective-permute-done.14.refs_2_
  42.4 0.2 shard_map.57
  42.6 0.1 collective-permute-start.15
  42.6 1.5 %collective-permute-start.16 = (f32[40,80]{1,0:T(8,128)S(1)}, f32[40,80]{1,0:T(8,128)S(1)}, u32[]{:S(2)}, u32[]{:S(2)}) collective-permute-start(f32[40,80]{1,0:T(8,128)S(1)} %get-tuple-element.55), channel_id=1, source_target_pairs={{0,2},{1,3},{2,0},{3,1},{4,6},{5,7},{6,4},{7,5},{8,10},{9,11},{10,... | collective-permute-start | bytes 38408 | tf_op jit(solution)/shard_map/ppermute | solution.py:17
  44.1 0.3 collective-permute-start.17
  44.5 1.6 %collective-permute-done.15.refs_0_ = f32[40,80]{1,0:T(8,128)S(1)} collective-permute-done((f32[40,80]{1,0:T(8,128)S(1)}, f32[40,80]{1,0:T(8,128)S(1)}, u32[]{:S(2)}, u32[]{:S(2)}) %collective-permute-start.15) | collective-permute-done | bytes 12832 | tf_op jit(solution)/shard_map/ppermute | solution.py:17
  46.0 0.4 collective-permute-done.16.refs_1_
  46.5 0.0 collective-permute-done.17.refs_2_
  46.5 1.5 %collective-permute-start.18 = (f32[40,80]{1,0:T(8,128)S(1)}, f32[40,80]{1,0:T(8,128)S(1)}, u32[]{:S(2)}, u32[]{:S(2)}) collective-permute-start(f32[40,80]{1,0:T(8,128)S(1)} %shard_map.58), channel_id=1, source_target_pairs={{0,16},{16,0},{1,17},{17,1},{2,18},{18,2},{3,19},{19,3},{4,20},{20... | collective-permute-start | bytes 38408 | tf_op jit(solution)/shard_map/ppermute | solution.py:17
  48.0 0.0 collective-permute-done.19.refs_2_
  48.0 0.0 collective-permute-done.20.refs_3_
  48.0 0.9 %shard_map.59 = bf16[12,20,1024]{2,1,0:T(8,128)(2,1)} custom-call(bf16[240,256]{1,0:T(8,128)(2,1)S(1)} %get-tuple-element.58.refs_0_, bf16[240,256]{1,0:T(8,128)(2,1)S(1)} %collective-permute-done.11.refs_9_.refs_1_, bf16[240,256]{1,0:T(8,128)(2,1)S(1)} %collective-permute-done.19.refs_2_, bf16[240,256]{1,0:T(8,128)(2,1)S(1)} %collective-permute-done.20.refs_3_), custom_call_target="tpu_custom_call" | custom-call | bytes 983040 | tf_op jit(solution)/shard_map/pallas_call | solution.py:46
  48.9 1.5 %collective-permute-done.18 = f32[40,80]{1,0:T(8,128)S(1)} collective-permute-done((f32[40,80]{1,0:T(8,128)S(1)}, f32[40,80]{1,0:T(8,128)S(1)}, u32[]{:S(2)}, u32[]{:S(2)}) %collective-permute-start.18) | collective-permute-done | bytes 12832 | tf_op jit(solution)/shard_map/ppermute | solution.py:17
  50.4 0.6 %fusion = (f32[20,80]{1,0:T(8,128)}, f32[20,80]{1,0:T(8,128)}) fusion(f32[40,80]{1,0:T(8,128)S(1)} %add.3), kind=kLoop, calls=%fused_computation | loop fusion | bytes 25600 | tf_op jit(solution)/shard_map/slice | solution.py:299
  (5 shorter events, 0.1 us)
Async XLA Ops:
  0.6 1.2 %copy-start = (bf16[20,20,1024]{2,1,0:T(8,128)(2,1)S(1)}, bf16[20,20,1024]{2,1,0:T(8,128)(2,1)}, u32[]{:S(2)}) copy-start(bf16[20,20,1024]{2,1,0:T(8,128)(2,1)} %slab_ref.3) | copy-start | bytes 2457604
  0.6 1.2 %copy-start.1 = (bf16[20,48]{1,0:T(8,128)(2,1)S(1)}, bf16[20,48]{1,0:T(8,128)(2,1)}, u32[]{:S(2)}) copy-start(bf16[20,48]{1,0:T(8,128)(2,1)} %refs_0_.1) | copy-start | bytes 5764
  2.0 16.2 %collective-permute-start.2 = (bf16[408,256]{1,0:T(8,128)(2,1)S(1)}, bf16[408,256]{1,0:T(8,128)(2,1)S(1)}, u32[]{:S(2)}, u32[]{:S(2)}) collective-permute-start(bf16[408,256]{1,0:T(8,128)(2,1)S(1)} %get-tuple-element.34), channel_id=1, source_target_pairs={{0,1},{1,0},{2,3},{3,2},{4,5},{5,4},{6,7},{7,6},{8,9},{9,8},{10,11... | collective-permute-start | bytes 626696 | tf_op jit(solution)/shard_map/ppermute | solution.py:17
  2.5 5.5 %collective-permute-start = (bf16[168,256]{1,0:T(8,128)(2,1)S(1)}, bf16[168,256]{1,0:T(8,128)(2,1)S(1)}, u32[]{:S(2)}, u32[]{:S(2)}) collective-permute-start(bf16[168,256]{1,0:T(8,128)(2,1)S(1)} %get-tuple-element.32), channel_id=1, source_target_pairs={{0,3},{1,2},{2,1},{3,0},{4,7},{5,6},{6,5},{7,4},{8,11},{9,10},{10,... | collective-permute-start | bytes 258056 | tf_op jit(solution)/shard_map/ppermute | solution.py:17
  8.0 15.1 %collective-permute-start.6 = (bf16[240,256]{1,0:T(8,128)(2,1)S(1)}, bf16[240,256]{1,0:T(8,128)(2,1)S(1)}, u32[]{:S(2)}, u32[]{:S(2)}) collective-permute-start(bf16[240,256]{1,0:T(8,128)(2,1)S(1)} %get-tuple-element.40), channel_id=1, source_target_pairs={{0,3},{1,2},{2,1},{3,0},{4,7},{5,6},{6,5},{7,4},{8,11},{9,10},{10,... | collective-permute-start | bytes 368648 | tf_op jit(solution)/shard_map/ppermute | solution.py:17
  9.4 13.7 %collective-permute-start.7 = (bf16[240,256]{1,0:T(8,128)(2,1)S(1)}, bf16[240,256]{1,0:T(8,128)(2,1)S(1)}, u32[]{:S(2)}, u32[]{:S(2)}) collective-permute-start(bf16[240,256]{1,0:T(8,128)(2,1)S(1)} %get-tuple-element.41), channel_id=1, source_target_pairs={{0,2},{1,3},{2,0},{3,1},{4,6},{5,7},{6,4},{7,5},{8,10},{9,11},{10,... | collective-permute-start | bytes 368648 | tf_op jit(solution)/shard_map/ppermute | solution.py:17
  9.8 8.4 %collective-permute-start.1 = (bf16[168,256]{1,0:T(8,128)(2,1)S(1)}, bf16[168,256]{1,0:T(8,128)(2,1)S(1)}, u32[]{:S(2)}, u32[]{:S(2)}) collective-permute-start(bf16[168,256]{1,0:T(8,128)(2,1)S(1)} %get-tuple-element.33), channel_id=1, source_target_pairs={{0,2},{1,3},{2,0},{3,1},{4,6},{5,7},{6,4},{7,5},{8,10},{9,11},{10,... | collective-permute-start | bytes 258056 | tf_op jit(solution)/shard_map/ppermute | solution.py:17
  18.6 8.5 %collective-permute-start.3 = (bf16[96,256]{1,0:T(8,128)(2,1)S(1)}, bf16[96,256]{1,0:T(8,128)(2,1)S(1)}, u32[]{:S(2)}, u32[]{:S(2)}) collective-permute-start(bf16[96,256]{1,0:T(8,128)(2,1)S(1)} %get-tuple-element.36), channel_id=1, source_target_pairs={{0,12},{4,8},{8,4},{12,0},{1,13},{5,9},{9,5},{13,1},{2,14},{6,10},... | collective-permute-start | bytes 147464 | tf_op jit(solution)/shard_map/ppermute | solution.py:17
  22.2 6.1 %collective-permute-start.4 = (bf16[96,256]{1,0:T(8,128)(2,1)S(1)}, bf16[96,256]{1,0:T(8,128)(2,1)S(1)}, u32[]{:S(2)}, u32[]{:S(2)}) collective-permute-start(bf16[96,256]{1,0:T(8,128)(2,1)S(1)} %get-tuple-element.37), channel_id=1, source_target_pairs={{0,8},{4,12},{8,0},{12,4},{1,9},{5,13},{9,1},{13,5},{2,10},{6,14},... | collective-permute-start | bytes 147464 | tf_op jit(solution)/shard_map/ppermute | solution.py:17
  22.2 6.1 %collective-permute-start.5 = (bf16[96,256]{1,0:T(8,128)(2,1)S(1)}, bf16[96,256]{1,0:T(8,128)(2,1)S(1)}, u32[]{:S(2)}, u32[]{:S(2)}) collective-permute-start(bf16[96,256]{1,0:T(8,128)(2,1)S(1)} %get-tuple-element.38), channel_id=1, source_target_pairs={{0,4},{4,0},{8,12},{12,8},{1,5},{5,1},{9,13},{13,9},{2,6},{6,2},{1... | collective-permute-start | bytes 147464 | tf_op jit(solution)/shard_map/ppermute | solution.py:17
  23.6 8.0 %collective-permute-start.8 = (bf16[144,256]{1,0:T(8,128)(2,1)S(1)}, bf16[144,256]{1,0:T(8,128)(2,1)S(1)}, u32[]{:S(2)}, u32[]{:S(2)}) collective-permute-start(bf16[144,256]{1,0:T(8,128)(2,1)S(1)} %get-tuple-element.43), channel_id=1, source_target_pairs={{0,12},{4,8},{8,4},{12,0},{1,13},{5,9},{9,5},{13,1},{2,14},{6,10},... | collective-permute-start | bytes 221192 | tf_op jit(solution)/shard_map/ppermute | solution.py:17
  28.4 7.0 %collective-permute-start.11 = (bf16[240,256]{1,0:T(8,128)(2,1)S(1)}, bf16[240,256]{1,0:T(8,128)(2,1)S(1)}, u32[]{:S(2)}, u32[]{:S(2)}) collective-permute-start(bf16[240,256]{1,0:T(8,128)(2,1)S(1)} %get-tuple-element.49), channel_id=1, source_target_pairs={{0,1},{1,0},{2,3},{3,2},{4,5},{5,4},{6,7},{7,6},{8,9},{9,8},{10,11... | collective-permute-start | bytes 368648 | tf_op jit(solution)/shard_map/ppermute | solution.py:17
  28.4 6.1 %collective-permute-start.9 = (bf16[144,256]{1,0:T(8,128)(2,1)S(1)}, bf16[144,256]{1,0:T(8,128)(2,1)S(1)}, u32[]{:S(2)}, u32[]{:S(2)}) collective-permute-start(bf16[144,256]{1,0:T(8,128)(2,1)S(1)} %get-tuple-element.44), channel_id=1, source_target_pairs={{0,8},{4,12},{8,0},{12,4},{1,9},{5,13},{9,1},{13,5},{2,10},{6,14},... | collective-permute-start | bytes 221192 | tf_op jit(solution)/shard_map/ppermute | solution.py:17
  29.4 5.9 %collective-permute-start.10 = (bf16[144,256]{1,0:T(8,128)(2,1)S(1)}, bf16[144,256]{1,0:T(8,128)(2,1)S(1)}, u32[]{:S(2)}, u32[]{:S(2)}) collective-permute-start(bf16[144,256]{1,0:T(8,128)(2,1)S(1)} %get-tuple-element.45), channel_id=1, source_target_pairs={{0,4},{4,0},{8,12},{12,8},{1,5},{5,1},{9,13},{13,9},{2,6},{6,2},{1... | collective-permute-start | bytes 221192 | tf_op jit(solution)/shard_map/ppermute | solution.py:17
  30.3 17.7 %collective-permute-start.19 = (bf16[240,256]{1,0:T(8,128)(2,1)S(1)}, bf16[240,256]{1,0:T(8,128)(2,1)S(1)}, u32[]{:S(2)}, u32[]{:S(2)}) collective-permute-start(bf16[240,256]{1,0:T(8,128)(2,1)S(1)} %get-tuple-element.59), channel_id=1, source_target_pairs={{0,2},{1,3},{2,0},{3,1},{4,6},{5,7},{6,4},{7,5},{8,10},{9,11},{10,... | collective-permute-start | bytes 368648 | tf_op jit(solution)/shard_map/ppermute | solution.py:17
  31.5 16.5 %collective-permute-start.20 = (bf16[240,256]{1,0:T(8,128)(2,1)S(1)}, bf16[240,256]{1,0:T(8,128)(2,1)S(1)}, u32[]{:S(2)}, u32[]{:S(2)}) collective-permute-start(bf16[240,256]{1,0:T(8,128)(2,1)S(1)} %get-tuple-element.60), channel_id=1, source_target_pairs={{0,3},{1,2},{2,1},{3,0},{4,7},{5,6},{6,5},{7,4},{8,11},{9,10},{10,... | collective-permute-start | bytes 368648 | tf_op jit(solution)/shard_map/ppermute | solution.py:17
  35.7 6.0 %collective-permute-start.12 = (f32[60,128]{1,0:T(8,128)S(1)}, f32[60,128]{1,0:T(8,128)S(1)}, u32[]{:S(2)}, u32[]{:S(2)}) collective-permute-start(f32[60,128]{1,0:T(8,128)S(1)} %get-tuple-element.50), channel_id=1, source_target_pairs={{0,12},{4,8},{8,4},{12,0},{1,13},{5,9},{9,5},{13,1},{2,14},{6,10},... | collective-permute-start | bytes 92168 | tf_op jit(solution)/shard_map/ppermute | solution.py:17
  37.2 5.2 %collective-permute-start.13 = (f32[60,128]{1,0:T(8,128)S(1)}, f32[60,128]{1,0:T(8,128)S(1)}, u32[]{:S(2)}, u32[]{:S(2)}) collective-permute-start(f32[60,128]{1,0:T(8,128)S(1)} %get-tuple-element.51), channel_id=1, source_target_pairs={{0,8},{4,12},{8,0},{12,4},{1,9},{5,13},{9,1},{13,5},{2,10},{6,14},... | collective-permute-start | bytes 92168 | tf_op jit(solution)/shard_map/ppermute | solution.py:17
  37.6 4.8 %collective-permute-start.14 = (f32[60,128]{1,0:T(8,128)S(1)}, f32[60,128]{1,0:T(8,128)S(1)}, u32[]{:S(2)}, u32[]{:S(2)}) collective-permute-start(f32[60,128]{1,0:T(8,128)S(1)} %get-tuple-element.52), channel_id=1, source_target_pairs={{0,4},{4,0},{8,12},{12,8},{1,5},{5,1},{9,13},{13,9},{2,6},{6,2},{1... | collective-permute-start | bytes 92168 | tf_op jit(solution)/shard_map/ppermute | solution.py:17
  42.6 3.5 %collective-permute-start.15 = (f32[40,80]{1,0:T(8,128)S(1)}, f32[40,80]{1,0:T(8,128)S(1)}, u32[]{:S(2)}, u32[]{:S(2)}) collective-permute-start(f32[40,80]{1,0:T(8,128)S(1)} %get-tuple-element.54), channel_id=1, source_target_pairs={{0,3},{1,2},{2,1},{3,0},{4,7},{5,6},{6,5},{7,4},{8,11},{9,10},{10,... | collective-permute-start | bytes 38408 | tf_op jit(solution)/shard_map/ppermute | solution.py:17
  42.6 3.8 %collective-permute-start.16 = (f32[40,80]{1,0:T(8,128)S(1)}, f32[40,80]{1,0:T(8,128)S(1)}, u32[]{:S(2)}, u32[]{:S(2)}) collective-permute-start(f32[40,80]{1,0:T(8,128)S(1)} %get-tuple-element.55), channel_id=1, source_target_pairs={{0,2},{1,3},{2,0},{3,1},{4,6},{5,7},{6,4},{7,5},{8,10},{9,11},{10,... | collective-permute-start | bytes 38408 | tf_op jit(solution)/shard_map/ppermute | solution.py:17
  44.1 2.3 %collective-permute-start.17 = (f32[40,80]{1,0:T(8,128)S(1)}, f32[40,80]{1,0:T(8,128)S(1)}, u32[]{:S(2)}, u32[]{:S(2)}) collective-permute-start(f32[40,80]{1,0:T(8,128)S(1)} %get-tuple-element.56), channel_id=1, source_target_pairs={{0,1},{1,0},{2,3},{3,2},{4,5},{5,4},{6,7},{7,6},{8,9},{9,8},{10,11... | collective-permute-start | bytes 38408 | tf_op jit(solution)/shard_map/ppermute | solution.py:17
  46.5 3.8 %collective-permute-start.18 = (f32[40,80]{1,0:T(8,128)S(1)}, f32[40,80]{1,0:T(8,128)S(1)}, u32[]{:S(2)}, u32[]{:S(2)}) collective-permute-start(f32[40,80]{1,0:T(8,128)S(1)} %shard_map.58), channel_id=1, source_target_pairs={{0,16},{16,0},{1,17},{17,1},{2,18},{18,2},{3,19},{19,3},{4,20},{20... | collective-permute-start | bytes 38408 | tf_op jit(solution)/shard_map/ppermute | solution.py:17

commit v3 on v2

--- a/solution.py
+++ b/solution.py
@@ -240,7 +240,7 @@
         outs = [sds((size * count, width), bf16)] * parts + [sds((parts, size * count, width), bf16)]
         if c == 0:
             outs += [sds((ranks, views_all), bf16)]
-        waits = [] if c else []
+        waits = lit[:1] if c else []
         made = call(
             functools.partial(
                 core_kernel, count, 0 if c else head, [0] * half + [tall[0] * c] * half, rows, ranks, views, parts,

time: 51.1 us -> 44 us (0.86)
  waiting for transfers between devices: 19.6 us -> 14.1 us
  starting transfers between devices: 25.7 us -> 24.2 us
    ppermute x21, waiting for transfers between devices: 19.6 us -> 14.1 us  [swap(): lax.ppermute(value, axis, [(i, i ^ step) for i in range(lax.axis_size(axi...]
    ppermute x21, starting transfers between devices: 25.7 us -> 24.2 us  [swap(): lax.ppermute(value, axis, [(i, i ^ step) for i in range(lax.axis_size(axi...]
  transfers between devices with their start and end apart: 21 -> 21, of which waited for: 10 -> 12; matrix products, arithmetic and copies ran while one was open for 0% -> 0% of each run, Pallas kernels for 6% -> 7%
where the time goes in v3:
time: 44 us; the launch traced here: 43.9 us
  starting transfers between devices  24.2 us (55%)
  waiting for transfers between devices  14.1 us (32%)
  Pallas kernels  3.07 us (7%)
  local copies, waits for them, and re-layouts  1.79 us (4%)
  between operations  0.73 us (2%)
    ppermute x21, starting transfers between devices, swap(): lax.ppermute(value, axis, [(i, i ^ step) for i in range(lax.axis_size(axi...  24.2 us
    ppermute x21, waiting for transfers between devices, swap(): lax.ppermute(value, axis, [(i, i ^ step) for i in range(lax.axis_size(axi...  14.1 us
    pallas_call x11, Pallas kernels, call(): pl.pallas_call(kernel, out_shape=out_shape, in_specs=[VMEM] * len(args) +...  3.07 us
    unnamed x4, local copies, waits for them, and re-layouts  1.18 us
  transfers between devices with their start and end apart: 21, of which 12 were waited for; matrix products, arithmetic and copies ran while one was open for 0% of the time, Pallas kernels for 7%

profile of v3, /device:TPU:0, one launch (start us, length us, event | category | flops | bytes accessed | tf_op | source)
XLA Modules:
  0.0 43.9 jit_solution(7805860145429034496)
XLA Ops:
  0.6 0.0 copy-start
  0.6 0.0 copy-start.1
  0.7 1.2 %copy-done = bf16[20,20,1024]{2,1,0:T(8,128)(2,1)S(1)} copy-done((bf16[20,20,1024]{2,1,0:T(8,128)(2,1)S(1)}, bf16[20,20,1024]{2,1,0:T(8,128)(2,1)}, u32[]{:S(2)}) %copy-start) | copy-done | bytes 819224
  1.8 0.0 copy-done.1
  1.8 0.1 shard_map.50
  2.0 0.5 %collective-permute-start.2 = (bf16[408,256]{1,0:T(8,128)(2,1)S(1)}, bf16[408,256]{1,0:T(8,128)(2,1)S(1)}, u32[]{:S(2)}, u32[]{:S(2)}) collective-permute-start(bf16[408,256]{1,0:T(8,128)(2,1)S(1)} %get-tuple-element.34), channel_id=1, source_target_pairs={{0,1},{1,0},{2,3},{3,2},{4,5},{5,4},{6,7},{7,6},{8,9},{9,8},{10,11... | collective-permute-start | bytes 626696 | tf_op jit(solution)/shard_map/ppermute | solution.py:17
  2.5 2.6 %collective-permute-start = (bf16[168,256]{1,0:T(8,128)(2,1)S(1)}, bf16[168,256]{1,0:T(8,128)(2,1)S(1)}, u32[]{:S(2)}, u32[]{:S(2)}) collective-permute-start(bf16[168,256]{1,0:T(8,128)(2,1)S(1)} %get-tuple-element.32), channel_id=1, source_target_pairs={{0,3},{1,2},{2,1},{3,0},{4,7},{5,6},{6,5},{7,4},{8,11},{9,10},{10,... | collective-permute-start | bytes 258056 | tf_op jit(solution)/shard_map/ppermute | solution.py:17
  5.1 0.0 collective-permute-start.1
  5.2 2.8 %collective-permute-done.refs_0_.refs_3_ = bf16[168,256]{1,0:T(8,128)(2,1)S(1)} collective-permute-done((bf16[168,256]{1,0:T(8,128)(2,1)S(1)}, bf16[168,256]{1,0:T(8,128)(2,1)S(1)}, u32[]{:S(2)}, u32[]{:S(2)}) %collective-permute-start) | collective-permute-done | bytes 86048 | tf_op jit(solution)/shard_map/ppermute | solution.py:17
  8.0 2.0 %collective-permute-start.6 = (bf16[240,256]{1,0:T(8,128)(2,1)S(1)}, bf16[240,256]{1,0:T(8,128)(2,1)S(1)}, u32[]{:S(2)}, u32[]{:S(2)}) collective-permute-start(bf16[240,256]{1,0:T(8,128)(2,1)S(1)} %get-tuple-element.40), channel_id=1, source_target_pairs={{0,3},{1,2},{2,1},{3,0},{4,7},{5,6},{6,5},{7,4},{8,11},{9,10},{10,... | collective-permute-start | bytes 368648 | tf_op jit(solution)/shard_map/ppermute | solution.py:17
  10.0 0.0 collective-permute-start.7
  10.0 0.0 collective-permute-done.1.refs_1_.refs_2_
  10.0 0.0 collective-permute-done.2.refs_2_.refs_1_
  10.0 0.5 %shard_map.51 = (bf16[96,256]{1,0:T(8,128)(2,1)S(1)}, bf16[96,256]{1,0:T(8,128)(2,1)S(1)}, bf16[96,256]{1,0:T(8,128)(2,1)S(1)}, bf16[96,256]{1,0:T(8,128)(2,1)S(...) custom-call(bf16[168,256]{1,0:T(8,128)(2,1)S(1)} %collective-permute-done.refs_0_.refs_3_, ...), custom_call_target="tpu_custom_call" | custom-call | flops 15728640 | bytes 990720 | tf_op jit(solution)/shard_map/pallas_call | solution.py:46
  10.5 4.1 %collective-permute-start.3 = (bf16[96,256]{1,0:T(8,128)(2,1)S(1)}, bf16[96,256]{1,0:T(8,128)(2,1)S(1)}, u32[]{:S(2)}, u32[]{:S(2)}) collective-permute-start(bf16[96,256]{1,0:T(8,128)(2,1)S(1)} %get-tuple-element.36), channel_id=1, source_target_pairs={{0,12},{4,8},{8,4},{12,0},{1,13},{5,9},{9,5},{13,1},{2,14},{6,10},... | collective-permute-start | bytes 147464 | tf_op jit(solution)/shard_map/ppermute | solution.py:17
  14.7 0.0 collective-permute-start.4
  14.7 0.6 %collective-permute-start.5 = (bf16[96,256]{1,0:T(8,128)(2,1)S(1)}, bf16[96,256]{1,0:T(8,128)(2,1)S(1)}, u32[]{:S(2)}, u32[]{:S(2)}) collective-permute-start(bf16[96,256]{1,0:T(8,128)(2,1)S(1)} %get-tuple-element.38), channel_id=1, source_target_pairs={{0,4},{4,0},{8,12},{12,8},{1,5},{5,1},{9,13},{13,9},{2,6},{6,2},{1... | collective-permute-start | bytes 147464 | tf_op jit(solution)/shard_map/ppermute | solution.py:17
  15.3 0.0 collective-permute-done.6.refs_0_.refs_5_
  15.3 1.2 %collective-permute-done.7.refs_1_.refs_4_ = bf16[240,256]{1,0:T(8,128)(2,1)S(1)} collective-permute-done((bf16[240,256]{1,0:T(8,128)(2,1)S(1)}, bf16[240,256]{1,0:T(8,128)(2,1)S(1)}, u32[]{:S(2)}, u32[]{:S(2)}) %collective-permute-start.7) | collective-permute-done | bytes 122912 | tf_op jit(solution)/shard_map/ppermute | solution.py:17
  16.5 0.5 %collective-permute-done.3.refs_5_.refs_2_.refs_0_ = bf16[96,256]{1,0:T(8,128)(2,1)S(1)} collective-permute-done((bf16[96,256]{1,0:T(8,128)(2,1)S(1)}, bf16[96,256]{1,0:T(8,128)(2,1)S(1)}, u32[]{:S(2)}, u32[]{:S(2)}) %collective-permute-start.3) | collective-permute-done | bytes 49184 | tf_op jit(solution)/shard_map/ppermute | solution.py:17
  17.0 0.5 %shard_map.53 = (bf16[144,256]{1,0:T(8,128)(2,1)S(1)}, bf16[144,256]{1,0:T(8,128)(2,1)S(1)}, bf16[144,256]{1,0:T(8,128)(2,1)S(1)}, bf16[144,256]{1,0:T(8,128)(2,1)S(1)}, bf16[4,144,256]{2,1,0:T(8,128)(2,1)S(1)}) custom-call(bf16[240,256]{1,0:T(8,128)(2,1)S(1)} %collective-permute-done.6.refs_0_.refs_5_, ...), custom_call_target="tpu_custom_call" | custom-call | flops 23592960 | bytes 1261056 | tf_op jit(solution)/shard_map/pallas_call | solution.py:46
  17.5 4.0 %collective-permute-start.8 = (bf16[144,256]{1,0:T(8,128)(2,1)S(1)}, bf16[144,256]{1,0:T(8,128)(2,1)S(1)}, u32[]{:S(2)}, u32[]{:S(2)}) collective-permute-start(bf16[144,256]{1,0:T(8,128)(2,1)S(1)} %get-tuple-element.43), channel_id=1, source_target_pairs={{0,12},{4,8},{8,4},{12,0},{1,13},{5,9},{9,5},{13,1},{2,14},{6,10},... | collective-permute-start | bytes 221192 | tf_op jit(solution)/shard_map/ppermute | solution.py:17
  21.5 0.0 collective-permute-done.4.refs_3_.refs_1_
  21.5 0.0 collective-permute-done.5.refs_4_.refs_2_
  21.5 0.1 collective-permute-start.11
  21.6 0.3 collective-permute-start.9
  21.9 0.5 %collective-permute-start.10 = (bf16[144,256]{1,0:T(8,128)(2,1)S(1)}, bf16[144,256]{1,0:T(8,128)(2,1)S(1)}, u32[]{:S(2)}, u32[]{:S(2)}) collective-permute-start(bf16[144,256]{1,0:T(8,128)(2,1)S(1)} %get-tuple-element.45), channel_id=1, source_target_pairs={{0,4},{4,0},{8,12},{12,8},{1,5},{5,1},{9,13},{13,9},{2,6},{6,2},{1... | collective-permute-start | bytes 221192 | tf_op jit(solution)/shard_map/ppermute | solution.py:17
  22.4 1.6 %collective-permute-start.19 = (bf16[240,256]{1,0:T(8,128)(2,1)S(1)}, bf16[240,256]{1,0:T(8,128)(2,1)S(1)}, u32[]{:S(2)}, u32[]{:S(2)}) collective-permute-start(bf16[240,256]{1,0:T(8,128)(2,1)S(1)} %get-tuple-element.59), channel_id=1, source_target_pairs={{0,2},{1,3},{2,0},{3,1},{4,6},{5,7},{6,4},{7,5},{8,10},{9,11},{10,... | collective-permute-start | bytes 368648 | tf_op jit(solution)/shard_map/ppermute | solution.py:17
  24.0 0.2 collective-permute-done.8.refs_4_
  24.2 0.0 collective-permute-start.20
  24.2 0.5 %shard_map.54.refs_8_ = f32[40,128]{1,0:T(8,128)S(1)} custom-call(bf16[408,256]{1,0:T(8,128)(2,1)S(1)} %get-tuple-element.35.refs_3_.refs_0_, bf16[408,256]{1,0:T(8,128)(2,1)S(1)} %collective-permute-done.2.refs_2_.refs_1_, bf16[168,256]{1,0:T(8,128)(2,1)S(1)} %collective-permute-done.1.refs_1_.refs_2_, ...), custom_call_target="tpu_custom_call" | custom-call | flops 65536000 | bytes 856064 | tf_op jit(solution)/shard_map/pallas_call | solution.py:46
  24.7 2.6 %collective-permute-done.9.refs_5_ = bf16[144,256]{1,0:T(8,128)(2,1)S(1)} collective-permute-done((bf16[144,256]{1,0:T(8,128)(2,1)S(1)}, bf16[144,256]{1,0:T(8,128)(2,1)S(1)}, u32[]{:S(2)}, u32[]{:S(2)}) %collective-permute-start.9) | collective-permute-done | bytes 73760 | tf_op jit(solution)/shard_map/ppermute | solution.py:17
  27.3 0.6 %collective-permute-done.10.refs_6_ = bf16[144,256]{1,0:T(8,128)(2,1)S(1)} collective-permute-done((bf16[144,256]{1,0:T(8,128)(2,1)S(1)}, bf16[144,256]{1,0:T(8,128)(2,1)S(1)}, u32[]{:S(2)}, u32[]{:S(2)}) %collective-permute-start.10) | collective-permute-done | bytes 73760 | tf_op jit(solution)/shard_map/ppermute | solution.py:17
  27.9 0.0 collective-permute-done.11.refs_9_.refs_1_
  27.9 0.3 shard_map.56
  28.2 2.0 %collective-permute-start.12 = (f32[60,128]{1,0:T(8,128)S(1)}, f32[60,128]{1,0:T(8,128)S(1)}, u32[]{:S(2)}, u32[]{:S(2)}) collective-permute-start(f32[60,128]{1,0:T(8,128)S(1)} %get-tuple-element.50), channel_id=1, source_target_pairs={{0,12},{4,8},{8,4},{12,0},{1,13},{5,9},{9,5},{13,1},{2,14},{6,10},... | collective-permute-start | bytes 92168 | tf_op jit(solution)/shard_map/ppermute | solution.py:17
  30.3 0.6 %collective-permute-start.13 = (f32[60,128]{1,0:T(8,128)S(1)}, f32[60,128]{1,0:T(8,128)S(1)}, u32[]{:S(2)}, u32[]{:S(2)}) collective-permute-start(f32[60,128]{1,0:T(8,128)S(1)} %get-tuple-element.51), channel_id=1, source_target_pairs={{0,8},{4,12},{8,0},{12,4},{1,9},{5,13},{9,1},{13,5},{2,10},{6,14},... | collective-permute-start | bytes 92168 | tf_op jit(solution)/shard_map/ppermute | solution.py:17
  30.9 1.8 %collective-permute-start.14 = (f32[60,128]{1,0:T(8,128)S(1)}, f32[60,128]{1,0:T(8,128)S(1)}, u32[]{:S(2)}, u32[]{:S(2)}) collective-permute-start(f32[60,128]{1,0:T(8,128)S(1)} %get-tuple-element.52), channel_id=1, source_target_pairs={{0,4},{4,0},{8,12},{12,8},{1,5},{5,1},{9,13},{13,9},{2,6},{6,2},{1... | collective-permute-start | bytes 92168 | tf_op jit(solution)/shard_map/ppermute | solution.py:17
  32.7 1.4 %collective-permute-done.12.refs_0_ = f32[60,128]{1,0:T(8,128)S(1)} collective-permute-done((f32[60,128]{1,0:T(8,128)S(1)}, f32[60,128]{1,0:T(8,128)S(1)}, u32[]{:S(2)}, u32[]{:S(2)}) %collective-permute-start.12) | collective-permute-done | bytes 30752 | tf_op jit(solution)/shard_map/ppermute | solution.py:17
  34.1 1.0 %collective-permute-done.13.refs_1_ = f32[60,128]{1,0:T(8,128)S(1)} collective-permute-done((f32[60,128]{1,0:T(8,128)S(1)}, f32[60,128]{1,0:T(8,128)S(1)}, u32[]{:S(2)}, u32[]{:S(2)}) %collective-permute-start.13) | collective-permute-done | bytes 30752 | tf_op jit(solution)/shard_map/ppermute | solution.py:17
  35.1 0.2 collective-permute-done.14.refs_2_
  35.3 0.2 shard_map.57
  35.5 0.1 collective-permute-start.15
  35.6 1.5 %collective-permute-start.16 = (f32[40,80]{1,0:T(8,128)S(1)}, f32[40,80]{1,0:T(8,128)S(1)}, u32[]{:S(2)}, u32[]{:S(2)}) collective-permute-start(f32[40,80]{1,0:T(8,128)S(1)} %get-tuple-element.55), channel_id=1, source_target_pairs={{0,2},{1,3},{2,0},{3,1},{4,6},{5,7},{6,4},{7,5},{8,10},{9,11},{10,... | collective-permute-start | bytes 38408 | tf_op jit(solution)/shard_map/ppermute | solution.py:17
  37.1 0.3 collective-permute-start.17
  37.4 1.6 %collective-permute-done.15.refs_0_ = f32[40,80]{1,0:T(8,128)S(1)} collective-permute-done((f32[40,80]{1,0:T(8,128)S(1)}, f32[40,80]{1,0:T(8,128)S(1)}, u32[]{:S(2)}, u32[]{:S(2)}) %collective-permute-start.15) | collective-permute-done | bytes 12832 | tf_op jit(solution)/shard_map/ppermute | solution.py:17
  39.0 0.4 %collective-permute-done.16.refs_1_ = f32[40,80]{1,0:T(8,128)S(1)} collective-permute-done((f32[40,80]{1,0:T(8,128)S(1)}, f32[40,80]{1,0:T(8,128)S(1)}, u32[]{:S(2)}, u32[]{:S(2)}) %collective-permute-start.16) | collective-permute-done | bytes 12832 | tf_op jit(solution)/shard_map/ppermute | solution.py:17
  39.4 0.0 collective-permute-done.17.refs_2_
  39.4 1.4 %collective-permute-start.18 = (f32[40,80]{1,0:T(8,128)S(1)}, f32[40,80]{1,0:T(8,128)S(1)}, u32[]{:S(2)}, u32[]{:S(2)}) collective-permute-start(f32[40,80]{1,0:T(8,128)S(1)} %shard_map.58), channel_id=1, source_target_pairs={{0,16},{16,0},{1,17},{17,1},{2,18},{18,2},{3,19},{19,3},{4,20},{20... | collective-permute-start | bytes 38408 | tf_op jit(solution)/shard_map/ppermute | solution.py:17
  40.9 0.0 collective-permute-done.19.refs_2_
  40.9 0.0 collective-permute-done.20.refs_3_
  40.9 0.9 %shard_map.59 = bf16[12,20,1024]{2,1,0:T(8,128)(2,1)} custom-call(bf16[240,256]{1,0:T(8,128)(2,1)S(1)} %get-tuple-element.58.refs_0_, bf16[240,256]{1,0:T(8,128)(2,1)S(1)} %collective-permute-done.11.refs_9_.refs_1_, bf16[240,256]{1,0:T(8,128)(2,1)S(1)} %collective-permute-done.19.refs_2_, bf16[240,256]{1,0:T(8,128)(2,1)S(1)} %collective-permute-done.20.refs_3_), custom_call_target="tpu_custom_call" | custom-call | bytes 983040 | tf_op jit(solution)/shard_map/pallas_call | solution.py:46
  41.8 1.5 %collective-permute-done.18 = f32[40,80]{1,0:T(8,128)S(1)} collective-permute-done((f32[40,80]{1,0:T(8,128)S(1)}, f32[40,80]{1,0:T(8,128)S(1)}, u32[]{:S(2)}, u32[]{:S(2)}) %collective-permute-start.18) | collective-permute-done | bytes 12832 | tf_op jit(solution)/shard_map/ppermute | solution.py:17
  43.3 0.6 %fusion = (f32[20,80]{1,0:T(8,128)}, f32[20,80]{1,0:T(8,128)}) fusion(f32[40,80]{1,0:T(8,128)S(1)} %add.3), kind=kLoop, calls=%fused_computation | loop fusion | bytes 25600 | tf_op jit(solution)/shard_map/slice | solution.py:299
  (5 shorter events, 0.1 us)
Async XLA Ops:
  0.6 1.2 %copy-start = (bf16[20,20,1024]{2,1,0:T(8,128)(2,1)S(1)}, bf16[20,20,1024]{2,1,0:T(8,128)(2,1)}, u32[]{:S(2)}) copy-start(bf16[20,20,1024]{2,1,0:T(8,128)(2,1)} %slab_ref.3) | copy-start | bytes 2457604
  0.6 1.2 %copy-start.1 = (bf16[20,48]{1,0:T(8,128)(2,1)S(1)}, bf16[20,48]{1,0:T(8,128)(2,1)}, u32[]{:S(2)}) copy-start(bf16[20,48]{1,0:T(8,128)(2,1)} %refs_0_.1) | copy-start | bytes 5764
  2.0 8.1 %collective-permute-start.2 = (bf16[408,256]{1,0:T(8,128)(2,1)S(1)}, bf16[408,256]{1,0:T(8,128)(2,1)S(1)}, u32[]{:S(2)}, u32[]{:S(2)}) collective-permute-start(bf16[408,256]{1,0:T(8,128)(2,1)S(1)} %get-tuple-element.34), channel_id=1, source_target_pairs={{0,1},{1,0},{2,3},{3,2},{4,5},{5,4},{6,7},{7,6},{8,9},{9,8},{10,11... | collective-permute-start | bytes 626696 | tf_op jit(solution)/shard_map/ppermute | solution.py:17
  2.5 5.5 %collective-permute-start = (bf16[168,256]{1,0:T(8,128)(2,1)S(1)}, bf16[168,256]{1,0:T(8,128)(2,1)S(1)}, u32[]{:S(2)}, u32[]{:S(2)}) collective-permute-start(bf16[168,256]{1,0:T(8,128)(2,1)S(1)} %get-tuple-element.32), channel_id=1, source_target_pairs={{0,3},{1,2},{2,1},{3,0},{4,7},{5,6},{6,5},{7,4},{8,11},{9,10},{10,... | collective-permute-start | bytes 258056 | tf_op jit(solution)/shard_map/ppermute | solution.py:17
  5.1 4.9 %collective-permute-start.1 = (bf16[168,256]{1,0:T(8,128)(2,1)S(1)}, bf16[168,256]{1,0:T(8,128)(2,1)S(1)}, u32[]{:S(2)}, u32[]{:S(2)}) collective-permute-start(bf16[168,256]{1,0:T(8,128)(2,1)S(1)} %get-tuple-element.33), channel_id=1, source_target_pairs={{0,2},{1,3},{2,0},{3,1},{4,6},{5,7},{6,4},{7,5},{8,10},{9,11},{10,... | collective-permute-start | bytes 258056 | tf_op jit(solution)/shard_map/ppermute | solution.py:17
  8.0 7.3 %collective-permute-start.6 = (bf16[240,256]{1,0:T(8,128)(2,1)S(1)}, bf16[240,256]{1,0:T(8,128)(2,1)S(1)}, u32[]{:S(2)}, u32[]{:S(2)}) collective-permute-start(bf16[240,256]{1,0:T(8,128)(2,1)S(1)} %get-tuple-element.40), channel_id=1, source_target_pairs={{0,3},{1,2},{2,1},{3,0},{4,7},{5,6},{6,5},{7,4},{8,11},{9,10},{10,... | collective-permute-start | bytes 368648 | tf_op jit(solution)/shard_map/ppermute | solution.py:17
  10.0 6.5 %collective-permute-start.7 = (bf16[240,256]{1,0:T(8,128)(2,1)S(1)}, bf16[240,256]{1,0:T(8,128)(2,1)S(1)}, u32[]{:S(2)}, u32[]{:S(2)}) collective-permute-start(bf16[240,256]{1,0:T(8,128)(2,1)S(1)} %get-tuple-element.41), channel_id=1, source_target_pairs={{0,2},{1,3},{2,0},{3,1},{4,6},{5,7},{6,4},{7,5},{8,10},{9,11},{10,... | collective-permute-start | bytes 368648 | tf_op jit(solution)/shard_map/ppermute | solution.py:17
  10.5 6.4 %collective-permute-start.3 = (bf16[96,256]{1,0:T(8,128)(2,1)S(1)}, bf16[96,256]{1,0:T(8,128)(2,1)S(1)}, u32[]{:S(2)}, u32[]{:S(2)}) collective-permute-start(bf16[96,256]{1,0:T(8,128)(2,1)S(1)} %get-tuple-element.36), channel_id=1, source_target_pairs={{0,12},{4,8},{8,4},{12,0},{1,13},{5,9},{9,5},{13,1},{2,14},{6,10},... | collective-permute-start | bytes 147464 | tf_op jit(solution)/shard_map/ppermute | solution.py:17
  14.7 6.8 %collective-permute-start.4 = (bf16[96,256]{1,0:T(8,128)(2,1)S(1)}, bf16[96,256]{1,0:T(8,128)(2,1)S(1)}, u32[]{:S(2)}, u32[]{:S(2)}) collective-permute-start(bf16[96,256]{1,0:T(8,128)(2,1)S(1)} %get-tuple-element.37), channel_id=1, source_target_pairs={{0,8},{4,12},{8,0},{12,4},{1,9},{5,13},{9,1},{13,5},{2,10},{6,14},... | collective-permute-start | bytes 147464 | tf_op jit(solution)/shard_map/ppermute | solution.py:17
  14.7 6.8 %collective-permute-start.5 = (bf16[96,256]{1,0:T(8,128)(2,1)S(1)}, bf16[96,256]{1,0:T(8,128)(2,1)S(1)}, u32[]{:S(2)}, u32[]{:S(2)}) collective-permute-start(bf16[96,256]{1,0:T(8,128)(2,1)S(1)} %get-tuple-element.38), channel_id=1, source_target_pairs={{0,4},{4,0},{8,12},{12,8},{1,5},{5,1},{9,13},{13,9},{2,6},{6,2},{1... | collective-permute-start | bytes 147464 | tf_op jit(solution)/shard_map/ppermute | solution.py:17
  17.5 6.7 %collective-permute-start.8 = (bf16[144,256]{1,0:T(8,128)(2,1)S(1)}, bf16[144,256]{1,0:T(8,128)(2,1)S(1)}, u32[]{:S(2)}, u32[]{:S(2)}) collective-permute-start(bf16[144,256]{1,0:T(8,128)(2,1)S(1)} %get-tuple-element.43), channel_id=1, source_target_pairs={{0,12},{4,8},{8,4},{12,0},{1,13},{5,9},{9,5},{13,1},{2,14},{6,10},... | collective-permute-start | bytes 221192 | tf_op jit(solution)/shard_map/ppermute | solution.py:17
  21.5 6.3 %collective-permute-start.11 = (bf16[240,256]{1,0:T(8,128)(2,1)S(1)}, bf16[240,256]{1,0:T(8,128)(2,1)S(1)}, u32[]{:S(2)}, u32[]{:S(2)}) collective-permute-start(bf16[240,256]{1,0:T(8,128)(2,1)S(1)} %get-tuple-element.49), channel_id=1, source_target_pairs={{0,1},{1,0},{2,3},{3,2},{4,5},{5,4},{6,7},{7,6},{8,9},{9,8},{10,11... | collective-permute-start | bytes 368648 | tf_op jit(solution)/shard_map/ppermute | solution.py:17
  21.6 5.7 %collective-permute-start.9 = (bf16[144,256]{1,0:T(8,128)(2,1)S(1)}, bf16[144,256]{1,0:T(8,128)(2,1)S(1)}, u32[]{:S(2)}, u32[]{:S(2)}) collective-permute-start(bf16[144,256]{1,0:T(8,128)(2,1)S(1)} %get-tuple-element.44), channel_id=1, source_target_pairs={{0,8},{4,12},{8,0},{12,4},{1,9},{5,13},{9,1},{13,5},{2,10},{6,14},... | collective-permute-start | bytes 221192 | tf_op jit(solution)/shard_map/ppermute | solution.py:17
  21.9 6.0 %collective-permute-start.10 = (bf16[144,256]{1,0:T(8,128)(2,1)S(1)}, bf16[144,256]{1,0:T(8,128)(2,1)S(1)}, u32[]{:S(2)}, u32[]{:S(2)}) collective-permute-start(bf16[144,256]{1,0:T(8,128)(2,1)S(1)} %get-tuple-element.45), channel_id=1, source_target_pairs={{0,4},{4,0},{8,12},{12,8},{1,5},{5,1},{9,13},{13,9},{2,6},{6,2},{1... | collective-permute-start | bytes 221192 | tf_op jit(solution)/shard_map/ppermute | solution.py:17
  22.4 18.5 %collective-permute-start.19 = (bf16[240,256]{1,0:T(8,128)(2,1)S(1)}, bf16[240,256]{1,0:T(8,128)(2,1)S(1)}, u32[]{:S(2)}, u32[]{:S(2)}) collective-permute-start(bf16[240,256]{1,0:T(8,128)(2,1)S(1)} %get-tuple-element.59), channel_id=1, source_target_pairs={{0,2},{1,3},{2,0},{3,1},{4,6},{5,7},{6,4},{7,5},{8,10},{9,11},{10,... | collective-permute-start | bytes 368648 | tf_op jit(solution)/shard_map/ppermute | solution.py:17
  24.2 16.7 %collective-permute-start.20 = (bf16[240,256]{1,0:T(8,128)(2,1)S(1)}, bf16[240,256]{1,0:T(8,128)(2,1)S(1)}, u32[]{:S(2)}, u32[]{:S(2)}) collective-permute-start(bf16[240,256]{1,0:T(8,128)(2,1)S(1)} %get-tuple-element.60), channel_id=1, source_target_pairs={{0,3},{1,2},{2,1},{3,0},{4,7},{5,6},{6,5},{7,4},{8,11},{9,10},{10,... | collective-permute-start | bytes 368648 | tf_op jit(solution)/shard_map/ppermute | solution.py:17
  28.2 5.9 %collective-permute-start.12 = (f32[60,128]{1,0:T(8,128)S(1)}, f32[60,128]{1,0:T(8,128)S(1)}, u32[]{:S(2)}, u32[]{:S(2)}) collective-permute-start(f32[60,128]{1,0:T(8,128)S(1)} %get-tuple-element.50), channel_id=1, source_target_pairs={{0,12},{4,8},{8,4},{12,0},{1,13},{5,9},{9,5},{13,1},{2,14},{6,10},... | collective-permute-start | bytes 92168 | tf_op jit(solution)/shard_map/ppermute | solution.py:17
  30.3 4.9 %collective-permute-start.13 = (f32[60,128]{1,0:T(8,128)S(1)}, f32[60,128]{1,0:T(8,128)S(1)}, u32[]{:S(2)}, u32[]{:S(2)}) collective-permute-start(f32[60,128]{1,0:T(8,128)S(1)} %get-tuple-element.51), channel_id=1, source_target_pairs={{0,8},{4,12},{8,0},{12,4},{1,9},{5,13},{9,1},{13,5},{2,10},{6,14},... | collective-permute-start | bytes 92168 | tf_op jit(solution)/shard_map/ppermute | solution.py:17
  30.9 4.5 %collective-permute-start.14 = (f32[60,128]{1,0:T(8,128)S(1)}, f32[60,128]{1,0:T(8,128)S(1)}, u32[]{:S(2)}, u32[]{:S(2)}) collective-permute-start(f32[60,128]{1,0:T(8,128)S(1)} %get-tuple-element.52), channel_id=1, source_target_pairs={{0,4},{4,0},{8,12},{12,8},{1,5},{5,1},{9,13},{13,9},{2,6},{6,2},{1... | collective-permute-start | bytes 92168 | tf_op jit(solution)/shard_map/ppermute | solution.py:17
  35.5 3.5 %collective-permute-start.15 = (f32[40,80]{1,0:T(8,128)S(1)}, f32[40,80]{1,0:T(8,128)S(1)}, u32[]{:S(2)}, u32[]{:S(2)}) collective-permute-start(f32[40,80]{1,0:T(8,128)S(1)} %get-tuple-element.54), channel_id=1, source_target_pairs={{0,3},{1,2},{2,1},{3,0},{4,7},{5,6},{6,5},{7,4},{8,11},{9,10},{10,... | collective-permute-start | bytes 38408 | tf_op jit(solution)/shard_map/ppermute | solution.py:17
  35.6 3.8 %collective-permute-start.16 = (f32[40,80]{1,0:T(8,128)S(1)}, f32[40,80]{1,0:T(8,128)S(1)}, u32[]{:S(2)}, u32[]{:S(2)}) collective-permute-start(f32[40,80]{1,0:T(8,128)S(1)} %get-tuple-element.55), channel_id=1, source_target_pairs={{0,2},{1,3},{2,0},{3,1},{4,6},{5,7},{6,4},{7,5},{8,10},{9,11},{10,... | collective-permute-start | bytes 38408 | tf_op jit(solution)/shard_map/ppermute | solution.py:17
  37.1 2.3 %collective-permute-start.17 = (f32[40,80]{1,0:T(8,128)S(1)}, f32[40,80]{1,0:T(8,128)S(1)}, u32[]{:S(2)}, u32[]{:S(2)}) collective-permute-start(f32[40,80]{1,0:T(8,128)S(1)} %get-tuple-element.56), channel_id=1, source_target_pairs={{0,1},{1,0},{2,3},{3,2},{4,5},{5,4},{6,7},{7,6},{8,9},{9,8},{10,11... | collective-permute-start | bytes 38408 | tf_op jit(solution)/shard_map/ppermute | solution.py:17
  39.4 3.8 %collective-permute-start.18 = (f32[40,80]{1,0:T(8,128)S(1)}, f32[40,80]{1,0:T(8,128)S(1)}, u32[]{:S(2)}, u32[]{:S(2)}) collective-permute-start(f32[40,80]{1,0:T(8,128)S(1)} %shard_map.58), channel_id=1, source_target_pairs={{0,16},{16,0},{1,17},{17,1},{2,18},{18,2},{3,19},{19,3},{4,20},{20... | collective-permute-start | bytes 38408 | tf_op jit(solution)/shard_map/ppermute | solution.py:17

commit v4 on v3

--- a/solution.py
+++ b/solution.py
@@ -31,14 +31,6 @@
     for value in values[-2::-1]:
         total = total + value
     return total
-
-
-def doubled(value, axis):
-    step = 1
-    while step < lax.axis_size(axis):
-        value = value + swap(value, axis, step)
-        step *= 2
-    return value
 
 
 def call(kernel, out_shape, scratch, flops, args, unused=()):
@@ -137,23 +129,40 @@
         gram += nt(page, page)
     gram *= scale
     half = views * rows // 2
-    quarters = jnp.concatenate([gram[:half], gram[half:, half:]], axis=1)
-    out[...] = jnp.pad(quarters, ((0, 0), (0, out.shape[1] - 3 * half)))
-
-
-def deal_kernel(lights, rows, views, *refs):
-    ins, outs, (blocks,) = cut(refs, len(refs) - views - 1, views)
-    v = lax.axis_index("view")
-    total = summed([ref[...] for ref in ins])
-    light, quarters = total[:lights, : outs[0].shape[1]], total[lights:]
-    half = views * rows // 2
-    cross = quarters[:, half : 2 * half]
-    lower = jnp.concatenate([cross.T, quarters[:, 2 * half : 3 * half]], axis=1)
-    gram = jnp.concatenate([quarters[:, : 2 * half], lower], axis=0)
-    for k in range(views):
-        blocks[k] = gram[k * rows : (k + 1) * rows]
-    for k in range(views):
-        outs[k][...] = jnp.concatenate([light, blocks[v ^ k]], axis=0)
+    left = jnp.zeros((out.shape[1], out.shape[2] - half), f32)
+    for p in range(2):
+        mine = jnp.concatenate([gram[k * rows : (k + 1) * rows] for k in range(p, views, 2)], axis=0)
+        mine = jnp.concatenate([mine[:, :half], mine[:, half:]], axis=0)
+        out[p] = jnp.concatenate([left, mine], axis=1)
+
+
+def deal_light_kernel(lights, parts, keep_ref, came_ref, *refs):
+    outs, blocks = refs[:-1], refs[-1]
+    z = lax.axis_index("light")
+    total = keep_ref[...] + came_ref[...]
+    wide = lights * parts
+    tall = total.shape[0] // 2
+    view = total[:, total.shape[1] - tall :]
+    view = jnp.concatenate([view[:tall], view[tall:]], axis=1)
+    for k in range(parts):
+        light = total[k * lights : (k + 1) * lights, :wide]
+        light = jnp.concatenate([light[:, : wide // 2], light[:, wide // 2 :]], axis=0)
+        blocks[k] = jnp.concatenate([view, light], axis=1)
+    for k in range(parts):
+        outs[k][...] = blocks[z ^ k]
+
+
+def deal_view_kernel(lights, rows, *refs):
+    total_ref, outs, blocks = refs[0], refs[1:-1], refs[-1]
+    u = lax.axis_index("view") // 2
+    total = total_ref[...]
+    wide = 2 * rows * len(outs)
+    light = total[:, wide:]
+    light = jnp.concatenate([light[:lights], light[lights:]], axis=1)
+    for m in range(len(outs)):
+        blocks[m] = jnp.concatenate([light, total[m * rows : (m + 1) * rows, :wide]], axis=0)
+    for m in range(len(outs)):
+        outs[m][...] = blocks[u ^ m]
 
 
 def sum_kernel(*refs):
@@ -161,7 +170,7 @@
 
 
 def light_kernel(counts, spare, parts, scale, *refs):
-    ins, (view,), _, outs, wholes, (blocks,) = cut(refs, parts * len(counts), 1, spare, parts, len(counts))
+    ins, (view,), _, (keep_out, send_out), wholes = cut(refs, parts * len(counts), 1, spare, 2)
     z, lights = lax.axis_index("light"), sum(counts)
     for c, whole in enumerate(wholes):
         for i, k in enumerate(farthest_first(parts)):
@@ -172,11 +181,10 @@
         page = jnp.concatenate(page, axis=0)
         gram += nt(page, page)
     gram *= scale
-    for k in range(parts):
-        blocks[k] = gram[k * lights : (k + 1) * lights]
-    for k in range(parts):
-        block = jnp.pad(blocks[z ^ k], ((0, 0), (0, view.shape[1] - parts * lights)))
-        outs[k][...] = jnp.concatenate([block, view[...]], axis=0)
+    gram = jnp.pad(gram, ((0, keep_out.shape[0] - gram.shape[0]), (0, keep_out.shape[1] - gram.shape[1])))
+    parity = lax.axis_index("view") % 2
+    keep_out[...] = gram + view[parity]
+    send_out[...] = gram + view[1 - parity]
 
 
 def place_kernel(counts, *refs):
@@ -262,33 +270,45 @@
         functools.partial(back_kernel, 2), [sds((size * lights, width), bf16)] * views, [], 0, pieces, lit[: parts - 1]
     )
     spans = [(k, 0) for k in range(half)] + [(k, c * tall[0]) for c in range(2) for k in range(half, views)]
-    wide = -(-max(3 * views_all // 2, lights_all) // 128) * 128
+    wide = lights_all + views_all // 2
+    both = max(lights_all, views_all)
     view_part = call(
         functools.partial(view_kernel, lights, rows, views, spans, view_scale),
-        sds((views_all // 2, wide), f32),
+        sds((2, both, wide), f32),
         [pltpu.VMEM((views, head + lights * rows, width), bf16)],
         2 * views_all * lights * width * views_all,
         near + whole[0] + whole[1],
     )
     returned = swaps(back, "view")
-    sums = call(
+    keep, send = call(
         functools.partial(light_kernel, counts, 1, parts, light_scale),
-        [sds((lights + views_all // 2, wide), f32)] * parts,
-        [pltpu.VMEM((parts, size * count, width), bf16) for count in counts]
-        + [pltpu.VMEM((parts, lights, lights_all), f32)],
+        [sds((both, wide), f32)] * 2,
+        [pltpu.VMEM((parts, size * count, width), bf16) for count in counts],
         2 * lights_all * lights_all * size * width,
         lit + [view_part],
         [returned[1]],
     )
     dealt = call(
-        functools.partial(deal_kernel, lights, rows, views),
-        [sds((lights + rows, lights_all), f32)] * views,
-        [pltpu.VMEM((views, rows, views_all), f32)],
-        0,
-        swaps(sums, "light")[::-1],
-    )
-    total = call(sum_kernel, sds((lights + rows, lights_all), f32), [], 0, swaps(dealt, "view")[::-1])
-    total = doubled(total, "texel")
+        functools.partial(deal_light_kernel, lights, parts),
+        [sds((views_all // 2, views_all + lights_all // 2), f32)] * parts,
+        [pltpu.VMEM((parts, views_all // 2, views_all + lights_all // 2), f32)],
+        0,
+        [keep, swap(send, "view", 1)],
+    )
+    total = call(sum_kernel, sds(dealt[0].shape, f32), [], 0, swaps(dealt, "light")[::-1])
+    texels, step = lax.axis_size("texel"), 2
+    while step < texels:
+        total = total + swap(total, "texel", step)
+        step *= 2
+    dealt = call(
+        functools.partial(deal_view_kernel, lights, rows),
+        [sds((lights + rows, views_all), f32)] * half,
+        [pltpu.VMEM((half, lights + rows, views_all), f32)],
+        0,
+        [total],
+    )
+    steps = [(t, m) for t in range(min(2, texels) - 1, -1, -1) for m in range(half - 1, -1, -1)]
+    total = summed([dealt[0]] + [swap(dealt[m], ("texel", "view"), t * views + 2 * m) for t, m in steps[:-1]])
     core = call(
         functools.partial(place_kernel, counts),
         sds((ranks // views, lights, columns), bf16),

time: 44 us -> 46.4 us (1.055)
  waiting for transfers between devices: 14.1 us -> 16.1 us
    ppermute x21, waiting for transfers between devices: 14.1 us -> 16.1 us  [swap(): lax.ppermute(value, axis, [(i, i ^ step) for i in range(lax.axis_size(axi...]
    pallas_call x11 -> x12, Pallas kernels: 3.07 us -> 3.21 us  [call(): pl.pallas_call(kernel, out_shape=out_shape, in_specs=[VMEM] * len(args) +...]
where the time goes in v4:
time: 46.4 us; the launch traced here: 46.2 us
  starting transfers between devices  24.4 us (53%)
  waiting for transfers between devices  16.1 us (35%)
  Pallas kernels  3.21 us (7%)
  local copies, waits for them, and re-layouts  1.79 us (4%)
  between operations  0.74 us (2%)
    ppermute x21, starting transfers between devices, swap(): lax.ppermute(value, axis, [(i, i ^ step) for i in range(lax.axis_size(axi...  24.4 us
    ppermute x21, waiting for transfers between devices, swap(): lax.ppermute(value, axis, [(i, i ^ step) for i in range(lax.axis_size(axi...  16.1 us
    pallas_call x12, Pallas kernels, call(): pl.pallas_call(kernel, out_shape=out_shape, in_specs=[VMEM] * len(args) +...  3.21 us
    unnamed x4, local copies, waits for them, and re-layouts  1.18 us
  transfers between devices with their start and end apart: 21, of which 12 were waited for; matrix products, arithmetic and copies ran while one was open for 0% of the time, Pallas kernels for 7%

profile of v4, /device:TPU:0, one launch (start us, length us, event | category | flops | bytes accessed | tf_op | source)
XLA Modules:
  0.0 46.2 jit_solution(11455572002744563053)
XLA Ops:
  0.6 0.0 copy-start
  0.6 0.0 copy-start.1
  0.7 1.2 %copy-done = bf16[20,20,1024]{2,1,0:T(8,128)(2,1)S(1)} copy-done((bf16[20,20,1024]{2,1,0:T(8,128)(2,1)S(1)}, bf16[20,20,1024]{2,1,0:T(8,128)(2,1)}, u32[]{:S(2)}) %copy-start) | copy-done | bytes 819224
  1.8 0.0 copy-done.1
  1.8 0.1 shard_map.50
  2.0 0.5 %collective-permute-start.2 = (bf16[408,256]{1,0:T(8,128)(2,1)S(1)}, bf16[408,256]{1,0:T(8,128)(2,1)S(1)}, u32[]{:S(2)}, u32[]{:S(2)}) collective-permute-start(bf16[408,256]{1,0:T(8,128)(2,1)S(1)} %get-tuple-element.34), channel_id=1, source_target_pairs={{0,1},{1,0},{2,3},{3,2},{4,5},{5,4},{6,7},{7,6},{8,9},{9,8},{10,11... | collective-permute-start | bytes 626696 | tf_op jit(solution)/shard_map/ppermute | solution.py:17
  2.5 2.6 %collective-permute-start = (bf16[168,256]{1,0:T(8,128)(2,1)S(1)}, bf16[168,256]{1,0:T(8,128)(2,1)S(1)}, u32[]{:S(2)}, u32[]{:S(2)}) collective-permute-start(bf16[168,256]{1,0:T(8,128)(2,1)S(1)} %get-tuple-element.32), channel_id=1, source_target_pairs={{0,3},{1,2},{2,1},{3,0},{4,7},{5,6},{6,5},{7,4},{8,11},{9,10},{10,... | collective-permute-start | bytes 258056 | tf_op jit(solution)/shard_map/ppermute | solution.py:17
  5.1 0.0 collective-permute-start.1
  5.2 2.8 %collective-permute-done.refs_0_.refs_3_ = bf16[168,256]{1,0:T(8,128)(2,1)S(1)} collective-permute-done((bf16[168,256]{1,0:T(8,128)(2,1)S(1)}, bf16[168,256]{1,0:T(8,128)(2,1)S(1)}, u32[]{:S(2)}, u32[]{:S(2)}) %collective-permute-start) | collective-permute-done | bytes 86048 | tf_op jit(solution)/shard_map/ppermute | solution.py:17
  8.0 2.0 %collective-permute-start.6 = (bf16[240,256]{1,0:T(8,128)(2,1)S(1)}, bf16[240,256]{1,0:T(8,128)(2,1)S(1)}, u32[]{:S(2)}, u32[]{:S(2)}) collective-permute-start(bf16[240,256]{1,0:T(8,128)(2,1)S(1)} %get-tuple-element.40), channel_id=1, source_target_pairs={{0,3},{1,2},{2,1},{3,0},{4,7},{5,6},{6,5},{7,4},{8,11},{9,10},{10,... | collective-permute-start | bytes 368648 | tf_op jit(solution)/shard_map/ppermute | solution.py:17
  10.0 0.0 collective-permute-start.7
  10.0 0.0 collective-permute-done.1.refs_1_.refs_2_
  10.0 0.0 collective-permute-done.2.refs_2_.refs_1_
  10.0 0.5 %shard_map.51 = (bf16[96,256]{1,0:T(8,128)(2,1)S(1)}, bf16[96,256]{1,0:T(8,128)(2,1)S(1)}, bf16[96,256]{1,0:T(8,128)(2,1)S(1)}, bf16[96,256]{1,0:T(8,128)(2,1)S(...) custom-call(bf16[168,256]{1,0:T(8,128)(2,1)S(1)} %collective-permute-done.refs_0_.refs_3_, ...), custom_call_target="tpu_custom_call" | custom-call | flops 15728640 | bytes 990720 | tf_op jit(solution)/shard_map/pallas_call | solution.py:38
  10.5 4.1 %collective-permute-start.3 = (bf16[96,256]{1,0:T(8,128)(2,1)S(1)}, bf16[96,256]{1,0:T(8,128)(2,1)S(1)}, u32[]{:S(2)}, u32[]{:S(2)}) collective-permute-start(bf16[96,256]{1,0:T(8,128)(2,1)S(1)} %get-tuple-element.36), channel_id=1, source_target_pairs={{0,12},{4,8},{8,4},{12,0},{1,13},{5,9},{9,5},{13,1},{2,14},{6,10},... | collective-permute-start | bytes 147464 | tf_op jit(solution)/shard_map/ppermute | solution.py:17
  14.7 0.0 collective-permute-start.4
  14.7 0.6 %collective-permute-start.5 = (bf16[96,256]{1,0:T(8,128)(2,1)S(1)}, bf16[96,256]{1,0:T(8,128)(2,1)S(1)}, u32[]{:S(2)}, u32[]{:S(2)}) collective-permute-start(bf16[96,256]{1,0:T(8,128)(2,1)S(1)} %get-tuple-element.38), channel_id=1, source_target_pairs={{0,4},{4,0},{8,12},{12,8},{1,5},{5,1},{9,13},{13,9},{2,6},{6,2},{1... | collective-permute-start | bytes 147464 | tf_op jit(solution)/shard_map/ppermute | solution.py:17
  15.3 0.0 collective-permute-done.6.refs_0_.refs_5_
  15.3 1.2 %collective-permute-done.7.refs_1_.refs_4_ = bf16[240,256]{1,0:T(8,128)(2,1)S(1)} collective-permute-done((bf16[240,256]{1,0:T(8,128)(2,1)S(1)}, bf16[240,256]{1,0:T(8,128)(2,1)S(1)}, u32[]{:S(2)}, u32[]{:S(2)}) %collective-permute-start.7) | collective-permute-done | bytes 122912 | tf_op jit(solution)/shard_map/ppermute | solution.py:17
  16.5 0.5 %collective-permute-done.3.refs_5_.refs_2_.refs_0_ = bf16[96,256]{1,0:T(8,128)(2,1)S(1)} collective-permute-done((bf16[96,256]{1,0:T(8,128)(2,1)S(1)}, bf16[96,256]{1,0:T(8,128)(2,1)S(1)}, u32[]{:S(2)}, u32[]{:S(2)}) %collective-permute-start.3) | collective-permute-done | bytes 49184 | tf_op jit(solution)/shard_map/ppermute | solution.py:17
  17.0 0.5 shard_map.53
  17.5 2.2 %collective-permute-done.4.refs_3_.refs_1_ = bf16[96,256]{1,0:T(8,128)(2,1)S(1)} collective-permute-done((bf16[96,256]{1,0:T(8,128)(2,1)S(1)}, bf16[96,256]{1,0:T(8,128)(2,1)S(1)}, u32[]{:S(2)}, u32[]{:S(2)}) %collective-permute-start.4) | collective-permute-done | bytes 49184 | tf_op jit(solution)/shard_map/ppermute | solution.py:17
  19.7 0.0 collective-permute-done.5.refs_4_.refs_2_
  19.7 0.1 collective-permute-start.11
  19.8 2.0 %collective-permute-start.8 = (bf16[144,256]{1,0:T(8,128)(2,1)S(1)}, bf16[144,256]{1,0:T(8,128)(2,1)S(1)}, u32[]{:S(2)}, u32[]{:S(2)}) collective-permute-start(bf16[144,256]{1,0:T(8,128)(2,1)S(1)} %get-tuple-element.43), channel_id=1, source_target_pairs={{0,12},{4,8},{8,4},{12,0},{1,13},{5,9},{9,5},{13,1},{2,14},{6,10},... | collective-permute-start | bytes 221192 | tf_op jit(solution)/shard_map/ppermute | solution.py:17
  21.8 0.1 collective-permute-start.9
  22.0 2.3 %collective-permute-start.10 = (bf16[144,256]{1,0:T(8,128)(2,1)S(1)}, bf16[144,256]{1,0:T(8,128)(2,1)S(1)}, u32[]{:S(2)}, u32[]{:S(2)}) collective-permute-start(bf16[144,256]{1,0:T(8,128)(2,1)S(1)} %get-tuple-element.45), channel_id=1, source_target_pairs={{0,4},{4,0},{8,12},{12,8},{1,5},{5,1},{9,13},{13,9},{2,6},{6,2},{1... | collective-permute-start | bytes 221192 | tf_op jit(solution)/shard_map/ppermute | solution.py:17
  24.3 1.5 %collective-permute-start.19 = (bf16[240,256]{1,0:T(8,128)(2,1)S(1)}, bf16[240,256]{1,0:T(8,128)(2,1)S(1)}, u32[]{:S(2)}, u32[]{:S(2)}) collective-permute-start(bf16[240,256]{1,0:T(8,128)(2,1)S(1)} %get-tuple-element.59), channel_id=1, source_target_pairs={{0,2},{1,3},{2,0},{3,1},{4,6},{5,7},{6,4},{7,5},{8,10},{9,11},{10,... | collective-permute-start | bytes 368648 | tf_op jit(solution)/shard_map/ppermute | solution.py:17
  25.8 1.1 %collective-permute-done.8.refs_4_ = bf16[144,256]{1,0:T(8,128)(2,1)S(1)} collective-permute-done((bf16[144,256]{1,0:T(8,128)(2,1)S(1)}, bf16[144,256]{1,0:T(8,128)(2,1)S(1)}, u32[]{:S(2)}, u32[]{:S(2)}) %collective-permute-start.8) | collective-permute-done | bytes 73760 | tf_op jit(solution)/shard_map/ppermute | solution.py:17
  26.8 0.2 collective-permute-start.20
  27.1 0.6 %shard_map.54.refs_8_ = f32[2,80,120]{2,1,0:T(8,128)S(1)} custom-call(bf16[408,256]{1,0:T(8,128)(2,1)S(1)} %get-tuple-element.35.refs_3_.refs_0_, bf16[408,256]{1,0:T(8,128)(2,1)S(1)} %collective-permute-done.2.refs_2_.refs_1_, bf16[168,256]{1,0:T(8,128)(2,1)S(1)} %collective-permute-done.1.refs_1_.refs_2_, ...), custom_call_target="tpu_custom_call" | custom-call | flops 65536000 | bytes 912384 | tf_op jit(solution)/shard_map/pallas_call | solution.py:38
  27.6 1.8 %collective-permute-done.9.refs_5_ = bf16[144,256]{1,0:T(8,128)(2,1)S(1)} collective-permute-done((bf16[144,256]{1,0:T(8,128)(2,1)S(1)}, bf16[144,256]{1,0:T(8,128)(2,1)S(1)}, u32[]{:S(2)}, u32[]{:S(2)}) %collective-permute-start.9) | collective-permute-done | bytes 73760 | tf_op jit(solution)/shard_map/ppermute | solution.py:17
  29.5 0.0 collective-permute-done.10.refs_6_
  29.5 0.0 collective-permute-done.11.refs_9_.refs_1_
  29.5 0.3 shard_map.56
  29.8 0.1 collective-permute-start.12
  30.0 1.2 %collective-permute-done.12.came_ref = f32[80,120]{1,0:T(8,128)S(1)} collective-permute-done((f32[80,120]{1,0:T(8,128)S(1)}, f32[80,120]{1,0:T(8,128)S(1)}, u32[]{:S(2)}, u32[]{:S(2)}) %collective-permute-start.12) | collective-permute-done | bytes 38432 | tf_op jit(solution)/shard_map/ppermute | solution.py:17
  31.1 0.2 shard_map.57
  31.3 2.7 %collective-permute-start.13 = (f32[40,120]{1,0:T(8,128)S(1)}, f32[40,120]{1,0:T(8,128)S(1)}, u32[]{:S(2)}, u32[]{:S(2)}) collective-permute-start(f32[40,120]{1,0:T(8,128)S(1)} %get-tuple-element.52), channel_id=1, source_target_pairs={{0,12},{4,8},{8,4},{12,0},{1,13},{5,9},{9,5},{13,1},{2,14},{6,10},... | collective-permute-start | bytes 57608 | tf_op jit(solution)/shard_map/ppermute | solution.py:17
  34.0 0.0 collective-permute-start.14
  34.0 1.7 %collective-permute-start.15 = (f32[40,120]{1,0:T(8,128)S(1)}, f32[40,120]{1,0:T(8,128)S(1)}, u32[]{:S(2)}, u32[]{:S(2)}) collective-permute-start(f32[40,120]{1,0:T(8,128)S(1)} %get-tuple-element.54), channel_id=1, source_target_pairs={{0,4},{4,0},{8,12},{12,8},{1,5},{5,1},{9,13},{13,9},{2,6},{6,2},{1... | collective-permute-start | bytes 57608 | tf_op jit(solution)/shard_map/ppermute | solution.py:17
  35.8 1.3 %collective-permute-done.13.refs_0_ = f32[40,120]{1,0:T(8,128)S(1)} collective-permute-done((f32[40,120]{1,0:T(8,128)S(1)}, f32[40,120]{1,0:T(8,128)S(1)}, u32[]{:S(2)}, u32[]{:S(2)}) %collective-permute-start.13) | collective-permute-done | bytes 19232 | tf_op jit(solution)/shard_map/ppermute | solution.py:17
  37.0 1.7 %collective-permute-done.14.refs_1_ = f32[40,120]{1,0:T(8,128)S(1)} collective-permute-done((f32[40,120]{1,0:T(8,128)S(1)}, f32[40,120]{1,0:T(8,128)S(1)}, u32[]{:S(2)}, u32[]{:S(2)}) %collective-permute-start.14) | collective-permute-done | bytes 19232 | tf_op jit(solution)/shard_map/ppermute | solution.py:17
  38.8 0.0 collective-permute-done.15.refs_2_
  38.8 0.1 shard_map.59
  38.9 2.4 %collective-permute-start.18 = (f32[40,80]{1,0:T(8,128)S(1)}, f32[40,80]{1,0:T(8,128)S(1)}, u32[]{:S(2)}, u32[]{:S(2)}) collective-permute-start(f32[40,80]{1,0:T(8,128)S(1)} %get-tuple-element.56), channel_id=1, source_target_pairs={{0,18},{1,19},{2,16},{3,17},{16,2},{17,3},{18,0},{19,1},{4,22},{5,... | collective-permute-start | bytes 38408 | tf_op jit(solution)/shard_map/ppermute | solution.py:17
  41.3 0.6 %collective-permute-start.16 = (f32[40,80]{1,0:T(8,128)S(1)}, f32[40,80]{1,0:T(8,128)S(1)}, u32[]{:S(2)}, u32[]{:S(2)}) collective-permute-start(f32[40,80]{1,0:T(8,128)S(1)} %get-tuple-element.56), channel_id=1, source_target_pairs={{0,2},{1,3},{2,0},{3,1},{16,18},{17,19},{18,16},{19,17},{4,6},{5,7... | collective-permute-start | bytes 38408 | tf_op jit(solution)/shard_map/ppermute | solution.py:17
  41.8 0.5 %collective-permute-start.17 = (f32[40,80]{1,0:T(8,128)S(1)}, f32[40,80]{1,0:T(8,128)S(1)}, u32[]{:S(2)}, u32[]{:S(2)}) collective-permute-start(f32[40,80]{1,0:T(8,128)S(1)} %get-tuple-element.57), channel_id=1, source_target_pairs={{0,16},{1,17},{2,18},{3,19},{16,0},{17,1},{18,2},{19,3},{4,20},{5,... | collective-permute-start | bytes 38408 | tf_op jit(solution)/shard_map/ppermute | solution.py:17
  42.4 0.0 collective-permute-done.19.refs_2_
  42.4 0.0 collective-permute-done.20.refs_3_
  42.4 0.9 %shard_map.60 = bf16[12,20,1024]{2,1,0:T(8,128)(2,1)} custom-call(bf16[240,256]{1,0:T(8,128)(2,1)S(1)} %get-tuple-element.58.refs_0_, bf16[240,256]{1,0:T(8,128)(2,1)S(1)} %collective-permute-done.11.refs_9_.refs_1_, bf16[240,256]{1,0:T(8,128)(2,1)S(1)} %collective-permute-done.19.refs_2_, bf16[240,256]{1,0:T(8,128)(2,1)S(1)} %collective-permute-done.20.refs_3_), custom_call_target="tpu_custom_call" | custom-call | bytes 983040 | tf_op jit(solution)/shard_map/pallas_call | solution.py:38
  43.3 0.3 collective-permute-done.18
  43.6 1.5 %collective-permute-done.16 = f32[40,80]{1,0:T(8,128)S(1)} collective-permute-done((f32[40,80]{1,0:T(8,128)S(1)}, f32[40,80]{1,0:T(8,128)S(1)}, u32[]{:S(2)}, u32[]{:S(2)}) %collective-permute-start.16) | collective-permute-done | bytes 12832 | tf_op jit(solution)/shard_map/ppermute | solution.py:17
  45.1 0.6 %collective-permute-done.17 = f32[40,80]{1,0:T(8,128)S(1)} collective-permute-done((f32[40,80]{1,0:T(8,128)S(1)}, f32[40,80]{1,0:T(8,128)S(1)}, u32[]{:S(2)}, u32[]{:S(2)}) %collective-permute-start.17) | collective-permute-done | bytes 12832 | tf_op jit(solution)/shard_map/ppermute | solution.py:17
  45.6 0.6 %fusion = (f32[20,80]{1,0:T(8,128)}, f32[20,80]{1,0:T(8,128)}) fusion(f32[40,80]{1,0:T(8,128)S(1)} %add_add_fusion), kind=kLoop, calls=%fused_computation.1 | loop fusion | bytes 25600 | tf_op jit(solution)/shard_map/slice | solution.py:319
  (5 shorter events, 0.1 us)
Async XLA Ops:
  0.6 1.2 %copy-start = (bf16[20,20,1024]{2,1,0:T(8,128)(2,1)S(1)}, bf16[20,20,1024]{2,1,0:T(8,128)(2,1)}, u32[]{:S(2)}) copy-start(bf16[20,20,1024]{2,1,0:T(8,128)(2,1)} %slab_ref.3) | copy-start | bytes 2457604
  0.6 1.2 %copy-start.1 = (bf16[20,48]{1,0:T(8,128)(2,1)S(1)}, bf16[20,48]{1,0:T(8,128)(2,1)}, u32[]{:S(2)}) copy-start(bf16[20,48]{1,0:T(8,128)(2,1)} %refs_0_.1) | copy-start | bytes 5764
  2.0 8.1 %collective-permute-start.2 = (bf16[408,256]{1,0:T(8,128)(2,1)S(1)}, bf16[408,256]{1,0:T(8,128)(2,1)S(1)}, u32[]{:S(2)}, u32[]{:S(2)}) collective-permute-start(bf16[408,256]{1,0:T(8,128)(2,1)S(1)} %get-tuple-element.34), channel_id=1, source_target_pairs={{0,1},{1,0},{2,3},{3,2},{4,5},{5,4},{6,7},{7,6},{8,9},{9,8},{10,11... | collective-permute-start | bytes 626696 | tf_op jit(solution)/shard_map/ppermute | solution.py:17
  2.5 5.5 %collective-permute-start = (bf16[168,256]{1,0:T(8,128)(2,1)S(1)}, bf16[168,256]{1,0:T(8,128)(2,1)S(1)}, u32[]{:S(2)}, u32[]{:S(2)}) collective-permute-start(bf16[168,256]{1,0:T(8,128)(2,1)S(1)} %get-tuple-element.32), channel_id=1, source_target_pairs={{0,3},{1,2},{2,1},{3,0},{4,7},{5,6},{6,5},{7,4},{8,11},{9,10},{10,... | collective-permute-start | bytes 258056 | tf_op jit(solution)/shard_map/ppermute | solution.py:17
  5.1 4.9 %collective-permute-start.1 = (bf16[168,256]{1,0:T(8,128)(2,1)S(1)}, bf16[168,256]{1,0:T(8,128)(2,1)S(1)}, u32[]{:S(2)}, u32[]{:S(2)}) collective-permute-start(bf16[168,256]{1,0:T(8,128)(2,1)S(1)} %get-tuple-element.33), channel_id=1, source_target_pairs={{0,2},{1,3},{2,0},{3,1},{4,6},{5,7},{6,4},{7,5},{8,10},{9,11},{10,... | collective-permute-start | bytes 258056 | tf_op jit(solution)/shard_map/ppermute | solution.py:17
  8.0 7.3 %collective-permute-start.6 = (bf16[240,256]{1,0:T(8,128)(2,1)S(1)}, bf16[240,256]{1,0:T(8,128)(2,1)S(1)}, u32[]{:S(2)}, u32[]{:S(2)}) collective-permute-start(bf16[240,256]{1,0:T(8,128)(2,1)S(1)} %get-tuple-element.40), channel_id=1, source_target_pairs={{0,3},{1,2},{2,1},{3,0},{4,7},{5,6},{6,5},{7,4},{8,11},{9,10},{10,... | collective-permute-start | bytes 368648 | tf_op jit(solution)/shard_map/ppermute | solution.py:17
  10.0 6.5 %collective-permute-start.7 = (bf16[240,256]{1,0:T(8,128)(2,1)S(1)}, bf16[240,256]{1,0:T(8,128)(2,1)S(1)}, u32[]{:S(2)}, u32[]{:S(2)}) collective-permute-start(bf16[240,256]{1,0:T(8,128)(2,1)S(1)} %get-tuple-element.41), channel_id=1, source_target_pairs={{0,2},{1,3},{2,0},{3,1},{4,6},{5,7},{6,4},{7,5},{8,10},{9,11},{10,... | collective-permute-start | bytes 368648 | tf_op jit(solution)/shard_map/ppermute | solution.py:17
  10.5 6.4 %collective-permute-start.3 = (bf16[96,256]{1,0:T(8,128)(2,1)S(1)}, bf16[96,256]{1,0:T(8,128)(2,1)S(1)}, u32[]{:S(2)}, u32[]{:S(2)}) collective-permute-start(bf16[96,256]{1,0:T(8,128)(2,1)S(1)} %get-tuple-element.36), channel_id=1, source_target_pairs={{0,12},{4,8},{8,4},{12,0},{1,13},{5,9},{9,5},{13,1},{2,14},{6,10},... | collective-permute-start | bytes 147464 | tf_op jit(solution)/shard_map/ppermute | solution.py:17
  14.7 5.0 %collective-permute-start.4 = (bf16[96,256]{1,0:T(8,128)(2,1)S(1)}, bf16[96,256]{1,0:T(8,128)(2,1)S(1)}, u32[]{:S(2)}, u32[]{:S(2)}) collective-permute-start(bf16[96,256]{1,0:T(8,128)(2,1)S(1)} %get-tuple-element.37), channel_id=1, source_target_pairs={{0,8},{4,12},{8,0},{12,4},{1,9},{5,13},{9,1},{13,5},{2,10},{6,14},... | collective-permute-start | bytes 147464 | tf_op jit(solution)/shard_map/ppermute | solution.py:17
  14.7 5.0 %collective-permute-start.5 = (bf16[96,256]{1,0:T(8,128)(2,1)S(1)}, bf16[96,256]{1,0:T(8,128)(2,1)S(1)}, u32[]{:S(2)}, u32[]{:S(2)}) collective-permute-start(bf16[96,256]{1,0:T(8,128)(2,1)S(1)} %get-tuple-element.38), channel_id=1, source_target_pairs={{0,4},{4,0},{8,12},{12,8},{1,5},{5,1},{9,13},{13,9},{2,6},{6,2},{1... | collective-permute-start | bytes 147464 | tf_op jit(solution)/shard_map/ppermute | solution.py:17
  19.7 9.8 %collective-permute-start.11 = (bf16[240,256]{1,0:T(8,128)(2,1)S(1)}, bf16[240,256]{1,0:T(8,128)(2,1)S(1)}, u32[]{:S(2)}, u32[]{:S(2)}) collective-permute-start(bf16[240,256]{1,0:T(8,128)(2,1)S(1)} %get-tuple-element.49), channel_id=1, source_target_pairs={{0,1},{1,0},{2,3},{3,2},{4,5},{5,4},{6,7},{7,6},{8,9},{9,8},{10,11... | collective-permute-start | bytes 368648 | tf_op jit(solution)/shard_map/ppermute | solution.py:17
  19.8 7.0 %collective-permute-start.8 = (bf16[144,256]{1,0:T(8,128)(2,1)S(1)}, bf16[144,256]{1,0:T(8,128)(2,1)S(1)}, u32[]{:S(2)}, u32[]{:S(2)}) collective-permute-start(bf16[144,256]{1,0:T(8,128)(2,1)S(1)} %get-tuple-element.43), channel_id=1, source_target_pairs={{0,12},{4,8},{8,4},{12,0},{1,13},{5,9},{9,5},{13,1},{2,14},{6,10},... | collective-permute-start | bytes 221192 | tf_op jit(solution)/shard_map/ppermute | solution.py:17
  21.8 7.7 %collective-permute-start.9 = (bf16[144,256]{1,0:T(8,128)(2,1)S(1)}, bf16[144,256]{1,0:T(8,128)(2,1)S(1)}, u32[]{:S(2)}, u32[]{:S(2)}) collective-permute-start(bf16[144,256]{1,0:T(8,128)(2,1)S(1)} %get-tuple-element.44), channel_id=1, source_target_pairs={{0,8},{4,12},{8,0},{12,4},{1,9},{5,13},{9,1},{13,5},{2,10},{6,14},... | collective-permute-start | bytes 221192 | tf_op jit(solution)/shard_map/ppermute | solution.py:17
  22.0 7.5 %collective-permute-start.10 = (bf16[144,256]{1,0:T(8,128)(2,1)S(1)}, bf16[144,256]{1,0:T(8,128)(2,1)S(1)}, u32[]{:S(2)}, u32[]{:S(2)}) collective-permute-start(bf16[144,256]{1,0:T(8,128)(2,1)S(1)} %get-tuple-element.45), channel_id=1, source_target_pairs={{0,4},{4,0},{8,12},{12,8},{1,5},{5,1},{9,13},{13,9},{2,6},{6,2},{1... | collective-permute-start | bytes 221192 | tf_op jit(solution)/shard_map/ppermute | solution.py:17
  24.3 18.1 %collective-permute-start.19 = (bf16[240,256]{1,0:T(8,128)(2,1)S(1)}, bf16[240,256]{1,0:T(8,128)(2,1)S(1)}, u32[]{:S(2)}, u32[]{:S(2)}) collective-permute-start(bf16[240,256]{1,0:T(8,128)(2,1)S(1)} %get-tuple-element.59), channel_id=1, source_target_pairs={{0,2},{1,3},{2,0},{3,1},{4,6},{5,7},{6,4},{7,5},{8,10},{9,11},{10,... | collective-permute-start | bytes 368648 | tf_op jit(solution)/shard_map/ppermute | solution.py:17
  26.8 15.6 %collective-permute-start.20 = (bf16[240,256]{1,0:T(8,128)(2,1)S(1)}, bf16[240,256]{1,0:T(8,128)(2,1)S(1)}, u32[]{:S(2)}, u32[]{:S(2)}) collective-permute-start(bf16[240,256]{1,0:T(8,128)(2,1)S(1)} %get-tuple-element.60), channel_id=1, source_target_pairs={{0,3},{1,2},{2,1},{3,0},{4,7},{5,6},{6,5},{7,4},{8,11},{9,10},{10,... | collective-permute-start | bytes 368648 | tf_op jit(solution)/shard_map/ppermute | solution.py:17
  29.8 1.3 %collective-permute-start.12 = (f32[80,120]{1,0:T(8,128)S(1)}, f32[80,120]{1,0:T(8,128)S(1)}, u32[]{:S(2)}, u32[]{:S(2)}) collective-permute-start(f32[80,120]{1,0:T(8,128)S(1)} %get-tuple-element.51), channel_id=1, source_target_pairs={{0,1},{1,0},{2,3},{3,2},{4,5},{5,4},{6,7},{7,6},{8,9},{9,8},{10,11... | collective-permute-start | bytes 115208 | tf_op jit(solution)/shard_map/ppermute | solution.py:17
  31.3 5.7 %collective-permute-start.13 = (f32[40,120]{1,0:T(8,128)S(1)}, f32[40,120]{1,0:T(8,128)S(1)}, u32[]{:S(2)}, u32[]{:S(2)}) collective-permute-start(f32[40,120]{1,0:T(8,128)S(1)} %get-tuple-element.52), channel_id=1, source_target_pairs={{0,12},{4,8},{8,4},{12,0},{1,13},{5,9},{9,5},{13,1},{2,14},{6,10},... | collective-permute-start | bytes 57608 | tf_op jit(solution)/shard_map/ppermute | solution.py:17
  34.0 4.7 %collective-permute-start.14 = (f32[40,120]{1,0:T(8,128)S(1)}, f32[40,120]{1,0:T(8,128)S(1)}, u32[]{:S(2)}, u32[]{:S(2)}) collective-permute-start(f32[40,120]{1,0:T(8,128)S(1)} %get-tuple-element.53), channel_id=1, source_target_pairs={{0,8},{4,12},{8,0},{12,4},{1,9},{5,13},{9,1},{13,5},{2,10},{6,14},... | collective-permute-start | bytes 57608 | tf_op jit(solution)/shard_map/ppermute | solution.py:17
  34.0 4.7 %collective-permute-start.15 = (f32[40,120]{1,0:T(8,128)S(1)}, f32[40,120]{1,0:T(8,128)S(1)}, u32[]{:S(2)}, u32[]{:S(2)}) collective-permute-start(f32[40,120]{1,0:T(8,128)S(1)} %get-tuple-element.54), channel_id=1, source_target_pairs={{0,4},{4,0},{8,12},{12,8},{1,5},{5,1},{9,13},{13,9},{2,6},{6,2},{1... | collective-permute-start | bytes 57608 | tf_op jit(solution)/shard_map/ppermute | solution.py:17
  38.9 4.7 %collective-permute-start.18 = (f32[40,80]{1,0:T(8,128)S(1)}, f32[40,80]{1,0:T(8,128)S(1)}, u32[]{:S(2)}, u32[]{:S(2)}) collective-permute-start(f32[40,80]{1,0:T(8,128)S(1)} %get-tuple-element.56), channel_id=1, source_target_pairs={{0,18},{1,19},{2,16},{3,17},{16,2},{17,3},{18,0},{19,1},{4,22},{5,... | collective-permute-start | bytes 38408 | tf_op jit(solution)/shard_map/ppermute | solution.py:17
  41.3 3.8 %collective-permute-start.16 = (f32[40,80]{1,0:T(8,128)S(1)}, f32[40,80]{1,0:T(8,128)S(1)}, u32[]{:S(2)}, u32[]{:S(2)}) collective-permute-start(f32[40,80]{1,0:T(8,128)S(1)} %get-tuple-element.56), channel_id=1, source_target_pairs={{0,2},{1,3},{2,0},{3,1},{16,18},{17,19},{18,16},{19,17},{4,6},{5,7... | collective-permute-start | bytes 38408 | tf_op jit(solution)/shard_map/ppermute | solution.py:17
  41.8 3.8 %collective-permute-start.17 = (f32[40,80]{1,0:T(8,128)S(1)}, f32[40,80]{1,0:T(8,128)S(1)}, u32[]{:S(2)}, u32[]{:S(2)}) collective-permute-start(f32[40,80]{1,0:T(8,128)S(1)} %get-tuple-element.57), channel_id=1, source_target_pairs={{0,16},{1,17},{2,18},{3,19},{16,0},{17,1},{18,2},{19,3},{4,20},{5,... | collective-permute-start | bytes 38408 | tf_op jit(solution)/shard_map/ppermute | solution.py:17

commit v5 on v4

--- a/solution.py
+++ b/solution.py
@@ -152,8 +152,8 @@
         outs[k][...] = blocks[z ^ k]
 
 
-def deal_view_kernel(lights, rows, *refs):
-    total_ref, outs, blocks = refs[0], refs[1:-1], refs[-1]
+def deal_view_kernel(lights, rows, spare, *refs):
+    total_ref, outs, blocks = refs[0], refs[1 + spare : -1], refs[-1]
     u = lax.axis_index("view") // 2
     total = total_ref[...]
     wide = 2 * rows * len(outs)
@@ -301,11 +301,12 @@
         total = total + swap(total, "texel", step)
         step *= 2
     dealt = call(
-        functools.partial(deal_view_kernel, lights, rows),
+        functools.partial(deal_view_kernel, lights, rows, 2),
         [sds((lights + rows, views_all), f32)] * half,
         [pltpu.VMEM((half, lights + rows, views_all), f32)],
         0,
         [total],
+        [returned[2], returned[3]],
     )
     steps = [(t, m) for t in range(min(2, texels) - 1, -1, -1) for m in range(half - 1, -1, -1)]
     total = summed([dealt[0]] + [swap(dealt[m], ("texel", "view"), t * views + 2 * m) for t, m in steps[:-1]])

time: 46.4 us -> 44 us (0.948)
  waiting for transfers between devices: 16.1 us -> 13.6 us
    ppermute x21, waiting for transfers between devices: 16.1 us -> 13.6 us  [swap(): lax.ppermute(value, axis, [(i, i ^ step) for i in range(lax.axis_size(axi...]
where the time goes in v5:
time: 44 us; the launch traced here: 43.9 us
  starting transfers between devices  24.5 us (56%)
  waiting for transfers between devices  13.6 us (31%)
  Pallas kernels  3.21 us (7%)
  local copies, waits for them, and re-layouts  1.79 us (4%)
  between operations  0.76 us (2%)
    ppermute x21, starting transfers between devices, swap(): lax.ppermute(value, axis, [(i, i ^ step) for i in range(lax.axis_size(axi...  24.5 us
    ppermute x21, waiting for transfers between devices, swap(): lax.ppermute(value, axis, [(i, i ^ step) for i in range(lax.axis_size(axi...  13.6 us
    pallas_call x12, Pallas kernels, call(): pl.pallas_call(kernel, out_shape=out_shape, in_specs=[VMEM] * len(args) +...  3.21 us
    unnamed x4, local copies, waits for them, and re-layouts  1.18 us
  transfers between devices with their start and end apart: 21, of which 12 were waited for; matrix products, arithmetic and copies ran while one was open for 0% of the time, Pallas kernels for 7%

profile of v5, /device:TPU:0, one launch (start us, length us, event | category | flops | bytes accessed | tf_op | source)
XLA Modules:
  0.0 43.9 jit_solution(2942846871866396074)
XLA Ops:
  0.6 0.0 copy-start
  0.6 0.0 copy-start.1
  0.7 1.2 %copy-done = bf16[20,20,1024]{2,1,0:T(8,128)(2,1)S(1)} copy-done((bf16[20,20,1024]{2,1,0:T(8,128)(2,1)S(1)}, bf16[20,20,1024]{2,1,0:T(8,128)(2,1)}, u32[]{:S(2)}) %copy-start) | copy-done | bytes 819224
  1.8 0.0 copy-done.1
  1.8 0.1 shard_map.50
  2.0 0.5 %collective-permute-start.2 = (bf16[408,256]{1,0:T(8,128)(2,1)S(1)}, bf16[408,256]{1,0:T(8,128)(2,1)S(1)}, u32[]{:S(2)}, u32[]{:S(2)}) collective-permute-start(bf16[408,256]{1,0:T(8,128)(2,1)S(1)} %get-tuple-element.34), channel_id=1, source_target_pairs={{0,1},{1,0},{2,3},{3,2},{4,5},{5,4},{6,7},{7,6},{8,9},{9,8},{10,11... | collective-permute-start | bytes 626696 | tf_op jit(solution)/shard_map/ppermute | solution.py:17
  2.5 2.6 %collective-permute-start = (bf16[168,256]{1,0:T(8,128)(2,1)S(1)}, bf16[168,256]{1,0:T(8,128)(2,1)S(1)}, u32[]{:S(2)}, u32[]{:S(2)}) collective-permute-start(bf16[168,256]{1,0:T(8,128)(2,1)S(1)} %get-tuple-element.32), channel_id=1, source_target_pairs={{0,3},{1,2},{2,1},{3,0},{4,7},{5,6},{6,5},{7,4},{8,11},{9,10},{10,... | collective-permute-start | bytes 258056 | tf_op jit(solution)/shard_map/ppermute | solution.py:17
  5.1 0.0 collective-permute-start.1
  5.2 2.8 %collective-permute-done.refs_0_.refs_3_ = bf16[168,256]{1,0:T(8,128)(2,1)S(1)} collective-permute-done((bf16[168,256]{1,0:T(8,128)(2,1)S(1)}, bf16[168,256]{1,0:T(8,128)(2,1)S(1)}, u32[]{:S(2)}, u32[]{:S(2)}) %collective-permute-start) | collective-permute-done | bytes 86048 | tf_op jit(solution)/shard_map/ppermute | solution.py:17
  8.0 2.0 %collective-permute-start.6 = (bf16[240,256]{1,0:T(8,128)(2,1)S(1)}, bf16[240,256]{1,0:T(8,128)(2,1)S(1)}, u32[]{:S(2)}, u32[]{:S(2)}) collective-permute-start(bf16[240,256]{1,0:T(8,128)(2,1)S(1)} %get-tuple-element.40), channel_id=1, source_target_pairs={{0,3},{1,2},{2,1},{3,0},{4,7},{5,6},{6,5},{7,4},{8,11},{9,10},{10,... | collective-permute-start | bytes 368648 | tf_op jit(solution)/shard_map/ppermute | solution.py:17
  10.0 0.0 collective-permute-start.7
  10.0 0.0 collective-permute-done.1.refs_1_.refs_2_
  10.0 0.0 collective-permute-done.2.refs_2_.refs_1_
  10.0 0.5 %shard_map.51 = (bf16[96,256]{1,0:T(8,128)(2,1)S(1)}, bf16[96,256]{1,0:T(8,128)(2,1)S(1)}, bf16[96,256]{1,0:T(8,128)(2,1)S(1)}, bf16[96,256]{1,0:T(8,128)(2,1)S(...) custom-call(bf16[168,256]{1,0:T(8,128)(2,1)S(1)} %collective-permute-done.refs_0_.refs_3_, ...), custom_call_target="tpu_custom_call" | custom-call | flops 15728640 | bytes 990720 | tf_op jit(solution)/shard_map/pallas_call | solution.py:38
  10.5 4.1 %collective-permute-start.3 = (bf16[96,256]{1,0:T(8,128)(2,1)S(1)}, bf16[96,256]{1,0:T(8,128)(2,1)S(1)}, u32[]{:S(2)}, u32[]{:S(2)}) collective-permute-start(bf16[96,256]{1,0:T(8,128)(2,1)S(1)} %get-tuple-element.36), channel_id=1, source_target_pairs={{0,12},{4,8},{8,4},{12,0},{1,13},{5,9},{9,5},{13,1},{2,14},{6,10},... | collective-permute-start | bytes 147464 | tf_op jit(solution)/shard_map/ppermute | solution.py:17
  14.7 0.0 collective-permute-start.4
  14.7 0.6 %collective-permute-start.5 = (bf16[96,256]{1,0:T(8,128)(2,1)S(1)}, bf16[96,256]{1,0:T(8,128)(2,1)S(1)}, u32[]{:S(2)}, u32[]{:S(2)}) collective-permute-start(bf16[96,256]{1,0:T(8,128)(2,1)S(1)} %get-tuple-element.38), channel_id=1, source_target_pairs={{0,4},{4,0},{8,12},{12,8},{1,5},{5,1},{9,13},{13,9},{2,6},{6,2},{1... | collective-permute-start | bytes 147464 | tf_op jit(solution)/shard_map/ppermute | solution.py:17
  15.3 0.0 collective-permute-done.6.refs_0_.refs_5_
  15.3 1.2 %collective-permute-done.7.refs_1_.refs_4_ = bf16[240,256]{1,0:T(8,128)(2,1)S(1)} collective-permute-done((bf16[240,256]{1,0:T(8,128)(2,1)S(1)}, bf16[240,256]{1,0:T(8,128)(2,1)S(1)}, u32[]{:S(2)}, u32[]{:S(2)}) %collective-permute-start.7) | collective-permute-done | bytes 122912 | tf_op jit(solution)/shard_map/ppermute | solution.py:17
  16.5 0.5 %collective-permute-done.3.refs_5_.refs_2_.refs_0_ = bf16[96,256]{1,0:T(8,128)(2,1)S(1)} collective-permute-done((bf16[96,256]{1,0:T(8,128)(2,1)S(1)}, bf16[96,256]{1,0:T(8,128)(2,1)S(1)}, u32[]{:S(2)}, u32[]{:S(2)}) %collective-permute-start.3) | collective-permute-done | bytes 49184 | tf_op jit(solution)/shard_map/ppermute | solution.py:17
  17.0 0.5 %shard_map.53 = (bf16[144,256]{1,0:T(8,128)(2,1)S(1)}, bf16[144,256]{1,0:T(8,128)(2,1)S(1)}, bf16[144,256]{1,0:T(8,128)(2,1)S(1)}, bf16[144,256]{1,0:T(8,128)(2,1)S(1)}, bf16[4,144,256]{2,1,0:T(8,128)(2,1)S(1)}) custom-call(bf16[240,256]{1,0:T(8,128)(2,1)S(1)} %collective-permute-done.6.refs_0_.refs_5_, ...), custom_call_target="tpu_custom_call" | custom-call | flops 23592960 | bytes 1261056 | tf_op jit(solution)/shard_map/pallas_call | solution.py:38
  17.5 4.0 %collective-permute-start.8 = (bf16[144,256]{1,0:T(8,128)(2,1)S(1)}, bf16[144,256]{1,0:T(8,128)(2,1)S(1)}, u32[]{:S(2)}, u32[]{:S(2)}) collective-permute-start(bf16[144,256]{1,0:T(8,128)(2,1)S(1)} %get-tuple-element.43), channel_id=1, source_target_pairs={{0,12},{4,8},{8,4},{12,0},{1,13},{5,9},{9,5},{13,1},{2,14},{6,10},... | collective-permute-start | bytes 221192 | tf_op jit(solution)/shard_map/ppermute | solution.py:17
  21.5 0.0 collective-permute-done.4.refs_3_.refs_1_
  21.5 0.0 collective-permute-done.5.refs_4_.refs_2_
  21.5 0.1 collective-permute-start.11
  21.6 0.3 collective-permute-start.9
  21.9 0.5 %collective-permute-start.10 = (bf16[144,256]{1,0:T(8,128)(2,1)S(1)}, bf16[144,256]{1,0:T(8,128)(2,1)S(1)}, u32[]{:S(2)}, u32[]{:S(2)}) collective-permute-start(bf16[144,256]{1,0:T(8,128)(2,1)S(1)} %get-tuple-element.45), channel_id=1, source_target_pairs={{0,4},{4,0},{8,12},{12,8},{1,5},{5,1},{9,13},{13,9},{2,6},{6,2},{1... | collective-permute-start | bytes 221192 | tf_op jit(solution)/shard_map/ppermute | solution.py:17
  22.4 1.6 %collective-permute-start.16 = (bf16[240,256]{1,0:T(8,128)(2,1)S(1)}, bf16[240,256]{1,0:T(8,128)(2,1)S(1)}, u32[]{:S(2)}, u32[]{:S(2)}) collective-permute-start(bf16[240,256]{1,0:T(8,128)(2,1)S(1)} %get-tuple-element.56), channel_id=1, source_target_pairs={{0,2},{1,3},{2,0},{3,1},{4,6},{5,7},{6,4},{7,5},{8,10},{9,11},{10,... | collective-permute-start | bytes 368648 | tf_op jit(solution)/shard_map/ppermute | solution.py:17
  24.0 0.2 collective-permute-done.8.refs_4_
  24.2 0.0 collective-permute-start.17
  24.2 0.6 %shard_map.54.refs_8_ = f32[2,80,120]{2,1,0:T(8,128)S(1)} custom-call(bf16[408,256]{1,0:T(8,128)(2,1)S(1)} %get-tuple-element.35.refs_3_.refs_0_, bf16[408,256]{1,0:T(8,128)(2,1)S(1)} %collective-permute-done.2.refs_2_.refs_1_, bf16[168,256]{1,0:T(8,128)(2,1)S(1)} %collective-permute-done.1.refs_1_.refs_2_, ...), custom_call_target="tpu_custom_call" | custom-call | flops 65536000 | bytes 912384 | tf_op jit(solution)/shard_map/pallas_call | solution.py:38
  24.8 2.5 %collective-permute-done.9.refs_5_ = bf16[144,256]{1,0:T(8,128)(2,1)S(1)} collective-permute-done((bf16[144,256]{1,0:T(8,128)(2,1)S(1)}, bf16[144,256]{1,0:T(8,128)(2,1)S(1)}, u32[]{:S(2)}, u32[]{:S(2)}) %collective-permute-start.9) | collective-permute-done | bytes 73760 | tf_op jit(solution)/shard_map/ppermute | solution.py:17
  27.3 0.6 %collective-permute-done.10.refs_6_ = bf16[144,256]{1,0:T(8,128)(2,1)S(1)} collective-permute-done((bf16[144,256]{1,0:T(8,128)(2,1)S(1)}, bf16[144,256]{1,0:T(8,128)(2,1)S(1)}, u32[]{:S(2)}, u32[]{:S(2)}) %collective-permute-start.10) | collective-permute-done | bytes 73760 | tf_op jit(solution)/shard_map/ppermute | solution.py:17
  27.9 0.0 collective-permute-done.11.refs_9_.refs_1_
  27.9 0.3 shard_map.56
  28.2 0.1 collective-permute-start.12
  28.3 1.2 %collective-permute-done.12.came_ref = f32[80,120]{1,0:T(8,128)S(1)} collective-permute-done((f32[80,120]{1,0:T(8,128)S(1)}, f32[80,120]{1,0:T(8,128)S(1)}, u32[]{:S(2)}, u32[]{:S(2)}) %collective-permute-start.12) | collective-permute-done | bytes 38432 | tf_op jit(solution)/shard_map/ppermute | solution.py:17
  29.5 0.2 shard_map.57
  29.7 2.0 %collective-permute-start.13 = (f32[40,120]{1,0:T(8,128)S(1)}, f32[40,120]{1,0:T(8,128)S(1)}, u32[]{:S(2)}, u32[]{:S(2)}) collective-permute-start(f32[40,120]{1,0:T(8,128)S(1)} %get-tuple-element.52), channel_id=1, source_target_pairs={{0,12},{4,8},{8,4},{12,0},{1,13},{5,9},{9,5},{13,1},{2,14},{6,10},... | collective-permute-start | bytes 57608 | tf_op jit(solution)/shard_map/ppermute | solution.py:17
  31.7 0.6 %collective-permute-start.14 = (f32[40,120]{1,0:T(8,128)S(1)}, f32[40,120]{1,0:T(8,128)S(1)}, u32[]{:S(2)}, u32[]{:S(2)}) collective-permute-start(f32[40,120]{1,0:T(8,128)S(1)} %get-tuple-element.53), channel_id=1, source_target_pairs={{0,8},{4,12},{8,0},{12,4},{1,9},{5,13},{9,1},{13,5},{2,10},{6,14},... | collective-permute-start | bytes 57608 | tf_op jit(solution)/shard_map/ppermute | solution.py:17
  32.3 1.8 %collective-permute-start.15 = (f32[40,120]{1,0:T(8,128)S(1)}, f32[40,120]{1,0:T(8,128)S(1)}, u32[]{:S(2)}, u32[]{:S(2)}) collective-permute-start(f32[40,120]{1,0:T(8,128)S(1)} %get-tuple-element.54), channel_id=1, source_target_pairs={{0,4},{4,0},{8,12},{12,8},{1,5},{5,1},{9,13},{13,9},{2,6},{6,2},{1... | collective-permute-start | bytes 57608 | tf_op jit(solution)/shard_map/ppermute | solution.py:17
  34.1 1.2 %collective-permute-done.13.refs_0_ = f32[40,120]{1,0:T(8,128)S(1)} collective-permute-done((f32[40,120]{1,0:T(8,128)S(1)}, f32[40,120]{1,0:T(8,128)S(1)}, u32[]{:S(2)}, u32[]{:S(2)}) %collective-permute-start.13) | collective-permute-done | bytes 19232 | tf_op jit(solution)/shard_map/ppermute | solution.py:17
  35.3 1.1 %collective-permute-done.14.refs_1_ = f32[40,120]{1,0:T(8,128)S(1)} collective-permute-done((f32[40,120]{1,0:T(8,128)S(1)}, f32[40,120]{1,0:T(8,128)S(1)}, u32[]{:S(2)}, u32[]{:S(2)}) %collective-permute-start.14) | collective-permute-done | bytes 19232 | tf_op jit(solution)/shard_map/ppermute | solution.py:17
  36.4 0.0 collective-permute-done.15.refs_2_
  36.4 0.0 collective-permute-done.16.refs_1_.refs_2_
  36.4 0.0 collective-permute-done.17.refs_2_.refs_3_
  36.4 0.1 shard_map.59
  36.5 2.5 %collective-permute-start.20 = (f32[40,80]{1,0:T(8,128)S(1)}, f32[40,80]{1,0:T(8,128)S(1)}, u32[]{:S(2)}, u32[]{:S(2)}) collective-permute-start(f32[40,80]{1,0:T(8,128)S(1)} %get-tuple-element.58), channel_id=1, source_target_pairs={{0,18},{1,19},{2,16},{3,17},{16,2},{17,3},{18,0},{19,1},{4,22},{5,... | collective-permute-start | bytes 38408 | tf_op jit(solution)/shard_map/ppermute | solution.py:17
  39.0 0.4 %collective-permute-start.18 = (f32[40,80]{1,0:T(8,128)S(1)}, f32[40,80]{1,0:T(8,128)S(1)}, u32[]{:S(2)}, u32[]{:S(2)}) collective-permute-start(f32[40,80]{1,0:T(8,128)S(1)} %get-tuple-element.58), channel_id=1, source_target_pairs={{0,2},{1,3},{2,0},{3,1},{16,18},{17,19},{18,16},{19,17},{4,6},{5,7... | collective-permute-start | bytes 38408 | tf_op jit(solution)/shard_map/ppermute | solution.py:17
  39.5 0.6 %collective-permute-start.19 = (f32[40,80]{1,0:T(8,128)S(1)}, f32[40,80]{1,0:T(8,128)S(1)}, u32[]{:S(2)}, u32[]{:S(2)}) collective-permute-start(f32[40,80]{1,0:T(8,128)S(1)} %get-tuple-element.59), channel_id=1, source_target_pairs={{0,16},{1,17},{2,18},{3,19},{16,0},{17,1},{18,2},{19,3},{4,20},{5,... | collective-permute-start | bytes 38408 | tf_op jit(solution)/shard_map/ppermute | solution.py:17
  40.0 0.9 %shard_map.60 = bf16[12,20,1024]{2,1,0:T(8,128)(2,1)} custom-call(bf16[240,256]{1,0:T(8,128)(2,1)S(1)} %get-tuple-element.60.refs_0_, bf16[240,256]{1,0:T(8,128)(2,1)S(1)} %collective-permute-done.11.refs_9_.refs_1_, bf16[240,256]{1,0:T(8,128)(2,1)S(1)} %collective-permute-done.16.refs_1_.refs_2_, bf16[240,256]{1,0:T(8,128)(2,1)S(1)} %collective-permute-done.17.refs_2_.refs_3_), custom_call_target="tpu_custom_call" | custom-call | bytes 983040 | tf_op jit(solution)/shard_map/pallas_call | solution.py:38
  40.9 0.3 collective-permute-done.20
  41.2 1.6 %collective-permute-done.18 = f32[40,80]{1,0:T(8,128)S(1)} collective-permute-done((f32[40,80]{1,0:T(8,128)S(1)}, f32[40,80]{1,0:T(8,128)S(1)}, u32[]{:S(2)}, u32[]{:S(2)}) %collective-permute-start.18) | collective-permute-done | bytes 12832 | tf_op jit(solution)/shard_map/ppermute | solution.py:17
  42.8 0.4 %collective-permute-done.19 = f32[40,80]{1,0:T(8,128)S(1)} collective-permute-done((f32[40,80]{1,0:T(8,128)S(1)}, f32[40,80]{1,0:T(8,128)S(1)}, u32[]{:S(2)}, u32[]{:S(2)}) %collective-permute-start.19) | collective-permute-done | bytes 12832 | tf_op jit(solution)/shard_map/ppermute | solution.py:17
  43.3 0.6 %fusion = (f32[20,80]{1,0:T(8,128)}, f32[20,80]{1,0:T(8,128)}) fusion(f32[40,80]{1,0:T(8,128)S(1)} %add_add_fusion), kind=kLoop, calls=%fused_computation.1 | loop fusion | bytes 25600 | tf_op jit(solution)/shard_map/slice | solution.py:320
  (5 shorter events, 0.1 us)
Async XLA Ops:
  0.6 1.2 %copy-start = (bf16[20,20,1024]{2,1,0:T(8,128)(2,1)S(1)}, bf16[20,20,1024]{2,1,0:T(8,128)(2,1)}, u32[]{:S(2)}) copy-start(bf16[20,20,1024]{2,1,0:T(8,128)(2,1)} %slab_ref.3) | copy-start | bytes 2457604
  0.6 1.2 %copy-start.1 = (bf16[20,48]{1,0:T(8,128)(2,1)S(1)}, bf16[20,48]{1,0:T(8,128)(2,1)}, u32[]{:S(2)}) copy-start(bf16[20,48]{1,0:T(8,128)(2,1)} %refs_0_.1) | copy-start | bytes 5764
  2.0 8.1 %collective-permute-start.2 = (bf16[408,256]{1,0:T(8,128)(2,1)S(1)}, bf16[408,256]{1,0:T(8,128)(2,1)S(1)}, u32[]{:S(2)}, u32[]{:S(2)}) collective-permute-start(bf16[408,256]{1,0:T(8,128)(2,1)S(1)} %get-tuple-element.34), channel_id=1, source_target_pairs={{0,1},{1,0},{2,3},{3,2},{4,5},{5,4},{6,7},{7,6},{8,9},{9,8},{10,11... | collective-permute-start | bytes 626696 | tf_op jit(solution)/shard_map/ppermute | solution.py:17
  2.5 5.5 %collective-permute-start = (bf16[168,256]{1,0:T(8,128)(2,1)S(1)}, bf16[168,256]{1,0:T(8,128)(2,1)S(1)}, u32[]{:S(2)}, u32[]{:S(2)}) collective-permute-start(bf16[168,256]{1,0:T(8,128)(2,1)S(1)} %get-tuple-element.32), channel_id=1, source_target_pairs={{0,3},{1,2},{2,1},{3,0},{4,7},{5,6},{6,5},{7,4},{8,11},{9,10},{10,... | collective-permute-start | bytes 258056 | tf_op jit(solution)/shard_map/ppermute | solution.py:17
  5.1 4.9 %collective-permute-start.1 = (bf16[168,256]{1,0:T(8,128)(2,1)S(1)}, bf16[168,256]{1,0:T(8,128)(2,1)S(1)}, u32[]{:S(2)}, u32[]{:S(2)}) collective-permute-start(bf16[168,256]{1,0:T(8,128)(2,1)S(1)} %get-tuple-element.33), channel_id=1, source_target_pairs={{0,2},{1,3},{2,0},{3,1},{4,6},{5,7},{6,4},{7,5},{8,10},{9,11},{10,... | collective-permute-start | bytes 258056 | tf_op jit(solution)/shard_map/ppermute | solution.py:17
  8.0 7.3 %collective-permute-start.6 = (bf16[240,256]{1,0:T(8,128)(2,1)S(1)}, bf16[240,256]{1,0:T(8,128)(2,1)S(1)}, u32[]{:S(2)}, u32[]{:S(2)}) collective-permute-start(bf16[240,256]{1,0:T(8,128)(2,1)S(1)} %get-tuple-element.40), channel_id=1, source_target_pairs={{0,3},{1,2},{2,1},{3,0},{4,7},{5,6},{6,5},{7,4},{8,11},{9,10},{10,... | collective-permute-start | bytes 368648 | tf_op jit(solution)/shard_map/ppermute | solution.py:17
  10.0 6.5 %collective-permute-start.7 = (bf16[240,256]{1,0:T(8,128)(2,1)S(1)}, bf16[240,256]{1,0:T(8,128)(2,1)S(1)}, u32[]{:S(2)}, u32[]{:S(2)}) collective-permute-start(bf16[240,256]{1,0:T(8,128)(2,1)S(1)} %get-tuple-element.41), channel_id=1, source_target_pairs={{0,2},{1,3},{2,0},{3,1},{4,6},{5,7},{6,4},{7,5},{8,10},{9,11},{10,... | collective-permute-start | bytes 368648 | tf_op jit(solution)/shard_map/ppermute | solution.py:17
  10.5 6.4 %collective-permute-start.3 = (bf16[96,256]{1,0:T(8,128)(2,1)S(1)}, bf16[96,256]{1,0:T(8,128)(2,1)S(1)}, u32[]{:S(2)}, u32[]{:S(2)}) collective-permute-start(bf16[96,256]{1,0:T(8,128)(2,1)S(1)} %get-tuple-element.36), channel_id=1, source_target_pairs={{0,12},{4,8},{8,4},{12,0},{1,13},{5,9},{9,5},{13,1},{2,14},{6,10},... | collective-permute-start | bytes 147464 | tf_op jit(solution)/shard_map/ppermute | solution.py:17
  14.7 6.8 %collective-permute-start.4 = (bf16[96,256]{1,0:T(8,128)(2,1)S(1)}, bf16[96,256]{1,0:T(8,128)(2,1)S(1)}, u32[]{:S(2)}, u32[]{:S(2)}) collective-permute-start(bf16[96,256]{1,0:T(8,128)(2,1)S(1)} %get-tuple-element.37), channel_id=1, source_target_pairs={{0,8},{4,12},{8,0},{12,4},{1,9},{5,13},{9,1},{13,5},{2,10},{6,14},... | collective-permute-start | bytes 147464 | tf_op jit(solution)/shard_map/ppermute | solution.py:17
  14.7 6.8 %collective-permute-start.5 = (bf16[96,256]{1,0:T(8,128)(2,1)S(1)}, bf16[96,256]{1,0:T(8,128)(2,1)S(1)}, u32[]{:S(2)}, u32[]{:S(2)}) collective-permute-start(bf16[96,256]{1,0:T(8,128)(2,1)S(1)} %get-tuple-element.38), channel_id=1, source_target_pairs={{0,4},{4,0},{8,12},{12,8},{1,5},{5,1},{9,13},{13,9},{2,6},{6,2},{1... | collective-permute-start | bytes 147464 | tf_op jit(solution)/shard_map/ppermute | solution.py:17
  17.5 6.7 %collective-permute-start.8 = (bf16[144,256]{1,0:T(8,128)(2,1)S(1)}, bf16[144,256]{1,0:T(8,128)(2,1)S(1)}, u32[]{:S(2)}, u32[]{:S(2)}) collective-permute-start(bf16[144,256]{1,0:T(8,128)(2,1)S(1)} %get-tuple-element.43), channel_id=1, source_target_pairs={{0,12},{4,8},{8,4},{12,0},{1,13},{5,9},{9,5},{13,1},{2,14},{6,10},... | collective-permute-start | bytes 221192 | tf_op jit(solution)/shard_map/ppermute | solution.py:17
  21.5 6.3 %collective-permute-start.11 = (bf16[240,256]{1,0:T(8,128)(2,1)S(1)}, bf16[240,256]{1,0:T(8,128)(2,1)S(1)}, u32[]{:S(2)}, u32[]{:S(2)}) collective-permute-start(bf16[240,256]{1,0:T(8,128)(2,1)S(1)} %get-tuple-element.49), channel_id=1, source_target_pairs={{0,1},{1,0},{2,3},{3,2},{4,5},{5,4},{6,7},{7,6},{8,9},{9,8},{10,11... | collective-permute-start | bytes 368648 | tf_op jit(solution)/shard_map/ppermute | solution.py:17
  21.6 5.7 %collective-permute-start.9 = (bf16[144,256]{1,0:T(8,128)(2,1)S(1)}, bf16[144,256]{1,0:T(8,128)(2,1)S(1)}, u32[]{:S(2)}, u32[]{:S(2)}) collective-permute-start(bf16[144,256]{1,0:T(8,128)(2,1)S(1)} %get-tuple-element.44), channel_id=1, source_target_pairs={{0,8},{4,12},{8,0},{12,4},{1,9},{5,13},{9,1},{13,5},{2,10},{6,14},... | collective-permute-start | bytes 221192 | tf_op jit(solution)/shard_map/ppermute | solution.py:17
  21.9 6.0 %collective-permute-start.10 = (bf16[144,256]{1,0:T(8,128)(2,1)S(1)}, bf16[144,256]{1,0:T(8,128)(2,1)S(1)}, u32[]{:S(2)}, u32[]{:S(2)}) collective-permute-start(bf16[144,256]{1,0:T(8,128)(2,1)S(1)} %get-tuple-element.45), channel_id=1, source_target_pairs={{0,4},{4,0},{8,12},{12,8},{1,5},{5,1},{9,13},{13,9},{2,6},{6,2},{1... | collective-permute-start | bytes 221192 | tf_op jit(solution)/shard_map/ppermute | solution.py:17
  22.4 14.0 %collective-permute-start.16 = (bf16[240,256]{1,0:T(8,128)(2,1)S(1)}, bf16[240,256]{1,0:T(8,128)(2,1)S(1)}, u32[]{:S(2)}, u32[]{:S(2)}) collective-permute-start(bf16[240,256]{1,0:T(8,128)(2,1)S(1)} %get-tuple-element.56), channel_id=1, source_target_pairs={{0,2},{1,3},{2,0},{3,1},{4,6},{5,7},{6,4},{7,5},{8,10},{9,11},{10,... | collective-permute-start | bytes 368648 | tf_op jit(solution)/shard_map/ppermute | solution.py:17
  24.2 12.2 %collective-permute-start.17 = (bf16[240,256]{1,0:T(8,128)(2,1)S(1)}, bf16[240,256]{1,0:T(8,128)(2,1)S(1)}, u32[]{:S(2)}, u32[]{:S(2)}) collective-permute-start(bf16[240,256]{1,0:T(8,128)(2,1)S(1)} %get-tuple-element.57), channel_id=1, source_target_pairs={{0,3},{1,2},{2,1},{3,0},{4,7},{5,6},{6,5},{7,4},{8,11},{9,10},{10,... | collective-permute-start | bytes 368648 | tf_op jit(solution)/shard_map/ppermute | solution.py:17
  28.2 1.3 %collective-permute-start.12 = (f32[80,120]{1,0:T(8,128)S(1)}, f32[80,120]{1,0:T(8,128)S(1)}, u32[]{:S(2)}, u32[]{:S(2)}) collective-permute-start(f32[80,120]{1,0:T(8,128)S(1)} %get-tuple-element.51), channel_id=1, source_target_pairs={{0,1},{1,0},{2,3},{3,2},{4,5},{5,4},{6,7},{7,6},{8,9},{9,8},{10,11... | collective-permute-start | bytes 115208 | tf_op jit(solution)/shard_map/ppermute | solution.py:17
  29.7 5.7 %collective-permute-start.13 = (f32[40,120]{1,0:T(8,128)S(1)}, f32[40,120]{1,0:T(8,128)S(1)}, u32[]{:S(2)}, u32[]{:S(2)}) collective-permute-start(f32[40,120]{1,0:T(8,128)S(1)} %get-tuple-element.52), channel_id=1, source_target_pairs={{0,12},{4,8},{8,4},{12,0},{1,13},{5,9},{9,5},{13,1},{2,14},{6,10},... | collective-permute-start | bytes 57608 | tf_op jit(solution)/shard_map/ppermute | solution.py:17
  31.7 4.7 %collective-permute-start.14 = (f32[40,120]{1,0:T(8,128)S(1)}, f32[40,120]{1,0:T(8,128)S(1)}, u32[]{:S(2)}, u32[]{:S(2)}) collective-permute-start(f32[40,120]{1,0:T(8,128)S(1)} %get-tuple-element.53), channel_id=1, source_target_pairs={{0,8},{4,12},{8,0},{12,4},{1,9},{5,13},{9,1},{13,5},{2,10},{6,14},... | collective-permute-start | bytes 57608 | tf_op jit(solution)/shard_map/ppermute | solution.py:17
  32.3 4.1 %collective-permute-start.15 = (f32[40,120]{1,0:T(8,128)S(1)}, f32[40,120]{1,0:T(8,128)S(1)}, u32[]{:S(2)}, u32[]{:S(2)}) collective-permute-start(f32[40,120]{1,0:T(8,128)S(1)} %get-tuple-element.54), channel_id=1, source_target_pairs={{0,4},{4,0},{8,12},{12,8},{1,5},{5,1},{9,13},{13,9},{2,6},{6,2},{1... | collective-permute-start | bytes 57608 | tf_op jit(solution)/shard_map/ppermute | solution.py:17
  36.5 4.7 %collective-permute-start.20 = (f32[40,80]{1,0:T(8,128)S(1)}, f32[40,80]{1,0:T(8,128)S(1)}, u32[]{:S(2)}, u32[]{:S(2)}) collective-permute-start(f32[40,80]{1,0:T(8,128)S(1)} %get-tuple-element.58), channel_id=1, source_target_pairs={{0,18},{1,19},{2,16},{3,17},{16,2},{17,3},{18,0},{19,1},{4,22},{5,... | collective-permute-start | bytes 38408 | tf_op jit(solution)/shard_map/ppermute | solution.py:17
  39.0 3.8 %collective-permute-start.18 = (f32[40,80]{1,0:T(8,128)S(1)}, f32[40,80]{1,0:T(8,128)S(1)}, u32[]{:S(2)}, u32[]{:S(2)}) collective-permute-start(f32[40,80]{1,0:T(8,128)S(1)} %get-tuple-element.58), channel_id=1, source_target_pairs={{0,2},{1,3},{2,0},{3,1},{16,18},{17,19},{18,16},{19,17},{4,6},{5,7... | collective-permute-start | bytes 38408 | tf_op jit(solution)/shard_map/ppermute | solution.py:17
  39.5 3.8 %collective-permute-start.19 = (f32[40,80]{1,0:T(8,128)S(1)}, f32[40,80]{1,0:T(8,128)S(1)}, u32[]{:S(2)}, u32[]{:S(2)}) collective-permute-start(f32[40,80]{1,0:T(8,128)S(1)} %get-tuple-element.59), channel_id=1, source_target_pairs={{0,16},{1,17},{2,18},{3,19},{16,0},{17,1},{18,2},{19,3},{4,20},{5,... | collective-permute-start | bytes 38408 | tf_op jit(solution)/shard_map/ppermute | solution.py:17

commit v6 on v3

--- a/solution.py
+++ b/solution.py
@@ -19,6 +19,10 @@
 
 def farthest_first(n):
     return list(range(n - 1, -1, -1))
+
+
+def middle_first(n):
+    return [n // 2] + [k for k in range(n - 1, -1, -1) if k != n // 2]
 
 
 def swaps(values, axis):
@@ -164,7 +168,7 @@
     ins, (view,), _, outs, wholes, (blocks,) = cut(refs, parts * len(counts), 1, spare, parts, len(counts))
     z, lights = lax.axis_index("light"), sum(counts)
     for c, whole in enumerate(wholes):
-        for i, k in enumerate(farthest_first(parts)):
+        for i, k in enumerate(middle_first(parts)):
             whole[z ^ k] = ins[c * parts + i][...]
     gram = jnp.zeros((parts * lights, parts * lights), f32)
     for r in range(wholes[0].shape[1] // counts[0]):
@@ -255,7 +259,8 @@
             whole[c][::-1] + near[::-1] + carried,
             waits,
         )
-        lit += swaps(made[:parts], "light")[::-1]
+        got = swaps(made[:parts], "light")
+        lit += [got[k] for k in middle_first(parts)]
         pieces.append(made[parts])
         carried = list(made[parts + 1 :])
     back = call(
@@ -280,12 +285,13 @@
         lit + [view_part],
         [returned[1]],
     )
+    got = swaps(sums, "light")
     dealt = call(
         functools.partial(deal_kernel, lights, rows, views),
         [sds((lights + rows, lights_all), f32)] * views,
         [pltpu.VMEM((views, rows, views_all), f32)],
         0,
-        swaps(sums, "light")[::-1],
+        [got[k] for k in middle_first(parts)],
     )
     total = call(sum_kernel, sds((lights + rows, lights_all), f32), [], 0, swaps(dealt, "view")[::-1])
     total = doubled(total, "texel")

time: 44 us -> 44.8 us (1.018)
  waiting for transfers between devices: 14.1 us -> 14.8 us
    ppermute x21, waiting for transfers between devices: 14.1 us -> 14.8 us  [swap(): lax.ppermute(value, axis, [(i, i ^ step) for i in range(lax.axis_size(axi...]
  transfers between devices with their start and end apart: 21 -> 21, of which waited for: 12 -> 9; matrix products, arithmetic and copies ran while one was open for 0% -> 0% of each run, Pallas kernels for 7% -> 7%
where the time goes in v6:
time: 44.8 us; the launch traced here: 44.6 us
  starting transfers between devices  24.2 us (54%)
  waiting for transfers between devices  14.8 us (33%)
  Pallas kernels  3.07 us (7%)
  local copies, waits for them, and re-layouts  1.79 us (4%)
  between operations  0.73 us (2%)
    ppermute x21, starting transfers between devices, swap(): lax.ppermute(value, axis, [(i, i ^ step) for i in range(lax.axis_size(axi...  24.2 us
    ppermute x21, waiting for transfers between devices, swap(): lax.ppermute(value, axis, [(i, i ^ step) for i in range(lax.axis_size(axi...  14.8 us
    pallas_call x11, Pallas kernels, call(): pl.pallas_call(kernel, out_shape=out_shape, in_specs=[VMEM] * len(args) +...  3.07 us
    unnamed x4, local copies, waits for them, and re-layouts  1.18 us
  transfers between devices with their start and end apart: 21, of which 9 were waited for; matrix products, arithmetic and copies ran while one was open for 0% of the time, Pallas kernels for 7%

profile of v6, /device:TPU:0, one launch (start us, length us, event | category | flops | bytes accessed | tf_op | source)
XLA Modules:
  0.0 44.6 jit_solution(3847456362410856341)
XLA Ops:
  0.6 0.0 copy-start
  0.6 0.0 copy-start.1
  0.7 1.2 %copy-done = bf16[20,20,1024]{2,1,0:T(8,128)(2,1)S(1)} copy-done((bf16[20,20,1024]{2,1,0:T(8,128)(2,1)S(1)}, bf16[20,20,1024]{2,1,0:T(8,128)(2,1)}, u32[]{:S(2)}) %copy-start) | copy-done | bytes 819224
  1.8 0.0 copy-done.1
  1.8 0.1 shard_map.50
  2.0 0.5 %collective-permute-start.2 = (bf16[408,256]{1,0:T(8,128)(2,1)S(1)}, bf16[408,256]{1,0:T(8,128)(2,1)S(1)}, u32[]{:S(2)}, u32[]{:S(2)}) collective-permute-start(bf16[408,256]{1,0:T(8,128)(2,1)S(1)} %get-tuple-element.34), channel_id=1, source_target_pairs={{0,1},{1,0},{2,3},{3,2},{4,5},{5,4},{6,7},{7,6},{8,9},{9,8},{10,11... | collective-permute-start | bytes 626696 | tf_op jit(solution)/shard_map/ppermute | solution.py:17
  2.5 2.6 %collective-permute-start = (bf16[168,256]{1,0:T(8,128)(2,1)S(1)}, bf16[168,256]{1,0:T(8,128)(2,1)S(1)}, u32[]{:S(2)}, u32[]{:S(2)}) collective-permute-start(bf16[168,256]{1,0:T(8,128)(2,1)S(1)} %get-tuple-element.32), channel_id=1, source_target_pairs={{0,3},{1,2},{2,1},{3,0},{4,7},{5,6},{6,5},{7,4},{8,11},{9,10},{10,... | collective-permute-start | bytes 258056 | tf_op jit(solution)/shard_map/ppermute | solution.py:17
  5.1 0.0 collective-permute-start.1
  5.2 2.8 %collective-permute-done.refs_0_.refs_3_ = bf16[168,256]{1,0:T(8,128)(2,1)S(1)} collective-permute-done((bf16[168,256]{1,0:T(8,128)(2,1)S(1)}, bf16[168,256]{1,0:T(8,128)(2,1)S(1)}, u32[]{:S(2)}, u32[]{:S(2)}) %collective-permute-start) | collective-permute-done | bytes 86048 | tf_op jit(solution)/shard_map/ppermute | solution.py:17
  8.0 2.0 %collective-permute-start.6 = (bf16[240,256]{1,0:T(8,128)(2,1)S(1)}, bf16[240,256]{1,0:T(8,128)(2,1)S(1)}, u32[]{:S(2)}, u32[]{:S(2)}) collective-permute-start(bf16[240,256]{1,0:T(8,128)(2,1)S(1)} %get-tuple-element.40), channel_id=1, source_target_pairs={{0,3},{1,2},{2,1},{3,0},{4,7},{5,6},{6,5},{7,4},{8,11},{9,10},{10,... | collective-permute-start | bytes 368648 | tf_op jit(solution)/shard_map/ppermute | solution.py:17
  10.0 0.0 collective-permute-start.7
  10.0 0.0 collective-permute-done.1.refs_1_.refs_2_
  10.0 0.0 collective-permute-done.2.refs_2_.refs_1_
  10.0 0.5 %shard_map.51 = (bf16[96,256]{1,0:T(8,128)(2,1)S(1)}, bf16[96,256]{1,0:T(8,128)(2,1)S(1)}, bf16[96,256]{1,0:T(8,128)(2,1)S(1)}, bf16[96,256]{1,0:T(8,128)(2,1)S(...) custom-call(bf16[168,256]{1,0:T(8,128)(2,1)S(1)} %collective-permute-done.refs_0_.refs_3_, ...), custom_call_target="tpu_custom_call" | custom-call | flops 15728640 | bytes 990720 | tf_op jit(solution)/shard_map/pallas_call | solution.py:50
  10.5 3.1 %collective-permute-start.3 = (bf16[96,256]{1,0:T(8,128)(2,1)S(1)}, bf16[96,256]{1,0:T(8,128)(2,1)S(1)}, u32[]{:S(2)}, u32[]{:S(2)}) collective-permute-start(bf16[96,256]{1,0:T(8,128)(2,1)S(1)} %get-tuple-element.36), channel_id=1, source_target_pairs={{0,8},{4,12},{8,0},{12,4},{1,9},{5,13},{9,1},{13,5},{2,10},{6,14},... | collective-permute-start | bytes 147464 | tf_op jit(solution)/shard_map/ppermute | solution.py:17
  13.7 1.3 %collective-permute-start.4 = (bf16[96,256]{1,0:T(8,128)(2,1)S(1)}, bf16[96,256]{1,0:T(8,128)(2,1)S(1)}, u32[]{:S(2)}, u32[]{:S(2)}) collective-permute-start(bf16[96,256]{1,0:T(8,128)(2,1)S(1)} %get-tuple-element.37), channel_id=1, source_target_pairs={{0,12},{4,8},{8,4},{12,0},{1,13},{5,9},{9,5},{13,1},{2,14},{6,10},... | collective-permute-start | bytes 147464 | tf_op jit(solution)/shard_map/ppermute | solution.py:17
  15.0 0.2 collective-permute-start.5
  15.3 0.0 collective-permute-done.6.refs_0_.refs_5_
  15.3 1.3 %collective-permute-done.7.refs_1_.refs_4_ = bf16[240,256]{1,0:T(8,128)(2,1)S(1)} collective-permute-done((bf16[240,256]{1,0:T(8,128)(2,1)S(1)}, bf16[240,256]{1,0:T(8,128)(2,1)S(1)}, u32[]{:S(2)}, u32[]{:S(2)}) %collective-permute-start.7) | collective-permute-done | bytes 122912 | tf_op jit(solution)/shard_map/ppermute | solution.py:17
  16.5 0.0 collective-permute-done.3.refs_5_.refs_2_.refs_0_
  16.5 0.5 %shard_map.53 = (bf16[144,256]{1,0:T(8,128)(2,1)S(1)}, bf16[144,256]{1,0:T(8,128)(2,1)S(1)}, bf16[144,256]{1,0:T(8,128)(2,1)S(1)}, bf16[144,256]{1,0:T(8,128)(2,1)S(1)}, bf16[4,144,256]{2,1,0:T(8,128)(2,1)S(1)}) custom-call(bf16[240,256]{1,0:T(8,128)(2,1)S(1)} %collective-permute-done.6.refs_0_.refs_5_, ...), custom_call_target="tpu_custom_call" | custom-call | flops 23592960 | bytes 1261056 | tf_op jit(solution)/shard_map/pallas_call | solution.py:50
  17.0 2.7 %collective-permute-start.8 = (bf16[144,256]{1,0:T(8,128)(2,1)S(1)}, bf16[144,256]{1,0:T(8,128)(2,1)S(1)}, u32[]{:S(2)}, u32[]{:S(2)}) collective-permute-start(bf16[144,256]{1,0:T(8,128)(2,1)S(1)} %get-tuple-element.43), channel_id=1, source_target_pairs={{0,8},{4,12},{8,0},{12,4},{1,9},{5,13},{9,1},{13,5},{2,10},{6,14},... | collective-permute-start | bytes 221192 | tf_op jit(solution)/shard_map/ppermute | solution.py:17
  19.7 0.0 collective-permute-done.4.refs_3_.refs_1_
  19.7 0.0 collective-permute-done.5.refs_4_.refs_2_
  19.8 0.1 collective-permute-start.11
  19.8 2.5 %collective-permute-start.9 = (bf16[144,256]{1,0:T(8,128)(2,1)S(1)}, bf16[144,256]{1,0:T(8,128)(2,1)S(1)}, u32[]{:S(2)}, u32[]{:S(2)}) collective-permute-start(bf16[144,256]{1,0:T(8,128)(2,1)S(1)} %get-tuple-element.44), channel_id=1, source_target_pairs={{0,12},{4,8},{8,4},{12,0},{1,13},{5,9},{9,5},{13,1},{2,14},{6,10},... | collective-permute-start | bytes 221192 | tf_op jit(solution)/shard_map/ppermute | solution.py:17
  22.3 0.6 %collective-permute-start.10 = (bf16[144,256]{1,0:T(8,128)(2,1)S(1)}, bf16[144,256]{1,0:T(8,128)(2,1)S(1)}, u32[]{:S(2)}, u32[]{:S(2)}) collective-permute-start(bf16[144,256]{1,0:T(8,128)(2,1)S(1)} %get-tuple-element.45), channel_id=1, source_target_pairs={{0,4},{4,0},{8,12},{12,8},{1,5},{5,1},{9,13},{13,9},{2,6},{6,2},{1... | collective-permute-start | bytes 221192 | tf_op jit(solution)/shard_map/ppermute | solution.py:17
  22.9 1.0 %collective-permute-start.19 = (bf16[240,256]{1,0:T(8,128)(2,1)S(1)}, bf16[240,256]{1,0:T(8,128)(2,1)S(1)}, u32[]{:S(2)}, u32[]{:S(2)}) collective-permute-start(bf16[240,256]{1,0:T(8,128)(2,1)S(1)} %get-tuple-element.59), channel_id=1, source_target_pairs={{0,2},{1,3},{2,0},{3,1},{4,6},{5,7},{6,4},{7,5},{8,10},{9,11},{10,... | collective-permute-start | bytes 368648 | tf_op jit(solution)/shard_map/ppermute | solution.py:17
  23.9 0.0 collective-permute-done.8.refs_4_
  23.9 0.4 collective-permute-start.20
  24.3 0.5 %shard_map.54.refs_8_ = f32[40,128]{1,0:T(8,128)S(1)} custom-call(bf16[408,256]{1,0:T(8,128)(2,1)S(1)} %get-tuple-element.35.refs_3_.refs_0_, bf16[408,256]{1,0:T(8,128)(2,1)S(1)} %collective-permute-done.2.refs_2_.refs_1_, bf16[168,256]{1,0:T(8,128)(2,1)S(1)} %collective-permute-done.1.refs_1_.refs_2_, ...), custom_call_target="tpu_custom_call" | custom-call | flops 65536000 | bytes 856064 | tf_op jit(solution)/shard_map/pallas_call | solution.py:50
  24.8 1.6 %collective-permute-done.9.refs_5_ = bf16[144,256]{1,0:T(8,128)(2,1)S(1)} collective-permute-done((bf16[144,256]{1,0:T(8,128)(2,1)S(1)}, bf16[144,256]{1,0:T(8,128)(2,1)S(1)}, u32[]{:S(2)}, u32[]{:S(2)}) %collective-permute-start.9) | collective-permute-done | bytes 73760 | tf_op jit(solution)/shard_map/ppermute | solution.py:17
  26.5 1.4 %collective-permute-done.10.refs_6_ = bf16[144,256]{1,0:T(8,128)(2,1)S(1)} collective-permute-done((bf16[144,256]{1,0:T(8,128)(2,1)S(1)}, bf16[144,256]{1,0:T(8,128)(2,1)S(1)}, u32[]{:S(2)}, u32[]{:S(2)}) %collective-permute-start.10) | collective-permute-done | bytes 73760 | tf_op jit(solution)/shard_map/ppermute | solution.py:17
  27.9 0.0 collective-permute-done.11.refs_9_.refs_1_
  27.9 0.3 shard_map.56
  28.3 1.7 %collective-permute-start.12 = (f32[60,128]{1,0:T(8,128)S(1)}, f32[60,128]{1,0:T(8,128)S(1)}, u32[]{:S(2)}, u32[]{:S(2)}) collective-permute-start(f32[60,128]{1,0:T(8,128)S(1)} %get-tuple-element.50), channel_id=1, source_target_pairs={{0,8},{4,12},{8,0},{12,4},{1,9},{5,13},{9,1},{13,5},{2,10},{6,14},... | collective-permute-start | bytes 92168 | tf_op jit(solution)/shard_map/ppermute | solution.py:17
  30.0 1.4 %collective-permute-start.13 = (f32[60,128]{1,0:T(8,128)S(1)}, f32[60,128]{1,0:T(8,128)S(1)}, u32[]{:S(2)}, u32[]{:S(2)}) collective-permute-start(f32[60,128]{1,0:T(8,128)S(1)} %get-tuple-element.51), channel_id=1, source_target_pairs={{0,12},{4,8},{8,4},{12,0},{1,13},{5,9},{9,5},{13,1},{2,14},{6,10},... | collective-permute-start | bytes 92168 | tf_op jit(solution)/shard_map/ppermute | solution.py:17
  31.3 0.5 %collective-permute-start.14 = (f32[60,128]{1,0:T(8,128)S(1)}, f32[60,128]{1,0:T(8,128)S(1)}, u32[]{:S(2)}, u32[]{:S(2)}) collective-permute-start(f32[60,128]{1,0:T(8,128)S(1)} %get-tuple-element.52), channel_id=1, source_target_pairs={{0,4},{4,0},{8,12},{12,8},{1,5},{5,1},{9,13},{13,9},{2,6},{6,2},{1... | collective-permute-start | bytes 92168 | tf_op jit(solution)/shard_map/ppermute | solution.py:17
  31.8 2.2 %collective-permute-done.12.refs_0_ = f32[60,128]{1,0:T(8,128)S(1)} collective-permute-done((f32[60,128]{1,0:T(8,128)S(1)}, f32[60,128]{1,0:T(8,128)S(1)}, u32[]{:S(2)}, u32[]{:S(2)}) %collective-permute-start.12) | collective-permute-done | bytes 30752 | tf_op jit(solution)/shard_map/ppermute | solution.py:17
  34.0 2.0 %collective-permute-done.13.refs_1_ = f32[60,128]{1,0:T(8,128)S(1)} collective-permute-done((f32[60,128]{1,0:T(8,128)S(1)}, f32[60,128]{1,0:T(8,128)S(1)}, u32[]{:S(2)}, u32[]{:S(2)}) %collective-permute-start.13) | collective-permute-done | bytes 30752 | tf_op jit(solution)/shard_map/ppermute | solution.py:17
  35.9 0.0 collective-permute-done.14.refs_2_
  35.9 0.2 shard_map.57
  36.1 0.1 collective-permute-start.15
  36.2 1.1 %collective-permute-start.16 = (f32[40,80]{1,0:T(8,128)S(1)}, f32[40,80]{1,0:T(8,128)S(1)}, u32[]{:S(2)}, u32[]{:S(2)}) collective-permute-start(f32[40,80]{1,0:T(8,128)S(1)} %get-tuple-element.55), channel_id=1, source_target_pairs={{0,2},{1,3},{2,0},{3,1},{4,6},{5,7},{6,4},{7,5},{8,10},{9,11},{10,... | collective-permute-start | bytes 38408 | tf_op jit(solution)/shard_map/ppermute | solution.py:17
  37.3 0.7 %collective-permute-start.17 = (f32[40,80]{1,0:T(8,128)S(1)}, f32[40,80]{1,0:T(8,128)S(1)}, u32[]{:S(2)}, u32[]{:S(2)}) collective-permute-start(f32[40,80]{1,0:T(8,128)S(1)} %get-tuple-element.56), channel_id=1, source_target_pairs={{0,1},{1,0},{2,3},{3,2},{4,5},{5,4},{6,7},{7,6},{8,9},{9,8},{10,11... | collective-permute-start | bytes 38408 | tf_op jit(solution)/shard_map/ppermute | solution.py:17
  38.0 1.3 %collective-permute-done.15.refs_0_ = f32[40,80]{1,0:T(8,128)S(1)} collective-permute-done((f32[40,80]{1,0:T(8,128)S(1)}, f32[40,80]{1,0:T(8,128)S(1)}, u32[]{:S(2)}, u32[]{:S(2)}) %collective-permute-start.15) | collective-permute-done | bytes 12832 | tf_op jit(solution)/shard_map/ppermute | solution.py:17
  39.4 0.7 %collective-permute-done.16.refs_1_ = f32[40,80]{1,0:T(8,128)S(1)} collective-permute-done((f32[40,80]{1,0:T(8,128)S(1)}, f32[40,80]{1,0:T(8,128)S(1)}, u32[]{:S(2)}, u32[]{:S(2)}) %collective-permute-start.16) | collective-permute-done | bytes 12832 | tf_op jit(solution)/shard_map/ppermute | solution.py:17
  40.1 0.0 collective-permute-done.17.refs_2_
  40.1 1.6 %collective-permute-start.18 = (f32[40,80]{1,0:T(8,128)S(1)}, f32[40,80]{1,0:T(8,128)S(1)}, u32[]{:S(2)}, u32[]{:S(2)}) collective-permute-start(f32[40,80]{1,0:T(8,128)S(1)} %shard_map.58), channel_id=1, source_target_pairs={{0,16},{16,0},{1,17},{17,1},{2,18},{18,2},{3,19},{19,3},{4,20},{20... | collective-permute-start | bytes 38408 | tf_op jit(solution)/shard_map/ppermute | solution.py:17
  41.7 0.0 collective-permute-done.19.refs_2_
  41.7 0.0 collective-permute-done.20.refs_3_
  41.7 0.9 %shard_map.59 = bf16[12,20,1024]{2,1,0:T(8,128)(2,1)} custom-call(bf16[240,256]{1,0:T(8,128)(2,1)S(1)} %get-tuple-element.58.refs_0_, bf16[240,256]{1,0:T(8,128)(2,1)S(1)} %collective-permute-done.11.refs_9_.refs_1_, bf16[240,256]{1,0:T(8,128)(2,1)S(1)} %collective-permute-done.19.refs_2_, bf16[240,256]{1,0:T(8,128)(2,1)S(1)} %collective-permute-done.20.refs_3_), custom_call_target="tpu_custom_call" | custom-call | bytes 983040 | tf_op jit(solution)/shard_map/pallas_call | solution.py:50
  42.6 1.4 %collective-permute-done.18 = f32[40,80]{1,0:T(8,128)S(1)} collective-permute-done((f32[40,80]{1,0:T(8,128)S(1)}, f32[40,80]{1,0:T(8,128)S(1)}, u32[]{:S(2)}, u32[]{:S(2)}) %collective-permute-start.18) | collective-permute-done | bytes 12832 | tf_op jit(solution)/shard_map/ppermute | solution.py:17
  44.0 0.6 %fusion = (f32[20,80]{1,0:T(8,128)}, f32[20,80]{1,0:T(8,128)}) fusion(f32[40,80]{1,0:T(8,128)S(1)} %add.3), kind=kLoop, calls=%fused_computation | loop fusion | bytes 25600 | tf_op jit(solution)/shard_map/slice | solution.py:305
  (5 shorter events, 0.1 us)
Async XLA Ops:
  0.6 1.2 %copy-start = (bf16[20,20,1024]{2,1,0:T(8,128)(2,1)S(1)}, bf16[20,20,1024]{2,1,0:T(8,128)(2,1)}, u32[]{:S(2)}) copy-start(bf16[20,20,1024]{2,1,0:T(8,128)(2,1)} %slab_ref.3) | copy-start | bytes 2457604
  0.6 1.2 %copy-start.1 = (bf16[20,48]{1,0:T(8,128)(2,1)S(1)}, bf16[20,48]{1,0:T(8,128)(2,1)}, u32[]{:S(2)}) copy-start(bf16[20,48]{1,0:T(8,128)(2,1)} %refs_0_.1) | copy-start | bytes 5764
  2.0 8.1 %collective-permute-start.2 = (bf16[408,256]{1,0:T(8,128)(2,1)S(1)}, bf16[408,256]{1,0:T(8,128)(2,1)S(1)}, u32[]{:S(2)}, u32[]{:S(2)}) collective-permute-start(bf16[408,256]{1,0:T(8,128)(2,1)S(1)} %get-tuple-element.34), channel_id=1, source_target_pairs={{0,1},{1,0},{2,3},{3,2},{4,5},{5,4},{6,7},{7,6},{8,9},{9,8},{10,11... | collective-permute-start | bytes 626696 | tf_op jit(solution)/shard_map/ppermute | solution.py:17
  2.5 5.5 %collective-permute-start = (bf16[168,256]{1,0:T(8,128)(2,1)S(1)}, bf16[168,256]{1,0:T(8,128)(2,1)S(1)}, u32[]{:S(2)}, u32[]{:S(2)}) collective-permute-start(bf16[168,256]{1,0:T(8,128)(2,1)S(1)} %get-tuple-element.32), channel_id=1, source_target_pairs={{0,3},{1,2},{2,1},{3,0},{4,7},{5,6},{6,5},{7,4},{8,11},{9,10},{10,... | collective-permute-start | bytes 258056 | tf_op jit(solution)/shard_map/ppermute | solution.py:17
  5.1 4.9 %collective-permute-start.1 = (bf16[168,256]{1,0:T(8,128)(2,1)S(1)}, bf16[168,256]{1,0:T(8,128)(2,1)S(1)}, u32[]{:S(2)}, u32[]{:S(2)}) collective-permute-start(bf16[168,256]{1,0:T(8,128)(2,1)S(1)} %get-tuple-element.33), channel_id=1, source_target_pairs={{0,2},{1,3},{2,0},{3,1},{4,6},{5,7},{6,4},{7,5},{8,10},{9,11},{10,... | collective-permute-start | bytes 258056 | tf_op jit(solution)/shard_map/ppermute | solution.py:17
  8.0 7.2 %collective-permute-start.6 = (bf16[240,256]{1,0:T(8,128)(2,1)S(1)}, bf16[240,256]{1,0:T(8,128)(2,1)S(1)}, u32[]{:S(2)}, u32[]{:S(2)}) collective-permute-start(bf16[240,256]{1,0:T(8,128)(2,1)S(1)} %get-tuple-element.40), channel_id=1, source_target_pairs={{0,3},{1,2},{2,1},{3,0},{4,7},{5,6},{6,5},{7,4},{8,11},{9,10},{10,... | collective-permute-start | bytes 368648 | tf_op jit(solution)/shard_map/ppermute | solution.py:17
  10.0 6.5 %collective-permute-start.7 = (bf16[240,256]{1,0:T(8,128)(2,1)S(1)}, bf16[240,256]{1,0:T(8,128)(2,1)S(1)}, u32[]{:S(2)}, u32[]{:S(2)}) collective-permute-start(bf16[240,256]{1,0:T(8,128)(2,1)S(1)} %get-tuple-element.41), channel_id=1, source_target_pairs={{0,2},{1,3},{2,0},{3,1},{4,6},{5,7},{6,4},{7,5},{8,10},{9,11},{10,... | collective-permute-start | bytes 368648 | tf_op jit(solution)/shard_map/ppermute | solution.py:17
  10.5 6.0 %collective-permute-start.3 = (bf16[96,256]{1,0:T(8,128)(2,1)S(1)}, bf16[96,256]{1,0:T(8,128)(2,1)S(1)}, u32[]{:S(2)}, u32[]{:S(2)}) collective-permute-start(bf16[96,256]{1,0:T(8,128)(2,1)S(1)} %get-tuple-element.36), channel_id=1, source_target_pairs={{0,8},{4,12},{8,0},{12,4},{1,9},{5,13},{9,1},{13,5},{2,10},{6,14},... | collective-permute-start | bytes 147464 | tf_op jit(solution)/shard_map/ppermute | solution.py:17
  13.7 6.0 %collective-permute-start.4 = (bf16[96,256]{1,0:T(8,128)(2,1)S(1)}, bf16[96,256]{1,0:T(8,128)(2,1)S(1)}, u32[]{:S(2)}, u32[]{:S(2)}) collective-permute-start(bf16[96,256]{1,0:T(8,128)(2,1)S(1)} %get-tuple-element.37), channel_id=1, source_target_pairs={{0,12},{4,8},{8,4},{12,0},{1,13},{5,9},{9,5},{13,1},{2,14},{6,10},... | collective-permute-start | bytes 147464 | tf_op jit(solution)/shard_map/ppermute | solution.py:17
  15.0 4.7 %collective-permute-start.5 = (bf16[96,256]{1,0:T(8,128)(2,1)S(1)}, bf16[96,256]{1,0:T(8,128)(2,1)S(1)}, u32[]{:S(2)}, u32[]{:S(2)}) collective-permute-start(bf16[96,256]{1,0:T(8,128)(2,1)S(1)} %get-tuple-element.38), channel_id=1, source_target_pairs={{0,4},{4,0},{8,12},{12,8},{1,5},{5,1},{9,13},{13,9},{2,6},{6,2},{1... | collective-permute-start | bytes 147464 | tf_op jit(solution)/shard_map/ppermute | solution.py:17
  17.0 6.9 %collective-permute-start.8 = (bf16[144,256]{1,0:T(8,128)(2,1)S(1)}, bf16[144,256]{1,0:T(8,128)(2,1)S(1)}, u32[]{:S(2)}, u32[]{:S(2)}) collective-permute-start(bf16[144,256]{1,0:T(8,128)(2,1)S(1)} %get-tuple-element.43), channel_id=1, source_target_pairs={{0,8},{4,12},{8,0},{12,4},{1,9},{5,13},{9,1},{13,5},{2,10},{6,14},... | collective-permute-start | bytes 221192 | tf_op jit(solution)/shard_map/ppermute | solution.py:17
  19.8 8.1 %collective-permute-start.11 = (bf16[240,256]{1,0:T(8,128)(2,1)S(1)}, bf16[240,256]{1,0:T(8,128)(2,1)S(1)}, u32[]{:S(2)}, u32[]{:S(2)}) collective-permute-start(bf16[240,256]{1,0:T(8,128)(2,1)S(1)} %get-tuple-element.49), channel_id=1, source_target_pairs={{0,1},{1,0},{2,3},{3,2},{4,5},{5,4},{6,7},{7,6},{8,9},{9,8},{10,11... | collective-permute-start | bytes 368648 | tf_op jit(solution)/shard_map/ppermute | solution.py:17
  19.8 6.6 %collective-permute-start.9 = (bf16[144,256]{1,0:T(8,128)(2,1)S(1)}, bf16[144,256]{1,0:T(8,128)(2,1)S(1)}, u32[]{:S(2)}, u32[]{:S(2)}) collective-permute-start(bf16[144,256]{1,0:T(8,128)(2,1)S(1)} %get-tuple-element.44), channel_id=1, source_target_pairs={{0,12},{4,8},{8,4},{12,0},{1,13},{5,9},{9,5},{13,1},{2,14},{6,10},... | collective-permute-start | bytes 221192 | tf_op jit(solution)/shard_map/ppermute | solution.py:17
  22.3 5.6 %collective-permute-start.10 = (bf16[144,256]{1,0:T(8,128)(2,1)S(1)}, bf16[144,256]{1,0:T(8,128)(2,1)S(1)}, u32[]{:S(2)}, u32[]{:S(2)}) collective-permute-start(bf16[144,256]{1,0:T(8,128)(2,1)S(1)} %get-tuple-element.45), channel_id=1, source_target_pairs={{0,4},{4,0},{8,12},{12,8},{1,5},{5,1},{9,13},{13,9},{2,6},{6,2},{1... | collective-permute-start | bytes 221192 | tf_op jit(solution)/shard_map/ppermute | solution.py:17
  22.9 18.8 %collective-permute-start.19 = (bf16[240,256]{1,0:T(8,128)(2,1)S(1)}, bf16[240,256]{1,0:T(8,128)(2,1)S(1)}, u32[]{:S(2)}, u32[]{:S(2)}) collective-permute-start(bf16[240,256]{1,0:T(8,128)(2,1)S(1)} %get-tuple-element.59), channel_id=1, source_target_pairs={{0,2},{1,3},{2,0},{3,1},{4,6},{5,7},{6,4},{7,5},{8,10},{9,11},{10,... | collective-permute-start | bytes 368648 | tf_op jit(solution)/shard_map/ppermute | solution.py:17
  23.9 17.8 %collective-permute-start.20 = (bf16[240,256]{1,0:T(8,128)(2,1)S(1)}, bf16[240,256]{1,0:T(8,128)(2,1)S(1)}, u32[]{:S(2)}, u32[]{:S(2)}) collective-permute-start(bf16[240,256]{1,0:T(8,128)(2,1)S(1)} %get-tuple-element.60), channel_id=1, source_target_pairs={{0,3},{1,2},{2,1},{3,0},{4,7},{5,6},{6,5},{7,4},{8,11},{9,10},{10,... | collective-permute-start | bytes 368648 | tf_op jit(solution)/shard_map/ppermute | solution.py:17
  28.3 5.7 %collective-permute-start.12 = (f32[60,128]{1,0:T(8,128)S(1)}, f32[60,128]{1,0:T(8,128)S(1)}, u32[]{:S(2)}, u32[]{:S(2)}) collective-permute-start(f32[60,128]{1,0:T(8,128)S(1)} %get-tuple-element.50), channel_id=1, source_target_pairs={{0,8},{4,12},{8,0},{12,4},{1,9},{5,13},{9,1},{13,5},{2,10},{6,14},... | collective-permute-start | bytes 92168 | tf_op jit(solution)/shard_map/ppermute | solution.py:17
  30.0 6.0 %collective-permute-start.13 = (f32[60,128]{1,0:T(8,128)S(1)}, f32[60,128]{1,0:T(8,128)S(1)}, u32[]{:S(2)}, u32[]{:S(2)}) collective-permute-start(f32[60,128]{1,0:T(8,128)S(1)} %get-tuple-element.51), channel_id=1, source_target_pairs={{0,12},{4,8},{8,4},{12,0},{1,13},{5,9},{9,5},{13,1},{2,14},{6,10},... | collective-permute-start | bytes 92168 | tf_op jit(solution)/shard_map/ppermute | solution.py:17
  31.3 4.6 %collective-permute-start.14 = (f32[60,128]{1,0:T(8,128)S(1)}, f32[60,128]{1,0:T(8,128)S(1)}, u32[]{:S(2)}, u32[]{:S(2)}) collective-permute-start(f32[60,128]{1,0:T(8,128)S(1)} %get-tuple-element.52), channel_id=1, source_target_pairs={{0,4},{4,0},{8,12},{12,8},{1,5},{5,1},{9,13},{13,9},{2,6},{6,2},{1... | collective-permute-start | bytes 92168 | tf_op jit(solution)/shard_map/ppermute | solution.py:17
  36.1 3.3 %collective-permute-start.15 = (f32[40,80]{1,0:T(8,128)S(1)}, f32[40,80]{1,0:T(8,128)S(1)}, u32[]{:S(2)}, u32[]{:S(2)}) collective-permute-start(f32[40,80]{1,0:T(8,128)S(1)} %get-tuple-element.54), channel_id=1, source_target_pairs={{0,3},{1,2},{2,1},{3,0},{4,7},{5,6},{6,5},{7,4},{8,11},{9,10},{10,... | collective-permute-start | bytes 38408 | tf_op jit(solution)/shard_map/ppermute | solution.py:17
  36.2 3.9 %collective-permute-start.16 = (f32[40,80]{1,0:T(8,128)S(1)}, f32[40,80]{1,0:T(8,128)S(1)}, u32[]{:S(2)}, u32[]{:S(2)}) collective-permute-start(f32[40,80]{1,0:T(8,128)S(1)} %get-tuple-element.55), channel_id=1, source_target_pairs={{0,2},{1,3},{2,0},{3,1},{4,6},{5,7},{6,4},{7,5},{8,10},{9,11},{10,... | collective-permute-start | bytes 38408 | tf_op jit(solution)/shard_map/ppermute | solution.py:17
  37.3 2.8 %collective-permute-start.17 = (f32[40,80]{1,0:T(8,128)S(1)}, f32[40,80]{1,0:T(8,128)S(1)}, u32[]{:S(2)}, u32[]{:S(2)}) collective-permute-start(f32[40,80]{1,0:T(8,128)S(1)} %get-tuple-element.56), channel_id=1, source_target_pairs={{0,1},{1,0},{2,3},{3,2},{4,5},{5,4},{6,7},{7,6},{8,9},{9,8},{10,11... | collective-permute-start | bytes 38408 | tf_op jit(solution)/shard_map/ppermute | solution.py:17
  40.1 3.8 %collective-permute-start.18 = (f32[40,80]{1,0:T(8,128)S(1)}, f32[40,80]{1,0:T(8,128)S(1)}, u32[]{:S(2)}, u32[]{:S(2)}) collective-permute-start(f32[40,80]{1,0:T(8,128)S(1)} %shard_map.58), channel_id=1, source_target_pairs={{0,16},{16,0},{1,17},{17,1},{2,18},{18,2},{3,19},{19,3},{4,20},{20... | collective-permute-start | bytes 38408 | tf_op jit(solution)/shard_map/ppermute | solution.py:17

commit v7 on v6

--- a/solution.py
+++ b/solution.py
@@ -96,7 +96,7 @@
     whole, turned = refs[-2:]
     v, z = lax.axis_index("view"), lax.axis_index("light")
     width = whole.shape[2]
-    for i, k in enumerate(farthest_first(views)):
+    for i, k in enumerate(middle_first(views)):
         whole[v ^ k] = ins[i][starts[i] : starts[i] + whole.shape[1], :]
     if first:
         deep = rows // groups
@@ -168,7 +168,7 @@
     ins, (view,), _, outs, wholes, (blocks,) = cut(refs, parts * len(counts), 1, spare, parts, len(counts))
     z, lights = lax.axis_index("light"), sum(counts)
     for c, whole in enumerate(wholes):
-        for i, k in enumerate(middle_first(parts)):
+        for i, k in enumerate(farthest_first(parts)):
             whole[z ^ k] = ins[c * parts + i][...]
     gram = jnp.zeros((parts * lights, parts * lights), f32)
     for r in range(wholes[0].shape[1] // counts[0]):
@@ -234,7 +234,7 @@
         [],
         0,
         [slab],
-        whole[0][1:],
+        whole[0][:1],
     )
     moved = {k: swap(packed[k - half], "view", k) for k in farthest_first(views)[:half]}
     whole.append([moved[k] for k in range(half, views)])
@@ -247,7 +247,7 @@
         waits = lit[:1] if c else []
         made = call(
             functools.partial(
-                core_kernel, count, 0 if c else head, [0] * half + [tall[0] * c] * half, rows, ranks, views, parts,
+                core_kernel, count, 0 if c else head, [0 if k >= half else tall[0] * c for k in middle_first(views)], rows, ranks, views, parts,
                 0 if c else groups, len(waits),
             ),
             outs,
@@ -256,11 +256,10 @@
                 pltpu.VMEM((width // 128, count * ranks, 128), f32),
             ],
             2 * views_all * count * width * ranks,
-            whole[c][::-1] + near[::-1] + carried,
+            [(near + whole[c])[k] for k in middle_first(views)] + carried,
             waits,
         )
-        got = swaps(made[:parts], "light")
-        lit += [got[k] for k in middle_first(parts)]
+        lit += swaps(made[:parts], "light")[::-1]
         pieces.append(made[parts])
         carried = list(made[parts + 1 :])
     back = call(
@@ -293,7 +292,9 @@
         0,
         [got[k] for k in middle_first(parts)],
     )
-    total = call(sum_kernel, sds((lights + rows, lights_all), f32), [], 0, swaps(dealt, "view")[::-1])
+    got = swaps(dealt, "view")
+    got = [got[k] for k in middle_first(views)]
+    total = call(sum_kernel, sds((lights + rows, lights_all), f32), [], 0, got)
     total = doubled(total, "texel")
     core = call(
         functools.partial(place_kernel, counts),

time: 44.8 us -> 44.9 us (level)
  waiting for transfers between devices: 14.8 us -> 15.7 us
  starting transfers between devices: 24.2 us -> 23.5 us
    ppermute x21, waiting for transfers between devices: 14.8 us -> 15.7 us  [swap(): lax.ppermute(value, axis, [(i, i ^ step) for i in range(lax.axis_size(axi...]
    ppermute x21, starting transfers between devices: 24.2 us -> 23.5 us  [swap(): lax.ppermute(value, axis, [(i, i ^ step) for i in range(lax.axis_size(axi...]
  transfers between devices with their start and end apart: 21 -> 21, of which waited for: 9 -> 12; matrix products, arithmetic and copies ran while one was open for 0% -> 0% of each run, Pallas kernels for 7% -> 7%
where the time goes in v7:
time: 44.9 us; the launch traced here: 44.8 us
  starting transfers between devices  23.5 us (52%)
  waiting for transfers between devices  15.7 us (35%)
  Pallas kernels  3.07 us (7%)
  local copies, waits for them, and re-layouts  1.79 us (4%)
  between operations  0.73 us (2%)
    ppermute x21, starting transfers between devices, swap(): lax.ppermute(value, axis, [(i, i ^ step) for i in range(lax.axis_size(axi...  23.5 us
    ppermute x21, waiting for transfers between devices, swap(): lax.ppermute(value, axis, [(i, i ^ step) for i in range(lax.axis_size(axi...  15.7 us
    pallas_call x11, Pallas kernels, call(): pl.pallas_call(kernel, out_shape=out_shape, in_specs=[VMEM] * len(args) +...  3.07 us
    unnamed x4, local copies, waits for them, and re-layouts  1.18 us
  transfers between devices with their start and end apart: 21, of which 12 were waited for; matrix products, arithmetic and copies ran while one was open for 0% of the time, Pallas kernels for 7%

profile of v7, /device:TPU:0, one launch (start us, length us, event | category | flops | bytes accessed | tf_op | source)
XLA Modules:
  0.0 44.8 jit_solution(6796687717097558405)
XLA Ops:
  0.6 0.0 copy-start
  0.6 0.0 copy-start.1
  0.7 1.2 %copy-done = bf16[20,20,1024]{2,1,0:T(8,128)(2,1)S(1)} copy-done((bf16[20,20,1024]{2,1,0:T(8,128)(2,1)S(1)}, bf16[20,20,1024]{2,1,0:T(8,128)(2,1)}, u32[]{:S(2)}) %copy-start) | copy-done | bytes 819224
  1.8 0.0 copy-done.1
  1.8 0.1 shard_map.50
  2.0 0.5 %collective-permute-start.2 = (bf16[408,256]{1,0:T(8,128)(2,1)S(1)}, bf16[408,256]{1,0:T(8,128)(2,1)S(1)}, u32[]{:S(2)}, u32[]{:S(2)}) collective-permute-start(bf16[408,256]{1,0:T(8,128)(2,1)S(1)} %get-tuple-element.34), channel_id=1, source_target_pairs={{0,1},{1,0},{2,3},{3,2},{4,5},{5,4},{6,7},{7,6},{8,9},{9,8},{10,11... | collective-permute-start | bytes 626696 | tf_op jit(solution)/shard_map/ppermute | solution.py:17
  2.5 2.6 %collective-permute-start = (bf16[168,256]{1,0:T(8,128)(2,1)S(1)}, bf16[168,256]{1,0:T(8,128)(2,1)S(1)}, u32[]{:S(2)}, u32[]{:S(2)}) collective-permute-start(bf16[168,256]{1,0:T(8,128)(2,1)S(1)} %get-tuple-element.32), channel_id=1, source_target_pairs={{0,2},{1,3},{2,0},{3,1},{4,6},{5,7},{6,4},{7,5},{8,10},{9,11},{10,... | collective-permute-start | bytes 258056 | tf_op jit(solution)/shard_map/ppermute | solution.py:17
  5.1 0.1 collective-permute-start.1
  5.1 3.1 %collective-permute-done.refs_0_.refs_2_ = bf16[168,256]{1,0:T(8,128)(2,1)S(1)} collective-permute-done((bf16[168,256]{1,0:T(8,128)(2,1)S(1)}, bf16[168,256]{1,0:T(8,128)(2,1)S(1)}, u32[]{:S(2)}, u32[]{:S(2)}) %collective-permute-start) | collective-permute-done | bytes 86048 | tf_op jit(solution)/shard_map/ppermute | solution.py:17
  8.3 2.2 %collective-permute-start.6 = (bf16[240,256]{1,0:T(8,128)(2,1)S(1)}, bf16[240,256]{1,0:T(8,128)(2,1)S(1)}, u32[]{:S(2)}, u32[]{:S(2)}) collective-permute-start(bf16[240,256]{1,0:T(8,128)(2,1)S(1)} %get-tuple-element.40), channel_id=1, source_target_pairs={{0,2},{1,3},{2,0},{3,1},{4,6},{5,7},{6,4},{7,5},{8,10},{9,11},{10,... | collective-permute-start | bytes 368648 | tf_op jit(solution)/shard_map/ppermute | solution.py:17
  10.5 0.0 collective-permute-start.7
  10.5 0.0 collective-permute-done.1.refs_1_.refs_3_
  10.5 0.0 collective-permute-done.2.refs_2_.refs_1_
  10.5 0.5 %shard_map.51 = (bf16[96,256]{1,0:T(8,128)(2,1)S(1)}, bf16[96,256]{1,0:T(8,128)(2,1)S(1)}, bf16[96,256]{1,0:T(8,128)(2,1)S(1)}, bf16[96,256]{1,0:T(8,128)(2,1)S(...) custom-call(bf16[168,256]{1,0:T(8,128)(2,1)S(1)} %collective-permute-done.refs_0_.refs_2_, ...), custom_call_target="tpu_custom_call" | custom-call | flops 15728640 | bytes 990720 | tf_op jit(solution)/shard_map/pallas_call | solution.py:50
  11.0 3.7 %collective-permute-start.3 = (bf16[96,256]{1,0:T(8,128)(2,1)S(1)}, bf16[96,256]{1,0:T(8,128)(2,1)S(1)}, u32[]{:S(2)}, u32[]{:S(2)}) collective-permute-start(bf16[96,256]{1,0:T(8,128)(2,1)S(1)} %get-tuple-element.36), channel_id=1, source_target_pairs={{0,12},{4,8},{8,4},{12,0},{1,13},{5,9},{9,5},{13,1},{2,14},{6,10},... | collective-permute-start | bytes 147464 | tf_op jit(solution)/shard_map/ppermute | solution.py:17
  14.7 0.0 collective-permute-start.4
  14.7 0.8 %collective-permute-start.5 = (bf16[96,256]{1,0:T(8,128)(2,1)S(1)}, bf16[96,256]{1,0:T(8,128)(2,1)S(1)}, u32[]{:S(2)}, u32[]{:S(2)}) collective-permute-start(bf16[96,256]{1,0:T(8,128)(2,1)S(1)} %get-tuple-element.38), channel_id=1, source_target_pairs={{0,4},{4,0},{8,12},{12,8},{1,5},{5,1},{9,13},{13,9},{2,6},{6,2},{1... | collective-permute-start | bytes 147464 | tf_op jit(solution)/shard_map/ppermute | solution.py:17
  15.5 0.0 collective-permute-done.6.refs_0_.refs_4_
  15.5 0.5 %collective-permute-done.7.refs_1_.refs_5_ = bf16[240,256]{1,0:T(8,128)(2,1)S(1)} collective-permute-done((bf16[240,256]{1,0:T(8,128)(2,1)S(1)}, bf16[240,256]{1,0:T(8,128)(2,1)S(1)}, u32[]{:S(2)}, u32[]{:S(2)}) %collective-permute-start.7) | collective-permute-done | bytes 122912 | tf_op jit(solution)/shard_map/ppermute | solution.py:17
  16.0 1.2 %collective-permute-done.3.refs_5_.refs_2_.refs_0_ = bf16[96,256]{1,0:T(8,128)(2,1)S(1)} collective-permute-done((bf16[96,256]{1,0:T(8,128)(2,1)S(1)}, bf16[96,256]{1,0:T(8,128)(2,1)S(1)}, u32[]{:S(2)}, u32[]{:S(2)}) %collective-permute-start.3) | collective-permute-done | bytes 49184 | tf_op jit(solution)/shard_map/ppermute | solution.py:17
  17.3 0.5 %shard_map.53 = (bf16[144,256]{1,0:T(8,128)(2,1)S(1)}, bf16[144,256]{1,0:T(8,128)(2,1)S(1)}, bf16[144,256]{1,0:T(8,128)(2,1)S(1)}, bf16[144,256]{1,0:T(8,128)(2,1)S(1)}, bf16[4,144,256]{2,1,0:T(8,128)(2,1)S(1)}) custom-call(bf16[240,256]{1,0:T(8,128)(2,1)S(1)} %collective-permute-done.6.refs_0_.refs_4_, ...), custom_call_target="tpu_custom_call" | custom-call | flops 23592960 | bytes 1261056 | tf_op jit(solution)/shard_map/pallas_call | solution.py:50
  17.7 3.9 %collective-permute-start.8 = (bf16[144,256]{1,0:T(8,128)(2,1)S(1)}, bf16[144,256]{1,0:T(8,128)(2,1)S(1)}, u32[]{:S(2)}, u32[]{:S(2)}) collective-permute-start(bf16[144,256]{1,0:T(8,128)(2,1)S(1)} %get-tuple-element.43), channel_id=1, source_target_pairs={{0,12},{4,8},{8,4},{12,0},{1,13},{5,9},{9,5},{13,1},{2,14},{6,10},... | collective-permute-start | bytes 221192 | tf_op jit(solution)/shard_map/ppermute | solution.py:17
  21.7 0.0 collective-permute-done.4.refs_3_.refs_1_
  21.7 0.0 collective-permute-done.5.refs_4_.refs_2_
  21.7 0.1 collective-permute-start.11
  21.8 0.1 collective-permute-start.9
  21.9 0.9 %collective-permute-start.10 = (bf16[144,256]{1,0:T(8,128)(2,1)S(1)}, bf16[144,256]{1,0:T(8,128)(2,1)S(1)}, u32[]{:S(2)}, u32[]{:S(2)}) collective-permute-start(bf16[144,256]{1,0:T(8,128)(2,1)S(1)} %get-tuple-element.45), channel_id=1, source_target_pairs={{0,4},{4,0},{8,12},{12,8},{1,5},{5,1},{9,13},{13,9},{2,6},{6,2},{1... | collective-permute-start | bytes 221192 | tf_op jit(solution)/shard_map/ppermute | solution.py:17
  22.8 1.3 %collective-permute-start.19 = (bf16[240,256]{1,0:T(8,128)(2,1)S(1)}, bf16[240,256]{1,0:T(8,128)(2,1)S(1)}, u32[]{:S(2)}, u32[]{:S(2)}) collective-permute-start(bf16[240,256]{1,0:T(8,128)(2,1)S(1)} %get-tuple-element.59), channel_id=1, source_target_pairs={{0,2},{1,3},{2,0},{3,1},{4,6},{5,7},{6,4},{7,5},{8,10},{9,11},{10,... | collective-permute-start | bytes 368648 | tf_op jit(solution)/shard_map/ppermute | solution.py:17
  24.1 0.3 collective-permute-done.8.refs_4_
  24.4 0.0 collective-permute-start.20
  24.4 0.5 %shard_map.54.refs_8_ = f32[40,128]{1,0:T(8,128)S(1)} custom-call(bf16[408,256]{1,0:T(8,128)(2,1)S(1)} %get-tuple-element.35.refs_3_.refs_0_, bf16[408,256]{1,0:T(8,128)(2,1)S(1)} %collective-permute-done.2.refs_2_.refs_1_, bf16[168,256]{1,0:T(8,128)(2,1)S(1)} %collective-permute-done.refs_0_.refs_2_, ...), custom_call_target="tpu_custom_call" | custom-call | flops 65536000 | bytes 856064 | tf_op jit(solution)/shard_map/pallas_call | solution.py:50
  24.9 3.0 %collective-permute-done.9.refs_5_ = bf16[144,256]{1,0:T(8,128)(2,1)S(1)} collective-permute-done((bf16[144,256]{1,0:T(8,128)(2,1)S(1)}, bf16[144,256]{1,0:T(8,128)(2,1)S(1)}, u32[]{:S(2)}, u32[]{:S(2)}) %collective-permute-start.9) | collective-permute-done | bytes 73760 | tf_op jit(solution)/shard_map/ppermute | solution.py:17
  27.9 0.2 collective-permute-done.10.refs_6_
  28.0 0.0 collective-permute-done.11.refs_9_.refs_1_
  28.0 0.3 shard_map.56
  28.4 1.3 %collective-permute-start.12 = (f32[60,128]{1,0:T(8,128)S(1)}, f32[60,128]{1,0:T(8,128)S(1)}, u32[]{:S(2)}, u32[]{:S(2)}) collective-permute-start(f32[60,128]{1,0:T(8,128)S(1)} %get-tuple-element.50), channel_id=1, source_target_pairs={{0,8},{4,12},{8,0},{12,4},{1,9},{5,13},{9,1},{13,5},{2,10},{6,14},... | collective-permute-start | bytes 92168 | tf_op jit(solution)/shard_map/ppermute | solution.py:17
  29.7 2.2 %collective-permute-start.13 = (f32[60,128]{1,0:T(8,128)S(1)}, f32[60,128]{1,0:T(8,128)S(1)}, u32[]{:S(2)}, u32[]{:S(2)}) collective-permute-start(f32[60,128]{1,0:T(8,128)S(1)} %get-tuple-element.51), channel_id=1, source_target_pairs={{0,12},{4,8},{8,4},{12,0},{1,13},{5,9},{9,5},{13,1},{2,14},{6,10},... | collective-permute-start | bytes 92168 | tf_op jit(solution)/shard_map/ppermute | solution.py:17
  31.9 0.0 collective-permute-start.14
  32.0 2.3 %collective-permute-done.12.refs_0_ = f32[60,128]{1,0:T(8,128)S(1)} collective-permute-done((f32[60,128]{1,0:T(8,128)S(1)}, f32[60,128]{1,0:T(8,128)S(1)}, u32[]{:S(2)}, u32[]{:S(2)}) %collective-permute-start.12) | collective-permute-done | bytes 30752 | tf_op jit(solution)/shard_map/ppermute | solution.py:17
  34.2 1.2 %collective-permute-done.13.refs_1_ = f32[60,128]{1,0:T(8,128)S(1)} collective-permute-done((f32[60,128]{1,0:T(8,128)S(1)}, f32[60,128]{1,0:T(8,128)S(1)}, u32[]{:S(2)}, u32[]{:S(2)}) %collective-permute-start.13) | collective-permute-done | bytes 30752 | tf_op jit(solution)/shard_map/ppermute | solution.py:17
  35.4 0.5 %collective-permute-done.14.refs_2_ = f32[60,128]{1,0:T(8,128)S(1)} collective-permute-done((f32[60,128]{1,0:T(8,128)S(1)}, f32[60,128]{1,0:T(8,128)S(1)}, u32[]{:S(2)}, u32[]{:S(2)}) %collective-permute-start.14) | collective-permute-done | bytes 30752 | tf_op jit(solution)/shard_map/ppermute | solution.py:17
  35.9 0.2 shard_map.57
  36.0 1.0 %collective-permute-start.15 = (f32[40,80]{1,0:T(8,128)S(1)}, f32[40,80]{1,0:T(8,128)S(1)}, u32[]{:S(2)}, u32[]{:S(2)}) collective-permute-start(f32[40,80]{1,0:T(8,128)S(1)} %get-tuple-element.54), channel_id=1, source_target_pairs={{0,2},{1,3},{2,0},{3,1},{4,6},{5,7},{6,4},{7,5},{8,10},{9,11},{10,... | collective-permute-start | bytes 38408 | tf_op jit(solution)/shard_map/ppermute | solution.py:17
  37.0 0.0 collective-permute-start.16
  37.0 1.2 %collective-permute-start.17 = (f32[40,80]{1,0:T(8,128)S(1)}, f32[40,80]{1,0:T(8,128)S(1)}, u32[]{:S(2)}, u32[]{:S(2)}) collective-permute-start(f32[40,80]{1,0:T(8,128)S(1)} %get-tuple-element.56), channel_id=1, source_target_pairs={{0,1},{1,0},{2,3},{3,2},{4,5},{5,4},{6,7},{7,6},{8,9},{9,8},{10,11... | collective-permute-start | bytes 38408 | tf_op jit(solution)/shard_map/ppermute | solution.py:17
  38.2 1.6 %collective-permute-done.15.refs_0_ = f32[40,80]{1,0:T(8,128)S(1)} collective-permute-done((f32[40,80]{1,0:T(8,128)S(1)}, f32[40,80]{1,0:T(8,128)S(1)}, u32[]{:S(2)}, u32[]{:S(2)}) %collective-permute-start.15) | collective-permute-done | bytes 12832 | tf_op jit(solution)/shard_map/ppermute | solution.py:17
  39.9 0.4 collective-permute-done.16.refs_1_
  40.3 0.0 collective-permute-done.17.refs_2_
  40.3 1.6 %collective-permute-start.18 = (f32[40,80]{1,0:T(8,128)S(1)}, f32[40,80]{1,0:T(8,128)S(1)}, u32[]{:S(2)}, u32[]{:S(2)}) collective-permute-start(f32[40,80]{1,0:T(8,128)S(1)} %shard_map.58), channel_id=1, source_target_pairs={{0,16},{16,0},{1,17},{17,1},{2,18},{18,2},{3,19},{19,3},{4,20},{20... | collective-permute-start | bytes 38408 | tf_op jit(solution)/shard_map/ppermute | solution.py:17
  41.9 0.0 collective-permute-done.19.refs_2_
  41.9 0.0 collective-permute-done.20.refs_3_
  41.9 0.9 %shard_map.59 = bf16[12,20,1024]{2,1,0:T(8,128)(2,1)} custom-call(bf16[240,256]{1,0:T(8,128)(2,1)S(1)} %get-tuple-element.58.refs_0_, bf16[240,256]{1,0:T(8,128)(2,1)S(1)} %collective-permute-done.11.refs_9_.refs_1_, bf16[240,256]{1,0:T(8,128)(2,1)S(1)} %collective-permute-done.19.refs_2_, bf16[240,256]{1,0:T(8,128)(2,1)S(1)} %collective-permute-done.20.refs_3_), custom_call_target="tpu_custom_call" | custom-call | bytes 983040 | tf_op jit(solution)/shard_map/pallas_call | solution.py:50
  42.8 1.4 %collective-permute-done.18 = f32[40,80]{1,0:T(8,128)S(1)} collective-permute-done((f32[40,80]{1,0:T(8,128)S(1)}, f32[40,80]{1,0:T(8,128)S(1)}, u32[]{:S(2)}, u32[]{:S(2)}) %collective-permute-start.18) | collective-permute-done | bytes 12832 | tf_op jit(solution)/shard_map/ppermute | solution.py:17
  44.2 0.6 %fusion = (f32[20,80]{1,0:T(8,128)}, f32[20,80]{1,0:T(8,128)}) fusion(f32[40,80]{1,0:T(8,128)S(1)} %add.3), kind=kLoop, calls=%fused_computation | loop fusion | bytes 25600 | tf_op jit(solution)/shard_map/slice | solution.py:306
  (5 shorter events, 0.1 us)
Async XLA Ops:
  0.6 1.2 %copy-start = (bf16[20,20,1024]{2,1,0:T(8,128)(2,1)S(1)}, bf16[20,20,1024]{2,1,0:T(8,128)(2,1)}, u32[]{:S(2)}) copy-start(bf16[20,20,1024]{2,1,0:T(8,128)(2,1)} %slab_ref.3) | copy-start | bytes 2457604
  0.6 1.2 %copy-start.1 = (bf16[20,48]{1,0:T(8,128)(2,1)S(1)}, bf16[20,48]{1,0:T(8,128)(2,1)}, u32[]{:S(2)}) copy-start(bf16[20,48]{1,0:T(8,128)(2,1)} %refs_0_.1) | copy-start | bytes 5764
  2.0 8.6 %collective-permute-start.2 = (bf16[408,256]{1,0:T(8,128)(2,1)S(1)}, bf16[408,256]{1,0:T(8,128)(2,1)S(1)}, u32[]{:S(2)}, u32[]{:S(2)}) collective-permute-start(bf16[408,256]{1,0:T(8,128)(2,1)S(1)} %get-tuple-element.34), channel_id=1, source_target_pairs={{0,1},{1,0},{2,3},{3,2},{4,5},{5,4},{6,7},{7,6},{8,9},{9,8},{10,11... | collective-permute-start | bytes 626696 | tf_op jit(solution)/shard_map/ppermute | solution.py:17
  2.5 5.8 %collective-permute-start = (bf16[168,256]{1,0:T(8,128)(2,1)S(1)}, bf16[168,256]{1,0:T(8,128)(2,1)S(1)}, u32[]{:S(2)}, u32[]{:S(2)}) collective-permute-start(bf16[168,256]{1,0:T(8,128)(2,1)S(1)} %get-tuple-element.32), channel_id=1, source_target_pairs={{0,2},{1,3},{2,0},{3,1},{4,6},{5,7},{6,4},{7,5},{8,10},{9,11},{10,... | collective-permute-start | bytes 258056 | tf_op jit(solution)/shard_map/ppermute | solution.py:17
  5.1 5.5 %collective-permute-start.1 = (bf16[168,256]{1,0:T(8,128)(2,1)S(1)}, bf16[168,256]{1,0:T(8,128)(2,1)S(1)}, u32[]{:S(2)}, u32[]{:S(2)}) collective-permute-start(bf16[168,256]{1,0:T(8,128)(2,1)S(1)} %get-tuple-element.33), channel_id=1, source_target_pairs={{0,3},{1,2},{2,1},{3,0},{4,7},{5,6},{6,5},{7,4},{8,11},{9,10},{10,... | collective-permute-start | bytes 258056 | tf_op jit(solution)/shard_map/ppermute | solution.py:17
  8.3 7.2 %collective-permute-start.6 = (bf16[240,256]{1,0:T(8,128)(2,1)S(1)}, bf16[240,256]{1,0:T(8,128)(2,1)S(1)}, u32[]{:S(2)}, u32[]{:S(2)}) collective-permute-start(bf16[240,256]{1,0:T(8,128)(2,1)S(1)} %get-tuple-element.40), channel_id=1, source_target_pairs={{0,2},{1,3},{2,0},{3,1},{4,6},{5,7},{6,4},{7,5},{8,10},{9,11},{10,... | collective-permute-start | bytes 368648 | tf_op jit(solution)/shard_map/ppermute | solution.py:17
  10.5 5.5 %collective-permute-start.7 = (bf16[240,256]{1,0:T(8,128)(2,1)S(1)}, bf16[240,256]{1,0:T(8,128)(2,1)S(1)}, u32[]{:S(2)}, u32[]{:S(2)}) collective-permute-start(bf16[240,256]{1,0:T(8,128)(2,1)S(1)} %get-tuple-element.41), channel_id=1, source_target_pairs={{0,3},{1,2},{2,1},{3,0},{4,7},{5,6},{6,5},{7,4},{8,11},{9,10},{10,... | collective-permute-start | bytes 368648 | tf_op jit(solution)/shard_map/ppermute | solution.py:17
  11.0 6.2 %collective-permute-start.3 = (bf16[96,256]{1,0:T(8,128)(2,1)S(1)}, bf16[96,256]{1,0:T(8,128)(2,1)S(1)}, u32[]{:S(2)}, u32[]{:S(2)}) collective-permute-start(bf16[96,256]{1,0:T(8,128)(2,1)S(1)} %get-tuple-element.36), channel_id=1, source_target_pairs={{0,12},{4,8},{8,4},{12,0},{1,13},{5,9},{9,5},{13,1},{2,14},{6,10},... | collective-permute-start | bytes 147464 | tf_op jit(solution)/shard_map/ppermute | solution.py:17
  14.7 7.0 %collective-permute-start.4 = (bf16[96,256]{1,0:T(8,128)(2,1)S(1)}, bf16[96,256]{1,0:T(8,128)(2,1)S(1)}, u32[]{:S(2)}, u32[]{:S(2)}) collective-permute-start(bf16[96,256]{1,0:T(8,128)(2,1)S(1)} %get-tuple-element.37), channel_id=1, source_target_pairs={{0,8},{4,12},{8,0},{12,4},{1,9},{5,13},{9,1},{13,5},{2,10},{6,14},... | collective-permute-start | bytes 147464 | tf_op jit(solution)/shard_map/ppermute | solution.py:17
  14.7 7.0 %collective-permute-start.5 = (bf16[96,256]{1,0:T(8,128)(2,1)S(1)}, bf16[96,256]{1,0:T(8,128)(2,1)S(1)}, u32[]{:S(2)}, u32[]{:S(2)}) collective-permute-start(bf16[96,256]{1,0:T(8,128)(2,1)S(1)} %get-tuple-element.38), channel_id=1, source_target_pairs={{0,4},{4,0},{8,12},{12,8},{1,5},{5,1},{9,13},{13,9},{2,6},{6,2},{1... | collective-permute-start | bytes 147464 | tf_op jit(solution)/shard_map/ppermute | solution.py:17
  17.7 6.6 %collective-permute-start.8 = (bf16[144,256]{1,0:T(8,128)(2,1)S(1)}, bf16[144,256]{1,0:T(8,128)(2,1)S(1)}, u32[]{:S(2)}, u32[]{:S(2)}) collective-permute-start(bf16[144,256]{1,0:T(8,128)(2,1)S(1)} %get-tuple-element.43), channel_id=1, source_target_pairs={{0,12},{4,8},{8,4},{12,0},{1,13},{5,9},{9,5},{13,1},{2,14},{6,10},... | collective-permute-start | bytes 221192 | tf_op jit(solution)/shard_map/ppermute | solution.py:17
  21.7 6.3 %collective-permute-start.11 = (bf16[240,256]{1,0:T(8,128)(2,1)S(1)}, bf16[240,256]{1,0:T(8,128)(2,1)S(1)}, u32[]{:S(2)}, u32[]{:S(2)}) collective-permute-start(bf16[240,256]{1,0:T(8,128)(2,1)S(1)} %get-tuple-element.49), channel_id=1, source_target_pairs={{0,1},{1,0},{2,3},{3,2},{4,5},{5,4},{6,7},{7,6},{8,9},{9,8},{10,11... | collective-permute-start | bytes 368648 | tf_op jit(solution)/shard_map/ppermute | solution.py:17
  21.8 6.1 %collective-permute-start.9 = (bf16[144,256]{1,0:T(8,128)(2,1)S(1)}, bf16[144,256]{1,0:T(8,128)(2,1)S(1)}, u32[]{:S(2)}, u32[]{:S(2)}) collective-permute-start(bf16[144,256]{1,0:T(8,128)(2,1)S(1)} %get-tuple-element.44), channel_id=1, source_target_pairs={{0,8},{4,12},{8,0},{12,4},{1,9},{5,13},{9,1},{13,5},{2,10},{6,14},... | collective-permute-start | bytes 221192 | tf_op jit(solution)/shard_map/ppermute | solution.py:17
  21.9 6.1 %collective-permute-start.10 = (bf16[144,256]{1,0:T(8,128)(2,1)S(1)}, bf16[144,256]{1,0:T(8,128)(2,1)S(1)}, u32[]{:S(2)}, u32[]{:S(2)}) collective-permute-start(bf16[144,256]{1,0:T(8,128)(2,1)S(1)} %get-tuple-element.45), channel_id=1, source_target_pairs={{0,4},{4,0},{8,12},{12,8},{1,5},{5,1},{9,13},{13,9},{2,6},{6,2},{1... | collective-permute-start | bytes 221192 | tf_op jit(solution)/shard_map/ppermute | solution.py:17
  22.8 19.1 %collective-permute-start.19 = (bf16[240,256]{1,0:T(8,128)(2,1)S(1)}, bf16[240,256]{1,0:T(8,128)(2,1)S(1)}, u32[]{:S(2)}, u32[]{:S(2)}) collective-permute-start(bf16[240,256]{1,0:T(8,128)(2,1)S(1)} %get-tuple-element.59), channel_id=1, source_target_pairs={{0,2},{1,3},{2,0},{3,1},{4,6},{5,7},{6,4},{7,5},{8,10},{9,11},{10,... | collective-permute-start | bytes 368648 | tf_op jit(solution)/shard_map/ppermute | solution.py:17
  24.4 17.5 %collective-permute-start.20 = (bf16[240,256]{1,0:T(8,128)(2,1)S(1)}, bf16[240,256]{1,0:T(8,128)(2,1)S(1)}, u32[]{:S(2)}, u32[]{:S(2)}) collective-permute-start(bf16[240,256]{1,0:T(8,128)(2,1)S(1)} %get-tuple-element.60), channel_id=1, source_target_pairs={{0,3},{1,2},{2,1},{3,0},{4,7},{5,6},{6,5},{7,4},{8,11},{9,10},{10,... | collective-permute-start | bytes 368648 | tf_op jit(solution)/shard_map/ppermute | solution.py:17
  28.4 5.8 %collective-permute-start.12 = (f32[60,128]{1,0:T(8,128)S(1)}, f32[60,128]{1,0:T(8,128)S(1)}, u32[]{:S(2)}, u32[]{:S(2)}) collective-permute-start(f32[60,128]{1,0:T(8,128)S(1)} %get-tuple-element.50), channel_id=1, source_target_pairs={{0,8},{4,12},{8,0},{12,4},{1,9},{5,13},{9,1},{13,5},{2,10},{6,14},... | collective-permute-start | bytes 92168 | tf_op jit(solution)/shard_map/ppermute | solution.py:17
  29.7 5.7 %collective-permute-start.13 = (f32[60,128]{1,0:T(8,128)S(1)}, f32[60,128]{1,0:T(8,128)S(1)}, u32[]{:S(2)}, u32[]{:S(2)}) collective-permute-start(f32[60,128]{1,0:T(8,128)S(1)} %get-tuple-element.51), channel_id=1, source_target_pairs={{0,12},{4,8},{8,4},{12,0},{1,13},{5,9},{9,5},{13,1},{2,14},{6,10},... | collective-permute-start | bytes 92168 | tf_op jit(solution)/shard_map/ppermute | solution.py:17
  31.9 3.9 %collective-permute-start.14 = (f32[60,128]{1,0:T(8,128)S(1)}, f32[60,128]{1,0:T(8,128)S(1)}, u32[]{:S(2)}, u32[]{:S(2)}) collective-permute-start(f32[60,128]{1,0:T(8,128)S(1)} %get-tuple-element.52), channel_id=1, source_target_pairs={{0,4},{4,0},{8,12},{12,8},{1,5},{5,1},{9,13},{13,9},{2,6},{6,2},{1... | collective-permute-start | bytes 92168 | tf_op jit(solution)/shard_map/ppermute | solution.py:17
  36.0 3.8 %collective-permute-start.15 = (f32[40,80]{1,0:T(8,128)S(1)}, f32[40,80]{1,0:T(8,128)S(1)}, u32[]{:S(2)}, u32[]{:S(2)}) collective-permute-start(f32[40,80]{1,0:T(8,128)S(1)} %get-tuple-element.54), channel_id=1, source_target_pairs={{0,2},{1,3},{2,0},{3,1},{4,6},{5,7},{6,4},{7,5},{8,10},{9,11},{10,... | collective-permute-start | bytes 38408 | tf_op jit(solution)/shard_map/ppermute | solution.py:17
  37.0 3.3 %collective-permute-start.16 = (f32[40,80]{1,0:T(8,128)S(1)}, f32[40,80]{1,0:T(8,128)S(1)}, u32[]{:S(2)}, u32[]{:S(2)}) collective-permute-start(f32[40,80]{1,0:T(8,128)S(1)} %get-tuple-element.55), channel_id=1, source_target_pairs={{0,3},{1,2},{2,1},{3,0},{4,7},{5,6},{6,5},{7,4},{8,11},{9,10},{10,... | collective-permute-start | bytes 38408 | tf_op jit(solution)/shard_map/ppermute | solution.py:17
  37.0 3.3 %collective-permute-start.17 = (f32[40,80]{1,0:T(8,128)S(1)}, f32[40,80]{1,0:T(8,128)S(1)}, u32[]{:S(2)}, u32[]{:S(2)}) collective-permute-start(f32[40,80]{1,0:T(8,128)S(1)} %get-tuple-element.56), channel_id=1, source_target_pairs={{0,1},{1,0},{2,3},{3,2},{4,5},{5,4},{6,7},{7,6},{8,9},{9,8},{10,11... | collective-permute-start | bytes 38408 | tf_op jit(solution)/shard_map/ppermute | solution.py:17
  40.3 3.8 %collective-permute-start.18 = (f32[40,80]{1,0:T(8,128)S(1)}, f32[40,80]{1,0:T(8,128)S(1)}, u32[]{:S(2)}, u32[]{:S(2)}) collective-permute-start(f32[40,80]{1,0:T(8,128)S(1)} %shard_map.58), channel_id=1, source_target_pairs={{0,16},{16,0},{1,17},{17,1},{2,18},{18,2},{3,19},{19,3},{4,20},{20... | collective-permute-start | bytes 38408 | tf_op jit(solution)/shard_map/ppermute | solution.py:17

commit v8 on v3

--- a/solution.py
+++ b/solution.py
@@ -80,7 +80,7 @@
         deep = rows // groups
         wide = refs[0][...].astype(f32)
         wide = jnp.concatenate([wide[g * deep : (g + 1) * deep] for g in range(groups)], axis=1)
-        head = [jnp.pad(wide, ((0, -deep % 8), (0, width - groups * ranks))).astype(bf16)]
+        head = [jnp.pad(wide, ((0, -deep % 16), (0, width - groups * ranks))).astype(bf16)]
     for (k, begin, count), out in zip(spans, outs):
         at = pl.ds(pl.multiple_of((me ^ k) * width, width), width)
         out[...] = jnp.concatenate(head + [slab_ref[l, :, at] for l in range(begin, begin + count)], axis=0)
@@ -204,7 +204,7 @@
     views_all, lights_all = views * rows, parts * lights
     size = ranks // parts
     groups = max(g for g in range(1, width // ranks + 1) if rows % g == 0)
-    head = -(-(rows // groups) // 8) * 8
+    head = -(-(rows // groups) // 16) * 16
 
     one = lights * 2 // 5 // 4 * 4
     counts, half = [one, lights - one], views // 2
@@ -249,7 +249,7 @@
             outs,
             [
                 pltpu.VMEM((views, tall[c], width), bf16),
-                pltpu.VMEM((width // 128, count * ranks, 128), f32),
+                pltpu.VMEM((width // 128, -(-count // 8) * 8 * ranks, 128), f32),
             ],
             2 * views_all * count * width * ranks,
             whole[c][::-1] + near[::-1] + carried,

time: 44 us -> 44 us (level)
  transfers between devices with their start and end apart: 21 -> 21, of which waited for: 12 -> 13; matrix products, arithmetic and copies ran while one was open for 0% -> 0% of each run, Pallas kernels for 7% -> 7%
where the time goes in v8:
time: 44 us; the launch traced here: 43.9 us
  starting transfers between devices  24.3 us (55%)
  waiting for transfers between devices  14 us (32%)
  Pallas kernels  3.08 us (7%)
  local copies, waits for them, and re-layouts  1.79 us (4%)
  between operations  0.73 us (2%)
    ppermute x21, starting transfers between devices, swap(): lax.ppermute(value, axis, [(i, i ^ step) for i in range(lax.axis_size(axi...  24.3 us
    ppermute x21, waiting for transfers between devices, swap(): lax.ppermute(value, axis, [(i, i ^ step) for i in range(lax.axis_size(axi...  14 us
    pallas_call x11, Pallas kernels, call(): pl.pallas_call(kernel, out_shape=out_shape, in_specs=[VMEM] * len(args) +...  3.08 us
    unnamed x4, local copies, waits for them, and re-layouts  1.18 us
  transfers between devices with their start and end apart: 21, of which 13 were waited for; matrix products, arithmetic and copies ran while one was open for 0% of the time, Pallas kernels for 7%

profile of v8, /device:TPU:0, one launch (start us, length us, event | category | flops | bytes accessed | tf_op | source)
XLA Modules:
  0.0 43.9 jit_solution(3866542868505535111)
XLA Ops:
  0.6 0.0 copy-start
  0.6 0.0 copy-start.1
  0.7 1.2 %copy-done = bf16[20,20,1024]{2,1,0:T(8,128)(2,1)S(1)} copy-done((bf16[20,20,1024]{2,1,0:T(8,128)(2,1)S(1)}, bf16[20,20,1024]{2,1,0:T(8,128)(2,1)}, u32[]{:S(2)}) %copy-start) | copy-done | bytes 819224
  1.8 0.0 copy-done.1
  1.8 0.1 shard_map.50
  2.0 0.5 %collective-permute-start.2 = (bf16[416,256]{1,0:T(8,128)(2,1)S(1)}, bf16[416,256]{1,0:T(8,128)(2,1)S(1)}, u32[]{:S(2)}, u32[]{:S(2)}) collective-permute-start(bf16[416,256]{1,0:T(8,128)(2,1)S(1)} %get-tuple-element.34), channel_id=1, source_target_pairs={{0,1},{1,0},{2,3},{3,2},{4,5},{5,4},{6,7},{7,6},{8,9},{9,8},{10,11... | collective-permute-start | bytes 638984 | tf_op jit(solution)/shard_map/ppermute | solution.py:17
  2.5 2.6 %collective-permute-start = (bf16[176,256]{1,0:T(8,128)(2,1)S(1)}, bf16[176,256]{1,0:T(8,128)(2,1)S(1)}, u32[]{:S(2)}, u32[]{:S(2)}) collective-permute-start(bf16[176,256]{1,0:T(8,128)(2,1)S(1)} %get-tuple-element.32), channel_id=1, source_target_pairs={{0,3},{1,2},{2,1},{3,0},{4,7},{5,6},{6,5},{7,4},{8,11},{9,10},{10,... | collective-permute-start | bytes 270344 | tf_op jit(solution)/shard_map/ppermute | solution.py:17
  5.1 0.0 collective-permute-start.1
  5.2 2.9 %collective-permute-done.refs_0_.refs_3_ = bf16[176,256]{1,0:T(8,128)(2,1)S(1)} collective-permute-done((bf16[176,256]{1,0:T(8,128)(2,1)S(1)}, bf16[176,256]{1,0:T(8,128)(2,1)S(1)}, u32[]{:S(2)}, u32[]{:S(2)}) %collective-permute-start) | collective-permute-done | bytes 90144 | tf_op jit(solution)/shard_map/ppermute | solution.py:17
  8.1 2.0 %collective-permute-start.6 = (bf16[240,256]{1,0:T(8,128)(2,1)S(1)}, bf16[240,256]{1,0:T(8,128)(2,1)S(1)}, u32[]{:S(2)}, u32[]{:S(2)}) collective-permute-start(bf16[240,256]{1,0:T(8,128)(2,1)S(1)} %get-tuple-element.40), channel_id=1, source_target_pairs={{0,3},{1,2},{2,1},{3,0},{4,7},{5,6},{6,5},{7,4},{8,11},{9,10},{10,... | collective-permute-start | bytes 368648 | tf_op jit(solution)/shard_map/ppermute | solution.py:17
  10.1 0.0 collective-permute-start.7
  10.1 0.1 collective-permute-done.1.refs_1_.refs_2_
  10.2 0.0 collective-permute-done.2.refs_2_.refs_1_
  10.2 0.5 %shard_map.51 = (bf16[96,256]{1,0:T(8,128)(2,1)S(1)}, bf16[96,256]{1,0:T(8,128)(2,1)S(1)}, bf16[96,256]{1,0:T(8,128)(2,1)S(1)}, bf16[96,256]{1,0:T(8,128)(2,1)S(...) custom-call(bf16[176,256]{1,0:T(8,128)(2,1)S(1)} %collective-permute-done.refs_0_.refs_3_, ...), custom_call_target="tpu_custom_call" | custom-call | flops 15728640 | bytes 1007104 | tf_op jit(solution)/shard_map/pallas_call | solution.py:46
  10.7 4.1 %collective-permute-start.3 = (bf16[96,256]{1,0:T(8,128)(2,1)S(1)}, bf16[96,256]{1,0:T(8,128)(2,1)S(1)}, u32[]{:S(2)}, u32[]{:S(2)}) collective-permute-start(bf16[96,256]{1,0:T(8,128)(2,1)S(1)} %get-tuple-element.36), channel_id=1, source_target_pairs={{0,12},{4,8},{8,4},{12,0},{1,13},{5,9},{9,5},{13,1},{2,14},{6,10},... | collective-permute-start | bytes 147464 | tf_op jit(solution)/shard_map/ppermute | solution.py:17
  14.8 0.0 collective-permute-start.4
  14.8 0.6 %collective-permute-start.5 = (bf16[96,256]{1,0:T(8,128)(2,1)S(1)}, bf16[96,256]{1,0:T(8,128)(2,1)S(1)}, u32[]{:S(2)}, u32[]{:S(2)}) collective-permute-start(bf16[96,256]{1,0:T(8,128)(2,1)S(1)} %get-tuple-element.38), channel_id=1, source_target_pairs={{0,4},{4,0},{8,12},{12,8},{1,5},{5,1},{9,13},{13,9},{2,6},{6,2},{1... | collective-permute-start | bytes 147464 | tf_op jit(solution)/shard_map/ppermute | solution.py:17
  15.4 0.0 collective-permute-done.6.refs_0_.refs_5_
  15.4 1.2 %collective-permute-done.7.refs_1_.refs_4_ = bf16[240,256]{1,0:T(8,128)(2,1)S(1)} collective-permute-done((bf16[240,256]{1,0:T(8,128)(2,1)S(1)}, bf16[240,256]{1,0:T(8,128)(2,1)S(1)}, u32[]{:S(2)}, u32[]{:S(2)}) %collective-permute-start.7) | collective-permute-done | bytes 122912 | tf_op jit(solution)/shard_map/ppermute | solution.py:17
  16.6 0.5 %collective-permute-done.3.refs_5_.refs_2_.refs_0_ = bf16[96,256]{1,0:T(8,128)(2,1)S(1)} collective-permute-done((bf16[96,256]{1,0:T(8,128)(2,1)S(1)}, bf16[96,256]{1,0:T(8,128)(2,1)S(1)}, u32[]{:S(2)}, u32[]{:S(2)}) %collective-permute-start.3) | collective-permute-done | bytes 49184 | tf_op jit(solution)/shard_map/ppermute | solution.py:17
  17.1 0.5 %shard_map.53 = (bf16[144,256]{1,0:T(8,128)(2,1)S(1)}, bf16[144,256]{1,0:T(8,128)(2,1)S(1)}, bf16[144,256]{1,0:T(8,128)(2,1)S(1)}, bf16[144,256]{1,0:T(8,128)(2,1)S(1)}, bf16[4,144,256]{2,1,0:T(8,128)(2,1)S(1)}) custom-call(bf16[240,256]{1,0:T(8,128)(2,1)S(1)} %collective-permute-done.6.refs_0_.refs_5_, ...), custom_call_target="tpu_custom_call" | custom-call | flops 23592960 | bytes 1269248 | tf_op jit(solution)/shard_map/pallas_call | solution.py:46
  17.5 4.0 %collective-permute-start.8 = (bf16[144,256]{1,0:T(8,128)(2,1)S(1)}, bf16[144,256]{1,0:T(8,128)(2,1)S(1)}, u32[]{:S(2)}, u32[]{:S(2)}) collective-permute-start(bf16[144,256]{1,0:T(8,128)(2,1)S(1)} %get-tuple-element.43), channel_id=1, source_target_pairs={{0,12},{4,8},{8,4},{12,0},{1,13},{5,9},{9,5},{13,1},{2,14},{6,10},... | collective-permute-start | bytes 221192 | tf_op jit(solution)/shard_map/ppermute | solution.py:17
  21.6 0.0 collective-permute-done.4.refs_3_.refs_1_
  21.6 0.0 collective-permute-done.5.refs_4_.refs_2_
  21.6 0.1 collective-permute-start.11
  21.7 0.3 collective-permute-start.9
  22.0 0.5 %collective-permute-start.10 = (bf16[144,256]{1,0:T(8,128)(2,1)S(1)}, bf16[144,256]{1,0:T(8,128)(2,1)S(1)}, u32[]{:S(2)}, u32[]{:S(2)}) collective-permute-start(bf16[144,256]{1,0:T(8,128)(2,1)S(1)} %get-tuple-element.45), channel_id=1, source_target_pairs={{0,4},{4,0},{8,12},{12,8},{1,5},{5,1},{9,13},{13,9},{2,6},{6,2},{1... | collective-permute-start | bytes 221192 | tf_op jit(solution)/shard_map/ppermute | solution.py:17
  22.5 1.6 %collective-permute-start.19 = (bf16[240,256]{1,0:T(8,128)(2,1)S(1)}, bf16[240,256]{1,0:T(8,128)(2,1)S(1)}, u32[]{:S(2)}, u32[]{:S(2)}) collective-permute-start(bf16[240,256]{1,0:T(8,128)(2,1)S(1)} %get-tuple-element.59), channel_id=1, source_target_pairs={{0,2},{1,3},{2,0},{3,1},{4,6},{5,7},{6,4},{7,5},{8,10},{9,11},{10,... | collective-permute-start | bytes 368648 | tf_op jit(solution)/shard_map/ppermute | solution.py:17
  24.1 0.2 collective-permute-done.8.refs_4_
  24.3 0.0 collective-permute-start.20
  24.3 0.5 %shard_map.54.refs_8_ = f32[40,128]{1,0:T(8,128)S(1)} custom-call(bf16[416,256]{1,0:T(8,128)(2,1)S(1)} %get-tuple-element.35.refs_3_.refs_0_, bf16[416,256]{1,0:T(8,128)(2,1)S(1)} %collective-permute-done.2.refs_2_.refs_1_, bf16[176,256]{1,0:T(8,128)(2,1)S(1)} %collective-permute-done.1.refs_1_.refs_2_, ...), custom_call_target="tpu_custom_call" | custom-call | flops 65536000 | bytes 872448 | tf_op jit(solution)/shard_map/pallas_call | solution.py:46
  24.8 2.6 %collective-permute-done.9.refs_5_ = bf16[144,256]{1,0:T(8,128)(2,1)S(1)} collective-permute-done((bf16[144,256]{1,0:T(8,128)(2,1)S(1)}, bf16[144,256]{1,0:T(8,128)(2,1)S(1)}, u32[]{:S(2)}, u32[]{:S(2)}) %collective-permute-start.9) | collective-permute-done | bytes 73760 | tf_op jit(solution)/shard_map/ppermute | solution.py:17
  27.4 0.6 %collective-permute-done.10.refs_6_ = bf16[144,256]{1,0:T(8,128)(2,1)S(1)} collective-permute-done((bf16[144,256]{1,0:T(8,128)(2,1)S(1)}, bf16[144,256]{1,0:T(8,128)(2,1)S(1)}, u32[]{:S(2)}, u32[]{:S(2)}) %collective-permute-start.10) | collective-permute-done | bytes 73760 | tf_op jit(solution)/shard_map/ppermute | solution.py:17
  28.0 0.0 collective-permute-done.11.refs_9_.refs_1_
  28.0 0.3 shard_map.56
  28.3 2.0 %collective-permute-start.12 = (f32[60,128]{1,0:T(8,128)S(1)}, f32[60,128]{1,0:T(8,128)S(1)}, u32[]{:S(2)}, u32[]{:S(2)}) collective-permute-start(f32[60,128]{1,0:T(8,128)S(1)} %get-tuple-element.50), channel_id=1, source_target_pairs={{0,12},{4,8},{8,4},{12,0},{1,13},{5,9},{9,5},{13,1},{2,14},{6,10},... | collective-permute-start | bytes 92168 | tf_op jit(solution)/shard_map/ppermute | solution.py:17
  30.3 0.6 %collective-permute-start.13 = (f32[60,128]{1,0:T(8,128)S(1)}, f32[60,128]{1,0:T(8,128)S(1)}, u32[]{:S(2)}, u32[]{:S(2)}) collective-permute-start(f32[60,128]{1,0:T(8,128)S(1)} %get-tuple-element.51), channel_id=1, source_target_pairs={{0,8},{4,12},{8,0},{12,4},{1,9},{5,13},{9,1},{13,5},{2,10},{6,14},... | collective-permute-start | bytes 92168 | tf_op jit(solution)/shard_map/ppermute | solution.py:17
  31.0 1.8 %collective-permute-start.14 = (f32[60,128]{1,0:T(8,128)S(1)}, f32[60,128]{1,0:T(8,128)S(1)}, u32[]{:S(2)}, u32[]{:S(2)}) collective-permute-start(f32[60,128]{1,0:T(8,128)S(1)} %get-tuple-element.52), channel_id=1, source_target_pairs={{0,4},{4,0},{8,12},{12,8},{1,5},{5,1},{9,13},{13,9},{2,6},{6,2},{1... | collective-permute-start | bytes 92168 | tf_op jit(solution)/shard_map/ppermute | solution.py:17
  32.8 1.4 %collective-permute-done.12.refs_0_ = f32[60,128]{1,0:T(8,128)S(1)} collective-permute-done((f32[60,128]{1,0:T(8,128)S(1)}, f32[60,128]{1,0:T(8,128)S(1)}, u32[]{:S(2)}, u32[]{:S(2)}) %collective-permute-start.12) | collective-permute-done | bytes 30752 | tf_op jit(solution)/shard_map/ppermute | solution.py:17
  34.2 1.0 %collective-permute-done.13.refs_1_ = f32[60,128]{1,0:T(8,128)S(1)} collective-permute-done((f32[60,128]{1,0:T(8,128)S(1)}, f32[60,128]{1,0:T(8,128)S(1)}, u32[]{:S(2)}, u32[]{:S(2)}) %collective-permute-start.13) | collective-permute-done | bytes 30752 | tf_op jit(solution)/shard_map/ppermute | solution.py:17
  35.2 0.1 collective-permute-done.14.refs_2_
  35.3 0.2 shard_map.57
  35.5 0.1 collective-permute-start.15
  35.6 1.7 %collective-permute-start.16 = (f32[40,80]{1,0:T(8,128)S(1)}, f32[40,80]{1,0:T(8,128)S(1)}, u32[]{:S(2)}, u32[]{:S(2)}) collective-permute-start(f32[40,80]{1,0:T(8,128)S(1)} %get-tuple-element.55), channel_id=1, source_target_pairs={{0,2},{1,3},{2,0},{3,1},{4,6},{5,7},{6,4},{7,5},{8,10},{9,11},{10,... | collective-permute-start | bytes 38408 | tf_op jit(solution)/shard_map/ppermute | solution.py:17
  37.2 0.2 collective-permute-start.17
  37.4 1.4 %collective-permute-done.15.refs_0_ = f32[40,80]{1,0:T(8,128)S(1)} collective-permute-done((f32[40,80]{1,0:T(8,128)S(1)}, f32[40,80]{1,0:T(8,128)S(1)}, u32[]{:S(2)}, u32[]{:S(2)}) %collective-permute-start.15) | collective-permute-done | bytes 12832 | tf_op jit(solution)/shard_map/ppermute | solution.py:17
  38.8 0.6 %collective-permute-done.16.refs_1_ = f32[40,80]{1,0:T(8,128)S(1)} collective-permute-done((f32[40,80]{1,0:T(8,128)S(1)}, f32[40,80]{1,0:T(8,128)S(1)}, u32[]{:S(2)}, u32[]{:S(2)}) %collective-permute-start.16) | collective-permute-done | bytes 12832 | tf_op jit(solution)/shard_map/ppermute | solution.py:17
  39.4 0.0 collective-permute-done.17.refs_2_
  39.4 1.5 %collective-permute-start.18 = (f32[40,80]{1,0:T(8,128)S(1)}, f32[40,80]{1,0:T(8,128)S(1)}, u32[]{:S(2)}, u32[]{:S(2)}) collective-permute-start(f32[40,80]{1,0:T(8,128)S(1)} %shard_map.58), channel_id=1, source_target_pairs={{0,16},{16,0},{1,17},{17,1},{2,18},{18,2},{3,19},{19,3},{4,20},{20... | collective-permute-start | bytes 38408 | tf_op jit(solution)/shard_map/ppermute | solution.py:17
  41.0 0.0 collective-permute-done.19.refs_2_
  41.0 0.0 collective-permute-done.20.refs_3_
  41.0 0.9 %shard_map.59 = bf16[12,20,1024]{2,1,0:T(8,128)(2,1)} custom-call(bf16[240,256]{1,0:T(8,128)(2,1)S(1)} %get-tuple-element.58.refs_0_, bf16[240,256]{1,0:T(8,128)(2,1)S(1)} %collective-permute-done.11.refs_9_.refs_1_, bf16[240,256]{1,0:T(8,128)(2,1)S(1)} %collective-permute-done.19.refs_2_, bf16[240,256]{1,0:T(8,128)(2,1)S(1)} %collective-permute-done.20.refs_3_), custom_call_target="tpu_custom_call" | custom-call | bytes 983040 | tf_op jit(solution)/shard_map/pallas_call | solution.py:46
  41.9 1.4 %collective-permute-done.18 = f32[40,80]{1,0:T(8,128)S(1)} collective-permute-done((f32[40,80]{1,0:T(8,128)S(1)}, f32[40,80]{1,0:T(8,128)S(1)}, u32[]{:S(2)}, u32[]{:S(2)}) %collective-permute-start.18) | collective-permute-done | bytes 12832 | tf_op jit(solution)/shard_map/ppermute | solution.py:17
  43.3 0.6 %fusion = (f32[20,80]{1,0:T(8,128)}, f32[20,80]{1,0:T(8,128)}) fusion(f32[40,80]{1,0:T(8,128)S(1)} %add.3), kind=kLoop, calls=%fused_computation | loop fusion | bytes 25600 | tf_op jit(solution)/shard_map/slice | solution.py:299
  (5 shorter events, 0.1 us)
Async XLA Ops:
  0.6 1.2 %copy-start = (bf16[20,20,1024]{2,1,0:T(8,128)(2,1)S(1)}, bf16[20,20,1024]{2,1,0:T(8,128)(2,1)}, u32[]{:S(2)}) copy-start(bf16[20,20,1024]{2,1,0:T(8,128)(2,1)} %slab_ref.3) | copy-start | bytes 2457604
  0.6 1.2 %copy-start.1 = (bf16[20,48]{1,0:T(8,128)(2,1)S(1)}, bf16[20,48]{1,0:T(8,128)(2,1)}, u32[]{:S(2)}) copy-start(bf16[20,48]{1,0:T(8,128)(2,1)} %refs_0_.1) | copy-start | bytes 5764
  2.0 8.3 %collective-permute-start.2 = (bf16[416,256]{1,0:T(8,128)(2,1)S(1)}, bf16[416,256]{1,0:T(8,128)(2,1)S(1)}, u32[]{:S(2)}, u32[]{:S(2)}) collective-permute-start(bf16[416,256]{1,0:T(8,128)(2,1)S(1)} %get-tuple-element.34), channel_id=1, source_target_pairs={{0,1},{1,0},{2,3},{3,2},{4,5},{5,4},{6,7},{7,6},{8,9},{9,8},{10,11... | collective-permute-start | bytes 638984 | tf_op jit(solution)/shard_map/ppermute | solution.py:17
  2.5 5.6 %collective-permute-start = (bf16[176,256]{1,0:T(8,128)(2,1)S(1)}, bf16[176,256]{1,0:T(8,128)(2,1)S(1)}, u32[]{:S(2)}, u32[]{:S(2)}) collective-permute-start(bf16[176,256]{1,0:T(8,128)(2,1)S(1)} %get-tuple-element.32), channel_id=1, source_target_pairs={{0,3},{1,2},{2,1},{3,0},{4,7},{5,6},{6,5},{7,4},{8,11},{9,10},{10,... | collective-permute-start | bytes 270344 | tf_op jit(solution)/shard_map/ppermute | solution.py:17
  5.1 5.1 %collective-permute-start.1 = (bf16[176,256]{1,0:T(8,128)(2,1)S(1)}, bf16[176,256]{1,0:T(8,128)(2,1)S(1)}, u32[]{:S(2)}, u32[]{:S(2)}) collective-permute-start(bf16[176,256]{1,0:T(8,128)(2,1)S(1)} %get-tuple-element.33), channel_id=1, source_target_pairs={{0,2},{1,3},{2,0},{3,1},{4,6},{5,7},{6,4},{7,5},{8,10},{9,11},{10,... | collective-permute-start | bytes 270344 | tf_op jit(solution)/shard_map/ppermute | solution.py:17
  8.1 7.3 %collective-permute-start.6 = (bf16[240,256]{1,0:T(8,128)(2,1)S(1)}, bf16[240,256]{1,0:T(8,128)(2,1)S(1)}, u32[]{:S(2)}, u32[]{:S(2)}) collective-permute-start(bf16[240,256]{1,0:T(8,128)(2,1)S(1)} %get-tuple-element.40), channel_id=1, source_target_pairs={{0,3},{1,2},{2,1},{3,0},{4,7},{5,6},{6,5},{7,4},{8,11},{9,10},{10,... | collective-permute-start | bytes 368648 | tf_op jit(solution)/shard_map/ppermute | solution.py:17
  10.1 6.5 %collective-permute-start.7 = (bf16[240,256]{1,0:T(8,128)(2,1)S(1)}, bf16[240,256]{1,0:T(8,128)(2,1)S(1)}, u32[]{:S(2)}, u32[]{:S(2)}) collective-permute-start(bf16[240,256]{1,0:T(8,128)(2,1)S(1)} %get-tuple-element.41), channel_id=1, source_target_pairs={{0,2},{1,3},{2,0},{3,1},{4,6},{5,7},{6,4},{7,5},{8,10},{9,11},{10,... | collective-permute-start | bytes 368648 | tf_op jit(solution)/shard_map/ppermute | solution.py:17
  10.7 6.4 %collective-permute-start.3 = (bf16[96,256]{1,0:T(8,128)(2,1)S(1)}, bf16[96,256]{1,0:T(8,128)(2,1)S(1)}, u32[]{:S(2)}, u32[]{:S(2)}) collective-permute-start(bf16[96,256]{1,0:T(8,128)(2,1)S(1)} %get-tuple-element.36), channel_id=1, source_target_pairs={{0,12},{4,8},{8,4},{12,0},{1,13},{5,9},{9,5},{13,1},{2,14},{6,10},... | collective-permute-start | bytes 147464 | tf_op jit(solution)/shard_map/ppermute | solution.py:17
  14.8 6.8 %collective-permute-start.4 = (bf16[96,256]{1,0:T(8,128)(2,1)S(1)}, bf16[96,256]{1,0:T(8,128)(2,1)S(1)}, u32[]{:S(2)}, u32[]{:S(2)}) collective-permute-start(bf16[96,256]{1,0:T(8,128)(2,1)S(1)} %get-tuple-element.37), channel_id=1, source_target_pairs={{0,8},{4,12},{8,0},{12,4},{1,9},{5,13},{9,1},{13,5},{2,10},{6,14},... | collective-permute-start | bytes 147464 | tf_op jit(solution)/shard_map/ppermute | solution.py:17
  14.8 6.8 %collective-permute-start.5 = (bf16[96,256]{1,0:T(8,128)(2,1)S(1)}, bf16[96,256]{1,0:T(8,128)(2,1)S(1)}, u32[]{:S(2)}, u32[]{:S(2)}) collective-permute-start(bf16[96,256]{1,0:T(8,128)(2,1)S(1)} %get-tuple-element.38), channel_id=1, source_target_pairs={{0,4},{4,0},{8,12},{12,8},{1,5},{5,1},{9,13},{13,9},{2,6},{6,2},{1... | collective-permute-start | bytes 147464 | tf_op jit(solution)/shard_map/ppermute | solution.py:17
  17.5 6.7 %collective-permute-start.8 = (bf16[144,256]{1,0:T(8,128)(2,1)S(1)}, bf16[144,256]{1,0:T(8,128)(2,1)S(1)}, u32[]{:S(2)}, u32[]{:S(2)}) collective-permute-start(bf16[144,256]{1,0:T(8,128)(2,1)S(1)} %get-tuple-element.43), channel_id=1, source_target_pairs={{0,12},{4,8},{8,4},{12,0},{1,13},{5,9},{9,5},{13,1},{2,14},{6,10},... | collective-permute-start | bytes 221192 | tf_op jit(solution)/shard_map/ppermute | solution.py:17
  21.6 6.3 %collective-permute-start.11 = (bf16[240,256]{1,0:T(8,128)(2,1)S(1)}, bf16[240,256]{1,0:T(8,128)(2,1)S(1)}, u32[]{:S(2)}, u32[]{:S(2)}) collective-permute-start(bf16[240,256]{1,0:T(8,128)(2,1)S(1)} %get-tuple-element.49), channel_id=1, source_target_pairs={{0,1},{1,0},{2,3},{3,2},{4,5},{5,4},{6,7},{7,6},{8,9},{9,8},{10,11... | collective-permute-start | bytes 368648 | tf_op jit(solution)/shard_map/ppermute | solution.py:17
  21.7 5.7 %collective-permute-start.9 = (bf16[144,256]{1,0:T(8,128)(2,1)S(1)}, bf16[144,256]{1,0:T(8,128)(2,1)S(1)}, u32[]{:S(2)}, u32[]{:S(2)}) collective-permute-start(bf16[144,256]{1,0:T(8,128)(2,1)S(1)} %get-tuple-element.44), channel_id=1, source_target_pairs={{0,8},{4,12},{8,0},{12,4},{1,9},{5,13},{9,1},{13,5},{2,10},{6,14},... | collective-permute-start | bytes 221192 | tf_op jit(solution)/shard_map/ppermute | solution.py:17
  22.0 6.0 %collective-permute-start.10 = (bf16[144,256]{1,0:T(8,128)(2,1)S(1)}, bf16[144,256]{1,0:T(8,128)(2,1)S(1)}, u32[]{:S(2)}, u32[]{:S(2)}) collective-permute-start(bf16[144,256]{1,0:T(8,128)(2,1)S(1)} %get-tuple-element.45), channel_id=1, source_target_pairs={{0,4},{4,0},{8,12},{12,8},{1,5},{5,1},{9,13},{13,9},{2,6},{6,2},{1... | collective-permute-start | bytes 221192 | tf_op jit(solution)/shard_map/ppermute | solution.py:17
  22.5 18.5 %collective-permute-start.19 = (bf16[240,256]{1,0:T(8,128)(2,1)S(1)}, bf16[240,256]{1,0:T(8,128)(2,1)S(1)}, u32[]{:S(2)}, u32[]{:S(2)}) collective-permute-start(bf16[240,256]{1,0:T(8,128)(2,1)S(1)} %get-tuple-element.59), channel_id=1, source_target_pairs={{0,2},{1,3},{2,0},{3,1},{4,6},{5,7},{6,4},{7,5},{8,10},{9,11},{10,... | collective-permute-start | bytes 368648 | tf_op jit(solution)/shard_map/ppermute | solution.py:17
  24.3 16.7 %collective-permute-start.20 = (bf16[240,256]{1,0:T(8,128)(2,1)S(1)}, bf16[240,256]{1,0:T(8,128)(2,1)S(1)}, u32[]{:S(2)}, u32[]{:S(2)}) collective-permute-start(bf16[240,256]{1,0:T(8,128)(2,1)S(1)} %get-tuple-element.60), channel_id=1, source_target_pairs={{0,3},{1,2},{2,1},{3,0},{4,7},{5,6},{6,5},{7,4},{8,11},{9,10},{10,... | collective-permute-start | bytes 368648 | tf_op jit(solution)/shard_map/ppermute | solution.py:17
  28.3 5.9 %collective-permute-start.12 = (f32[60,128]{1,0:T(8,128)S(1)}, f32[60,128]{1,0:T(8,128)S(1)}, u32[]{:S(2)}, u32[]{:S(2)}) collective-permute-start(f32[60,128]{1,0:T(8,128)S(1)} %get-tuple-element.50), channel_id=1, source_target_pairs={{0,12},{4,8},{8,4},{12,0},{1,13},{5,9},{9,5},{13,1},{2,14},{6,10},... | collective-permute-start | bytes 92168 | tf_op jit(solution)/shard_map/ppermute | solution.py:17
  30.3 4.9 %collective-permute-start.13 = (f32[60,128]{1,0:T(8,128)S(1)}, f32[60,128]{1,0:T(8,128)S(1)}, u32[]{:S(2)}, u32[]{:S(2)}) collective-permute-start(f32[60,128]{1,0:T(8,128)S(1)} %get-tuple-element.51), channel_id=1, source_target_pairs={{0,8},{4,12},{8,0},{12,4},{1,9},{5,13},{9,1},{13,5},{2,10},{6,14},... | collective-permute-start | bytes 92168 | tf_op jit(solution)/shard_map/ppermute | solution.py:17
  31.0 4.4 %collective-permute-start.14 = (f32[60,128]{1,0:T(8,128)S(1)}, f32[60,128]{1,0:T(8,128)S(1)}, u32[]{:S(2)}, u32[]{:S(2)}) collective-permute-start(f32[60,128]{1,0:T(8,128)S(1)} %get-tuple-element.52), channel_id=1, source_target_pairs={{0,4},{4,0},{8,12},{12,8},{1,5},{5,1},{9,13},{13,9},{2,6},{6,2},{1... | collective-permute-start | bytes 92168 | tf_op jit(solution)/shard_map/ppermute | solution.py:17
  35.5 3.3 %collective-permute-start.15 = (f32[40,80]{1,0:T(8,128)S(1)}, f32[40,80]{1,0:T(8,128)S(1)}, u32[]{:S(2)}, u32[]{:S(2)}) collective-permute-start(f32[40,80]{1,0:T(8,128)S(1)} %get-tuple-element.54), channel_id=1, source_target_pairs={{0,3},{1,2},{2,1},{3,0},{4,7},{5,6},{6,5},{7,4},{8,11},{9,10},{10,... | collective-permute-start | bytes 38408 | tf_op jit(solution)/shard_map/ppermute | solution.py:17
  35.6 3.8 %collective-permute-start.16 = (f32[40,80]{1,0:T(8,128)S(1)}, f32[40,80]{1,0:T(8,128)S(1)}, u32[]{:S(2)}, u32[]{:S(2)}) collective-permute-start(f32[40,80]{1,0:T(8,128)S(1)} %get-tuple-element.55), channel_id=1, source_target_pairs={{0,2},{1,3},{2,0},{3,1},{4,6},{5,7},{6,4},{7,5},{8,10},{9,11},{10,... | collective-permute-start | bytes 38408 | tf_op jit(solution)/shard_map/ppermute | solution.py:17
  37.2 2.2 %collective-permute-start.17 = (f32[40,80]{1,0:T(8,128)S(1)}, f32[40,80]{1,0:T(8,128)S(1)}, u32[]{:S(2)}, u32[]{:S(2)}) collective-permute-start(f32[40,80]{1,0:T(8,128)S(1)} %get-tuple-element.56), channel_id=1, source_target_pairs={{0,1},{1,0},{2,3},{3,2},{4,5},{5,4},{6,7},{7,6},{8,9},{9,8},{10,11... | collective-permute-start | bytes 38408 | tf_op jit(solution)/shard_map/ppermute | solution.py:17
  39.4 3.8 %collective-permute-start.18 = (f32[40,80]{1,0:T(8,128)S(1)}, f32[40,80]{1,0:T(8,128)S(1)}, u32[]{:S(2)}, u32[]{:S(2)}) collective-permute-start(f32[40,80]{1,0:T(8,128)S(1)} %shard_map.58), channel_id=1, source_target_pairs={{0,16},{16,0},{1,17},{17,1},{2,18},{18,2},{3,19},{19,3},{4,20},{20... | collective-permute-start | bytes 38408 | tf_op jit(solution)/shard_map/ppermute | solution.py:17

commit v9 on v8

--- a/solution.py
+++ b/solution.py
@@ -118,10 +118,15 @@
         outs[0][...] = basis
 
 
-def back_kernel(chunks, *refs):
-    v, outs = lax.axis_index("view"), refs[-refs[0].shape[0] :]
-    for k, out in enumerate(outs):
-        out[...] = jnp.concatenate([ref[v ^ k] for ref in refs[:chunks]], axis=0)
+def back_kernel(chunks, near, *refs):
+    views = refs[0].shape[0]
+    v, outs = lax.axis_index("view"), refs[-(views + near - 1) :]
+    for k in range(views):
+        page = jnp.concatenate([ref[v ^ k] for ref in refs[:chunks]], axis=0)
+        outs[0][...] = page[: outs[0].shape[0]]
+        if 0 < k < near:
+            outs[1][...] = page[page.shape[0] - outs[1].shape[0] :]
+        outs = outs[2 if 0 < k < near else 1 :]
 
 
 def view_kernel(lights, rows, views, spans, scale, *refs):
@@ -179,10 +184,15 @@
         outs[k][...] = jnp.concatenate([block, view[...]], axis=0)
 
 
-def place_kernel(counts, *refs):
+def place_kernel(counts, halves, *refs):
     ins, core_ref = refs[:-1], refs[-1]
     v = lax.axis_index("view")
     ranks, width = core_ref.shape[0], ins[0].shape[1]
+    tall = ranks * sum(counts)
+    ins = [
+        part[0] if len(part) == 1 else jnp.concatenate([part[0][...], part[1][2 * part[1].shape[0] - tall :]], axis=0)
+        for part in cut(ins, *halves)[:-1]
+    ]
     for k in range(len(ins)):
         at = pl.ds(pl.multiple_of((v ^ k) * width, width), width)
         for r in range(ranks):
@@ -258,9 +268,6 @@
         lit += swaps(made[:parts], "light")[::-1]
         pieces.append(made[parts])
         carried = list(made[parts + 1 :])
-    back = call(
-        functools.partial(back_kernel, 2), [sds((size * lights, width), bf16)] * views, [], 0, pieces, lit[: parts - 1]
-    )
     spans = [(k, 0) for k in range(half)] + [(k, c * tall[0]) for c in range(2) for k in range(half, views)]
     wide = -(-max(3 * views_all // 2, lights_all) // 128) * 128
     view_part = call(
@@ -270,15 +277,26 @@
         2 * views_all * lights * width * views_all,
         near + whole[0] + whole[1],
     )
-    returned = swaps(back, "view")
+    halves = [2 if 0 < k < half else 1 for k in range(views)]
+    back = call(
+        functools.partial(back_kernel, len(pieces), half),
+        [sds((size * (counts[-1] if n > 1 else lights), width), bf16) for n in halves for _ in range(n)],
+        [],
+        0,
+        pieces,
+        lit[: parts - 1] + [view_part],
+    )
+    back = cut(back, *halves)[:-1]
+    moved = {k: [swap(part, "view", k) for part in back[k]] for k in farthest_first(views)[:-1]}
+    returned = [list(back[0])] + [moved[k] for k in range(1, views)]
     sums = call(
-        functools.partial(light_kernel, counts, 1, parts, light_scale),
+        functools.partial(light_kernel, counts, 2, parts, light_scale),
         [sds((lights + views_all // 2, wide), f32)] * parts,
         [pltpu.VMEM((parts, size * count, width), bf16) for count in counts]
         + [pltpu.VMEM((parts, lights, lights_all), f32)],
         2 * lights_all * lights_all * size * width,
         lit + [view_part],
-        [returned[1]],
+        returned[1],
     )
     dealt = call(
         functools.partial(deal_kernel, lights, rows, views),
@@ -290,11 +308,11 @@
     total = call(sum_kernel, sds((lights + rows, lights_all), f32), [], 0, swaps(dealt, "view")[::-1])
     total = doubled(total, "texel")
     core = call(
-        functools.partial(place_kernel, counts),
+        functools.partial(place_kernel, counts, halves),
         sds((ranks // views, lights, columns), bf16),
         [],
         0,
-        returned,
+        sum(returned, []),
     )
     return (total[lights:], core, total[:lights])
 

time: 44 us -> 46.3 us (1.052)
  waiting for transfers between devices: 14 us -> 16.2 us
    ppermute x21 -> x22, waiting for transfers between devices: 14 us -> 16.2 us  [swap(): lax.ppermute(value, axis, [(i, i ^ step) for i in range(lax.axis_size(axi...]
    ppermute x21 -> x22, starting transfers between devices: 24.3 us -> 24.3 us  [swap(): lax.ppermute(value, axis, [(i, i ^ step) for i in range(lax.axis_size(axi...]
  transfers between devices with their start and end apart: 21 -> 22, of which waited for: 13 -> 11; matrix products, arithmetic and copies ran while one was open for 0% -> 0% of each run, Pallas kernels for 7% -> 6%
where the time goes in v9:
time: 46.3 us; the launch traced here: 46.2 us
  starting transfers between devices  24.3 us (52%)
  waiting for transfers between devices  16.2 us (35%)
  Pallas kernels  3.07 us (7%)
  local copies, waits for them, and re-layouts  1.79 us (4%)
  between operations  0.74 us (2%)
    ppermute x22, starting transfers between devices, swap(): lax.ppermute(value, axis, [(i, i ^ step) for i in range(lax.axis_size(axi...  24.3 us
    ppermute x22, waiting for transfers between devices, swap(): lax.ppermute(value, axis, [(i, i ^ step) for i in range(lax.axis_size(axi...  16.2 us
    pallas_call x11, Pallas kernels, call(): pl.pallas_call(kernel, out_shape=out_shape, in_specs=[VMEM] * len(args) +...  3.07 us
    unnamed x4, local copies, waits for them, and re-layouts  1.18 us
  transfers between devices with their start and end apart: 22, of which 11 were waited for; matrix products, arithmetic and copies ran while one was open for 0% of the time, Pallas kernels for 6%

profile of v9, /device:TPU:0, one launch (start us, length us, event | category | flops | bytes accessed | tf_op | source)
XLA Modules:
  0.0 46.2 jit_solution(9145509691271669060)
XLA Ops:
  0.6 0.0 copy-start
  0.6 0.0 copy-start.1
  0.7 1.2 %copy-done = bf16[20,20,1024]{2,1,0:T(8,128)(2,1)S(1)} copy-done((bf16[20,20,1024]{2,1,0:T(8,128)(2,1)S(1)}, bf16[20,20,1024]{2,1,0:T(8,128)(2,1)}, u32[]{:S(2)}) %copy-start) | copy-done | bytes 819224
  1.8 0.0 copy-done.1
  1.8 0.1 shard_map.50
  2.0 0.5 %collective-permute-start.2 = (bf16[416,256]{1,0:T(8,128)(2,1)S(1)}, bf16[416,256]{1,0:T(8,128)(2,1)S(1)}, u32[]{:S(2)}, u32[]{:S(2)}) collective-permute-start(bf16[416,256]{1,0:T(8,128)(2,1)S(1)} %get-tuple-element.35), channel_id=1, source_target_pairs={{0,1},{1,0},{2,3},{3,2},{4,5},{5,4},{6,7},{7,6},{8,9},{9,8},{10,11... | collective-permute-start | bytes 638984 | tf_op jit(solution)/shard_map/ppermute | solution.py:17
  2.5 2.6 %collective-permute-start = (bf16[176,256]{1,0:T(8,128)(2,1)S(1)}, bf16[176,256]{1,0:T(8,128)(2,1)S(1)}, u32[]{:S(2)}, u32[]{:S(2)}) collective-permute-start(bf16[176,256]{1,0:T(8,128)(2,1)S(1)} %get-tuple-element.33), channel_id=1, source_target_pairs={{0,3},{1,2},{2,1},{3,0},{4,7},{5,6},{6,5},{7,4},{8,11},{9,10},{10,... | collective-permute-start | bytes 270344 | tf_op jit(solution)/shard_map/ppermute | solution.py:17
  5.1 0.0 collective-permute-start.1
  5.2 2.9 %collective-permute-done.refs_0_.refs_3_ = bf16[176,256]{1,0:T(8,128)(2,1)S(1)} collective-permute-done((bf16[176,256]{1,0:T(8,128)(2,1)S(1)}, bf16[176,256]{1,0:T(8,128)(2,1)S(1)}, u32[]{:S(2)}, u32[]{:S(2)}) %collective-permute-start) | collective-permute-done | bytes 90144 | tf_op jit(solution)/shard_map/ppermute | solution.py:17
  8.1 2.0 %collective-permute-start.6 = (bf16[240,256]{1,0:T(8,128)(2,1)S(1)}, bf16[240,256]{1,0:T(8,128)(2,1)S(1)}, u32[]{:S(2)}, u32[]{:S(2)}) collective-permute-start(bf16[240,256]{1,0:T(8,128)(2,1)S(1)} %get-tuple-element.41), channel_id=1, source_target_pairs={{0,3},{1,2},{2,1},{3,0},{4,7},{5,6},{6,5},{7,4},{8,11},{9,10},{10,... | collective-permute-start | bytes 368648 | tf_op jit(solution)/shard_map/ppermute | solution.py:17
  10.1 0.0 collective-permute-start.7
  10.1 0.1 collective-permute-done.1.refs_1_.refs_2_
  10.2 0.0 collective-permute-done.2.refs_2_.refs_1_
  10.2 0.5 %shard_map.51 = (bf16[96,256]{1,0:T(8,128)(2,1)S(1)}, bf16[96,256]{1,0:T(8,128)(2,1)S(1)}, bf16[96,256]{1,0:T(8,128)(2,1)S(1)}, bf16[96,256]{1,0:T(8,128)(2,1)S(...) custom-call(bf16[176,256]{1,0:T(8,128)(2,1)S(1)} %collective-permute-done.refs_0_.refs_3_, ...), custom_call_target="tpu_custom_call" | custom-call | flops 15728640 | bytes 1007104 | tf_op jit(solution)/shard_map/pallas_call | solution.py:46
  10.7 4.1 %collective-permute-start.3 = (bf16[96,256]{1,0:T(8,128)(2,1)S(1)}, bf16[96,256]{1,0:T(8,128)(2,1)S(1)}, u32[]{:S(2)}, u32[]{:S(2)}) collective-permute-start(bf16[96,256]{1,0:T(8,128)(2,1)S(1)} %get-tuple-element.37), channel_id=1, source_target_pairs={{0,12},{4,8},{8,4},{12,0},{1,13},{5,9},{9,5},{13,1},{2,14},{6,10},... | collective-permute-start | bytes 147464 | tf_op jit(solution)/shard_map/ppermute | solution.py:17
  14.8 0.0 collective-permute-start.4
  14.8 0.6 %collective-permute-start.5 = (bf16[96,256]{1,0:T(8,128)(2,1)S(1)}, bf16[96,256]{1,0:T(8,128)(2,1)S(1)}, u32[]{:S(2)}, u32[]{:S(2)}) collective-permute-start(bf16[96,256]{1,0:T(8,128)(2,1)S(1)} %get-tuple-element.39), channel_id=1, source_target_pairs={{0,4},{4,0},{8,12},{12,8},{1,5},{5,1},{9,13},{13,9},{2,6},{6,2},{1... | collective-permute-start | bytes 147464 | tf_op jit(solution)/shard_map/ppermute | solution.py:17
  15.4 0.0 collective-permute-done.6.refs_0_.refs_5_
  15.4 1.2 %collective-permute-done.7.refs_1_.refs_4_ = bf16[240,256]{1,0:T(8,128)(2,1)S(1)} collective-permute-done((bf16[240,256]{1,0:T(8,128)(2,1)S(1)}, bf16[240,256]{1,0:T(8,128)(2,1)S(1)}, u32[]{:S(2)}, u32[]{:S(2)}) %collective-permute-start.7) | collective-permute-done | bytes 122912 | tf_op jit(solution)/shard_map/ppermute | solution.py:17
  16.6 0.5 %shard_map.54.refs_5_.refs_8_ = f32[40,128]{1,0:T(8,128)S(1)} custom-call(bf16[416,256]{1,0:T(8,128)(2,1)S(1)} %get-tuple-element.36.refs_3_.refs_0_, bf16[416,256]{1,0:T(8,128)(2,1)S(1)} %collective-permute-done.2.refs_2_.refs_1_, bf16[176,256]{1,0:T(8,128)(2,1)S(1)} %collective-permute-done.1.refs_1_.refs_2_, ...), custom_call_target="tpu_custom_call" | custom-call | flops 65536000 | bytes 872448 | tf_op jit(solution)/shard_map/pallas_call | solution.py:46
  17.1 0.0 collective-permute-done.3.refs_5_.refs_2_.refs_0_
  17.1 0.5 %shard_map.53 = (bf16[144,256]{1,0:T(8,128)(2,1)S(1)}, bf16[144,256]{1,0:T(8,128)(2,1)S(1)}, bf16[144,256]{1,0:T(8,128)(2,1)S(1)}, bf16[144,256]{1,0:T(8,128)(2,1)S(1)}, bf16[4,144,256]{2,1,0:T(8,128)(2,1)S(1)}) custom-call(bf16[240,256]{1,0:T(8,128)(2,1)S(1)} %collective-permute-done.6.refs_0_.refs_5_, ...), custom_call_target="tpu_custom_call" | custom-call | flops 23592960 | bytes 1269248 | tf_op jit(solution)/shard_map/pallas_call | solution.py:46
  17.6 2.2 %collective-permute-done.4.refs_3_.refs_1_ = bf16[96,256]{1,0:T(8,128)(2,1)S(1)} collective-permute-done((bf16[96,256]{1,0:T(8,128)(2,1)S(1)}, bf16[96,256]{1,0:T(8,128)(2,1)S(1)}, u32[]{:S(2)}, u32[]{:S(2)}) %collective-permute-start.4) | collective-permute-done | bytes 49184 | tf_op jit(solution)/shard_map/ppermute | solution.py:17
  19.8 0.0 collective-permute-done.5.refs_4_.refs_2_
  19.8 0.1 collective-permute-start.11
  19.9 0.5 %collective-permute-start.12 = (bf16[144,256]{1,0:T(8,128)(2,1)S(1)}, bf16[144,256]{1,0:T(8,128)(2,1)S(1)}, u32[]{:S(2)}, u32[]{:S(2)}) collective-permute-start(bf16[144,256]{1,0:T(8,128)(2,1)S(1)} %get-tuple-element.51), channel_id=1, source_target_pairs={{0,1},{1,0},{2,3},{3,2},{4,5},{5,4},{6,7},{7,6},{8,9},{9,8},{10,11... | collective-permute-start | bytes 221192 | tf_op jit(solution)/shard_map/ppermute | solution.py:17
  20.4 2.0 %collective-permute-start.8 = (bf16[144,256]{1,0:T(8,128)(2,1)S(1)}, bf16[144,256]{1,0:T(8,128)(2,1)S(1)}, u32[]{:S(2)}, u32[]{:S(2)}) collective-permute-start(bf16[144,256]{1,0:T(8,128)(2,1)S(1)} %get-tuple-element.44), channel_id=1, source_target_pairs={{0,12},{4,8},{8,4},{12,0},{1,13},{5,9},{9,5},{13,1},{2,14},{6,10},... | collective-permute-start | bytes 221192 | tf_op jit(solution)/shard_map/ppermute | solution.py:17
  22.3 0.1 collective-permute-start.9
  22.4 2.4 %collective-permute-start.10 = (bf16[144,256]{1,0:T(8,128)(2,1)S(1)}, bf16[144,256]{1,0:T(8,128)(2,1)S(1)}, u32[]{:S(2)}, u32[]{:S(2)}) collective-permute-start(bf16[144,256]{1,0:T(8,128)(2,1)S(1)} %get-tuple-element.46), channel_id=1, source_target_pairs={{0,4},{4,0},{8,12},{12,8},{1,5},{5,1},{9,13},{13,9},{2,6},{6,2},{1... | collective-permute-start | bytes 221192 | tf_op jit(solution)/shard_map/ppermute | solution.py:17
  24.8 0.0 collective-permute-done.11.refs_9_.refs_1_
  24.8 1.5 %collective-permute-start.20 = (bf16[240,256]{1,0:T(8,128)(2,1)S(1)}, bf16[240,256]{1,0:T(8,128)(2,1)S(1)}, u32[]{:S(2)}, u32[]{:S(2)}) collective-permute-start(bf16[240,256]{1,0:T(8,128)(2,1)S(1)} %get-tuple-element.61), channel_id=1, source_target_pairs={{0,2},{1,3},{2,0},{3,1},{4,6},{5,7},{6,4},{7,5},{8,10},{9,11},{10,... | collective-permute-start | bytes 368648 | tf_op jit(solution)/shard_map/ppermute | solution.py:17
  26.3 0.0 collective-permute-done.12.refs_10_.refs_2_
  26.3 0.0 collective-permute-start.21
  26.3 1.0 %collective-permute-done.8.refs_4_ = bf16[144,256]{1,0:T(8,128)(2,1)S(1)} collective-permute-done((bf16[144,256]{1,0:T(8,128)(2,1)S(1)}, bf16[144,256]{1,0:T(8,128)(2,1)S(1)}, u32[]{:S(2)}, u32[]{:S(2)}) %collective-permute-start.8) | collective-permute-done | bytes 73760 | tf_op jit(solution)/shard_map/ppermute | solution.py:17
  27.3 2.3 %collective-permute-done.9.refs_5_ = bf16[144,256]{1,0:T(8,128)(2,1)S(1)} collective-permute-done((bf16[144,256]{1,0:T(8,128)(2,1)S(1)}, bf16[144,256]{1,0:T(8,128)(2,1)S(1)}, u32[]{:S(2)}, u32[]{:S(2)}) %collective-permute-start.9) | collective-permute-done | bytes 73760 | tf_op jit(solution)/shard_map/ppermute | solution.py:17
  29.7 0.0 collective-permute-done.10.refs_6_
  29.7 0.3 shard_map.56
  30.0 2.8 %collective-permute-start.13 = (f32[60,128]{1,0:T(8,128)S(1)}, f32[60,128]{1,0:T(8,128)S(1)}, u32[]{:S(2)}, u32[]{:S(2)}) collective-permute-start(f32[60,128]{1,0:T(8,128)S(1)} %get-tuple-element.52), channel_id=1, source_target_pairs={{0,12},{4,8},{8,4},{12,0},{1,13},{5,9},{9,5},{13,1},{2,14},{6,10},... | collective-permute-start | bytes 92168 | tf_op jit(solution)/shard_map/ppermute | solution.py:17
  32.8 0.0 collective-permute-start.14
  32.8 1.7 %collective-permute-start.15 = (f32[60,128]{1,0:T(8,128)S(1)}, f32[60,128]{1,0:T(8,128)S(1)}, u32[]{:S(2)}, u32[]{:S(2)}) collective-permute-start(f32[60,128]{1,0:T(8,128)S(1)} %get-tuple-element.54), channel_id=1, source_target_pairs={{0,4},{4,0},{8,12},{12,8},{1,5},{5,1},{9,13},{13,9},{2,6},{6,2},{1... | collective-permute-start | bytes 92168 | tf_op jit(solution)/shard_map/ppermute | solution.py:17
  34.5 1.4 %collective-permute-done.13.refs_0_ = f32[60,128]{1,0:T(8,128)S(1)} collective-permute-done((f32[60,128]{1,0:T(8,128)S(1)}, f32[60,128]{1,0:T(8,128)S(1)}, u32[]{:S(2)}, u32[]{:S(2)}) %collective-permute-start.13) | collective-permute-done | bytes 30752 | tf_op jit(solution)/shard_map/ppermute | solution.py:17
  35.9 1.7 %collective-permute-done.14.refs_1_ = f32[60,128]{1,0:T(8,128)S(1)} collective-permute-done((f32[60,128]{1,0:T(8,128)S(1)}, f32[60,128]{1,0:T(8,128)S(1)}, u32[]{:S(2)}, u32[]{:S(2)}) %collective-permute-start.14) | collective-permute-done | bytes 30752 | tf_op jit(solution)/shard_map/ppermute | solution.py:17
  37.6 0.0 collective-permute-done.15.refs_2_
  37.6 0.2 shard_map.57
  37.7 0.1 collective-permute-start.16
  37.8 1.5 %collective-permute-start.17 = (f32[40,80]{1,0:T(8,128)S(1)}, f32[40,80]{1,0:T(8,128)S(1)}, u32[]{:S(2)}, u32[]{:S(2)}) collective-permute-start(f32[40,80]{1,0:T(8,128)S(1)} %get-tuple-element.57), channel_id=1, source_target_pairs={{0,2},{1,3},{2,0},{3,1},{4,6},{5,7},{6,4},{7,5},{8,10},{9,11},{10,... | collective-permute-start | bytes 38408 | tf_op jit(solution)/shard_map/ppermute | solution.py:17
  39.4 0.3 collective-permute-start.18
  39.7 1.5 %collective-permute-done.16.refs_0_ = f32[40,80]{1,0:T(8,128)S(1)} collective-permute-done((f32[40,80]{1,0:T(8,128)S(1)}, f32[40,80]{1,0:T(8,128)S(1)}, u32[]{:S(2)}, u32[]{:S(2)}) %collective-permute-start.16) | collective-permute-done | bytes 12832 | tf_op jit(solution)/shard_map/ppermute | solution.py:17
  41.2 0.5 %collective-permute-done.17.refs_1_ = f32[40,80]{1,0:T(8,128)S(1)} collective-permute-done((f32[40,80]{1,0:T(8,128)S(1)}, f32[40,80]{1,0:T(8,128)S(1)}, u32[]{:S(2)}, u32[]{:S(2)}) %collective-permute-start.17) | collective-permute-done | bytes 12832 | tf_op jit(solution)/shard_map/ppermute | solution.py:17
  41.7 0.0 collective-permute-done.18.refs_2_
  41.7 1.6 %collective-permute-start.19 = (f32[40,80]{1,0:T(8,128)S(1)}, f32[40,80]{1,0:T(8,128)S(1)}, u32[]{:S(2)}, u32[]{:S(2)}) collective-permute-start(f32[40,80]{1,0:T(8,128)S(1)} %shard_map.58), channel_id=1, source_target_pairs={{0,16},{16,0},{1,17},{17,1},{2,18},{18,2},{3,19},{19,3},{4,20},{20... | collective-permute-start | bytes 38408 | tf_op jit(solution)/shard_map/ppermute | solution.py:17
  43.3 0.0 collective-permute-done.20.refs_3_
  43.3 0.0 collective-permute-done.21.refs_4_
  43.3 0.9 %shard_map.59 = bf16[12,20,1024]{2,1,0:T(8,128)(2,1)} custom-call(bf16[240,256]{1,0:T(8,128)(2,1)S(1)} %get-tuple-element.60.refs_0_, bf16[144,256]{1,0:T(8,128)(2,1)S(1)} %collective-permute-done.11.refs_9_.refs_1_, bf16[144,256]{1,0:T(8,128)(2,1)S(1)} %collective-permute-done.12.refs_10_.refs_2_, bf16[240,256]{1,0:T(8,128)(2,1)S(1)} %collective-permute-done.20.refs_3_, ...), custom_call_target="tpu_custom_call" | custom-call | bytes 1007616 | tf_op jit(solution)/shard_map/pallas_call | solution.py:46
  44.2 1.4 %collective-permute-done.19 = f32[40,80]{1,0:T(8,128)S(1)} collective-permute-done((f32[40,80]{1,0:T(8,128)S(1)}, f32[40,80]{1,0:T(8,128)S(1)}, u32[]{:S(2)}, u32[]{:S(2)}) %collective-permute-start.19) | collective-permute-done | bytes 12832 | tf_op jit(solution)/shard_map/ppermute | solution.py:17
  45.6 0.6 %fusion = (f32[20,80]{1,0:T(8,128)}, f32[20,80]{1,0:T(8,128)}) fusion(f32[40,80]{1,0:T(8,128)S(1)} %add.3), kind=kLoop, calls=%fused_computation | loop fusion | bytes 25600 | tf_op jit(solution)/shard_map/slice | solution.py:317
  (5 shorter events, 0.1 us)
Async XLA Ops:
  0.6 1.2 %copy-start = (bf16[20,20,1024]{2,1,0:T(8,128)(2,1)S(1)}, bf16[20,20,1024]{2,1,0:T(8,128)(2,1)}, u32[]{:S(2)}) copy-start(bf16[20,20,1024]{2,1,0:T(8,128)(2,1)} %slab_ref.3) | copy-start | bytes 2457604
  0.6 1.2 %copy-start.1 = (bf16[20,48]{1,0:T(8,128)(2,1)S(1)}, bf16[20,48]{1,0:T(8,128)(2,1)}, u32[]{:S(2)}) copy-start(bf16[20,48]{1,0:T(8,128)(2,1)} %refs_0_.1) | copy-start | bytes 5764
  2.0 8.3 %collective-permute-start.2 = (bf16[416,256]{1,0:T(8,128)(2,1)S(1)}, bf16[416,256]{1,0:T(8,128)(2,1)S(1)}, u32[]{:S(2)}, u32[]{:S(2)}) collective-permute-start(bf16[416,256]{1,0:T(8,128)(2,1)S(1)} %get-tuple-element.35), channel_id=1, source_target_pairs={{0,1},{1,0},{2,3},{3,2},{4,5},{5,4},{6,7},{7,6},{8,9},{9,8},{10,11... | collective-permute-start | bytes 638984 | tf_op jit(solution)/shard_map/ppermute | solution.py:17
  2.5 5.6 %collective-permute-start = (bf16[176,256]{1,0:T(8,128)(2,1)S(1)}, bf16[176,256]{1,0:T(8,128)(2,1)S(1)}, u32[]{:S(2)}, u32[]{:S(2)}) collective-permute-start(bf16[176,256]{1,0:T(8,128)(2,1)S(1)} %get-tuple-element.33), channel_id=1, source_target_pairs={{0,3},{1,2},{2,1},{3,0},{4,7},{5,6},{6,5},{7,4},{8,11},{9,10},{10,... | collective-permute-start | bytes 270344 | tf_op jit(solution)/shard_map/ppermute | solution.py:17
  5.1 5.1 %collective-permute-start.1 = (bf16[176,256]{1,0:T(8,128)(2,1)S(1)}, bf16[176,256]{1,0:T(8,128)(2,1)S(1)}, u32[]{:S(2)}, u32[]{:S(2)}) collective-permute-start(bf16[176,256]{1,0:T(8,128)(2,1)S(1)} %get-tuple-element.34), channel_id=1, source_target_pairs={{0,2},{1,3},{2,0},{3,1},{4,6},{5,7},{6,4},{7,5},{8,10},{9,11},{10,... | collective-permute-start | bytes 270344 | tf_op jit(solution)/shard_map/ppermute | solution.py:17
  8.1 7.3 %collective-permute-start.6 = (bf16[240,256]{1,0:T(8,128)(2,1)S(1)}, bf16[240,256]{1,0:T(8,128)(2,1)S(1)}, u32[]{:S(2)}, u32[]{:S(2)}) collective-permute-start(bf16[240,256]{1,0:T(8,128)(2,1)S(1)} %get-tuple-element.41), channel_id=1, source_target_pairs={{0,3},{1,2},{2,1},{3,0},{4,7},{5,6},{6,5},{7,4},{8,11},{9,10},{10,... | collective-permute-start | bytes 368648 | tf_op jit(solution)/shard_map/ppermute | solution.py:17
  10.1 6.5 %collective-permute-start.7 = (bf16[240,256]{1,0:T(8,128)(2,1)S(1)}, bf16[240,256]{1,0:T(8,128)(2,1)S(1)}, u32[]{:S(2)}, u32[]{:S(2)}) collective-permute-start(bf16[240,256]{1,0:T(8,128)(2,1)S(1)} %get-tuple-element.42), channel_id=1, source_target_pairs={{0,2},{1,3},{2,0},{3,1},{4,6},{5,7},{6,4},{7,5},{8,10},{9,11},{10,... | collective-permute-start | bytes 368648 | tf_op jit(solution)/shard_map/ppermute | solution.py:17
  10.7 6.4 %collective-permute-start.3 = (bf16[96,256]{1,0:T(8,128)(2,1)S(1)}, bf16[96,256]{1,0:T(8,128)(2,1)S(1)}, u32[]{:S(2)}, u32[]{:S(2)}) collective-permute-start(bf16[96,256]{1,0:T(8,128)(2,1)S(1)} %get-tuple-element.37), channel_id=1, source_target_pairs={{0,12},{4,8},{8,4},{12,0},{1,13},{5,9},{9,5},{13,1},{2,14},{6,10},... | collective-permute-start | bytes 147464 | tf_op jit(solution)/shard_map/ppermute | solution.py:17
  14.8 5.0 %collective-permute-start.4 = (bf16[96,256]{1,0:T(8,128)(2,1)S(1)}, bf16[96,256]{1,0:T(8,128)(2,1)S(1)}, u32[]{:S(2)}, u32[]{:S(2)}) collective-permute-start(bf16[96,256]{1,0:T(8,128)(2,1)S(1)} %get-tuple-element.38), channel_id=1, source_target_pairs={{0,8},{4,12},{8,0},{12,4},{1,9},{5,13},{9,1},{13,5},{2,10},{6,14},... | collective-permute-start | bytes 147464 | tf_op jit(solution)/shard_map/ppermute | solution.py:17
  14.8 5.0 %collective-permute-start.5 = (bf16[96,256]{1,0:T(8,128)(2,1)S(1)}, bf16[96,256]{1,0:T(8,128)(2,1)S(1)}, u32[]{:S(2)}, u32[]{:S(2)}) collective-permute-start(bf16[96,256]{1,0:T(8,128)(2,1)S(1)} %get-tuple-element.39), channel_id=1, source_target_pairs={{0,4},{4,0},{8,12},{12,8},{1,5},{5,1},{9,13},{13,9},{2,6},{6,2},{1... | collective-permute-start | bytes 147464 | tf_op jit(solution)/shard_map/ppermute | solution.py:17
  19.8 5.0 %collective-permute-start.11 = (bf16[144,256]{1,0:T(8,128)(2,1)S(1)}, bf16[144,256]{1,0:T(8,128)(2,1)S(1)}, u32[]{:S(2)}, u32[]{:S(2)}) collective-permute-start(bf16[144,256]{1,0:T(8,128)(2,1)S(1)} %get-tuple-element.50), channel_id=1, source_target_pairs={{0,1},{1,0},{2,3},{3,2},{4,5},{5,4},{6,7},{7,6},{8,9},{9,8},{10,11... | collective-permute-start | bytes 221192 | tf_op jit(solution)/shard_map/ppermute | solution.py:17
  19.9 6.4 %collective-permute-start.12 = (bf16[144,256]{1,0:T(8,128)(2,1)S(1)}, bf16[144,256]{1,0:T(8,128)(2,1)S(1)}, u32[]{:S(2)}, u32[]{:S(2)}) collective-permute-start(bf16[144,256]{1,0:T(8,128)(2,1)S(1)} %get-tuple-element.51), channel_id=1, source_target_pairs={{0,1},{1,0},{2,3},{3,2},{4,5},{5,4},{6,7},{7,6},{8,9},{9,8},{10,11... | collective-permute-start | bytes 221192 | tf_op jit(solution)/shard_map/ppermute | solution.py:17
  20.4 6.9 %collective-permute-start.8 = (bf16[144,256]{1,0:T(8,128)(2,1)S(1)}, bf16[144,256]{1,0:T(8,128)(2,1)S(1)}, u32[]{:S(2)}, u32[]{:S(2)}) collective-permute-start(bf16[144,256]{1,0:T(8,128)(2,1)S(1)} %get-tuple-element.44), channel_id=1, source_target_pairs={{0,12},{4,8},{8,4},{12,0},{1,13},{5,9},{9,5},{13,1},{2,14},{6,10},... | collective-permute-start | bytes 221192 | tf_op jit(solution)/shard_map/ppermute | solution.py:17
  22.3 7.3 %collective-permute-start.9 = (bf16[144,256]{1,0:T(8,128)(2,1)S(1)}, bf16[144,256]{1,0:T(8,128)(2,1)S(1)}, u32[]{:S(2)}, u32[]{:S(2)}) collective-permute-start(bf16[144,256]{1,0:T(8,128)(2,1)S(1)} %get-tuple-element.45), channel_id=1, source_target_pairs={{0,8},{4,12},{8,0},{12,4},{1,9},{5,13},{9,1},{13,5},{2,10},{6,14},... | collective-permute-start | bytes 221192 | tf_op jit(solution)/shard_map/ppermute | solution.py:17
  22.4 7.2 %collective-permute-start.10 = (bf16[144,256]{1,0:T(8,128)(2,1)S(1)}, bf16[144,256]{1,0:T(8,128)(2,1)S(1)}, u32[]{:S(2)}, u32[]{:S(2)}) collective-permute-start(bf16[144,256]{1,0:T(8,128)(2,1)S(1)} %get-tuple-element.46), channel_id=1, source_target_pairs={{0,4},{4,0},{8,12},{12,8},{1,5},{5,1},{9,13},{13,9},{2,6},{6,2},{1... | collective-permute-start | bytes 221192 | tf_op jit(solution)/shard_map/ppermute | solution.py:17
  24.8 18.5 %collective-permute-start.20 = (bf16[240,256]{1,0:T(8,128)(2,1)S(1)}, bf16[240,256]{1,0:T(8,128)(2,1)S(1)}, u32[]{:S(2)}, u32[]{:S(2)}) collective-permute-start(bf16[240,256]{1,0:T(8,128)(2,1)S(1)} %get-tuple-element.61), channel_id=1, source_target_pairs={{0,2},{1,3},{2,0},{3,1},{4,6},{5,7},{6,4},{7,5},{8,10},{9,11},{10,... | collective-permute-start | bytes 368648 | tf_op jit(solution)/shard_map/ppermute | solution.py:17
  26.3 17.0 %collective-permute-start.21 = (bf16[240,256]{1,0:T(8,128)(2,1)S(1)}, bf16[240,256]{1,0:T(8,128)(2,1)S(1)}, u32[]{:S(2)}, u32[]{:S(2)}) collective-permute-start(bf16[240,256]{1,0:T(8,128)(2,1)S(1)} %get-tuple-element.62), channel_id=1, source_target_pairs={{0,3},{1,2},{2,1},{3,0},{4,7},{5,6},{6,5},{7,4},{8,11},{9,10},{10,... | collective-permute-start | bytes 368648 | tf_op jit(solution)/shard_map/ppermute | solution.py:17
  30.0 5.9 %collective-permute-start.13 = (f32[60,128]{1,0:T(8,128)S(1)}, f32[60,128]{1,0:T(8,128)S(1)}, u32[]{:S(2)}, u32[]{:S(2)}) collective-permute-start(f32[60,128]{1,0:T(8,128)S(1)} %get-tuple-element.52), channel_id=1, source_target_pairs={{0,12},{4,8},{8,4},{12,0},{1,13},{5,9},{9,5},{13,1},{2,14},{6,10},... | collective-permute-start | bytes 92168 | tf_op jit(solution)/shard_map/ppermute | solution.py:17
  32.8 4.8 %collective-permute-start.14 = (f32[60,128]{1,0:T(8,128)S(1)}, f32[60,128]{1,0:T(8,128)S(1)}, u32[]{:S(2)}, u32[]{:S(2)}) collective-permute-start(f32[60,128]{1,0:T(8,128)S(1)} %get-tuple-element.53), channel_id=1, source_target_pairs={{0,8},{4,12},{8,0},{12,4},{1,9},{5,13},{9,1},{13,5},{2,10},{6,14},... | collective-permute-start | bytes 92168 | tf_op jit(solution)/shard_map/ppermute | solution.py:17
  32.8 4.8 %collective-permute-start.15 = (f32[60,128]{1,0:T(8,128)S(1)}, f32[60,128]{1,0:T(8,128)S(1)}, u32[]{:S(2)}, u32[]{:S(2)}) collective-permute-start(f32[60,128]{1,0:T(8,128)S(1)} %get-tuple-element.54), channel_id=1, source_target_pairs={{0,4},{4,0},{8,12},{12,8},{1,5},{5,1},{9,13},{13,9},{2,6},{6,2},{1... | collective-permute-start | bytes 92168 | tf_op jit(solution)/shard_map/ppermute | solution.py:17
  37.7 3.5 %collective-permute-start.16 = (f32[40,80]{1,0:T(8,128)S(1)}, f32[40,80]{1,0:T(8,128)S(1)}, u32[]{:S(2)}, u32[]{:S(2)}) collective-permute-start(f32[40,80]{1,0:T(8,128)S(1)} %get-tuple-element.56), channel_id=1, source_target_pairs={{0,3},{1,2},{2,1},{3,0},{4,7},{5,6},{6,5},{7,4},{8,11},{9,10},{10,... | collective-permute-start | bytes 38408 | tf_op jit(solution)/shard_map/ppermute | solution.py:17
  37.8 3.8 %collective-permute-start.17 = (f32[40,80]{1,0:T(8,128)S(1)}, f32[40,80]{1,0:T(8,128)S(1)}, u32[]{:S(2)}, u32[]{:S(2)}) collective-permute-start(f32[40,80]{1,0:T(8,128)S(1)} %get-tuple-element.57), channel_id=1, source_target_pairs={{0,2},{1,3},{2,0},{3,1},{4,6},{5,7},{6,4},{7,5},{8,10},{9,11},{10,... | collective-permute-start | bytes 38408 | tf_op jit(solution)/shard_map/ppermute | solution.py:17
  39.4 2.3 %collective-permute-start.18 = (f32[40,80]{1,0:T(8,128)S(1)}, f32[40,80]{1,0:T(8,128)S(1)}, u32[]{:S(2)}, u32[]{:S(2)}) collective-permute-start(f32[40,80]{1,0:T(8,128)S(1)} %get-tuple-element.58), channel_id=1, source_target_pairs={{0,1},{1,0},{2,3},{3,2},{4,5},{5,4},{6,7},{7,6},{8,9},{9,8},{10,11... | collective-permute-start | bytes 38408 | tf_op jit(solution)/shard_map/ppermute | solution.py:17
  41.7 3.9 %collective-permute-start.19 = (f32[40,80]{1,0:T(8,128)S(1)}, f32[40,80]{1,0:T(8,128)S(1)}, u32[]{:S(2)}, u32[]{:S(2)}) collective-permute-start(f32[40,80]{1,0:T(8,128)S(1)} %shard_map.58), channel_id=1, source_target_pairs={{0,16},{16,0},{1,17},{17,1},{2,18},{18,2},{3,19},{19,3},{4,20},{20... | collective-permute-start | bytes 38408 | tf_op jit(solution)/shard_map/ppermute | solution.py:17

commit v10 on v8

--- a/solution.py
+++ b/solution.py
@@ -230,7 +230,7 @@
         [],
         0,
         [slab],
-        whole[0][1:],
+        near[1:],
     )
     moved = {k: swap(packed[k - half], "view", k) for k in farthest_first(views)[:half]}
     whole.append([moved[k] for k in range(half, views)])

time: 44 us -> 44.4 us (level)
  waiting for transfers between devices: 14 us -> 14.7 us
    ppermute x21, waiting for transfers between devices: 14 us -> 14.7 us  [swap(): lax.ppermute(value, axis, [(i, i ^ step) for i in range(lax.axis_size(axi...]
  transfers between devices with their start and end apart: 21 -> 21, of which waited for: 13 -> 12; matrix products, arithmetic and copies ran while one was open for 0% -> 0% of each run, Pallas kernels for 7% -> 7%
where the time goes in v10:
time: 44.4 us; the launch traced here: 44.3 us
  starting transfers between devices  24 us (54%)
  waiting for transfers between devices  14.7 us (33%)
  Pallas kernels  3.07 us (7%)
  local copies, waits for them, and re-layouts  1.79 us (4%)
  between operations  0.73 us (2%)
    ppermute x21, starting transfers between devices, swap(): lax.ppermute(value, axis, [(i, i ^ step) for i in range(lax.axis_size(axi...  24 us
    ppermute x21, waiting for transfers between devices, swap(): lax.ppermute(value, axis, [(i, i ^ step) for i in range(lax.axis_size(axi...  14.7 us
    pallas_call x11, Pallas kernels, call(): pl.pallas_call(kernel, out_shape=out_shape, in_specs=[VMEM] * len(args) +...  3.07 us
    unnamed x4, local copies, waits for them, and re-layouts  1.18 us
  transfers between devices with their start and end apart: 21, of which 12 were waited for; matrix products, arithmetic and copies ran while one was open for 0% of the time, Pallas kernels for 7%

profile of v10, /device:TPU:0, one launch (start us, length us, event | category | flops | bytes accessed | tf_op | source)
XLA Modules:
  0.0 44.3 jit_solution(4784194556011142726)
XLA Ops:
  0.6 0.0 copy-start
  0.6 0.0 copy-start.1
  0.7 1.2 %copy-done = bf16[20,20,1024]{2,1,0:T(8,128)(2,1)S(1)} copy-done((bf16[20,20,1024]{2,1,0:T(8,128)(2,1)S(1)}, bf16[20,20,1024]{2,1,0:T(8,128)(2,1)}, u32[]{:S(2)}) %copy-start) | copy-done | bytes 819224
  1.8 0.0 copy-done.1
  1.8 0.1 shard_map.50
  2.0 0.5 %collective-permute-start.2 = (bf16[416,256]{1,0:T(8,128)(2,1)S(1)}, bf16[416,256]{1,0:T(8,128)(2,1)S(1)}, u32[]{:S(2)}, u32[]{:S(2)}) collective-permute-start(bf16[416,256]{1,0:T(8,128)(2,1)S(1)} %get-tuple-element.34), channel_id=1, source_target_pairs={{0,1},{1,0},{2,3},{3,2},{4,5},{5,4},{6,7},{7,6},{8,9},{9,8},{10,11... | collective-permute-start | bytes 638984 | tf_op jit(solution)/shard_map/ppermute | solution.py:17
  2.5 2.6 %collective-permute-start = (bf16[176,256]{1,0:T(8,128)(2,1)S(1)}, bf16[176,256]{1,0:T(8,128)(2,1)S(1)}, u32[]{:S(2)}, u32[]{:S(2)}) collective-permute-start(bf16[176,256]{1,0:T(8,128)(2,1)S(1)} %get-tuple-element.32), channel_id=1, source_target_pairs={{0,3},{1,2},{2,1},{3,0},{4,7},{5,6},{6,5},{7,4},{8,11},{9,10},{10,... | collective-permute-start | bytes 270344 | tf_op jit(solution)/shard_map/ppermute | solution.py:17
  5.1 0.0 collective-permute-start.1
  5.2 0.0 collective-permute-done.2.refs_2_.refs_0_.refs_1_
  5.2 1.4 %collective-permute-start.6 = (bf16[240,256]{1,0:T(8,128)(2,1)S(1)}, bf16[240,256]{1,0:T(8,128)(2,1)S(1)}, u32[]{:S(2)}, u32[]{:S(2)}) collective-permute-start(bf16[240,256]{1,0:T(8,128)(2,1)S(1)} %get-tuple-element.40), channel_id=1, source_target_pairs={{0,3},{1,2},{2,1},{3,0},{4,7},{5,6},{6,5},{7,4},{8,11},{9,10},{10,... | collective-permute-start | bytes 368648 | tf_op jit(solution)/shard_map/ppermute | solution.py:17
  6.7 0.7 %collective-permute-start.7 = (bf16[240,256]{1,0:T(8,128)(2,1)S(1)}, bf16[240,256]{1,0:T(8,128)(2,1)S(1)}, u32[]{:S(2)}, u32[]{:S(2)}) collective-permute-start(bf16[240,256]{1,0:T(8,128)(2,1)S(1)} %get-tuple-element.41), channel_id=1, source_target_pairs={{0,2},{1,3},{2,0},{3,1},{4,6},{5,7},{6,4},{7,5},{8,10},{9,11},{10,... | collective-permute-start | bytes 368648 | tf_op jit(solution)/shard_map/ppermute | solution.py:17
  7.3 0.7 %collective-permute-done.refs_0_.refs_3_ = bf16[176,256]{1,0:T(8,128)(2,1)S(1)} collective-permute-done((bf16[176,256]{1,0:T(8,128)(2,1)S(1)}, bf16[176,256]{1,0:T(8,128)(2,1)S(1)}, u32[]{:S(2)}, u32[]{:S(2)}) %collective-permute-start) | collective-permute-done | bytes 90144 | tf_op jit(solution)/shard_map/ppermute | solution.py:17
  8.1 2.6 %collective-permute-done.1.refs_1_.refs_2_ = bf16[176,256]{1,0:T(8,128)(2,1)S(1)} collective-permute-done((bf16[176,256]{1,0:T(8,128)(2,1)S(1)}, bf16[176,256]{1,0:T(8,128)(2,1)S(1)}, u32[]{:S(2)}, u32[]{:S(2)}) %collective-permute-start.1) | collective-permute-done | bytes 90144 | tf_op jit(solution)/shard_map/ppermute | solution.py:17
  10.7 0.5 %shard_map.51 = (bf16[96,256]{1,0:T(8,128)(2,1)S(1)}, bf16[96,256]{1,0:T(8,128)(2,1)S(1)}, bf16[96,256]{1,0:T(8,128)(2,1)S(1)}, bf16[96,256]{1,0:T(8,128)(2,1)S(...) custom-call(bf16[176,256]{1,0:T(8,128)(2,1)S(1)} %collective-permute-done.refs_0_.refs_3_, ...), custom_call_target="tpu_custom_call" | custom-call | flops 15728640 | bytes 1007104 | tf_op jit(solution)/shard_map/pallas_call | solution.py:46
  11.2 4.0 %collective-permute-start.3 = (bf16[96,256]{1,0:T(8,128)(2,1)S(1)}, bf16[96,256]{1,0:T(8,128)(2,1)S(1)}, u32[]{:S(2)}, u32[]{:S(2)}) collective-permute-start(bf16[96,256]{1,0:T(8,128)(2,1)S(1)} %get-tuple-element.36), channel_id=1, source_target_pairs={{0,12},{4,8},{8,4},{12,0},{1,13},{5,9},{9,5},{13,1},{2,14},{6,10},... | collective-permute-start | bytes 147464 | tf_op jit(solution)/shard_map/ppermute | solution.py:17
  15.1 0.0 collective-permute-start.4
  15.1 0.6 %collective-permute-start.5 = (bf16[96,256]{1,0:T(8,128)(2,1)S(1)}, bf16[96,256]{1,0:T(8,128)(2,1)S(1)}, u32[]{:S(2)}, u32[]{:S(2)}) collective-permute-start(bf16[96,256]{1,0:T(8,128)(2,1)S(1)} %get-tuple-element.38), channel_id=1, source_target_pairs={{0,4},{4,0},{8,12},{12,8},{1,5},{5,1},{9,13},{13,9},{2,6},{6,2},{1... | collective-permute-start | bytes 147464 | tf_op jit(solution)/shard_map/ppermute | solution.py:17
  15.8 1.7 %collective-permute-done.3.refs_5_.refs_2_.refs_0_ = bf16[96,256]{1,0:T(8,128)(2,1)S(1)} collective-permute-done((bf16[96,256]{1,0:T(8,128)(2,1)S(1)}, bf16[96,256]{1,0:T(8,128)(2,1)S(1)}, u32[]{:S(2)}, u32[]{:S(2)}) %collective-permute-start.3) | collective-permute-done | bytes 49184 | tf_op jit(solution)/shard_map/ppermute | solution.py:17
  17.5 0.0 collective-permute-done.6.refs_0_.refs_5_
  17.5 0.0 collective-permute-done.7.refs_1_.refs_4_
  17.5 0.5 %shard_map.53 = (bf16[144,256]{1,0:T(8,128)(2,1)S(1)}, bf16[144,256]{1,0:T(8,128)(2,1)S(1)}, bf16[144,256]{1,0:T(8,128)(2,1)S(1)}, bf16[144,256]{1,0:T(8,128)(2,1)S(1)}, bf16[4,144,256]{2,1,0:T(8,128)(2,1)S(1)}) custom-call(bf16[240,256]{1,0:T(8,128)(2,1)S(1)} %collective-permute-done.6.refs_0_.refs_5_, ...), custom_call_target="tpu_custom_call" | custom-call | flops 23592960 | bytes 1269248 | tf_op jit(solution)/shard_map/pallas_call | solution.py:46
  18.0 3.7 %collective-permute-start.8 = (bf16[144,256]{1,0:T(8,128)(2,1)S(1)}, bf16[144,256]{1,0:T(8,128)(2,1)S(1)}, u32[]{:S(2)}, u32[]{:S(2)}) collective-permute-start(bf16[144,256]{1,0:T(8,128)(2,1)S(1)} %get-tuple-element.43), channel_id=1, source_target_pairs={{0,12},{4,8},{8,4},{12,0},{1,13},{5,9},{9,5},{13,1},{2,14},{6,10},... | collective-permute-start | bytes 221192 | tf_op jit(solution)/shard_map/ppermute | solution.py:17
  21.7 0.0 collective-permute-done.4.refs_3_.refs_1_
  21.7 0.0 collective-permute-done.5.refs_4_.refs_2_
  21.7 0.1 collective-permute-start.11
  21.8 0.6 %collective-permute-start.9 = (bf16[144,256]{1,0:T(8,128)(2,1)S(1)}, bf16[144,256]{1,0:T(8,128)(2,1)S(1)}, u32[]{:S(2)}, u32[]{:S(2)}) collective-permute-start(bf16[144,256]{1,0:T(8,128)(2,1)S(1)} %get-tuple-element.44), channel_id=1, source_target_pairs={{0,8},{4,12},{8,0},{12,4},{1,9},{5,13},{9,1},{13,5},{2,10},{6,14},... | collective-permute-start | bytes 221192 | tf_op jit(solution)/shard_map/ppermute | solution.py:17
  22.4 0.2 collective-permute-start.10
  22.6 1.5 %collective-permute-start.19 = (bf16[240,256]{1,0:T(8,128)(2,1)S(1)}, bf16[240,256]{1,0:T(8,128)(2,1)S(1)}, u32[]{:S(2)}, u32[]{:S(2)}) collective-permute-start(bf16[240,256]{1,0:T(8,128)(2,1)S(1)} %get-tuple-element.59), channel_id=1, source_target_pairs={{0,2},{1,3},{2,0},{3,1},{4,6},{5,7},{6,4},{7,5},{8,10},{9,11},{10,... | collective-permute-start | bytes 368648 | tf_op jit(solution)/shard_map/ppermute | solution.py:17
  24.1 0.4 collective-permute-done.8.refs_4_
  24.5 0.0 collective-permute-start.20
  24.6 0.5 %shard_map.54.refs_8_ = f32[40,128]{1,0:T(8,128)S(1)} custom-call(bf16[416,256]{1,0:T(8,128)(2,1)S(1)} %get-tuple-element.35.refs_3_.refs_0_, bf16[416,256]{1,0:T(8,128)(2,1)S(1)} %collective-permute-done.2.refs_2_.refs_0_.refs_1_, bf16[176,256]{1,0:T(8,128)(2,1)S(1)} %collective-permute-done.1.refs_1_.refs_2_, ...), custom_call_target="tpu_custom_call" | custom-call | flops 65536000 | bytes 872448 | tf_op jit(solution)/shard_map/pallas_call | solution.py:46
  25.1 2.4 %collective-permute-done.9.refs_5_ = bf16[144,256]{1,0:T(8,128)(2,1)S(1)} collective-permute-done((bf16[144,256]{1,0:T(8,128)(2,1)S(1)}, bf16[144,256]{1,0:T(8,128)(2,1)S(1)}, u32[]{:S(2)}, u32[]{:S(2)}) %collective-permute-start.9) | collective-permute-done | bytes 73760 | tf_op jit(solution)/shard_map/ppermute | solution.py:17
  27.5 0.9 %collective-permute-done.10.refs_6_ = bf16[144,256]{1,0:T(8,128)(2,1)S(1)} collective-permute-done((bf16[144,256]{1,0:T(8,128)(2,1)S(1)}, bf16[144,256]{1,0:T(8,128)(2,1)S(1)}, u32[]{:S(2)}, u32[]{:S(2)}) %collective-permute-start.10) | collective-permute-done | bytes 73760 | tf_op jit(solution)/shard_map/ppermute | solution.py:17
  28.4 0.0 collective-permute-done.11.refs_9_.refs_1_
  28.4 0.3 shard_map.56
  28.7 1.6 %collective-permute-start.12 = (f32[60,128]{1,0:T(8,128)S(1)}, f32[60,128]{1,0:T(8,128)S(1)}, u32[]{:S(2)}, u32[]{:S(2)}) collective-permute-start(f32[60,128]{1,0:T(8,128)S(1)} %get-tuple-element.50), channel_id=1, source_target_pairs={{0,12},{4,8},{8,4},{12,0},{1,13},{5,9},{9,5},{13,1},{2,14},{6,10},... | collective-permute-start | bytes 92168 | tf_op jit(solution)/shard_map/ppermute | solution.py:17
  30.3 0.8 %collective-permute-start.13 = (f32[60,128]{1,0:T(8,128)S(1)}, f32[60,128]{1,0:T(8,128)S(1)}, u32[]{:S(2)}, u32[]{:S(2)}) collective-permute-start(f32[60,128]{1,0:T(8,128)S(1)} %get-tuple-element.51), channel_id=1, source_target_pairs={{0,8},{4,12},{8,0},{12,4},{1,9},{5,13},{9,1},{13,5},{2,10},{6,14},... | collective-permute-start | bytes 92168 | tf_op jit(solution)/shard_map/ppermute | solution.py:17
  31.1 2.1 %collective-permute-start.14 = (f32[60,128]{1,0:T(8,128)S(1)}, f32[60,128]{1,0:T(8,128)S(1)}, u32[]{:S(2)}, u32[]{:S(2)}) collective-permute-start(f32[60,128]{1,0:T(8,128)S(1)} %get-tuple-element.52), channel_id=1, source_target_pairs={{0,4},{4,0},{8,12},{12,8},{1,5},{5,1},{9,13},{13,9},{2,6},{6,2},{1... | collective-permute-start | bytes 92168 | tf_op jit(solution)/shard_map/ppermute | solution.py:17
  33.2 1.3 %collective-permute-done.12.refs_0_ = f32[60,128]{1,0:T(8,128)S(1)} collective-permute-done((f32[60,128]{1,0:T(8,128)S(1)}, f32[60,128]{1,0:T(8,128)S(1)}, u32[]{:S(2)}, u32[]{:S(2)}) %collective-permute-start.12) | collective-permute-done | bytes 30752 | tf_op jit(solution)/shard_map/ppermute | solution.py:17
  34.5 1.1 %collective-permute-done.13.refs_1_ = f32[60,128]{1,0:T(8,128)S(1)} collective-permute-done((f32[60,128]{1,0:T(8,128)S(1)}, f32[60,128]{1,0:T(8,128)S(1)}, u32[]{:S(2)}, u32[]{:S(2)}) %collective-permute-start.13) | collective-permute-done | bytes 30752 | tf_op jit(solution)/shard_map/ppermute | solution.py:17
  35.7 0.1 collective-permute-done.14.refs_2_
  35.7 0.2 shard_map.57
  35.9 0.1 collective-permute-start.15
  36.0 1.5 %collective-permute-start.16 = (f32[40,80]{1,0:T(8,128)S(1)}, f32[40,80]{1,0:T(8,128)S(1)}, u32[]{:S(2)}, u32[]{:S(2)}) collective-permute-start(f32[40,80]{1,0:T(8,128)S(1)} %get-tuple-element.55), channel_id=1, source_target_pairs={{0,2},{1,3},{2,0},{3,1},{4,6},{5,7},{6,4},{7,5},{8,10},{9,11},{10,... | collective-permute-start | bytes 38408 | tf_op jit(solution)/shard_map/ppermute | solution.py:17
  37.5 0.3 collective-permute-start.17
  37.8 1.5 %collective-permute-done.15.refs_0_ = f32[40,80]{1,0:T(8,128)S(1)} collective-permute-done((f32[40,80]{1,0:T(8,128)S(1)}, f32[40,80]{1,0:T(8,128)S(1)}, u32[]{:S(2)}, u32[]{:S(2)}) %collective-permute-start.15) | collective-permute-done | bytes 12832 | tf_op jit(solution)/shard_map/ppermute | solution.py:17
  39.3 0.5 %collective-permute-done.16.refs_1_ = f32[40,80]{1,0:T(8,128)S(1)} collective-permute-done((f32[40,80]{1,0:T(8,128)S(1)}, f32[40,80]{1,0:T(8,128)S(1)}, u32[]{:S(2)}, u32[]{:S(2)}) %collective-permute-start.16) | collective-permute-done | bytes 12832 | tf_op jit(solution)/shard_map/ppermute | solution.py:17
  39.8 0.0 collective-permute-done.17.refs_2_
  39.8 1.6 %collective-permute-start.18 = (f32[40,80]{1,0:T(8,128)S(1)}, f32[40,80]{1,0:T(8,128)S(1)}, u32[]{:S(2)}, u32[]{:S(2)}) collective-permute-start(f32[40,80]{1,0:T(8,128)S(1)} %shard_map.58), channel_id=1, source_target_pairs={{0,16},{16,0},{1,17},{17,1},{2,18},{18,2},{3,19},{19,3},{4,20},{20... | collective-permute-start | bytes 38408 | tf_op jit(solution)/shard_map/ppermute | solution.py:17
  41.4 0.0 collective-permute-done.19.refs_2_
  41.4 0.0 collective-permute-done.20.refs_3_
  41.4 0.9 %shard_map.59 = bf16[12,20,1024]{2,1,0:T(8,128)(2,1)} custom-call(bf16[240,256]{1,0:T(8,128)(2,1)S(1)} %get-tuple-element.58.refs_0_, bf16[240,256]{1,0:T(8,128)(2,1)S(1)} %collective-permute-done.11.refs_9_.refs_1_, bf16[240,256]{1,0:T(8,128)(2,1)S(1)} %collective-permute-done.19.refs_2_, bf16[240,256]{1,0:T(8,128)(2,1)S(1)} %collective-permute-done.20.refs_3_), custom_call_target="tpu_custom_call" | custom-call | bytes 983040 | tf_op jit(solution)/shard_map/pallas_call | solution.py:46
  42.3 1.4 %collective-permute-done.18 = f32[40,80]{1,0:T(8,128)S(1)} collective-permute-done((f32[40,80]{1,0:T(8,128)S(1)}, f32[40,80]{1,0:T(8,128)S(1)}, u32[]{:S(2)}, u32[]{:S(2)}) %collective-permute-start.18) | collective-permute-done | bytes 12832 | tf_op jit(solution)/shard_map/ppermute | solution.py:17
  43.7 0.6 %fusion = (f32[20,80]{1,0:T(8,128)}, f32[20,80]{1,0:T(8,128)}) fusion(f32[40,80]{1,0:T(8,128)S(1)} %add.3), kind=kLoop, calls=%fused_computation | loop fusion | bytes 25600 | tf_op jit(solution)/shard_map/slice | solution.py:299
  (5 shorter events, 0.1 us)
Async XLA Ops:
  0.6 1.2 %copy-start = (bf16[20,20,1024]{2,1,0:T(8,128)(2,1)S(1)}, bf16[20,20,1024]{2,1,0:T(8,128)(2,1)}, u32[]{:S(2)}) copy-start(bf16[20,20,1024]{2,1,0:T(8,128)(2,1)} %slab_ref.3) | copy-start | bytes 2457604
  0.6 1.2 %copy-start.1 = (bf16[20,48]{1,0:T(8,128)(2,1)S(1)}, bf16[20,48]{1,0:T(8,128)(2,1)}, u32[]{:S(2)}) copy-start(bf16[20,48]{1,0:T(8,128)(2,1)} %refs_0_.1) | copy-start | bytes 5764
  2.0 3.2 %collective-permute-start.2 = (bf16[416,256]{1,0:T(8,128)(2,1)S(1)}, bf16[416,256]{1,0:T(8,128)(2,1)S(1)}, u32[]{:S(2)}, u32[]{:S(2)}) collective-permute-start(bf16[416,256]{1,0:T(8,128)(2,1)S(1)} %get-tuple-element.34), channel_id=1, source_target_pairs={{0,1},{1,0},{2,3},{3,2},{4,5},{5,4},{6,7},{7,6},{8,9},{9,8},{10,11... | collective-permute-start | bytes 638984 | tf_op jit(solution)/shard_map/ppermute | solution.py:17
  2.5 5.6 %collective-permute-start = (bf16[176,256]{1,0:T(8,128)(2,1)S(1)}, bf16[176,256]{1,0:T(8,128)(2,1)S(1)}, u32[]{:S(2)}, u32[]{:S(2)}) collective-permute-start(bf16[176,256]{1,0:T(8,128)(2,1)S(1)} %get-tuple-element.32), channel_id=1, source_target_pairs={{0,3},{1,2},{2,1},{3,0},{4,7},{5,6},{6,5},{7,4},{8,11},{9,10},{10,... | collective-permute-start | bytes 270344 | tf_op jit(solution)/shard_map/ppermute | solution.py:17
  5.1 5.6 %collective-permute-start.1 = (bf16[176,256]{1,0:T(8,128)(2,1)S(1)}, bf16[176,256]{1,0:T(8,128)(2,1)S(1)}, u32[]{:S(2)}, u32[]{:S(2)}) collective-permute-start(bf16[176,256]{1,0:T(8,128)(2,1)S(1)} %get-tuple-element.33), channel_id=1, source_target_pairs={{0,2},{1,3},{2,0},{3,1},{4,6},{5,7},{6,4},{7,5},{8,10},{9,11},{10,... | collective-permute-start | bytes 270344 | tf_op jit(solution)/shard_map/ppermute | solution.py:17
  5.2 12.3 %collective-permute-start.6 = (bf16[240,256]{1,0:T(8,128)(2,1)S(1)}, bf16[240,256]{1,0:T(8,128)(2,1)S(1)}, u32[]{:S(2)}, u32[]{:S(2)}) collective-permute-start(bf16[240,256]{1,0:T(8,128)(2,1)S(1)} %get-tuple-element.40), channel_id=1, source_target_pairs={{0,3},{1,2},{2,1},{3,0},{4,7},{5,6},{6,5},{7,4},{8,11},{9,10},{10,... | collective-permute-start | bytes 368648 | tf_op jit(solution)/shard_map/ppermute | solution.py:17
  6.7 10.8 %collective-permute-start.7 = (bf16[240,256]{1,0:T(8,128)(2,1)S(1)}, bf16[240,256]{1,0:T(8,128)(2,1)S(1)}, u32[]{:S(2)}, u32[]{:S(2)}) collective-permute-start(bf16[240,256]{1,0:T(8,128)(2,1)S(1)} %get-tuple-element.41), channel_id=1, source_target_pairs={{0,2},{1,3},{2,0},{3,1},{4,6},{5,7},{6,4},{7,5},{8,10},{9,11},{10,... | collective-permute-start | bytes 368648 | tf_op jit(solution)/shard_map/ppermute | solution.py:17
  11.2 6.3 %collective-permute-start.3 = (bf16[96,256]{1,0:T(8,128)(2,1)S(1)}, bf16[96,256]{1,0:T(8,128)(2,1)S(1)}, u32[]{:S(2)}, u32[]{:S(2)}) collective-permute-start(bf16[96,256]{1,0:T(8,128)(2,1)S(1)} %get-tuple-element.36), channel_id=1, source_target_pairs={{0,12},{4,8},{8,4},{12,0},{1,13},{5,9},{9,5},{13,1},{2,14},{6,10},... | collective-permute-start | bytes 147464 | tf_op jit(solution)/shard_map/ppermute | solution.py:17
  15.1 6.5 %collective-permute-start.4 = (bf16[96,256]{1,0:T(8,128)(2,1)S(1)}, bf16[96,256]{1,0:T(8,128)(2,1)S(1)}, u32[]{:S(2)}, u32[]{:S(2)}) collective-permute-start(bf16[96,256]{1,0:T(8,128)(2,1)S(1)} %get-tuple-element.37), channel_id=1, source_target_pairs={{0,8},{4,12},{8,0},{12,4},{1,9},{5,13},{9,1},{13,5},{2,10},{6,14},... | collective-permute-start | bytes 147464 | tf_op jit(solution)/shard_map/ppermute | solution.py:17
  15.1 6.5 %collective-permute-start.5 = (bf16[96,256]{1,0:T(8,128)(2,1)S(1)}, bf16[96,256]{1,0:T(8,128)(2,1)S(1)}, u32[]{:S(2)}, u32[]{:S(2)}) collective-permute-start(bf16[96,256]{1,0:T(8,128)(2,1)S(1)} %get-tuple-element.38), channel_id=1, source_target_pairs={{0,4},{4,0},{8,12},{12,8},{1,5},{5,1},{9,13},{13,9},{2,6},{6,2},{1... | collective-permute-start | bytes 147464 | tf_op jit(solution)/shard_map/ppermute | solution.py:17
  18.0 6.6 %collective-permute-start.8 = (bf16[144,256]{1,0:T(8,128)(2,1)S(1)}, bf16[144,256]{1,0:T(8,128)(2,1)S(1)}, u32[]{:S(2)}, u32[]{:S(2)}) collective-permute-start(bf16[144,256]{1,0:T(8,128)(2,1)S(1)} %get-tuple-element.43), channel_id=1, source_target_pairs={{0,12},{4,8},{8,4},{12,0},{1,13},{5,9},{9,5},{13,1},{2,14},{6,10},... | collective-permute-start | bytes 221192 | tf_op jit(solution)/shard_map/ppermute | solution.py:17
  21.7 6.6 %collective-permute-start.11 = (bf16[240,256]{1,0:T(8,128)(2,1)S(1)}, bf16[240,256]{1,0:T(8,128)(2,1)S(1)}, u32[]{:S(2)}, u32[]{:S(2)}) collective-permute-start(bf16[240,256]{1,0:T(8,128)(2,1)S(1)} %get-tuple-element.49), channel_id=1, source_target_pairs={{0,1},{1,0},{2,3},{3,2},{4,5},{5,4},{6,7},{7,6},{8,9},{9,8},{10,11... | collective-permute-start | bytes 368648 | tf_op jit(solution)/shard_map/ppermute | solution.py:17
  21.8 5.7 %collective-permute-start.9 = (bf16[144,256]{1,0:T(8,128)(2,1)S(1)}, bf16[144,256]{1,0:T(8,128)(2,1)S(1)}, u32[]{:S(2)}, u32[]{:S(2)}) collective-permute-start(bf16[144,256]{1,0:T(8,128)(2,1)S(1)} %get-tuple-element.44), channel_id=1, source_target_pairs={{0,8},{4,12},{8,0},{12,4},{1,9},{5,13},{9,1},{13,5},{2,10},{6,14},... | collective-permute-start | bytes 221192 | tf_op jit(solution)/shard_map/ppermute | solution.py:17
  22.4 5.9 %collective-permute-start.10 = (bf16[144,256]{1,0:T(8,128)(2,1)S(1)}, bf16[144,256]{1,0:T(8,128)(2,1)S(1)}, u32[]{:S(2)}, u32[]{:S(2)}) collective-permute-start(bf16[144,256]{1,0:T(8,128)(2,1)S(1)} %get-tuple-element.45), channel_id=1, source_target_pairs={{0,4},{4,0},{8,12},{12,8},{1,5},{5,1},{9,13},{13,9},{2,6},{6,2},{1... | collective-permute-start | bytes 221192 | tf_op jit(solution)/shard_map/ppermute | solution.py:17
  22.6 18.8 %collective-permute-start.19 = (bf16[240,256]{1,0:T(8,128)(2,1)S(1)}, bf16[240,256]{1,0:T(8,128)(2,1)S(1)}, u32[]{:S(2)}, u32[]{:S(2)}) collective-permute-start(bf16[240,256]{1,0:T(8,128)(2,1)S(1)} %get-tuple-element.59), channel_id=1, source_target_pairs={{0,2},{1,3},{2,0},{3,1},{4,6},{5,7},{6,4},{7,5},{8,10},{9,11},{10,... | collective-permute-start | bytes 368648 | tf_op jit(solution)/shard_map/ppermute | solution.py:17
  24.5 16.8 %collective-permute-start.20 = (bf16[240,256]{1,0:T(8,128)(2,1)S(1)}, bf16[240,256]{1,0:T(8,128)(2,1)S(1)}, u32[]{:S(2)}, u32[]{:S(2)}) collective-permute-start(bf16[240,256]{1,0:T(8,128)(2,1)S(1)} %get-tuple-element.60), channel_id=1, source_target_pairs={{0,3},{1,2},{2,1},{3,0},{4,7},{5,6},{6,5},{7,4},{8,11},{9,10},{10,... | collective-permute-start | bytes 368648 | tf_op jit(solution)/shard_map/ppermute | solution.py:17
  28.7 5.8 %collective-permute-start.12 = (f32[60,128]{1,0:T(8,128)S(1)}, f32[60,128]{1,0:T(8,128)S(1)}, u32[]{:S(2)}, u32[]{:S(2)}) collective-permute-start(f32[60,128]{1,0:T(8,128)S(1)} %get-tuple-element.50), channel_id=1, source_target_pairs={{0,12},{4,8},{8,4},{12,0},{1,13},{5,9},{9,5},{13,1},{2,14},{6,10},... | collective-permute-start | bytes 92168 | tf_op jit(solution)/shard_map/ppermute | solution.py:17
  30.3 5.3 %collective-permute-start.13 = (f32[60,128]{1,0:T(8,128)S(1)}, f32[60,128]{1,0:T(8,128)S(1)}, u32[]{:S(2)}, u32[]{:S(2)}) collective-permute-start(f32[60,128]{1,0:T(8,128)S(1)} %get-tuple-element.51), channel_id=1, source_target_pairs={{0,8},{4,12},{8,0},{12,4},{1,9},{5,13},{9,1},{13,5},{2,10},{6,14},... | collective-permute-start | bytes 92168 | tf_op jit(solution)/shard_map/ppermute | solution.py:17
  31.1 4.6 %collective-permute-start.14 = (f32[60,128]{1,0:T(8,128)S(1)}, f32[60,128]{1,0:T(8,128)S(1)}, u32[]{:S(2)}, u32[]{:S(2)}) collective-permute-start(f32[60,128]{1,0:T(8,128)S(1)} %get-tuple-element.52), channel_id=1, source_target_pairs={{0,4},{4,0},{8,12},{12,8},{1,5},{5,1},{9,13},{13,9},{2,6},{6,2},{1... | collective-permute-start | bytes 92168 | tf_op jit(solution)/shard_map/ppermute | solution.py:17
  35.9 3.4 %collective-permute-start.15 = (f32[40,80]{1,0:T(8,128)S(1)}, f32[40,80]{1,0:T(8,128)S(1)}, u32[]{:S(2)}, u32[]{:S(2)}) collective-permute-start(f32[40,80]{1,0:T(8,128)S(1)} %get-tuple-element.54), channel_id=1, source_target_pairs={{0,3},{1,2},{2,1},{3,0},{4,7},{5,6},{6,5},{7,4},{8,11},{9,10},{10,... | collective-permute-start | bytes 38408 | tf_op jit(solution)/shard_map/ppermute | solution.py:17
  36.0 3.8 %collective-permute-start.16 = (f32[40,80]{1,0:T(8,128)S(1)}, f32[40,80]{1,0:T(8,128)S(1)}, u32[]{:S(2)}, u32[]{:S(2)}) collective-permute-start(f32[40,80]{1,0:T(8,128)S(1)} %get-tuple-element.55), channel_id=1, source_target_pairs={{0,2},{1,3},{2,0},{3,1},{4,6},{5,7},{6,4},{7,5},{8,10},{9,11},{10,... | collective-permute-start | bytes 38408 | tf_op jit(solution)/shard_map/ppermute | solution.py:17
  37.5 2.3 %collective-permute-start.17 = (f32[40,80]{1,0:T(8,128)S(1)}, f32[40,80]{1,0:T(8,128)S(1)}, u32[]{:S(2)}, u32[]{:S(2)}) collective-permute-start(f32[40,80]{1,0:T(8,128)S(1)} %get-tuple-element.56), channel_id=1, source_target_pairs={{0,1},{1,0},{2,3},{3,2},{4,5},{5,4},{6,7},{7,6},{8,9},{9,8},{10,11... | collective-permute-start | bytes 38408 | tf_op jit(solution)/shard_map/ppermute | solution.py:17
  39.8 3.8 %collective-permute-start.18 = (f32[40,80]{1,0:T(8,128)S(1)}, f32[40,80]{1,0:T(8,128)S(1)}, u32[]{:S(2)}, u32[]{:S(2)}) collective-permute-start(f32[40,80]{1,0:T(8,128)S(1)} %shard_map.58), channel_id=1, source_target_pairs={{0,16},{16,0},{1,17},{17,1},{2,18},{18,2},{3,19},{19,3},{4,20},{20... | collective-permute-start | bytes 38408 | tf_op jit(solution)/shard_map/ppermute | solution.py:17

commit v11 on v5

--- a/solution.py
+++ b/solution.py
@@ -72,7 +72,7 @@
         deep = rows // groups
         wide = refs[0][...].astype(f32)
         wide = jnp.concatenate([wide[g * deep : (g + 1) * deep] for g in range(groups)], axis=1)
-        head = [jnp.pad(wide, ((0, -deep % 8), (0, width - groups * ranks))).astype(bf16)]
+        head = [jnp.pad(wide, ((0, -deep % 16), (0, width - groups * ranks))).astype(bf16)]
     for (k, begin, count), out in zip(spans, outs):
         at = pl.ds(pl.multiple_of((me ^ k) * width, width), width)
         out[...] = jnp.concatenate(head + [slab_ref[l, :, at] for l in range(begin, begin + count)], axis=0)
@@ -212,7 +212,7 @@
     views_all, lights_all = views * rows, parts * lights
     size = ranks // parts
     groups = max(g for g in range(1, width // ranks + 1) if rows % g == 0)
-    head = -(-(rows // groups) // 8) * 8
+    head = -(-(rows // groups) // 16) * 16
 
     one = lights * 2 // 5 // 4 * 4
     counts, half = [one, lights - one], views // 2
@@ -257,7 +257,7 @@
             outs,
             [
                 pltpu.VMEM((views, tall[c], width), bf16),
-                pltpu.VMEM((width // 128, count * ranks, 128), f32),
+                pltpu.VMEM((width // 128, -(-count // 8) * 8 * ranks, 128), f32),
             ],
             2 * views_all * count * width * ranks,
             whole[c][::-1] + near[::-1] + carried,
@@ -309,7 +309,8 @@
         [returned[2], returned[3]],
     )
     steps = [(t, m) for t in range(min(2, texels) - 1, -1, -1) for m in range(half - 1, -1, -1)]
-    total = summed([dealt[0]] + [swap(dealt[m], ("texel", "view"), t * views + 2 * m) for t, m in steps[:-1]])
+    came = [swap(dealt[m], ("texel", "view"), t * views + 2 * m) for t, m in steps[:-1]]
+    total = summed([dealt[0]] + came[::-1])
     core = call(
         functools.partial(place_kernel, counts),
         sds((ranks // views, lights, columns), bf16),

time: 44 us -> 44.1 us (level)
  no operation moved by 1% of the time
where the time goes in v11:
time: 44.1 us; the launch traced here: 44 us
  starting transfers between devices  24.5 us (56%)
  waiting for transfers between devices  13.7 us (31%)
  Pallas kernels  3.22 us (7%)
  local copies, waits for them, and re-layouts  1.79 us (4%)
  between operations  0.76 us (2%)
    ppermute x21, starting transfers between devices, swap(): lax.ppermute(value, axis, [(i, i ^ step) for i in range(lax.axis_size(axi...  24.5 us
    ppermute x21, waiting for transfers between devices, swap(): lax.ppermute(value, axis, [(i, i ^ step) for i in range(lax.axis_size(axi...  13.7 us
    pallas_call x12, Pallas kernels, call(): pl.pallas_call(kernel, out_shape=out_shape, in_specs=[VMEM] * len(args) +...  3.22 us
    unnamed x4, local copies, waits for them, and re-layouts  1.18 us
  transfers between devices with their start and end apart: 21, of which 12 were waited for; matrix products, arithmetic and copies ran while one was open for 0% of the time, Pallas kernels for 7%

profile of v11, /device:TPU:0, one launch (start us, length us, event | category | flops | bytes accessed | tf_op | source)
XLA Modules:
  0.0 44.0 jit_solution(6957141776720537894)
XLA Ops:
  0.6 0.0 copy-start
  0.6 0.0 copy-start.1
  0.7 1.2 %copy-done = bf16[20,20,1024]{2,1,0:T(8,128)(2,1)S(1)} copy-done((bf16[20,20,1024]{2,1,0:T(8,128)(2,1)S(1)}, bf16[20,20,1024]{2,1,0:T(8,128)(2,1)}, u32[]{:S(2)}) %copy-start) | copy-done | bytes 819224
  1.8 0.0 copy-done.1
  1.8 0.1 shard_map.50
  2.0 0.5 %collective-permute-start.2 = (bf16[416,256]{1,0:T(8,128)(2,1)S(1)}, bf16[416,256]{1,0:T(8,128)(2,1)S(1)}, u32[]{:S(2)}, u32[]{:S(2)}) collective-permute-start(bf16[416,256]{1,0:T(8,128)(2,1)S(1)} %get-tuple-element.34), channel_id=1, source_target_pairs={{0,1},{1,0},{2,3},{3,2},{4,5},{5,4},{6,7},{7,6},{8,9},{9,8},{10,11... | collective-permute-start | bytes 638984 | tf_op jit(solution)/shard_map/ppermute | solution.py:17
  2.5 2.6 %collective-permute-start = (bf16[176,256]{1,0:T(8,128)(2,1)S(1)}, bf16[176,256]{1,0:T(8,128)(2,1)S(1)}, u32[]{:S(2)}, u32[]{:S(2)}) collective-permute-start(bf16[176,256]{1,0:T(8,128)(2,1)S(1)} %get-tuple-element.32), channel_id=1, source_target_pairs={{0,3},{1,2},{2,1},{3,0},{4,7},{5,6},{6,5},{7,4},{8,11},{9,10},{10,... | collective-permute-start | bytes 270344 | tf_op jit(solution)/shard_map/ppermute | solution.py:17
  5.1 0.0 collective-permute-start.1
  5.2 2.9 %collective-permute-done.refs_0_.refs_3_ = bf16[176,256]{1,0:T(8,128)(2,1)S(1)} collective-permute-done((bf16[176,256]{1,0:T(8,128)(2,1)S(1)}, bf16[176,256]{1,0:T(8,128)(2,1)S(1)}, u32[]{:S(2)}, u32[]{:S(2)}) %collective-permute-start) | collective-permute-done | bytes 90144 | tf_op jit(solution)/shard_map/ppermute | solution.py:17
  8.1 2.0 %collective-permute-start.6 = (bf16[240,256]{1,0:T(8,128)(2,1)S(1)}, bf16[240,256]{1,0:T(8,128)(2,1)S(1)}, u32[]{:S(2)}, u32[]{:S(2)}) collective-permute-start(bf16[240,256]{1,0:T(8,128)(2,1)S(1)} %get-tuple-element.40), channel_id=1, source_target_pairs={{0,3},{1,2},{2,1},{3,0},{4,7},{5,6},{6,5},{7,4},{8,11},{9,10},{10,... | collective-permute-start | bytes 368648 | tf_op jit(solution)/shard_map/ppermute | solution.py:17
  10.1 0.0 collective-permute-start.7
  10.1 0.1 collective-permute-done.1.refs_1_.refs_2_
  10.2 0.0 collective-permute-done.2.refs_2_.refs_1_
  10.2 0.5 %shard_map.51 = (bf16[96,256]{1,0:T(8,128)(2,1)S(1)}, bf16[96,256]{1,0:T(8,128)(2,1)S(1)}, bf16[96,256]{1,0:T(8,128)(2,1)S(1)}, bf16[96,256]{1,0:T(8,128)(2,1)S(...) custom-call(bf16[176,256]{1,0:T(8,128)(2,1)S(1)} %collective-permute-done.refs_0_.refs_3_, ...), custom_call_target="tpu_custom_call" | custom-call | flops 15728640 | bytes 1007104 | tf_op jit(solution)/shard_map/pallas_call | solution.py:38
  10.7 4.1 %collective-permute-start.3 = (bf16[96,256]{1,0:T(8,128)(2,1)S(1)}, bf16[96,256]{1,0:T(8,128)(2,1)S(1)}, u32[]{:S(2)}, u32[]{:S(2)}) collective-permute-start(bf16[96,256]{1,0:T(8,128)(2,1)S(1)} %get-tuple-element.36), channel_id=1, source_target_pairs={{0,12},{4,8},{8,4},{12,0},{1,13},{5,9},{9,5},{13,1},{2,14},{6,10},... | collective-permute-start | bytes 147464 | tf_op jit(solution)/shard_map/ppermute | solution.py:17
  14.8 0.0 collective-permute-start.4
  14.8 0.6 %collective-permute-start.5 = (bf16[96,256]{1,0:T(8,128)(2,1)S(1)}, bf16[96,256]{1,0:T(8,128)(2,1)S(1)}, u32[]{:S(2)}, u32[]{:S(2)}) collective-permute-start(bf16[96,256]{1,0:T(8,128)(2,1)S(1)} %get-tuple-element.38), channel_id=1, source_target_pairs={{0,4},{4,0},{8,12},{12,8},{1,5},{5,1},{9,13},{13,9},{2,6},{6,2},{1... | collective-permute-start | bytes 147464 | tf_op jit(solution)/shard_map/ppermute | solution.py:17
  15.4 0.0 collective-permute-done.6.refs_0_.refs_5_
  15.4 1.2 %collective-permute-done.7.refs_1_.refs_4_ = bf16[240,256]{1,0:T(8,128)(2,1)S(1)} collective-permute-done((bf16[240,256]{1,0:T(8,128)(2,1)S(1)}, bf16[240,256]{1,0:T(8,128)(2,1)S(1)}, u32[]{:S(2)}, u32[]{:S(2)}) %collective-permute-start.7) | collective-permute-done | bytes 122912 | tf_op jit(solution)/shard_map/ppermute | solution.py:17
  16.6 0.5 %collective-permute-done.3.refs_5_.refs_2_.refs_0_ = bf16[96,256]{1,0:T(8,128)(2,1)S(1)} collective-permute-done((bf16[96,256]{1,0:T(8,128)(2,1)S(1)}, bf16[96,256]{1,0:T(8,128)(2,1)S(1)}, u32[]{:S(2)}, u32[]{:S(2)}) %collective-permute-start.3) | collective-permute-done | bytes 49184 | tf_op jit(solution)/shard_map/ppermute | solution.py:17
  17.1 0.5 %shard_map.53 = (bf16[144,256]{1,0:T(8,128)(2,1)S(1)}, bf16[144,256]{1,0:T(8,128)(2,1)S(1)}, bf16[144,256]{1,0:T(8,128)(2,1)S(1)}, bf16[144,256]{1,0:T(8,128)(2,1)S(1)}, bf16[4,144,256]{2,1,0:T(8,128)(2,1)S(1)}) custom-call(bf16[240,256]{1,0:T(8,128)(2,1)S(1)} %collective-permute-done.6.refs_0_.refs_5_, ...), custom_call_target="tpu_custom_call" | custom-call | flops 23592960 | bytes 1269248 | tf_op jit(solution)/shard_map/pallas_call | solution.py:38
  17.6 4.0 %collective-permute-start.8 = (bf16[144,256]{1,0:T(8,128)(2,1)S(1)}, bf16[144,256]{1,0:T(8,128)(2,1)S(1)}, u32[]{:S(2)}, u32[]{:S(2)}) collective-permute-start(bf16[144,256]{1,0:T(8,128)(2,1)S(1)} %get-tuple-element.43), channel_id=1, source_target_pairs={{0,12},{4,8},{8,4},{12,0},{1,13},{5,9},{9,5},{13,1},{2,14},{6,10},... | collective-permute-start | bytes 221192 | tf_op jit(solution)/shard_map/ppermute | solution.py:17
  21.6 0.0 collective-permute-done.4.refs_3_.refs_1_
  21.6 0.0 collective-permute-done.5.refs_4_.refs_2_
  21.6 0.1 collective-permute-start.11
  21.7 0.3 collective-permute-start.9
  22.0 0.5 %collective-permute-start.10 = (bf16[144,256]{1,0:T(8,128)(2,1)S(1)}, bf16[144,256]{1,0:T(8,128)(2,1)S(1)}, u32[]{:S(2)}, u32[]{:S(2)}) collective-permute-start(bf16[144,256]{1,0:T(8,128)(2,1)S(1)} %get-tuple-element.45), channel_id=1, source_target_pairs={{0,4},{4,0},{8,12},{12,8},{1,5},{5,1},{9,13},{13,9},{2,6},{6,2},{1... | collective-permute-start | bytes 221192 | tf_op jit(solution)/shard_map/ppermute | solution.py:17
  22.5 1.6 %collective-permute-start.16 = (bf16[240,256]{1,0:T(8,128)(2,1)S(1)}, bf16[240,256]{1,0:T(8,128)(2,1)S(1)}, u32[]{:S(2)}, u32[]{:S(2)}) collective-permute-start(bf16[240,256]{1,0:T(8,128)(2,1)S(1)} %get-tuple-element.56), channel_id=1, source_target_pairs={{0,2},{1,3},{2,0},{3,1},{4,6},{5,7},{6,4},{7,5},{8,10},{9,11},{10,... | collective-permute-start | bytes 368648 | tf_op jit(solution)/shard_map/ppermute | solution.py:17
  24.1 0.2 collective-permute-done.8.refs_4_
  24.3 0.0 collective-permute-start.17
  24.3 0.6 %shard_map.54.refs_8_ = f32[2,80,120]{2,1,0:T(8,128)S(1)} custom-call(bf16[416,256]{1,0:T(8,128)(2,1)S(1)} %get-tuple-element.35.refs_3_.refs_0_, bf16[416,256]{1,0:T(8,128)(2,1)S(1)} %collective-permute-done.2.refs_2_.refs_1_, bf16[176,256]{1,0:T(8,128)(2,1)S(1)} %collective-permute-done.1.refs_1_.refs_2_, ...), custom_call_target="tpu_custom_call" | custom-call | flops 65536000 | bytes 928768 | tf_op jit(solution)/shard_map/pallas_call | solution.py:38
  24.9 2.5 %collective-permute-done.9.refs_5_ = bf16[144,256]{1,0:T(8,128)(2,1)S(1)} collective-permute-done((bf16[144,256]{1,0:T(8,128)(2,1)S(1)}, bf16[144,256]{1,0:T(8,128)(2,1)S(1)}, u32[]{:S(2)}, u32[]{:S(2)}) %collective-permute-start.9) | collective-permute-done | bytes 73760 | tf_op jit(solution)/shard_map/ppermute | solution.py:17
  27.4 0.6 %collective-permute-done.10.refs_6_ = bf16[144,256]{1,0:T(8,128)(2,1)S(1)} collective-permute-done((bf16[144,256]{1,0:T(8,128)(2,1)S(1)}, bf16[144,256]{1,0:T(8,128)(2,1)S(1)}, u32[]{:S(2)}, u32[]{:S(2)}) %collective-permute-start.10) | collective-permute-done | bytes 73760 | tf_op jit(solution)/shard_map/ppermute | solution.py:17
  28.0 0.0 collective-permute-done.11.refs_9_.refs_1_
  28.0 0.3 shard_map.56
  28.3 0.1 collective-permute-start.12
  28.4 1.2 %collective-permute-done.12.came_ref = f32[80,120]{1,0:T(8,128)S(1)} collective-permute-done((f32[80,120]{1,0:T(8,128)S(1)}, f32[80,120]{1,0:T(8,128)S(1)}, u32[]{:S(2)}, u32[]{:S(2)}) %collective-permute-start.12) | collective-permute-done | bytes 38432 | tf_op jit(solution)/shard_map/ppermute | solution.py:17
  29.6 0.2 shard_map.57
  29.8 2.0 %collective-permute-start.13 = (f32[40,120]{1,0:T(8,128)S(1)}, f32[40,120]{1,0:T(8,128)S(1)}, u32[]{:S(2)}, u32[]{:S(2)}) collective-permute-start(f32[40,120]{1,0:T(8,128)S(1)} %get-tuple-element.52), channel_id=1, source_target_pairs={{0,12},{4,8},{8,4},{12,0},{1,13},{5,9},{9,5},{13,1},{2,14},{6,10},... | collective-permute-start | bytes 57608 | tf_op jit(solution)/shard_map/ppermute | solution.py:17
  31.8 0.6 %collective-permute-start.14 = (f32[40,120]{1,0:T(8,128)S(1)}, f32[40,120]{1,0:T(8,128)S(1)}, u32[]{:S(2)}, u32[]{:S(2)}) collective-permute-start(f32[40,120]{1,0:T(8,128)S(1)} %get-tuple-element.53), channel_id=1, source_target_pairs={{0,8},{4,12},{8,0},{12,4},{1,9},{5,13},{9,1},{13,5},{2,10},{6,14},... | collective-permute-start | bytes 57608 | tf_op jit(solution)/shard_map/ppermute | solution.py:17
  32.4 1.8 %collective-permute-start.15 = (f32[40,120]{1,0:T(8,128)S(1)}, f32[40,120]{1,0:T(8,128)S(1)}, u32[]{:S(2)}, u32[]{:S(2)}) collective-permute-start(f32[40,120]{1,0:T(8,128)S(1)} %get-tuple-element.54), channel_id=1, source_target_pairs={{0,4},{4,0},{8,12},{12,8},{1,5},{5,1},{9,13},{13,9},{2,6},{6,2},{1... | collective-permute-start | bytes 57608 | tf_op jit(solution)/shard_map/ppermute | solution.py:17
  34.2 1.3 %collective-permute-done.13.refs_0_ = f32[40,120]{1,0:T(8,128)S(1)} collective-permute-done((f32[40,120]{1,0:T(8,128)S(1)}, f32[40,120]{1,0:T(8,128)S(1)}, u32[]{:S(2)}, u32[]{:S(2)}) %collective-permute-start.13) | collective-permute-done | bytes 19232 | tf_op jit(solution)/shard_map/ppermute | solution.py:17
  35.5 1.0 %collective-permute-done.14.refs_1_ = f32[40,120]{1,0:T(8,128)S(1)} collective-permute-done((f32[40,120]{1,0:T(8,128)S(1)}, f32[40,120]{1,0:T(8,128)S(1)}, u32[]{:S(2)}, u32[]{:S(2)}) %collective-permute-start.14) | collective-permute-done | bytes 19232 | tf_op jit(solution)/shard_map/ppermute | solution.py:17
  36.5 0.0 collective-permute-done.15.refs_2_
  36.5 0.0 collective-permute-done.16.refs_1_.refs_2_
  36.5 0.0 collective-permute-done.17.refs_2_.refs_3_
  36.5 0.1 shard_map.59
  36.6 1.7 %collective-permute-start.20 = (f32[40,80]{1,0:T(8,128)S(1)}, f32[40,80]{1,0:T(8,128)S(1)}, u32[]{:S(2)}, u32[]{:S(2)}) collective-permute-start(f32[40,80]{1,0:T(8,128)S(1)} %get-tuple-element.58), channel_id=1, source_target_pairs={{0,2},{1,3},{2,0},{3,1},{16,18},{17,19},{18,16},{19,17},{4,6},{5,7... | collective-permute-start | bytes 38408 | tf_op jit(solution)/shard_map/ppermute | solution.py:17
  38.3 1.3 %collective-permute-start.18 = (f32[40,80]{1,0:T(8,128)S(1)}, f32[40,80]{1,0:T(8,128)S(1)}, u32[]{:S(2)}, u32[]{:S(2)}) collective-permute-start(f32[40,80]{1,0:T(8,128)S(1)} %get-tuple-element.58), channel_id=1, source_target_pairs={{0,18},{1,19},{2,16},{3,17},{16,2},{17,3},{18,0},{19,1},{4,22},{5,... | collective-permute-start | bytes 38408 | tf_op jit(solution)/shard_map/ppermute | solution.py:17
  39.6 0.5 %collective-permute-start.19 = (f32[40,80]{1,0:T(8,128)S(1)}, f32[40,80]{1,0:T(8,128)S(1)}, u32[]{:S(2)}, u32[]{:S(2)}) collective-permute-start(f32[40,80]{1,0:T(8,128)S(1)} %get-tuple-element.59), channel_id=1, source_target_pairs={{0,16},{1,17},{2,18},{3,19},{16,0},{17,1},{18,2},{19,3},{4,20},{5,... | collective-permute-start | bytes 38408 | tf_op jit(solution)/shard_map/ppermute | solution.py:17
  40.1 0.9 %shard_map.60 = bf16[12,20,1024]{2,1,0:T(8,128)(2,1)} custom-call(bf16[240,256]{1,0:T(8,128)(2,1)S(1)} %get-tuple-element.60.refs_0_, bf16[240,256]{1,0:T(8,128)(2,1)S(1)} %collective-permute-done.11.refs_9_.refs_1_, bf16[240,256]{1,0:T(8,128)(2,1)S(1)} %collective-permute-done.16.refs_1_.refs_2_, bf16[240,256]{1,0:T(8,128)(2,1)S(1)} %collective-permute-done.17.refs_2_.refs_3_), custom_call_target="tpu_custom_call" | custom-call | bytes 983040 | tf_op jit(solution)/shard_map/pallas_call | solution.py:38
  41.0 0.0 collective-permute-done.20
  41.0 1.9 %collective-permute-done.18 = f32[40,80]{1,0:T(8,128)S(1)} collective-permute-done((f32[40,80]{1,0:T(8,128)S(1)}, f32[40,80]{1,0:T(8,128)S(1)}, u32[]{:S(2)}, u32[]{:S(2)}) %collective-permute-start.18) | collective-permute-done | bytes 12832 | tf_op jit(solution)/shard_map/ppermute | solution.py:17
  42.9 0.4 collective-permute-done.19
  43.4 0.6 %fusion = (f32[20,80]{1,0:T(8,128)}, f32[20,80]{1,0:T(8,128)}) fusion(f32[40,80]{1,0:T(8,128)S(1)} %add_add_fusion), kind=kLoop, calls=%fused_computation.1 | loop fusion | bytes 25600 | tf_op jit(solution)/shard_map/slice | solution.py:321
  (5 shorter events, 0.1 us)
Async XLA Ops:
  0.6 1.2 %copy-start = (bf16[20,20,1024]{2,1,0:T(8,128)(2,1)S(1)}, bf16[20,20,1024]{2,1,0:T(8,128)(2,1)}, u32[]{:S(2)}) copy-start(bf16[20,20,1024]{2,1,0:T(8,128)(2,1)} %slab_ref.3) | copy-start | bytes 2457604
  0.6 1.2 %copy-start.1 = (bf16[20,48]{1,0:T(8,128)(2,1)S(1)}, bf16[20,48]{1,0:T(8,128)(2,1)}, u32[]{:S(2)}) copy-start(bf16[20,48]{1,0:T(8,128)(2,1)} %refs_0_.1) | copy-start | bytes 5764
  2.0 8.3 %collective-permute-start.2 = (bf16[416,256]{1,0:T(8,128)(2,1)S(1)}, bf16[416,256]{1,0:T(8,128)(2,1)S(1)}, u32[]{:S(2)}, u32[]{:S(2)}) collective-permute-start(bf16[416,256]{1,0:T(8,128)(2,1)S(1)} %get-tuple-element.34), channel_id=1, source_target_pairs={{0,1},{1,0},{2,3},{3,2},{4,5},{5,4},{6,7},{7,6},{8,9},{9,8},{10,11... | collective-permute-start | bytes 638984 | tf_op jit(solution)/shard_map/ppermute | solution.py:17
  2.5 5.6 %collective-permute-start = (bf16[176,256]{1,0:T(8,128)(2,1)S(1)}, bf16[176,256]{1,0:T(8,128)(2,1)S(1)}, u32[]{:S(2)}, u32[]{:S(2)}) collective-permute-start(bf16[176,256]{1,0:T(8,128)(2,1)S(1)} %get-tuple-element.32), channel_id=1, source_target_pairs={{0,3},{1,2},{2,1},{3,0},{4,7},{5,6},{6,5},{7,4},{8,11},{9,10},{10,... | collective-permute-start | bytes 270344 | tf_op jit(solution)/shard_map/ppermute | solution.py:17
  5.1 5.1 %collective-permute-start.1 = (bf16[176,256]{1,0:T(8,128)(2,1)S(1)}, bf16[176,256]{1,0:T(8,128)(2,1)S(1)}, u32[]{:S(2)}, u32[]{:S(2)}) collective-permute-start(bf16[176,256]{1,0:T(8,128)(2,1)S(1)} %get-tuple-element.33), channel_id=1, source_target_pairs={{0,2},{1,3},{2,0},{3,1},{4,6},{5,7},{6,4},{7,5},{8,10},{9,11},{10,... | collective-permute-start | bytes 270344 | tf_op jit(solution)/shard_map/ppermute | solution.py:17
  8.1 7.3 %collective-permute-start.6 = (bf16[240,256]{1,0:T(8,128)(2,1)S(1)}, bf16[240,256]{1,0:T(8,128)(2,1)S(1)}, u32[]{:S(2)}, u32[]{:S(2)}) collective-permute-start(bf16[240,256]{1,0:T(8,128)(2,1)S(1)} %get-tuple-element.40), channel_id=1, source_target_pairs={{0,3},{1,2},{2,1},{3,0},{4,7},{5,6},{6,5},{7,4},{8,11},{9,10},{10,... | collective-permute-start | bytes 368648 | tf_op jit(solution)/shard_map/ppermute | solution.py:17
  10.1 6.5 %collective-permute-start.7 = (bf16[240,256]{1,0:T(8,128)(2,1)S(1)}, bf16[240,256]{1,0:T(8,128)(2,1)S(1)}, u32[]{:S(2)}, u32[]{:S(2)}) collective-permute-start(bf16[240,256]{1,0:T(8,128)(2,1)S(1)} %get-tuple-element.41), channel_id=1, source_target_pairs={{0,2},{1,3},{2,0},{3,1},{4,6},{5,7},{6,4},{7,5},{8,10},{9,11},{10,... | collective-permute-start | bytes 368648 | tf_op jit(solution)/shard_map/ppermute | solution.py:17
  10.7 6.4 %collective-permute-start.3 = (bf16[96,256]{1,0:T(8,128)(2,1)S(1)}, bf16[96,256]{1,0:T(8,128)(2,1)S(1)}, u32[]{:S(2)}, u32[]{:S(2)}) collective-permute-start(bf16[96,256]{1,0:T(8,128)(2,1)S(1)} %get-tuple-element.36), channel_id=1, source_target_pairs={{0,12},{4,8},{8,4},{12,0},{1,13},{5,9},{9,5},{13,1},{2,14},{6,10},... | collective-permute-start | bytes 147464 | tf_op jit(solution)/shard_map/ppermute | solution.py:17
  14.8 6.8 %collective-permute-start.4 = (bf16[96,256]{1,0:T(8,128)(2,1)S(1)}, bf16[96,256]{1,0:T(8,128)(2,1)S(1)}, u32[]{:S(2)}, u32[]{:S(2)}) collective-permute-start(bf16[96,256]{1,0:T(8,128)(2,1)S(1)} %get-tuple-element.37), channel_id=1, source_target_pairs={{0,8},{4,12},{8,0},{12,4},{1,9},{5,13},{9,1},{13,5},{2,10},{6,14},... | collective-permute-start | bytes 147464 | tf_op jit(solution)/shard_map/ppermute | solution.py:17
  14.8 6.8 %collective-permute-start.5 = (bf16[96,256]{1,0:T(8,128)(2,1)S(1)}, bf16[96,256]{1,0:T(8,128)(2,1)S(1)}, u32[]{:S(2)}, u32[]{:S(2)}) collective-permute-start(bf16[96,256]{1,0:T(8,128)(2,1)S(1)} %get-tuple-element.38), channel_id=1, source_target_pairs={{0,4},{4,0},{8,12},{12,8},{1,5},{5,1},{9,13},{13,9},{2,6},{6,2},{1... | collective-permute-start | bytes 147464 | tf_op jit(solution)/shard_map/ppermute | solution.py:17
  17.6 6.7 %collective-permute-start.8 = (bf16[144,256]{1,0:T(8,128)(2,1)S(1)}, bf16[144,256]{1,0:T(8,128)(2,1)S(1)}, u32[]{:S(2)}, u32[]{:S(2)}) collective-permute-start(bf16[144,256]{1,0:T(8,128)(2,1)S(1)} %get-tuple-element.43), channel_id=1, source_target_pairs={{0,12},{4,8},{8,4},{12,0},{1,13},{5,9},{9,5},{13,1},{2,14},{6,10},... | collective-permute-start | bytes 221192 | tf_op jit(solution)/shard_map/ppermute | solution.py:17
  21.6 6.3 %collective-permute-start.11 = (bf16[240,256]{1,0:T(8,128)(2,1)S(1)}, bf16[240,256]{1,0:T(8,128)(2,1)S(1)}, u32[]{:S(2)}, u32[]{:S(2)}) collective-permute-start(bf16[240,256]{1,0:T(8,128)(2,1)S(1)} %get-tuple-element.49), channel_id=1, source_target_pairs={{0,1},{1,0},{2,3},{3,2},{4,5},{5,4},{6,7},{7,6},{8,9},{9,8},{10,11... | collective-permute-start | bytes 368648 | tf_op jit(solution)/shard_map/ppermute | solution.py:17
  21.7 5.7 %collective-permute-start.9 = (bf16[144,256]{1,0:T(8,128)(2,1)S(1)}, bf16[144,256]{1,0:T(8,128)(2,1)S(1)}, u32[]{:S(2)}, u32[]{:S(2)}) collective-permute-start(bf16[144,256]{1,0:T(8,128)(2,1)S(1)} %get-tuple-element.44), channel_id=1, source_target_pairs={{0,8},{4,12},{8,0},{12,4},{1,9},{5,13},{9,1},{13,5},{2,10},{6,14},... | collective-permute-start | bytes 221192 | tf_op jit(solution)/shard_map/ppermute | solution.py:17
  22.0 6.0 %collective-permute-start.10 = (bf16[144,256]{1,0:T(8,128)(2,1)S(1)}, bf16[144,256]{1,0:T(8,128)(2,1)S(1)}, u32[]{:S(2)}, u32[]{:S(2)}) collective-permute-start(bf16[144,256]{1,0:T(8,128)(2,1)S(1)} %get-tuple-element.45), channel_id=1, source_target_pairs={{0,4},{4,0},{8,12},{12,8},{1,5},{5,1},{9,13},{13,9},{2,6},{6,2},{1... | collective-permute-start | bytes 221192 | tf_op jit(solution)/shard_map/ppermute | solution.py:17
  22.5 14.0 %collective-permute-start.16 = (bf16[240,256]{1,0:T(8,128)(2,1)S(1)}, bf16[240,256]{1,0:T(8,128)(2,1)S(1)}, u32[]{:S(2)}, u32[]{:S(2)}) collective-permute-start(bf16[240,256]{1,0:T(8,128)(2,1)S(1)} %get-tuple-element.56), channel_id=1, source_target_pairs={{0,2},{1,3},{2,0},{3,1},{4,6},{5,7},{6,4},{7,5},{8,10},{9,11},{10,... | collective-permute-start | bytes 368648 | tf_op jit(solution)/shard_map/ppermute | solution.py:17
  24.3 12.2 %collective-permute-start.17 = (bf16[240,256]{1,0:T(8,128)(2,1)S(1)}, bf16[240,256]{1,0:T(8,128)(2,1)S(1)}, u32[]{:S(2)}, u32[]{:S(2)}) collective-permute-start(bf16[240,256]{1,0:T(8,128)(2,1)S(1)} %get-tuple-element.57), channel_id=1, source_target_pairs={{0,3},{1,2},{2,1},{3,0},{4,7},{5,6},{6,5},{7,4},{8,11},{9,10},{10,... | collective-permute-start | bytes 368648 | tf_op jit(solution)/shard_map/ppermute | solution.py:17
  28.3 1.3 %collective-permute-start.12 = (f32[80,120]{1,0:T(8,128)S(1)}, f32[80,120]{1,0:T(8,128)S(1)}, u32[]{:S(2)}, u32[]{:S(2)}) collective-permute-start(f32[80,120]{1,0:T(8,128)S(1)} %get-tuple-element.51), channel_id=1, source_target_pairs={{0,1},{1,0},{2,3},{3,2},{4,5},{5,4},{6,7},{7,6},{8,9},{9,8},{10,11... | collective-permute-start | bytes 115208 | tf_op jit(solution)/shard_map/ppermute | solution.py:17
  29.8 5.7 %collective-permute-start.13 = (f32[40,120]{1,0:T(8,128)S(1)}, f32[40,120]{1,0:T(8,128)S(1)}, u32[]{:S(2)}, u32[]{:S(2)}) collective-permute-start(f32[40,120]{1,0:T(8,128)S(1)} %get-tuple-element.52), channel_id=1, source_target_pairs={{0,12},{4,8},{8,4},{12,0},{1,13},{5,9},{9,5},{13,1},{2,14},{6,10},... | collective-permute-start | bytes 57608 | tf_op jit(solution)/shard_map/ppermute | solution.py:17
  31.8 4.7 %collective-permute-start.14 = (f32[40,120]{1,0:T(8,128)S(1)}, f32[40,120]{1,0:T(8,128)S(1)}, u32[]{:S(2)}, u32[]{:S(2)}) collective-permute-start(f32[40,120]{1,0:T(8,128)S(1)} %get-tuple-element.53), channel_id=1, source_target_pairs={{0,8},{4,12},{8,0},{12,4},{1,9},{5,13},{9,1},{13,5},{2,10},{6,14},... | collective-permute-start | bytes 57608 | tf_op jit(solution)/shard_map/ppermute | solution.py:17
  32.4 4.1 %collective-permute-start.15 = (f32[40,120]{1,0:T(8,128)S(1)}, f32[40,120]{1,0:T(8,128)S(1)}, u32[]{:S(2)}, u32[]{:S(2)}) collective-permute-start(f32[40,120]{1,0:T(8,128)S(1)} %get-tuple-element.54), channel_id=1, source_target_pairs={{0,4},{4,0},{8,12},{12,8},{1,5},{5,1},{9,13},{13,9},{2,6},{6,2},{1... | collective-permute-start | bytes 57608 | tf_op jit(solution)/shard_map/ppermute | solution.py:17
  36.6 4.4 %collective-permute-start.20 = (f32[40,80]{1,0:T(8,128)S(1)}, f32[40,80]{1,0:T(8,128)S(1)}, u32[]{:S(2)}, u32[]{:S(2)}) collective-permute-start(f32[40,80]{1,0:T(8,128)S(1)} %get-tuple-element.58), channel_id=1, source_target_pairs={{0,2},{1,3},{2,0},{3,1},{16,18},{17,19},{18,16},{19,17},{4,6},{5,7... | collective-permute-start | bytes 38408 | tf_op jit(solution)/shard_map/ppermute | solution.py:17
  38.3 4.7 %collective-permute-start.18 = (f32[40,80]{1,0:T(8,128)S(1)}, f32[40,80]{1,0:T(8,128)S(1)}, u32[]{:S(2)}, u32[]{:S(2)}) collective-permute-start(f32[40,80]{1,0:T(8,128)S(1)} %get-tuple-element.58), channel_id=1, source_target_pairs={{0,18},{1,19},{2,16},{3,17},{16,2},{17,3},{18,0},{19,1},{4,22},{5,... | collective-permute-start | bytes 38408 | tf_op jit(solution)/shard_map/ppermute | solution.py:17
  39.6 3.8 %collective-permute-start.19 = (f32[40,80]{1,0:T(8,128)S(1)}, f32[40,80]{1,0:T(8,128)S(1)}, u32[]{:S(2)}, u32[]{:S(2)}) collective-permute-start(f32[40,80]{1,0:T(8,128)S(1)} %get-tuple-element.59), channel_id=1, source_target_pairs={{0,16},{1,17},{2,18},{3,19},{16,0},{17,1},{18,2},{19,3},{4,20},{5,... | collective-permute-start | bytes 38408 | tf_op jit(solution)/shard_map/ppermute | solution.py:17

commit v12 on v11

--- a/solution.py
+++ b/solution.py
@@ -266,9 +266,6 @@
         lit += swaps(made[:parts], "light")[::-1]
         pieces.append(made[parts])
         carried = list(made[parts + 1 :])
-    back = call(
-        functools.partial(back_kernel, 2), [sds((size * lights, width), bf16)] * views, [], 0, pieces, lit[: parts - 1]
-    )
     spans = [(k, 0) for k in range(half)] + [(k, c * tall[0]) for c in range(2) for k in range(half, views)]
     wide = lights_all + views_all // 2
     both = max(lights_all, views_all)
@@ -279,6 +276,9 @@
         2 * views_all * lights * width * views_all,
         near + whole[0] + whole[1],
     )
+    back = call(
+        functools.partial(back_kernel, 2), [sds((size * lights, width), bf16)] * views, [], 0, pieces, lit[: parts - 1] + [view_part]
+    )
     returned = swaps(back, "view")
     keep, send = call(
         functools.partial(light_kernel, counts, 1, parts, light_scale),

time: 44.1 us -> 44.8 us (1.016)
  waiting for transfers between devices: 13.7 us -> 14.4 us
    ppermute x21, waiting for transfers between devices: 13.7 us -> 14.4 us  [swap(): lax.ppermute(value, axis, [(i, i ^ step) for i in range(lax.axis_size(axi...]
  transfers between devices with their start and end apart: 21 -> 21, of which waited for: 12 -> 11; matrix products, arithmetic and copies ran while one was open for 0% -> 0% of each run, Pallas kernels for 7% -> 7%
where the time goes in v12:
time: 44.8 us; the launch traced here: 44.7 us
  starting transfers between devices  24.4 us (54%)
  waiting for transfers between devices  14.4 us (32%)
  Pallas kernels  3.22 us (7%)
  local copies, waits for them, and re-layouts  1.79 us (4%)
  between operations  0.78 us (2%)
    ppermute x21, starting transfers between devices, swap(): lax.ppermute(value, axis, [(i, i ^ step) for i in range(lax.axis_size(axi...  24.4 us
    ppermute x21, waiting for transfers between devices, swap(): lax.ppermute(value, axis, [(i, i ^ step) for i in range(lax.axis_size(axi...  14.4 us
    pallas_call x12, Pallas kernels, call(): pl.pallas_call(kernel, out_shape=out_shape, in_specs=[VMEM] * len(args) +...  3.22 us
    unnamed x4, local copies, waits for them, and re-layouts  1.18 us
  transfers between devices with their start and end apart: 21, of which 11 were waited for; matrix products, arithmetic and copies ran while one was open for 0% of the time, Pallas kernels for 7%

profile of v12, /device:TPU:0, one launch (start us, length us, event | category | flops | bytes accessed | tf_op | source)
XLA Modules:
  0.0 44.7 jit_solution(5846825177219362403)
XLA Ops:
  0.6 0.0 copy-start
  0.6 0.0 copy-start.1
  0.7 1.2 %copy-done = bf16[20,20,1024]{2,1,0:T(8,128)(2,1)S(1)} copy-done((bf16[20,20,1024]{2,1,0:T(8,128)(2,1)S(1)}, bf16[20,20,1024]{2,1,0:T(8,128)(2,1)}, u32[]{:S(2)}) %copy-start) | copy-done | bytes 819224
  1.8 0.0 copy-done.1
  1.8 0.1 shard_map.50
  2.0 0.5 %collective-permute-start.2 = (bf16[416,256]{1,0:T(8,128)(2,1)S(1)}, bf16[416,256]{1,0:T(8,128)(2,1)S(1)}, u32[]{:S(2)}, u32[]{:S(2)}) collective-permute-start(bf16[416,256]{1,0:T(8,128)(2,1)S(1)} %get-tuple-element.34), channel_id=1, source_target_pairs={{0,1},{1,0},{2,3},{3,2},{4,5},{5,4},{6,7},{7,6},{8,9},{9,8},{10,11... | collective-permute-start | bytes 638984 | tf_op jit(solution)/shard_map/ppermute | solution.py:17
  2.5 2.6 %collective-permute-start = (bf16[176,256]{1,0:T(8,128)(2,1)S(1)}, bf16[176,256]{1,0:T(8,128)(2,1)S(1)}, u32[]{:S(2)}, u32[]{:S(2)}) collective-permute-start(bf16[176,256]{1,0:T(8,128)(2,1)S(1)} %get-tuple-element.32), channel_id=1, source_target_pairs={{0,3},{1,2},{2,1},{3,0},{4,7},{5,6},{6,5},{7,4},{8,11},{9,10},{10,... | collective-permute-start | bytes 270344 | tf_op jit(solution)/shard_map/ppermute | solution.py:17
  5.1 0.0 collective-permute-start.1
  5.2 2.9 %collective-permute-done.refs_0_.refs_3_ = bf16[176,256]{1,0:T(8,128)(2,1)S(1)} collective-permute-done((bf16[176,256]{1,0:T(8,128)(2,1)S(1)}, bf16[176,256]{1,0:T(8,128)(2,1)S(1)}, u32[]{:S(2)}, u32[]{:S(2)}) %collective-permute-start) | collective-permute-done | bytes 90144 | tf_op jit(solution)/shard_map/ppermute | solution.py:17
  8.1 2.0 %collective-permute-start.6 = (bf16[240,256]{1,0:T(8,128)(2,1)S(1)}, bf16[240,256]{1,0:T(8,128)(2,1)S(1)}, u32[]{:S(2)}, u32[]{:S(2)}) collective-permute-start(bf16[240,256]{1,0:T(8,128)(2,1)S(1)} %get-tuple-element.40), channel_id=1, source_target_pairs={{0,3},{1,2},{2,1},{3,0},{4,7},{5,6},{6,5},{7,4},{8,11},{9,10},{10,... | collective-permute-start | bytes 368648 | tf_op jit(solution)/shard_map/ppermute | solution.py:17
  10.1 0.0 collective-permute-start.7
  10.1 0.1 collective-permute-done.1.refs_1_.refs_2_
  10.2 0.0 collective-permute-done.2.refs_2_.refs_1_
  10.2 0.5 %shard_map.51 = (bf16[96,256]{1,0:T(8,128)(2,1)S(1)}, bf16[96,256]{1,0:T(8,128)(2,1)S(1)}, bf16[96,256]{1,0:T(8,128)(2,1)S(1)}, bf16[96,256]{1,0:T(8,128)(2,1)S(...) custom-call(bf16[176,256]{1,0:T(8,128)(2,1)S(1)} %collective-permute-done.refs_0_.refs_3_, ...), custom_call_target="tpu_custom_call" | custom-call | flops 15728640 | bytes 1007104 | tf_op jit(solution)/shard_map/pallas_call | solution.py:38
  10.7 4.1 %collective-permute-start.3 = (bf16[96,256]{1,0:T(8,128)(2,1)S(1)}, bf16[96,256]{1,0:T(8,128)(2,1)S(1)}, u32[]{:S(2)}, u32[]{:S(2)}) collective-permute-start(bf16[96,256]{1,0:T(8,128)(2,1)S(1)} %get-tuple-element.36), channel_id=1, source_target_pairs={{0,12},{4,8},{8,4},{12,0},{1,13},{5,9},{9,5},{13,1},{2,14},{6,10},... | collective-permute-start | bytes 147464 | tf_op jit(solution)/shard_map/ppermute | solution.py:17
  14.8 0.0 collective-permute-start.4
  14.8 0.6 %collective-permute-start.5 = (bf16[96,256]{1,0:T(8,128)(2,1)S(1)}, bf16[96,256]{1,0:T(8,128)(2,1)S(1)}, u32[]{:S(2)}, u32[]{:S(2)}) collective-permute-start(bf16[96,256]{1,0:T(8,128)(2,1)S(1)} %get-tuple-element.38), channel_id=1, source_target_pairs={{0,4},{4,0},{8,12},{12,8},{1,5},{5,1},{9,13},{13,9},{2,6},{6,2},{1... | collective-permute-start | bytes 147464 | tf_op jit(solution)/shard_map/ppermute | solution.py:17
  15.4 0.0 collective-permute-done.6.refs_0_.refs_5_
  15.4 1.2 %collective-permute-done.7.refs_1_.refs_4_ = bf16[240,256]{1,0:T(8,128)(2,1)S(1)} collective-permute-done((bf16[240,256]{1,0:T(8,128)(2,1)S(1)}, bf16[240,256]{1,0:T(8,128)(2,1)S(1)}, u32[]{:S(2)}, u32[]{:S(2)}) %collective-permute-start.7) | collective-permute-done | bytes 122912 | tf_op jit(solution)/shard_map/ppermute | solution.py:17
  16.6 0.5 %collective-permute-done.3.refs_5_.refs_2_.refs_0_ = bf16[96,256]{1,0:T(8,128)(2,1)S(1)} collective-permute-done((bf16[96,256]{1,0:T(8,128)(2,1)S(1)}, bf16[96,256]{1,0:T(8,128)(2,1)S(1)}, u32[]{:S(2)}, u32[]{:S(2)}) %collective-permute-start.3) | collective-permute-done | bytes 49184 | tf_op jit(solution)/shard_map/ppermute | solution.py:17
  17.1 0.5 %shard_map.53 = (bf16[144,256]{1,0:T(8,128)(2,1)S(1)}, bf16[144,256]{1,0:T(8,128)(2,1)S(1)}, bf16[144,256]{1,0:T(8,128)(2,1)S(1)}, bf16[144,256]{1,0:T(8,128)(2,1)S(1)}, bf16[4,144,256]{2,1,0:T(8,128)(2,1)S(1)}) custom-call(bf16[240,256]{1,0:T(8,128)(2,1)S(1)} %collective-permute-done.6.refs_0_.refs_5_, ...), custom_call_target="tpu_custom_call" | custom-call | flops 23592960 | bytes 1269248 | tf_op jit(solution)/shard_map/pallas_call | solution.py:38
  17.6 4.0 %collective-permute-start.8 = (bf16[144,256]{1,0:T(8,128)(2,1)S(1)}, bf16[144,256]{1,0:T(8,128)(2,1)S(1)}, u32[]{:S(2)}, u32[]{:S(2)}) collective-permute-start(bf16[144,256]{1,0:T(8,128)(2,1)S(1)} %get-tuple-element.43), channel_id=1, source_target_pairs={{0,12},{4,8},{8,4},{12,0},{1,13},{5,9},{9,5},{13,1},{2,14},{6,10},... | collective-permute-start | bytes 221192 | tf_op jit(solution)/shard_map/ppermute | solution.py:17
  21.6 0.6 %shard_map.54.refs_5_.refs_8_ = f32[2,80,120]{2,1,0:T(8,128)S(1)} custom-call(bf16[416,256]{1,0:T(8,128)(2,1)S(1)} %get-tuple-element.35.refs_3_.refs_0_, bf16[416,256]{1,0:T(8,128)(2,1)S(1)} %collective-permute-done.2.refs_2_.refs_1_, bf16[176,256]{1,0:T(8,128)(2,1)S(1)} %collective-permute-done.1.refs_1_.refs_2_, ...), custom_call_target="tpu_custom_call" | custom-call | flops 65536000 | bytes 928768 | tf_op jit(solution)/shard_map/pallas_call | solution.py:38
  22.1 0.0 collective-permute-done.4.refs_3_.refs_1_
  22.2 0.0 collective-permute-done.5.refs_4_.refs_2_
  22.2 0.1 collective-permute-start.11
  22.3 0.1 collective-permute-start.9
  22.4 0.6 %collective-permute-start.10 = (bf16[144,256]{1,0:T(8,128)(2,1)S(1)}, bf16[144,256]{1,0:T(8,128)(2,1)S(1)}, u32[]{:S(2)}, u32[]{:S(2)}) collective-permute-start(bf16[144,256]{1,0:T(8,128)(2,1)S(1)} %get-tuple-element.45), channel_id=1, source_target_pairs={{0,4},{4,0},{8,12},{12,8},{1,5},{5,1},{9,13},{13,9},{2,6},{6,2},{1... | collective-permute-start | bytes 221192 | tf_op jit(solution)/shard_map/ppermute | solution.py:17
  22.9 1.8 %collective-permute-start.16 = (bf16[240,256]{1,0:T(8,128)(2,1)S(1)}, bf16[240,256]{1,0:T(8,128)(2,1)S(1)}, u32[]{:S(2)}, u32[]{:S(2)}) collective-permute-start(bf16[240,256]{1,0:T(8,128)(2,1)S(1)} %get-tuple-element.56), channel_id=1, source_target_pairs={{0,2},{1,3},{2,0},{3,1},{4,6},{5,7},{6,4},{7,5},{8,10},{9,11},{10,... | collective-permute-start | bytes 368648 | tf_op jit(solution)/shard_map/ppermute | solution.py:17
  24.7 0.0 collective-permute-done.8.refs_4_
  24.7 0.0 collective-permute-start.17
  24.7 3.3 %collective-permute-done.9.refs_5_ = bf16[144,256]{1,0:T(8,128)(2,1)S(1)} collective-permute-done((bf16[144,256]{1,0:T(8,128)(2,1)S(1)}, bf16[144,256]{1,0:T(8,128)(2,1)S(1)}, u32[]{:S(2)}, u32[]{:S(2)}) %collective-permute-start.9) | collective-permute-done | bytes 73760 | tf_op jit(solution)/shard_map/ppermute | solution.py:17
  28.0 0.6 %collective-permute-done.10.refs_6_ = bf16[144,256]{1,0:T(8,128)(2,1)S(1)} collective-permute-done((bf16[144,256]{1,0:T(8,128)(2,1)S(1)}, bf16[144,256]{1,0:T(8,128)(2,1)S(1)}, u32[]{:S(2)}, u32[]{:S(2)}) %collective-permute-start.10) | collective-permute-done | bytes 73760 | tf_op jit(solution)/shard_map/ppermute | solution.py:17
  28.6 0.0 collective-permute-done.11.refs_9_.refs_1_
  28.6 0.3 shard_map.56
  28.9 0.1 collective-permute-start.12
  29.0 1.2 %collective-permute-done.12.came_ref = f32[80,120]{1,0:T(8,128)S(1)} collective-permute-done((f32[80,120]{1,0:T(8,128)S(1)}, f32[80,120]{1,0:T(8,128)S(1)}, u32[]{:S(2)}, u32[]{:S(2)}) %collective-permute-start.12) | collective-permute-done | bytes 38432 | tf_op jit(solution)/shard_map/ppermute | solution.py:17
  30.2 0.2 shard_map.57
  30.4 1.9 %collective-permute-start.13 = (f32[40,120]{1,0:T(8,128)S(1)}, f32[40,120]{1,0:T(8,128)S(1)}, u32[]{:S(2)}, u32[]{:S(2)}) collective-permute-start(f32[40,120]{1,0:T(8,128)S(1)} %get-tuple-element.52), channel_id=1, source_target_pairs={{0,12},{4,8},{8,4},{12,0},{1,13},{5,9},{9,5},{13,1},{2,14},{6,10},... | collective-permute-start | bytes 57608 | tf_op jit(solution)/shard_map/ppermute | solution.py:17
  32.3 0.2 collective-permute-start.14
  32.5 2.3 %collective-permute-start.15 = (f32[40,120]{1,0:T(8,128)S(1)}, f32[40,120]{1,0:T(8,128)S(1)}, u32[]{:S(2)}, u32[]{:S(2)}) collective-permute-start(f32[40,120]{1,0:T(8,128)S(1)} %get-tuple-element.54), channel_id=1, source_target_pairs={{0,4},{4,0},{8,12},{12,8},{1,5},{5,1},{9,13},{13,9},{2,6},{6,2},{1... | collective-permute-start | bytes 57608 | tf_op jit(solution)/shard_map/ppermute | solution.py:17
  34.8 1.3 %collective-permute-done.13.refs_0_ = f32[40,120]{1,0:T(8,128)S(1)} collective-permute-done((f32[40,120]{1,0:T(8,128)S(1)}, f32[40,120]{1,0:T(8,128)S(1)}, u32[]{:S(2)}, u32[]{:S(2)}) %collective-permute-start.13) | collective-permute-done | bytes 19232 | tf_op jit(solution)/shard_map/ppermute | solution.py:17
  36.1 0.9 %collective-permute-done.14.refs_1_ = f32[40,120]{1,0:T(8,128)S(1)} collective-permute-done((f32[40,120]{1,0:T(8,128)S(1)}, f32[40,120]{1,0:T(8,128)S(1)}, u32[]{:S(2)}, u32[]{:S(2)}) %collective-permute-start.14) | collective-permute-done | bytes 19232 | tf_op jit(solution)/shard_map/ppermute | solution.py:17
  37.0 0.0 collective-permute-done.15.refs_2_
  37.0 0.0 collective-permute-done.16.refs_1_.refs_2_
  37.0 0.0 collective-permute-done.17.refs_2_.refs_3_
  37.0 0.1 shard_map.59
  37.1 1.7 %collective-permute-start.20 = (f32[40,80]{1,0:T(8,128)S(1)}, f32[40,80]{1,0:T(8,128)S(1)}, u32[]{:S(2)}, u32[]{:S(2)}) collective-permute-start(f32[40,80]{1,0:T(8,128)S(1)} %get-tuple-element.58), channel_id=1, source_target_pairs={{0,2},{1,3},{2,0},{3,1},{16,18},{17,19},{18,16},{19,17},{4,6},{5,7... | collective-permute-start | bytes 38408 | tf_op jit(solution)/shard_map/ppermute | solution.py:17
  38.8 1.5 %collective-permute-start.18 = (f32[40,80]{1,0:T(8,128)S(1)}, f32[40,80]{1,0:T(8,128)S(1)}, u32[]{:S(2)}, u32[]{:S(2)}) collective-permute-start(f32[40,80]{1,0:T(8,128)S(1)} %get-tuple-element.58), channel_id=1, source_target_pairs={{0,18},{1,19},{2,16},{3,17},{16,2},{17,3},{18,0},{19,1},{4,22},{5,... | collective-permute-start | bytes 38408 | tf_op jit(solution)/shard_map/ppermute | solution.py:17
  40.3 0.3 collective-permute-start.19
  40.6 0.9 %shard_map.60 = bf16[12,20,1024]{2,1,0:T(8,128)(2,1)} custom-call(bf16[240,256]{1,0:T(8,128)(2,1)S(1)} %get-tuple-element.60.refs_0_, bf16[240,256]{1,0:T(8,128)(2,1)S(1)} %collective-permute-done.11.refs_9_.refs_1_, bf16[240,256]{1,0:T(8,128)(2,1)S(1)} %collective-permute-done.16.refs_1_.refs_2_, bf16[240,256]{1,0:T(8,128)(2,1)S(1)} %collective-permute-done.17.refs_2_.refs_3_), custom_call_target="tpu_custom_call" | custom-call | bytes 983040 | tf_op jit(solution)/shard_map/pallas_call | solution.py:38
  41.5 0.0 collective-permute-done.20
  41.5 2.0 %collective-permute-done.18 = f32[40,80]{1,0:T(8,128)S(1)} collective-permute-done((f32[40,80]{1,0:T(8,128)S(1)}, f32[40,80]{1,0:T(8,128)S(1)}, u32[]{:S(2)}, u32[]{:S(2)}) %collective-permute-start.18) | collective-permute-done | bytes 12832 | tf_op jit(solution)/shard_map/ppermute | solution.py:17
  43.5 0.6 %collective-permute-done.19 = f32[40,80]{1,0:T(8,128)S(1)} collective-permute-done((f32[40,80]{1,0:T(8,128)S(1)}, f32[40,80]{1,0:T(8,128)S(1)}, u32[]{:S(2)}, u32[]{:S(2)}) %collective-permute-start.19) | collective-permute-done | bytes 12832 | tf_op jit(solution)/shard_map/ppermute | solution.py:17
  44.1 0.6 %fusion = (f32[20,80]{1,0:T(8,128)}, f32[20,80]{1,0:T(8,128)}) fusion(f32[40,80]{1,0:T(8,128)S(1)} %add_add_fusion), kind=kLoop, calls=%fused_computation.1 | loop fusion | bytes 25600 | tf_op jit(solution)/shard_map/slice | solution.py:321
  (5 shorter events, 0.1 us)
Async XLA Ops:
  0.6 1.2 %copy-start = (bf16[20,20,1024]{2,1,0:T(8,128)(2,1)S(1)}, bf16[20,20,1024]{2,1,0:T(8,128)(2,1)}, u32[]{:S(2)}) copy-start(bf16[20,20,1024]{2,1,0:T(8,128)(2,1)} %slab_ref.3) | copy-start | bytes 2457604
  0.6 1.2 %copy-start.1 = (bf16[20,48]{1,0:T(8,128)(2,1)S(1)}, bf16[20,48]{1,0:T(8,128)(2,1)}, u32[]{:S(2)}) copy-start(bf16[20,48]{1,0:T(8,128)(2,1)} %refs_0_.1) | copy-start | bytes 5764
  2.0 8.3 %collective-permute-start.2 = (bf16[416,256]{1,0:T(8,128)(2,1)S(1)}, bf16[416,256]{1,0:T(8,128)(2,1)S(1)}, u32[]{:S(2)}, u32[]{:S(2)}) collective-permute-start(bf16[416,256]{1,0:T(8,128)(2,1)S(1)} %get-tuple-element.34), channel_id=1, source_target_pairs={{0,1},{1,0},{2,3},{3,2},{4,5},{5,4},{6,7},{7,6},{8,9},{9,8},{10,11... | collective-permute-start | bytes 638984 | tf_op jit(solution)/shard_map/ppermute | solution.py:17
  2.5 5.6 %collective-permute-start = (bf16[176,256]{1,0:T(8,128)(2,1)S(1)}, bf16[176,256]{1,0:T(8,128)(2,1)S(1)}, u32[]{:S(2)}, u32[]{:S(2)}) collective-permute-start(bf16[176,256]{1,0:T(8,128)(2,1)S(1)} %get-tuple-element.32), channel_id=1, source_target_pairs={{0,3},{1,2},{2,1},{3,0},{4,7},{5,6},{6,5},{7,4},{8,11},{9,10},{10,... | collective-permute-start | bytes 270344 | tf_op jit(solution)/shard_map/ppermute | solution.py:17
  5.1 5.1 %collective-permute-start.1 = (bf16[176,256]{1,0:T(8,128)(2,1)S(1)}, bf16[176,256]{1,0:T(8,128)(2,1)S(1)}, u32[]{:S(2)}, u32[]{:S(2)}) collective-permute-start(bf16[176,256]{1,0:T(8,128)(2,1)S(1)} %get-tuple-element.33), channel_id=1, source_target_pairs={{0,2},{1,3},{2,0},{3,1},{4,6},{5,7},{6,4},{7,5},{8,10},{9,11},{10,... | collective-permute-start | bytes 270344 | tf_op jit(solution)/shard_map/ppermute | solution.py:17
  8.1 7.3 %collective-permute-start.6 = (bf16[240,256]{1,0:T(8,128)(2,1)S(1)}, bf16[240,256]{1,0:T(8,128)(2,1)S(1)}, u32[]{:S(2)}, u32[]{:S(2)}) collective-permute-start(bf16[240,256]{1,0:T(8,128)(2,1)S(1)} %get-tuple-element.40), channel_id=1, source_target_pairs={{0,3},{1,2},{2,1},{3,0},{4,7},{5,6},{6,5},{7,4},{8,11},{9,10},{10,... | collective-permute-start | bytes 368648 | tf_op jit(solution)/shard_map/ppermute | solution.py:17
  10.1 6.5 %collective-permute-start.7 = (bf16[240,256]{1,0:T(8,128)(2,1)S(1)}, bf16[240,256]{1,0:T(8,128)(2,1)S(1)}, u32[]{:S(2)}, u32[]{:S(2)}) collective-permute-start(bf16[240,256]{1,0:T(8,128)(2,1)S(1)} %get-tuple-element.41), channel_id=1, source_target_pairs={{0,2},{1,3},{2,0},{3,1},{4,6},{5,7},{6,4},{7,5},{8,10},{9,11},{10,... | collective-permute-start | bytes 368648 | tf_op jit(solution)/shard_map/ppermute | solution.py:17
  10.7 6.4 %collective-permute-start.3 = (bf16[96,256]{1,0:T(8,128)(2,1)S(1)}, bf16[96,256]{1,0:T(8,128)(2,1)S(1)}, u32[]{:S(2)}, u32[]{:S(2)}) collective-permute-start(bf16[96,256]{1,0:T(8,128)(2,1)S(1)} %get-tuple-element.36), channel_id=1, source_target_pairs={{0,12},{4,8},{8,4},{12,0},{1,13},{5,9},{9,5},{13,1},{2,14},{6,10},... | collective-permute-start | bytes 147464 | tf_op jit(solution)/shard_map/ppermute | solution.py:17
  14.8 7.4 %collective-permute-start.4 = (bf16[96,256]{1,0:T(8,128)(2,1)S(1)}, bf16[96,256]{1,0:T(8,128)(2,1)S(1)}, u32[]{:S(2)}, u32[]{:S(2)}) collective-permute-start(bf16[96,256]{1,0:T(8,128)(2,1)S(1)} %get-tuple-element.37), channel_id=1, source_target_pairs={{0,8},{4,12},{8,0},{12,4},{1,9},{5,13},{9,1},{13,5},{2,10},{6,14},... | collective-permute-start | bytes 147464 | tf_op jit(solution)/shard_map/ppermute | solution.py:17
  14.8 7.4 %collective-permute-start.5 = (bf16[96,256]{1,0:T(8,128)(2,1)S(1)}, bf16[96,256]{1,0:T(8,128)(2,1)S(1)}, u32[]{:S(2)}, u32[]{:S(2)}) collective-permute-start(bf16[96,256]{1,0:T(8,128)(2,1)S(1)} %get-tuple-element.38), channel_id=1, source_target_pairs={{0,4},{4,0},{8,12},{12,8},{1,5},{5,1},{9,13},{13,9},{2,6},{6,2},{1... | collective-permute-start | bytes 147464 | tf_op jit(solution)/shard_map/ppermute | solution.py:17
  17.6 7.2 %collective-permute-start.8 = (bf16[144,256]{1,0:T(8,128)(2,1)S(1)}, bf16[144,256]{1,0:T(8,128)(2,1)S(1)}, u32[]{:S(2)}, u32[]{:S(2)}) collective-permute-start(bf16[144,256]{1,0:T(8,128)(2,1)S(1)} %get-tuple-element.43), channel_id=1, source_target_pairs={{0,12},{4,8},{8,4},{12,0},{1,13},{5,9},{9,5},{13,1},{2,14},{6,10},... | collective-permute-start | bytes 221192 | tf_op jit(solution)/shard_map/ppermute | solution.py:17
  22.2 6.3 %collective-permute-start.11 = (bf16[240,256]{1,0:T(8,128)(2,1)S(1)}, bf16[240,256]{1,0:T(8,128)(2,1)S(1)}, u32[]{:S(2)}, u32[]{:S(2)}) collective-permute-start(bf16[240,256]{1,0:T(8,128)(2,1)S(1)} %get-tuple-element.49), channel_id=1, source_target_pairs={{0,1},{1,0},{2,3},{3,2},{4,5},{5,4},{6,7},{7,6},{8,9},{9,8},{10,11... | collective-permute-start | bytes 368648 | tf_op jit(solution)/shard_map/ppermute | solution.py:17
  22.3 5.7 %collective-permute-start.9 = (bf16[144,256]{1,0:T(8,128)(2,1)S(1)}, bf16[144,256]{1,0:T(8,128)(2,1)S(1)}, u32[]{:S(2)}, u32[]{:S(2)}) collective-permute-start(bf16[144,256]{1,0:T(8,128)(2,1)S(1)} %get-tuple-element.44), channel_id=1, source_target_pairs={{0,8},{4,12},{8,0},{12,4},{1,9},{5,13},{9,1},{13,5},{2,10},{6,14},... | collective-permute-start | bytes 221192 | tf_op jit(solution)/shard_map/ppermute | solution.py:17
  22.4 6.2 %collective-permute-start.10 = (bf16[144,256]{1,0:T(8,128)(2,1)S(1)}, bf16[144,256]{1,0:T(8,128)(2,1)S(1)}, u32[]{:S(2)}, u32[]{:S(2)}) collective-permute-start(bf16[144,256]{1,0:T(8,128)(2,1)S(1)} %get-tuple-element.45), channel_id=1, source_target_pairs={{0,4},{4,0},{8,12},{12,8},{1,5},{5,1},{9,13},{13,9},{2,6},{6,2},{1... | collective-permute-start | bytes 221192 | tf_op jit(solution)/shard_map/ppermute | solution.py:17
  22.9 14.0 %collective-permute-start.16 = (bf16[240,256]{1,0:T(8,128)(2,1)S(1)}, bf16[240,256]{1,0:T(8,128)(2,1)S(1)}, u32[]{:S(2)}, u32[]{:S(2)}) collective-permute-start(bf16[240,256]{1,0:T(8,128)(2,1)S(1)} %get-tuple-element.56), channel_id=1, source_target_pairs={{0,2},{1,3},{2,0},{3,1},{4,6},{5,7},{6,4},{7,5},{8,10},{9,11},{10,... | collective-permute-start | bytes 368648 | tf_op jit(solution)/shard_map/ppermute | solution.py:17
  24.7 12.3 %collective-permute-start.17 = (bf16[240,256]{1,0:T(8,128)(2,1)S(1)}, bf16[240,256]{1,0:T(8,128)(2,1)S(1)}, u32[]{:S(2)}, u32[]{:S(2)}) collective-permute-start(bf16[240,256]{1,0:T(8,128)(2,1)S(1)} %get-tuple-element.57), channel_id=1, source_target_pairs={{0,3},{1,2},{2,1},{3,0},{4,7},{5,6},{6,5},{7,4},{8,11},{9,10},{10,... | collective-permute-start | bytes 368648 | tf_op jit(solution)/shard_map/ppermute | solution.py:17
  28.9 1.3 %collective-permute-start.12 = (f32[80,120]{1,0:T(8,128)S(1)}, f32[80,120]{1,0:T(8,128)S(1)}, u32[]{:S(2)}, u32[]{:S(2)}) collective-permute-start(f32[80,120]{1,0:T(8,128)S(1)} %get-tuple-element.51), channel_id=1, source_target_pairs={{0,1},{1,0},{2,3},{3,2},{4,5},{5,4},{6,7},{7,6},{8,9},{9,8},{10,11... | collective-permute-start | bytes 115208 | tf_op jit(solution)/shard_map/ppermute | solution.py:17
  30.4 5.7 %collective-permute-start.13 = (f32[40,120]{1,0:T(8,128)S(1)}, f32[40,120]{1,0:T(8,128)S(1)}, u32[]{:S(2)}, u32[]{:S(2)}) collective-permute-start(f32[40,120]{1,0:T(8,128)S(1)} %get-tuple-element.52), channel_id=1, source_target_pairs={{0,12},{4,8},{8,4},{12,0},{1,13},{5,9},{9,5},{13,1},{2,14},{6,10},... | collective-permute-start | bytes 57608 | tf_op jit(solution)/shard_map/ppermute | solution.py:17
  32.3 4.7 %collective-permute-start.14 = (f32[40,120]{1,0:T(8,128)S(1)}, f32[40,120]{1,0:T(8,128)S(1)}, u32[]{:S(2)}, u32[]{:S(2)}) collective-permute-start(f32[40,120]{1,0:T(8,128)S(1)} %get-tuple-element.53), channel_id=1, source_target_pairs={{0,8},{4,12},{8,0},{12,4},{1,9},{5,13},{9,1},{13,5},{2,10},{6,14},... | collective-permute-start | bytes 57608 | tf_op jit(solution)/shard_map/ppermute | solution.py:17
  32.5 4.5 %collective-permute-start.15 = (f32[40,120]{1,0:T(8,128)S(1)}, f32[40,120]{1,0:T(8,128)S(1)}, u32[]{:S(2)}, u32[]{:S(2)}) collective-permute-start(f32[40,120]{1,0:T(8,128)S(1)} %get-tuple-element.54), channel_id=1, source_target_pairs={{0,4},{4,0},{8,12},{12,8},{1,5},{5,1},{9,13},{13,9},{2,6},{6,2},{1... | collective-permute-start | bytes 57608 | tf_op jit(solution)/shard_map/ppermute | solution.py:17
  37.1 4.4 %collective-permute-start.20 = (f32[40,80]{1,0:T(8,128)S(1)}, f32[40,80]{1,0:T(8,128)S(1)}, u32[]{:S(2)}, u32[]{:S(2)}) collective-permute-start(f32[40,80]{1,0:T(8,128)S(1)} %get-tuple-element.58), channel_id=1, source_target_pairs={{0,2},{1,3},{2,0},{3,1},{16,18},{17,19},{18,16},{19,17},{4,6},{5,7... | collective-permute-start | bytes 38408 | tf_op jit(solution)/shard_map/ppermute | solution.py:17
  38.8 4.7 %collective-permute-start.18 = (f32[40,80]{1,0:T(8,128)S(1)}, f32[40,80]{1,0:T(8,128)S(1)}, u32[]{:S(2)}, u32[]{:S(2)}) collective-permute-start(f32[40,80]{1,0:T(8,128)S(1)} %get-tuple-element.58), channel_id=1, source_target_pairs={{0,18},{1,19},{2,16},{3,17},{16,2},{17,3},{18,0},{19,1},{4,22},{5,... | collective-permute-start | bytes 38408 | tf_op jit(solution)/shard_map/ppermute | solution.py:17
  40.3 3.8 %collective-permute-start.19 = (f32[40,80]{1,0:T(8,128)S(1)}, f32[40,80]{1,0:T(8,128)S(1)}, u32[]{:S(2)}, u32[]{:S(2)}) collective-permute-start(f32[40,80]{1,0:T(8,128)S(1)} %get-tuple-element.59), channel_id=1, source_target_pairs={{0,16},{1,17},{2,18},{3,19},{16,0},{17,1},{18,2},{19,3},{4,20},{5,... | collective-permute-start | bytes 38408 | tf_op jit(solution)/shard_map/ppermute | solution.py:17

commit v13 on v11

--- a/solution.py
+++ b/solution.py
@@ -310,7 +310,7 @@
     )
     steps = [(t, m) for t in range(min(2, texels) - 1, -1, -1) for m in range(half - 1, -1, -1)]
     came = [swap(dealt[m], ("texel", "view"), t * views + 2 * m) for t, m in steps[:-1]]
-    total = summed([dealt[0]] + came[::-1])
+    total = summed([dealt[0], *came[2:], *came[:2]])
     core = call(
         functools.partial(place_kernel, counts),
         sds((ranks // views, lights, columns), bf16),

time: 44.1 us -> 45.2 us (1.025)
  waiting for transfers between devices: 13.7 us -> 14.8 us
    ppermute x21, waiting for transfers between devices: 13.7 us -> 14.8 us  [swap(): lax.ppermute(value, axis, [(i, i ^ step) for i in range(lax.axis_size(axi...]
where the time goes in v13:
time: 45.2 us; the launch traced here: 45.1 us
  starting transfers between devices  24.5 us (54%)
  waiting for transfers between devices  14.8 us (33%)
  Pallas kernels  3.22 us (7%)
  local copies, waits for them, and re-layouts  1.79 us (4%)
  between operations  0.76 us (2%)
    ppermute x21, starting transfers between devices, swap(): lax.ppermute(value, axis, [(i, i ^ step) for i in range(lax.axis_size(axi...  24.5 us
    ppermute x21, waiting for transfers between devices, swap(): lax.ppermute(value, axis, [(i, i ^ step) for i in range(lax.axis_size(axi...  14.8 us
    pallas_call x12, Pallas kernels, call(): pl.pallas_call(kernel, out_shape=out_shape, in_specs=[VMEM] * len(args) +...  3.22 us
    unnamed x4, local copies, waits for them, and re-layouts  1.18 us
  transfers between devices with their start and end apart: 21, of which 12 were waited for; matrix products, arithmetic and copies ran while one was open for 0% of the time, Pallas kernels for 7%

profile of v13, /device:TPU:0, one launch (start us, length us, event | category | flops | bytes accessed | tf_op | source)
XLA Modules:
  0.0 45.1 jit_solution(3164612406910745120)
XLA Ops:
  0.6 0.0 copy-start
  0.6 0.0 copy-start.1
  0.7 1.2 %copy-done = bf16[20,20,1024]{2,1,0:T(8,128)(2,1)S(1)} copy-done((bf16[20,20,1024]{2,1,0:T(8,128)(2,1)S(1)}, bf16[20,20,1024]{2,1,0:T(8,128)(2,1)}, u32[]{:S(2)}) %copy-start) | copy-done | bytes 819224
  1.8 0.0 copy-done.1
  1.8 0.1 shard_map.50
  2.0 0.5 %collective-permute-start.2 = (bf16[416,256]{1,0:T(8,128)(2,1)S(1)}, bf16[416,256]{1,0:T(8,128)(2,1)S(1)}, u32[]{:S(2)}, u32[]{:S(2)}) collective-permute-start(bf16[416,256]{1,0:T(8,128)(2,1)S(1)} %get-tuple-element.34), channel_id=1, source_target_pairs={{0,1},{1,0},{2,3},{3,2},{4,5},{5,4},{6,7},{7,6},{8,9},{9,8},{10,11... | collective-permute-start | bytes 638984 | tf_op jit(solution)/shard_map/ppermute | solution.py:17
  2.5 2.6 %collective-permute-start = (bf16[176,256]{1,0:T(8,128)(2,1)S(1)}, bf16[176,256]{1,0:T(8,128)(2,1)S(1)}, u32[]{:S(2)}, u32[]{:S(2)}) collective-permute-start(bf16[176,256]{1,0:T(8,128)(2,1)S(1)} %get-tuple-element.32), channel_id=1, source_target_pairs={{0,3},{1,2},{2,1},{3,0},{4,7},{5,6},{6,5},{7,4},{8,11},{9,10},{10,... | collective-permute-start | bytes 270344 | tf_op jit(solution)/shard_map/ppermute | solution.py:17
  5.1 0.0 collective-permute-start.1
  5.2 2.9 %collective-permute-done.refs_0_.refs_3_ = bf16[176,256]{1,0:T(8,128)(2,1)S(1)} collective-permute-done((bf16[176,256]{1,0:T(8,128)(2,1)S(1)}, bf16[176,256]{1,0:T(8,128)(2,1)S(1)}, u32[]{:S(2)}, u32[]{:S(2)}) %collective-permute-start) | collective-permute-done | bytes 90144 | tf_op jit(solution)/shard_map/ppermute | solution.py:17
  8.1 2.0 %collective-permute-start.6 = (bf16[240,256]{1,0:T(8,128)(2,1)S(1)}, bf16[240,256]{1,0:T(8,128)(2,1)S(1)}, u32[]{:S(2)}, u32[]{:S(2)}) collective-permute-start(bf16[240,256]{1,0:T(8,128)(2,1)S(1)} %get-tuple-element.40), channel_id=1, source_target_pairs={{0,3},{1,2},{2,1},{3,0},{4,7},{5,6},{6,5},{7,4},{8,11},{9,10},{10,... | collective-permute-start | bytes 368648 | tf_op jit(solution)/shard_map/ppermute | solution.py:17
  10.1 0.0 collective-permute-start.7
  10.1 0.1 collective-permute-done.1.refs_1_.refs_2_
  10.2 0.0 collective-permute-done.2.refs_2_.refs_1_
  10.2 0.5 %shard_map.51 = (bf16[96,256]{1,0:T(8,128)(2,1)S(1)}, bf16[96,256]{1,0:T(8,128)(2,1)S(1)}, bf16[96,256]{1,0:T(8,128)(2,1)S(1)}, bf16[96,256]{1,0:T(8,128)(2,1)S(...) custom-call(bf16[176,256]{1,0:T(8,128)(2,1)S(1)} %collective-permute-done.refs_0_.refs_3_, ...), custom_call_target="tpu_custom_call" | custom-call | flops 15728640 | bytes 1007104 | tf_op jit(solution)/shard_map/pallas_call | solution.py:38
  10.7 4.1 %collective-permute-start.3 = (bf16[96,256]{1,0:T(8,128)(2,1)S(1)}, bf16[96,256]{1,0:T(8,128)(2,1)S(1)}, u32[]{:S(2)}, u32[]{:S(2)}) collective-permute-start(bf16[96,256]{1,0:T(8,128)(2,1)S(1)} %get-tuple-element.36), channel_id=1, source_target_pairs={{0,12},{4,8},{8,4},{12,0},{1,13},{5,9},{9,5},{13,1},{2,14},{6,10},... | collective-permute-start | bytes 147464 | tf_op jit(solution)/shard_map/ppermute | solution.py:17
  14.8 0.0 collective-permute-start.4
  14.8 0.6 %collective-permute-start.5 = (bf16[96,256]{1,0:T(8,128)(2,1)S(1)}, bf16[96,256]{1,0:T(8,128)(2,1)S(1)}, u32[]{:S(2)}, u32[]{:S(2)}) collective-permute-start(bf16[96,256]{1,0:T(8,128)(2,1)S(1)} %get-tuple-element.38), channel_id=1, source_target_pairs={{0,4},{4,0},{8,12},{12,8},{1,5},{5,1},{9,13},{13,9},{2,6},{6,2},{1... | collective-permute-start | bytes 147464 | tf_op jit(solution)/shard_map/ppermute | solution.py:17
  15.4 0.0 collective-permute-done.6.refs_0_.refs_5_
  15.4 1.2 %collective-permute-done.7.refs_1_.refs_4_ = bf16[240,256]{1,0:T(8,128)(2,1)S(1)} collective-permute-done((bf16[240,256]{1,0:T(8,128)(2,1)S(1)}, bf16[240,256]{1,0:T(8,128)(2,1)S(1)}, u32[]{:S(2)}, u32[]{:S(2)}) %collective-permute-start.7) | collective-permute-done | bytes 122912 | tf_op jit(solution)/shard_map/ppermute | solution.py:17
  16.6 0.5 %collective-permute-done.3.refs_5_.refs_2_.refs_0_ = bf16[96,256]{1,0:T(8,128)(2,1)S(1)} collective-permute-done((bf16[96,256]{1,0:T(8,128)(2,1)S(1)}, bf16[96,256]{1,0:T(8,128)(2,1)S(1)}, u32[]{:S(2)}, u32[]{:S(2)}) %collective-permute-start.3) | collective-permute-done | bytes 49184 | tf_op jit(solution)/shard_map/ppermute | solution.py:17
  17.1 0.5 %shard_map.53 = (bf16[144,256]{1,0:T(8,128)(2,1)S(1)}, bf16[144,256]{1,0:T(8,128)(2,1)S(1)}, bf16[144,256]{1,0:T(8,128)(2,1)S(1)}, bf16[144,256]{1,0:T(8,128)(2,1)S(1)}, bf16[4,144,256]{2,1,0:T(8,128)(2,1)S(1)}) custom-call(bf16[240,256]{1,0:T(8,128)(2,1)S(1)} %collective-permute-done.6.refs_0_.refs_5_, ...), custom_call_target="tpu_custom_call" | custom-call | flops 23592960 | bytes 1269248 | tf_op jit(solution)/shard_map/pallas_call | solution.py:38
  17.6 4.0 %collective-permute-start.8 = (bf16[144,256]{1,0:T(8,128)(2,1)S(1)}, bf16[144,256]{1,0:T(8,128)(2,1)S(1)}, u32[]{:S(2)}, u32[]{:S(2)}) collective-permute-start(bf16[144,256]{1,0:T(8,128)(2,1)S(1)} %get-tuple-element.43), channel_id=1, source_target_pairs={{0,12},{4,8},{8,4},{12,0},{1,13},{5,9},{9,5},{13,1},{2,14},{6,10},... | collective-permute-start | bytes 221192 | tf_op jit(solution)/shard_map/ppermute | solution.py:17
  21.6 0.0 collective-permute-done.4.refs_3_.refs_1_
  21.6 0.0 collective-permute-done.5.refs_4_.refs_2_
  21.6 0.1 collective-permute-start.11
  21.7 0.3 collective-permute-start.9
  22.0 0.5 %collective-permute-start.10 = (bf16[144,256]{1,0:T(8,128)(2,1)S(1)}, bf16[144,256]{1,0:T(8,128)(2,1)S(1)}, u32[]{:S(2)}, u32[]{:S(2)}) collective-permute-start(bf16[144,256]{1,0:T(8,128)(2,1)S(1)} %get-tuple-element.45), channel_id=1, source_target_pairs={{0,4},{4,0},{8,12},{12,8},{1,5},{5,1},{9,13},{13,9},{2,6},{6,2},{1... | collective-permute-start | bytes 221192 | tf_op jit(solution)/shard_map/ppermute | solution.py:17
  22.5 1.6 %collective-permute-start.16 = (bf16[240,256]{1,0:T(8,128)(2,1)S(1)}, bf16[240,256]{1,0:T(8,128)(2,1)S(1)}, u32[]{:S(2)}, u32[]{:S(2)}) collective-permute-start(bf16[240,256]{1,0:T(8,128)(2,1)S(1)} %get-tuple-element.56), channel_id=1, source_target_pairs={{0,2},{1,3},{2,0},{3,1},{4,6},{5,7},{6,4},{7,5},{8,10},{9,11},{10,... | collective-permute-start | bytes 368648 | tf_op jit(solution)/shard_map/ppermute | solution.py:17
  24.1 0.2 collective-permute-done.8.refs_4_
  24.3 0.0 collective-permute-start.17
  24.3 0.6 %shard_map.54.refs_8_ = f32[2,80,120]{2,1,0:T(8,128)S(1)} custom-call(bf16[416,256]{1,0:T(8,128)(2,1)S(1)} %get-tuple-element.35.refs_3_.refs_0_, bf16[416,256]{1,0:T(8,128)(2,1)S(1)} %collective-permute-done.2.refs_2_.refs_1_, bf16[176,256]{1,0:T(8,128)(2,1)S(1)} %collective-permute-done.1.refs_1_.refs_2_, ...), custom_call_target="tpu_custom_call" | custom-call | flops 65536000 | bytes 928768 | tf_op jit(solution)/shard_map/pallas_call | solution.py:38
  24.9 2.5 %collective-permute-done.9.refs_5_ = bf16[144,256]{1,0:T(8,128)(2,1)S(1)} collective-permute-done((bf16[144,256]{1,0:T(8,128)(2,1)S(1)}, bf16[144,256]{1,0:T(8,128)(2,1)S(1)}, u32[]{:S(2)}, u32[]{:S(2)}) %collective-permute-start.9) | collective-permute-done | bytes 73760 | tf_op jit(solution)/shard_map/ppermute | solution.py:17
  27.4 0.6 %collective-permute-done.10.refs_6_ = bf16[144,256]{1,0:T(8,128)(2,1)S(1)} collective-permute-done((bf16[144,256]{1,0:T(8,128)(2,1)S(1)}, bf16[144,256]{1,0:T(8,128)(2,1)S(1)}, u32[]{:S(2)}, u32[]{:S(2)}) %collective-permute-start.10) | collective-permute-done | bytes 73760 | tf_op jit(solution)/shard_map/ppermute | solution.py:17
  28.0 0.0 collective-permute-done.11.refs_9_.refs_1_
  28.0 0.3 shard_map.56
  28.3 0.1 collective-permute-start.12
  28.4 1.2 %collective-permute-done.12.came_ref = f32[80,120]{1,0:T(8,128)S(1)} collective-permute-done((f32[80,120]{1,0:T(8,128)S(1)}, f32[80,120]{1,0:T(8,128)S(1)}, u32[]{:S(2)}, u32[]{:S(2)}) %collective-permute-start.12) | collective-permute-done | bytes 38432 | tf_op jit(solution)/shard_map/ppermute | solution.py:17
  29.6 0.2 shard_map.57
  29.8 2.0 %collective-permute-start.13 = (f32[40,120]{1,0:T(8,128)S(1)}, f32[40,120]{1,0:T(8,128)S(1)}, u32[]{:S(2)}, u32[]{:S(2)}) collective-permute-start(f32[40,120]{1,0:T(8,128)S(1)} %get-tuple-element.52), channel_id=1, source_target_pairs={{0,12},{4,8},{8,4},{12,0},{1,13},{5,9},{9,5},{13,1},{2,14},{6,10},... | collective-permute-start | bytes 57608 | tf_op jit(solution)/shard_map/ppermute | solution.py:17
  31.8 0.6 %collective-permute-start.14 = (f32[40,120]{1,0:T(8,128)S(1)}, f32[40,120]{1,0:T(8,128)S(1)}, u32[]{:S(2)}, u32[]{:S(2)}) collective-permute-start(f32[40,120]{1,0:T(8,128)S(1)} %get-tuple-element.53), channel_id=1, source_target_pairs={{0,8},{4,12},{8,0},{12,4},{1,9},{5,13},{9,1},{13,5},{2,10},{6,14},... | collective-permute-start | bytes 57608 | tf_op jit(solution)/shard_map/ppermute | solution.py:17
  32.4 1.8 %collective-permute-start.15 = (f32[40,120]{1,0:T(8,128)S(1)}, f32[40,120]{1,0:T(8,128)S(1)}, u32[]{:S(2)}, u32[]{:S(2)}) collective-permute-start(f32[40,120]{1,0:T(8,128)S(1)} %get-tuple-element.54), channel_id=1, source_target_pairs={{0,4},{4,0},{8,12},{12,8},{1,5},{5,1},{9,13},{13,9},{2,6},{6,2},{1... | collective-permute-start | bytes 57608 | tf_op jit(solution)/shard_map/ppermute | solution.py:17
  34.2 1.3 %collective-permute-done.13.refs_0_ = f32[40,120]{1,0:T(8,128)S(1)} collective-permute-done((f32[40,120]{1,0:T(8,128)S(1)}, f32[40,120]{1,0:T(8,128)S(1)}, u32[]{:S(2)}, u32[]{:S(2)}) %collective-permute-start.13) | collective-permute-done | bytes 19232 | tf_op jit(solution)/shard_map/ppermute | solution.py:17
  35.5 1.0 %collective-permute-done.14.refs_1_ = f32[40,120]{1,0:T(8,128)S(1)} collective-permute-done((f32[40,120]{1,0:T(8,128)S(1)}, f32[40,120]{1,0:T(8,128)S(1)}, u32[]{:S(2)}, u32[]{:S(2)}) %collective-permute-start.14) | collective-permute-done | bytes 19232 | tf_op jit(solution)/shard_map/ppermute | solution.py:17
  36.5 0.0 collective-permute-done.15.refs_2_
  36.5 0.0 collective-permute-done.16.refs_1_.refs_2_
  36.5 0.0 collective-permute-done.17.refs_2_.refs_3_
  36.5 0.1 shard_map.59
  36.6 1.5 %collective-permute-start.18 = (f32[40,80]{1,0:T(8,128)S(1)}, f32[40,80]{1,0:T(8,128)S(1)}, u32[]{:S(2)}, u32[]{:S(2)}) collective-permute-start(f32[40,80]{1,0:T(8,128)S(1)} %get-tuple-element.58), channel_id=1, source_target_pairs={{0,16},{1,17},{2,18},{3,19},{16,0},{17,1},{18,2},{19,3},{4,20},{5,... | collective-permute-start | bytes 38408 | tf_op jit(solution)/shard_map/ppermute | solution.py:17
  38.1 1.6 %collective-permute-start.20 = (f32[40,80]{1,0:T(8,128)S(1)}, f32[40,80]{1,0:T(8,128)S(1)}, u32[]{:S(2)}, u32[]{:S(2)}) collective-permute-start(f32[40,80]{1,0:T(8,128)S(1)} %get-tuple-element.59), channel_id=1, source_target_pairs={{0,2},{1,3},{2,0},{3,1},{16,18},{17,19},{18,16},{19,17},{4,6},{5,7... | collective-permute-start | bytes 38408 | tf_op jit(solution)/shard_map/ppermute | solution.py:17
  39.8 0.4 collective-permute-start.19
  40.1 0.9 %shard_map.60 = bf16[12,20,1024]{2,1,0:T(8,128)(2,1)} custom-call(bf16[240,256]{1,0:T(8,128)(2,1)S(1)} %get-tuple-element.60.refs_0_, bf16[240,256]{1,0:T(8,128)(2,1)S(1)} %collective-permute-done.11.refs_9_.refs_1_, bf16[240,256]{1,0:T(8,128)(2,1)S(1)} %collective-permute-done.16.refs_1_.refs_2_, bf16[240,256]{1,0:T(8,128)(2,1)S(1)} %collective-permute-done.17.refs_2_.refs_3_), custom_call_target="tpu_custom_call" | custom-call | bytes 983040 | tf_op jit(solution)/shard_map/pallas_call | solution.py:38
  41.0 0.0 collective-permute-done.18
  41.0 1.1 %collective-permute-done.20 = f32[40,80]{1,0:T(8,128)S(1)} collective-permute-done((f32[40,80]{1,0:T(8,128)S(1)}, f32[40,80]{1,0:T(8,128)S(1)}, u32[]{:S(2)}, u32[]{:S(2)}) %collective-permute-start.20) | collective-permute-done | bytes 12832 | tf_op jit(solution)/shard_map/ppermute | solution.py:17
  42.1 2.3 %collective-permute-done.19 = f32[40,80]{1,0:T(8,128)S(1)} collective-permute-done((f32[40,80]{1,0:T(8,128)S(1)}, f32[40,80]{1,0:T(8,128)S(1)}, u32[]{:S(2)}, u32[]{:S(2)}) %collective-permute-start.19) | collective-permute-done | bytes 12832 | tf_op jit(solution)/shard_map/ppermute | solution.py:17
  44.5 0.6 %fusion = (f32[20,80]{1,0:T(8,128)}, f32[20,80]{1,0:T(8,128)}) fusion(f32[40,80]{1,0:T(8,128)S(1)} %add_add_fusion), kind=kLoop, calls=%fused_computation.1 | loop fusion | bytes 25600 | tf_op jit(solution)/shard_map/slice | solution.py:321
  (5 shorter events, 0.1 us)
Async XLA Ops:
  0.6 1.2 %copy-start = (bf16[20,20,1024]{2,1,0:T(8,128)(2,1)S(1)}, bf16[20,20,1024]{2,1,0:T(8,128)(2,1)}, u32[]{:S(2)}) copy-start(bf16[20,20,1024]{2,1,0:T(8,128)(2,1)} %slab_ref.3) | copy-start | bytes 2457604
  0.6 1.2 %copy-start.1 = (bf16[20,48]{1,0:T(8,128)(2,1)S(1)}, bf16[20,48]{1,0:T(8,128)(2,1)}, u32[]{:S(2)}) copy-start(bf16[20,48]{1,0:T(8,128)(2,1)} %refs_0_.1) | copy-start | bytes 5764
  2.0 8.3 %collective-permute-start.2 = (bf16[416,256]{1,0:T(8,128)(2,1)S(1)}, bf16[416,256]{1,0:T(8,128)(2,1)S(1)}, u32[]{:S(2)}, u32[]{:S(2)}) collective-permute-start(bf16[416,256]{1,0:T(8,128)(2,1)S(1)} %get-tuple-element.34), channel_id=1, source_target_pairs={{0,1},{1,0},{2,3},{3,2},{4,5},{5,4},{6,7},{7,6},{8,9},{9,8},{10,11... | collective-permute-start | bytes 638984 | tf_op jit(solution)/shard_map/ppermute | solution.py:17
  2.5 5.6 %collective-permute-start = (bf16[176,256]{1,0:T(8,128)(2,1)S(1)}, bf16[176,256]{1,0:T(8,128)(2,1)S(1)}, u32[]{:S(2)}, u32[]{:S(2)}) collective-permute-start(bf16[176,256]{1,0:T(8,128)(2,1)S(1)} %get-tuple-element.32), channel_id=1, source_target_pairs={{0,3},{1,2},{2,1},{3,0},{4,7},{5,6},{6,5},{7,4},{8,11},{9,10},{10,... | collective-permute-start | bytes 270344 | tf_op jit(solution)/shard_map/ppermute | solution.py:17
  5.1 5.1 %collective-permute-start.1 = (bf16[176,256]{1,0:T(8,128)(2,1)S(1)}, bf16[176,256]{1,0:T(8,128)(2,1)S(1)}, u32[]{:S(2)}, u32[]{:S(2)}) collective-permute-start(bf16[176,256]{1,0:T(8,128)(2,1)S(1)} %get-tuple-element.33), channel_id=1, source_target_pairs={{0,2},{1,3},{2,0},{3,1},{4,6},{5,7},{6,4},{7,5},{8,10},{9,11},{10,... | collective-permute-start | bytes 270344 | tf_op jit(solution)/shard_map/ppermute | solution.py:17
  8.1 7.3 %collective-permute-start.6 = (bf16[240,256]{1,0:T(8,128)(2,1)S(1)}, bf16[240,256]{1,0:T(8,128)(2,1)S(1)}, u32[]{:S(2)}, u32[]{:S(2)}) collective-permute-start(bf16[240,256]{1,0:T(8,128)(2,1)S(1)} %get-tuple-element.40), channel_id=1, source_target_pairs={{0,3},{1,2},{2,1},{3,0},{4,7},{5,6},{6,5},{7,4},{8,11},{9,10},{10,... | collective-permute-start | bytes 368648 | tf_op jit(solution)/shard_map/ppermute | solution.py:17
  10.1 6.5 %collective-permute-start.7 = (bf16[240,256]{1,0:T(8,128)(2,1)S(1)}, bf16[240,256]{1,0:T(8,128)(2,1)S(1)}, u32[]{:S(2)}, u32[]{:S(2)}) collective-permute-start(bf16[240,256]{1,0:T(8,128)(2,1)S(1)} %get-tuple-element.41), channel_id=1, source_target_pairs={{0,2},{1,3},{2,0},{3,1},{4,6},{5,7},{6,4},{7,5},{8,10},{9,11},{10,... | collective-permute-start | bytes 368648 | tf_op jit(solution)/shard_map/ppermute | solution.py:17
  10.7 6.4 %collective-permute-start.3 = (bf16[96,256]{1,0:T(8,128)(2,1)S(1)}, bf16[96,256]{1,0:T(8,128)(2,1)S(1)}, u32[]{:S(2)}, u32[]{:S(2)}) collective-permute-start(bf16[96,256]{1,0:T(8,128)(2,1)S(1)} %get-tuple-element.36), channel_id=1, source_target_pairs={{0,12},{4,8},{8,4},{12,0},{1,13},{5,9},{9,5},{13,1},{2,14},{6,10},... | collective-permute-start | bytes 147464 | tf_op jit(solution)/shard_map/ppermute | solution.py:17
  14.8 6.8 %collective-permute-start.4 = (bf16[96,256]{1,0:T(8,128)(2,1)S(1)}, bf16[96,256]{1,0:T(8,128)(2,1)S(1)}, u32[]{:S(2)}, u32[]{:S(2)}) collective-permute-start(bf16[96,256]{1,0:T(8,128)(2,1)S(1)} %get-tuple-element.37), channel_id=1, source_target_pairs={{0,8},{4,12},{8,0},{12,4},{1,9},{5,13},{9,1},{13,5},{2,10},{6,14},... | collective-permute-start | bytes 147464 | tf_op jit(solution)/shard_map/ppermute | solution.py:17
  14.8 6.8 %collective-permute-start.5 = (bf16[96,256]{1,0:T(8,128)(2,1)S(1)}, bf16[96,256]{1,0:T(8,128)(2,1)S(1)}, u32[]{:S(2)}, u32[]{:S(2)}) collective-permute-start(bf16[96,256]{1,0:T(8,128)(2,1)S(1)} %get-tuple-element.38), channel_id=1, source_target_pairs={{0,4},{4,0},{8,12},{12,8},{1,5},{5,1},{9,13},{13,9},{2,6},{6,2},{1... | collective-permute-start | bytes 147464 | tf_op jit(solution)/shard_map/ppermute | solution.py:17
  17.6 6.7 %collective-permute-start.8 = (bf16[144,256]{1,0:T(8,128)(2,1)S(1)}, bf16[144,256]{1,0:T(8,128)(2,1)S(1)}, u32[]{:S(2)}, u32[]{:S(2)}) collective-permute-start(bf16[144,256]{1,0:T(8,128)(2,1)S(1)} %get-tuple-element.43), channel_id=1, source_target_pairs={{0,12},{4,8},{8,4},{12,0},{1,13},{5,9},{9,5},{13,1},{2,14},{6,10},... | collective-permute-start | bytes 221192 | tf_op jit(solution)/shard_map/ppermute | solution.py:17
  21.6 6.3 %collective-permute-start.11 = (bf16[240,256]{1,0:T(8,128)(2,1)S(1)}, bf16[240,256]{1,0:T(8,128)(2,1)S(1)}, u32[]{:S(2)}, u32[]{:S(2)}) collective-permute-start(bf16[240,256]{1,0:T(8,128)(2,1)S(1)} %get-tuple-element.49), channel_id=1, source_target_pairs={{0,1},{1,0},{2,3},{3,2},{4,5},{5,4},{6,7},{7,6},{8,9},{9,8},{10,11... | collective-permute-start | bytes 368648 | tf_op jit(solution)/shard_map/ppermute | solution.py:17
  21.7 5.7 %collective-permute-start.9 = (bf16[144,256]{1,0:T(8,128)(2,1)S(1)}, bf16[144,256]{1,0:T(8,128)(2,1)S(1)}, u32[]{:S(2)}, u32[]{:S(2)}) collective-permute-start(bf16[144,256]{1,0:T(8,128)(2,1)S(1)} %get-tuple-element.44), channel_id=1, source_target_pairs={{0,8},{4,12},{8,0},{12,4},{1,9},{5,13},{9,1},{13,5},{2,10},{6,14},... | collective-permute-start | bytes 221192 | tf_op jit(solution)/shard_map/ppermute | solution.py:17
  22.0 6.0 %collective-permute-start.10 = (bf16[144,256]{1,0:T(8,128)(2,1)S(1)}, bf16[144,256]{1,0:T(8,128)(2,1)S(1)}, u32[]{:S(2)}, u32[]{:S(2)}) collective-permute-start(bf16[144,256]{1,0:T(8,128)(2,1)S(1)} %get-tuple-element.45), channel_id=1, source_target_pairs={{0,4},{4,0},{8,12},{12,8},{1,5},{5,1},{9,13},{13,9},{2,6},{6,2},{1... | collective-permute-start | bytes 221192 | tf_op jit(solution)/shard_map/ppermute | solution.py:17
  22.5 14.0 %collective-permute-start.16 = (bf16[240,256]{1,0:T(8,128)(2,1)S(1)}, bf16[240,256]{1,0:T(8,128)(2,1)S(1)}, u32[]{:S(2)}, u32[]{:S(2)}) collective-permute-start(bf16[240,256]{1,0:T(8,128)(2,1)S(1)} %get-tuple-element.56), channel_id=1, source_target_pairs={{0,2},{1,3},{2,0},{3,1},{4,6},{5,7},{6,4},{7,5},{8,10},{9,11},{10,... | collective-permute-start | bytes 368648 | tf_op jit(solution)/shard_map/ppermute | solution.py:17
  24.3 12.2 %collective-permute-start.17 = (bf16[240,256]{1,0:T(8,128)(2,1)S(1)}, bf16[240,256]{1,0:T(8,128)(2,1)S(1)}, u32[]{:S(2)}, u32[]{:S(2)}) collective-permute-start(bf16[240,256]{1,0:T(8,128)(2,1)S(1)} %get-tuple-element.57), channel_id=1, source_target_pairs={{0,3},{1,2},{2,1},{3,0},{4,7},{5,6},{6,5},{7,4},{8,11},{9,10},{10,... | collective-permute-start | bytes 368648 | tf_op jit(solution)/shard_map/ppermute | solution.py:17
  28.3 1.3 %collective-permute-start.12 = (f32[80,120]{1,0:T(8,128)S(1)}, f32[80,120]{1,0:T(8,128)S(1)}, u32[]{:S(2)}, u32[]{:S(2)}) collective-permute-start(f32[80,120]{1,0:T(8,128)S(1)} %get-tuple-element.51), channel_id=1, source_target_pairs={{0,1},{1,0},{2,3},{3,2},{4,5},{5,4},{6,7},{7,6},{8,9},{9,8},{10,11... | collective-permute-start | bytes 115208 | tf_op jit(solution)/shard_map/ppermute | solution.py:17
  29.8 5.7 %collective-permute-start.13 = (f32[40,120]{1,0:T(8,128)S(1)}, f32[40,120]{1,0:T(8,128)S(1)}, u32[]{:S(2)}, u32[]{:S(2)}) collective-permute-start(f32[40,120]{1,0:T(8,128)S(1)} %get-tuple-element.52), channel_id=1, source_target_pairs={{0,12},{4,8},{8,4},{12,0},{1,13},{5,9},{9,5},{13,1},{2,14},{6,10},... | collective-permute-start | bytes 57608 | tf_op jit(solution)/shard_map/ppermute | solution.py:17
  31.8 4.7 %collective-permute-start.14 = (f32[40,120]{1,0:T(8,128)S(1)}, f32[40,120]{1,0:T(8,128)S(1)}, u32[]{:S(2)}, u32[]{:S(2)}) collective-permute-start(f32[40,120]{1,0:T(8,128)S(1)} %get-tuple-element.53), channel_id=1, source_target_pairs={{0,8},{4,12},{8,0},{12,4},{1,9},{5,13},{9,1},{13,5},{2,10},{6,14},... | collective-permute-start | bytes 57608 | tf_op jit(solution)/shard_map/ppermute | solution.py:17
  32.4 4.1 %collective-permute-start.15 = (f32[40,120]{1,0:T(8,128)S(1)}, f32[40,120]{1,0:T(8,128)S(1)}, u32[]{:S(2)}, u32[]{:S(2)}) collective-permute-start(f32[40,120]{1,0:T(8,128)S(1)} %get-tuple-element.54), channel_id=1, source_target_pairs={{0,4},{4,0},{8,12},{12,8},{1,5},{5,1},{9,13},{13,9},{2,6},{6,2},{1... | collective-permute-start | bytes 57608 | tf_op jit(solution)/shard_map/ppermute | solution.py:17
  36.6 4.4 %collective-permute-start.18 = (f32[40,80]{1,0:T(8,128)S(1)}, f32[40,80]{1,0:T(8,128)S(1)}, u32[]{:S(2)}, u32[]{:S(2)}) collective-permute-start(f32[40,80]{1,0:T(8,128)S(1)} %get-tuple-element.58), channel_id=1, source_target_pairs={{0,16},{1,17},{2,18},{3,19},{16,0},{17,1},{18,2},{19,3},{4,20},{5,... | collective-permute-start | bytes 38408 | tf_op jit(solution)/shard_map/ppermute | solution.py:17
  38.1 4.0 %collective-permute-start.20 = (f32[40,80]{1,0:T(8,128)S(1)}, f32[40,80]{1,0:T(8,128)S(1)}, u32[]{:S(2)}, u32[]{:S(2)}) collective-permute-start(f32[40,80]{1,0:T(8,128)S(1)} %get-tuple-element.59), channel_id=1, source_target_pairs={{0,2},{1,3},{2,0},{3,1},{16,18},{17,19},{18,16},{19,17},{4,6},{5,7... | collective-permute-start | bytes 38408 | tf_op jit(solution)/shard_map/ppermute | solution.py:17
  39.8 4.7 %collective-permute-start.19 = (f32[40,80]{1,0:T(8,128)S(1)}, f32[40,80]{1,0:T(8,128)S(1)}, u32[]{:S(2)}, u32[]{:S(2)}) collective-permute-start(f32[40,80]{1,0:T(8,128)S(1)} %get-tuple-element.59), channel_id=1, source_target_pairs={{0,18},{1,19},{2,16},{3,17},{16,2},{17,3},{18,0},{19,1},{4,22},{5,... | collective-permute-start | bytes 38408 | tf_op jit(solution)/shard_map/ppermute | solution.py:17
